TPU v7x, 32 devices: a whole 2x2x4 slice. The times are simulated.
32 devices in a mesh: row: 4 (over z), col: 8 (over y, x, core).
Axes of the slice: x: 2, y: 2, z: 4, core: 2. Of those that a mesh axis runs over, the one named last changes fastest.
Arguments:
- activations: bfloat16 [256, 28672], P('row', 'col'), may hold values from -0.375 to 0.375
- cotangent: bfloat16 [256, 16384], P('col', 'row'), may hold values from -6 to 6
- down_weight: bfloat16 [28672, 16384], P('col', 'row'), may hold values from -0.046875 to 0.046875
- row_order: int32 [256], replicated, may hold values from 0 to 255, each once
Outputs:
- weight_grad: bfloat16 [28672, 16384], P('col', 'row')
- input_grad: bfloat16 [256, 28672], P('row', 'col')
Inputs may be any that keep to these rules, and one draw needn't show every extreme that they name: `row_order`: each of the 256 rows is named exactly once.
All inputs are finite; a program needn't handle non-finite values.
Results may differ from a plain program's by a relative error of at most 0.001.
Values may be sent and summed in bfloat16 or wider, within the bound.
No kernel may reach another device: no remote copies, remote signals or barrier semaphores. Data moves between devices by JAX's collectives and lax.ppermute only.
A program may use at most 128 MiB of HBM per device.

v0:
```python
import jax
import jax.numpy as jnp
from jax import lax
from jax.sharding import PartitionSpec as P


def contract_rows(left, right):
    return lax.dot_general(
        left, right, (((0,), (0,)), ((), ())), preferred_element_type=jnp.float32
    )


def contract_cols(left, right):
    return lax.dot_general(
        left, right, (((1,), (1,)), ((), ())), preferred_element_type=jnp.float32
    )


def body(activations, cotangent, down_weight, row_order):
    gathered = lax.all_gather(cotangent, "col", axis=0, tiled=True)
    aligned = jnp.take(gathered, row_order, axis=0)
    all_rows = lax.all_gather(activations, "row", axis=0, tiled=True)
    weight_total = contract_rows(all_rows, aligned)
    weight_grad = weight_total.astype(jnp.bfloat16)
    partial_sums = contract_cols(aligned, down_weight)
    summed = lax.psum_scatter(partial_sums, "row", scatter_dimension=0, tiled=True)
    input_grad = summed.astype(jnp.bfloat16)
    return (weight_grad, input_grad)


def solution(mesh):
    in_specs = (P("row", "col"), P("col", "row"), P("col", "row"), P())
    out_specs = (P("col", "row"), P("row", "col"))
    return jax.shard_map(body, mesh=mesh, in_specs=in_specs, out_specs=out_specs, check_vma=False)
```

profile of v0, /device:TPU:0, one launch (start us, length us, event | category | flops | bytes accessed | tf_op | source)
XLA Modules:
  0.0 161.7 jit_solution(7355669282448734595)
XLA Ops:
  7.2 0.0 all-gather.3.cloned.1.call-start
  7.2 0.7 all-gather.3.cloned.1.call-update
  7.9 0.0 all-gather.5.cloned.1.call-start
  7.9 0.7 all-gather.5.cloned.1.call-update
  8.6 0.0 reduce-scatter.2.cloned.1.call-start
  8.7 0.7 compare_select_fusion
  9.4 0.7 compare_and_fusion
  10.1 30.4 %all-gather.3.cloned.1.call-done = bf16[256,4096]{1,0:T(8,128)(2,1)} async-done(((bf16[32,4096]{1,0:T(8,128)(2,1)}), bf16[256,4096]{1,0:T(8,128)(2,1)}) %all-gather.3.cloned.1.call-update) | async-done | bytes 2097168 | tf_op jit(solution)/shard_map/all_gather | solution.py:20
  40.5 5.7 %gather_fusion = bf16[256,4096]{1,0:T(8,128)(2,1)S(1)} fusion(bf16[256,4096]{1,0:T(8,128)(2,1)} %all-gather.3.cloned.1.call-done, s32[1024]{0:T(1024)S(1)} %pad_clamp_fusion), kind=kCustom, calls=%fused_computation | custom fusion | bytes 4195328 | tf_op jit(solution)/shard_map/jit(_take)/gather | solution.py:21
  46.3 15.8 %fusion.1 = f32[256,3584]{1,0:T(8,128)} fusion(bf16[3584,4096]{1,0:T(8,128)(2,1)} %param.6, bf16[256,4096]{1,0:T(8,128)(2,1)S(1)} %gather_fusion, pred[256]{0:T(512)(128)(4,1)S(1)} %compare_and_fusion), kind=kOutput, calls=%fused_computation.4 | convolution fusion | flops 7517241344 | bytes 35127552 | tf_op jit(solution)/shard_map/dot_general | solution.py:14
  62.1 0.0 reduce-scatter.2.cloned.1.call-update
  62.1 21.4 %all-gather.5.cloned.1.call-done = bf16[256,3584]{1,0:T(8,128)(2,1)} async-done(((bf16[64,3584]{1,0:T(8,128)(2,1)}), bf16[256,3584]{1,0:T(8,128)(2,1)}) %all-gather.5.cloned.1.call-update) | async-done | bytes 1835024 | tf_op jit(solution)/shard_map/all_gather | solution.py:22
  83.5 14.3 %fusion = bf16[3584,4096]{0,1:T(8,128)(2,1)} fusion(bf16[256,3584]{1,0:T(8,128)(2,1)} %all-gather.5.cloned.1.call-done, bf16[256,4096]{1,0:T(8,128)(2,1)S(1)} %gather_fusion, pred[256]{0:T(512)(128)(4,1)S(1)} %compare_and_fusion), kind=kOutput, calls=%fused_computation.2 | convolution fusion | flops 7531921408 | bytes 33292544 | tf_op jit(solution)/shard_map/dot_general | solution.py:8
  97.8 39.6 %copy.6 = bf16[3584,4096]{1,0:T(8,128)(2,1)} copy(bf16[3584,4096]{0,1:T(8,128)(2,1)} %fusion) | data formatting | bytes 58720256
  137.4 15.7 %reduce-scatter.2.cloned.1.call-done = f32[64,3584]{1,0:T(8,128)} async-done(((f32[256,3584]{1,0:T(8,128)}), f32[64,3584]{1,0:T(8,128)}) %reduce-scatter.2.cloned.1.call-update) | async-done | bytes 917520 | tf_op jit(solution)/shard_map/reduce_scatter | solution.py:26
  153.1 2.0 %convert_element_type.11 = bf16[64,3584]{1,0:T(8,128)(2,1)} convert(f32[64,3584]{1,0:T(8,128)} %reduce-scatter.2.cloned.1.call-done) | non-fusion elementwise | flops 229376 | bytes 1376256 | tf_op jit(solution)/shard_map/convert_element_type | solution.py:27
  (1 shorter events, 0.0 us)
Async XLA Ops:
  7.2 33.4 %all-gather.3.cloned.1.call-start = ((), (), s32[]{:S(2)}) async-start(), calls=%async_computation.1 | async-start | bytes 2359296 | tf_op jit(solution)/shard_map/all_gather | solution.py:20
  7.9 75.6 %all-gather.5.cloned.1.call-start = ((), (), s32[]{:S(2)}) async-start(), calls=%async_computation.2 | async-start | bytes 2293760 | tf_op jit(solution)/shard_map/all_gather | solution.py:22
  8.6 144.5 %reduce-scatter.2.cloned.1.call-start = ((), (), s32[]{:S(2)}) async-start(), calls=%async_computation.3 | async-start | bytes 4587520 | tf_op jit(solution)/shard_map/reduce_scatter | solution.py:26
Sparse Core Ops, SparseCore 0:
  9.9 30.5 all-gather.2
  42.1 41.3 all-gather.4
  85.8 67.2 reduce-scatter.1
where the time goes:
time: 163 us; the launch traced here: 162 us
  waiting for transfers between devices  69 us (42%)
  local copies, waits for them, and re-layouts  45.4 us (28%)
  matrix products  30.1 us (18%)
  between operations  13.8 us (8%)
  other arithmetic  3.37 us (2%)
    unnamed x1, local copies, waits for them, and re-layouts  39.6 us
    all_gather x1, waiting for transfers between devices, body(): gathered = lax.all_gather(cotangent, 'col', axis=0, tiled=True)  30.4 us
    all_gather x1, waiting for transfers between devices, body(): all_rows = lax.all_gather(activations, 'row', axis=0, tiled=True)  21.4 us
    dot_general x1, matrix products, contract_cols(): lax.dot_general(left, right, (((1,), (1,)), ((), ())), preferred_element_...  15.8 us
    reduce_scatter x1, waiting for transfers between devices, body(): lax.psum_scatter(partial_sums, 'row', scatter_dimension=0, tiled=True)  15.7 us
    dot_general x1, matrix products, contract_rows(): lax.dot_general(left, right, (((0,), (0,)), ((), ())), preferred_element_...  14.3 us
    gather x1, local copies, waits for them, and re-layouts, body(): aligned = jnp.take(gathered, row_order, axis=0)  5.74 us
  transfers between devices with their start and end apart: 3, of which 3 were waited for; matrix products, arithmetic and copies ran while one was open for 48% of the time, Pallas kernels for 0%

commit v1 on v0

v1 whole, which is shorter than its diff:
```python
import functools

import jax
import jax.numpy as jnp
from jax import lax
from jax.experimental import pallas as pl
from jax.experimental.pallas import tpu as pltpu
from jax.sharding import PartitionSpec as P

LANES = 128
STEPS_PER_OCTAVE = 128.0
TOP = 32766.0
LEAST = 2.0 ** -120
VMEM_LIMIT = 50 * 1024 * 1024


def tile_of(size, largest):
    tile = largest
    while size % tile:
        tile //= 2
    return tile


def dot(left, right, dims):
    return lax.dot_general(left, right, (dims, ((), ())), preferred_element_type=jnp.float32)


def encode(values):
    most = jnp.maximum(jnp.max(jnp.abs(values), axis=1, keepdims=True), LEAST)
    level = jnp.ceil(jnp.log2(most) * STEPS_PER_OCTAVE) + 1.0
    codes = jnp.round(values * jnp.exp2(level * (-1.0 / STEPS_PER_OCTAVE)) * TOP)
    return codes.astype(jnp.int32).astype(jnp.int16), level


def decode(codes, levels):
    scale = jnp.exp2(levels.astype(jnp.int32).astype(jnp.float32) * (1.0 / STEPS_PER_OCTAVE)) * (1.0 / TOP)
    return codes.astype(jnp.int32).astype(jnp.float32) * scale


def partial_kernel(n_pieces, n_groups, tile, *refs):
    pick_ref, weight_ref = refs[:2]
    pieces = refs[2:2 + n_pieces]
    aligned_ref, own_ref = refs[2 + n_pieces:4 + n_pieces]
    sent = refs[4 + n_pieces:3 + n_pieces + n_groups]
    levels_ref = refs[-1]
    step = pl.program_id(0)
    rows = own_ref.shape[0]
    width = sent[0].shape[1] - LANES
    depth = aligned_ref.shape[1]

    @pl.when(step == 0)
    def _():
        chunk = tile_of(depth, 512)
        for at in range(0, depth, chunk):
            cols = slice(at, at + chunk)
            gathered = jnp.concatenate([piece[:, cols] for piece in pieces], axis=0)
            aligned_ref[:, cols] = dot(pick_ref[...], gathered, ((1,), (0,))).astype(jnp.bfloat16)
        levels_ref[...] = jnp.zeros_like(levels_ref)

    sums = dot(aligned_ref[...], weight_ref[...], ((1,), (1,)))
    own_ref[...] = sums[:rows]
    codes, level = encode(sums[rows:])
    here = lax.broadcasted_iota(jnp.int32, levels_ref.shape, 1) == step
    levels_ref[...] = jnp.where(here, level, levels_ref[...])
    cols = pl.ds(pl.multiple_of(step * tile, tile), tile)
    for at, ref in enumerate(sent):
        ref[:, cols] = codes[at * rows:(at + 1) * rows]

    @pl.when(step == pl.num_programs(0) - 1)
    def _():
        for at, ref in enumerate(sent):
            ref[:, width:] = levels_ref[at * rows:(at + 1) * rows].astype(jnp.int32).astype(jnp.int16)


def partial_sums(pick, weight, pieces, n_groups):
    hidden, depth = weight.shape
    total = pick.shape[0]
    rows = total // n_groups
    tile = tile_of(hidden, 256)
    whole = lambda i: (0, 0)
    return pl.pallas_call(
        functools.partial(partial_kernel, len(pieces), n_groups, tile),
        grid=(hidden // tile,),
        in_specs=[
            pl.BlockSpec(pick.shape, whole),
            pl.BlockSpec((tile, depth), lambda i: (i, 0)),
        ] + [pl.BlockSpec(piece.shape, whole) for piece in pieces],
        out_specs=[
            pl.BlockSpec((total, depth), whole),
            pl.BlockSpec((rows, tile), lambda i: (0, i)),
        ] + [pl.BlockSpec((rows, hidden + LANES), whole)] * (n_groups - 1),
        out_shape=[
            jax.ShapeDtypeStruct((total, depth), jnp.bfloat16),
            jax.ShapeDtypeStruct((rows, hidden), jnp.float32),
        ] + [jax.ShapeDtypeStruct((rows, hidden + LANES), jnp.int16)] * (n_groups - 1),
        scratch_shapes=[pltpu.VMEM((total - rows, LANES), jnp.float32)],
        compiler_params=pltpu.CompilerParams(vmem_limit_bytes=VMEM_LIMIT),
        cost_estimate=pl.CostEstimate(
            flops=2 * total * hidden * depth, bytes_accessed=2 * hidden * depth + 6 * total * depth, transcendentals=0),
        name="partial_sums",
    )(pick, weight, *pieces)


def weight_kernel(n_groups, *refs):
    aligned_ref = refs[0]
    pieces = refs[1:1 + n_groups]
    out_ref = refs[-1]
    left = jnp.concatenate([piece[...] for piece in pieces], axis=0)
    depth = out_ref.shape[1]
    chunk = tile_of(depth, 1024)
    for at in range(0, depth, chunk):
        cols = slice(at, at + chunk)
        out_ref[:, cols] = dot(left, aligned_ref[:, cols], ((0,), (0,))).astype(jnp.bfloat16)


def weight_grads(aligned, pieces):
    total, depth = aligned.shape
    rows, hidden = pieces[0].shape
    tile = tile_of(hidden, 256)
    return pl.pallas_call(
        functools.partial(weight_kernel, len(pieces)),
        grid=(hidden // tile,),
        in_specs=[pl.BlockSpec((total, depth), lambda i: (0, 0))]
        + [pl.BlockSpec((rows, tile), lambda i: (0, i))] * len(pieces),
        out_specs=pl.BlockSpec((tile, depth), lambda i: (i, 0)),
        out_shape=jax.ShapeDtypeStruct((hidden, depth), jnp.bfloat16),
        compiler_params=pltpu.CompilerParams(vmem_limit_bytes=VMEM_LIMIT),
        cost_estimate=pl.CostEstimate(
            flops=2 * total * hidden * depth, bytes_accessed=2 * hidden * depth + 2 * total * (depth + hidden), transcendentals=0),
        name="weight_grads",
    )(aligned, *pieces)


def total_kernel(tile, own_ref, *refs):
    received, out_ref = refs[:-1], refs[-1]
    width = own_ref.shape[1]
    for at in range(width // tile):
        cols = slice(at * tile, (at + 1) * tile)
        total = own_ref[:, cols]
        for ref in received:
            total = total + decode(ref[:, cols], ref[:, width:][:, at:at + 1])
        out_ref[:, cols] = total.astype(jnp.bfloat16)


def totals(own, received):
    rows, hidden = own.shape
    return pl.pallas_call(
        functools.partial(total_kernel, tile_of(hidden, 256)),
        out_shape=jax.ShapeDtypeStruct((rows, hidden), jnp.bfloat16),
        compiler_params=pltpu.CompilerParams(vmem_limit_bytes=VMEM_LIMIT),
        cost_estimate=pl.CostEstimate(
            flops=rows * hidden * 8, bytes_accessed=rows * hidden * (6 + 2 * len(received)), transcendentals=0),
        name="totals",
    )(own, *received)


def gather_cotangent(cotangent, n_col):
    pieces, owners = [cotangent], [0]
    for flip in range(2, n_col, 2):
        pieces.append(lax.ppermute(cotangent, "col", [(i, i ^ flip) for i in range(n_col)]))
        owners.append(flip)
    swap = [(i, i ^ 1) for i in range(n_col)]
    pieces += [lax.ppermute(piece, "col", swap) for piece in pieces]
    owners += [flip ^ 1 for flip in owners]
    return pieces, owners


def gather_activations(activations, n_row):
    last = n_row - 1
    pieces = [activations]
    for o in range(1, n_row):
        pairs = [((i + o) % n_row, i) for i in range(n_row)]
        pairs = [pair for pair in pairs if abs(pair[0] - pair[1]) < max(last, 2)]
        pieces.append(lax.ppermute(activations, "row", pairs))
    if last >= 3:
        me = lax.axis_index("row")
        held = pieces[2] if n_row == 4 else jnp.where(me == 1, pieces[n_row - 2], pieces[2])
        far = lax.ppermute(held, "row", [(1, 0), (last - 1, last)])
        pieces[last] = jnp.where(me == 0, far, pieces[last])
        pieces[1] = jnp.where(me == last, far, pieces[1])
    return pieces


def body(n_row, n_col, activations, cotangent, down_weight, row_order):
    rows = activations.shape[0]
    shard = cotangent.shape[0]
    mine_row, mine_col = lax.axis_index("row"), lax.axis_index("col")

    cot_pieces, owners = gather_cotangent(cotangent, n_col)
    act_pieces = gather_activations(activations, n_row)

    order = row_order.reshape(n_row, rows)
    order = jnp.roll(order, -mine_row, axis=0).reshape(n_row * rows)
    owner = mine_col ^ jnp.asarray(owners, jnp.int32)
    named = (owner[:, None] * shard + jnp.arange(shard, dtype=jnp.int32)[None, :]).reshape(-1)
    pick = (order[:, None] == named[None, :]).astype(jnp.bfloat16)

    aligned, own, *sent = partial_sums(pick, down_weight, cot_pieces, n_row)
    received = [
        lax.ppermute(message, "row", [(i, (i + o) % n_row) for i in range(n_row)])
        for o, message in enumerate(sent, 1)
    ]
    weight_grad = weight_grads(aligned, act_pieces)
    input_grad = totals(own, received)
    return weight_grad, input_grad


def solution(mesh):
    in_specs = (P("row", "col"), P("col", "row"), P("col", "row"), P())
    out_specs = (P("col", "row"), P("row", "col"))
    fn = functools.partial(body, mesh.shape["row"], mesh.shape["col"])
    return jax.shard_map(fn, mesh=mesh, in_specs=in_specs, out_specs=out_specs, check_vma=False)
```

time: 163 us -> 100 us (0.61)
  the two profiles are of different devices: /device:TPU:0 before, /device:TPU:11 now
where the time goes in v1:
time: 100 us; the launch traced here: 99.5 us
  Pallas kernels  37.5 us (38%)
  waiting for transfers between devices  37.2 us (37%)
  starting transfers between devices  19.7 us (20%)
  local copies, waits for them, and re-layouts  3.47 us (3%)
    ppermute x3, waiting for transfers between devices, body(): lax.ppermute(message, 'row', [(i, (i + o) % n_row) for i in range(n_row)])  24 us
    pallas_call x1, Pallas kernels, partial_sums(): pl.pallas_call(functools.partial(partial_kernel, len(pieces), n_groups, t...  21 us
    pallas_call x1, Pallas kernels, weight_grads(): pl.pallas_call(functools.partial(weight_kernel, len(pieces)), grid=(hidde...  15.2 us
    ppermute x3, waiting for transfers between devices, gather_activations(): pieces.append(lax.ppermute(activations, 'row', pairs))  8.88 us
    ppermute x3, starting transfers between devices, gather_activations(): pieces.append(lax.ppermute(activations, 'row', pairs))  6.3 us
    ppermute x4, starting transfers between devices, gather_cotangent(): pieces += [lax.ppermute(piece, 'col', swap) for piece in pieces]  4.8 us
    ppermute x3, waiting for transfers between devices, gather_cotangent(): lax.ppermute(cotangent, 'col', [(i, i ^ flip) for i in range(n_col)])  4.28 us
    ppermute x1, starting transfers between devices, gather_activations(): far = lax.ppermute(held, 'row', [(1, 0), (last - 1, last)])  3.41 us
  transfers between devices with their start and end apart: 14, of which 5 were waited for; matrix products, arithmetic and copies ran while one was open for 2% of the time, Pallas kernels for 36%

profile of v1, /device:TPU:11, one launch (start us, length us, event | category | flops | bytes accessed | tf_op | source)
XLA Modules:
  0.0 99.5 jit_solution(12768066357430189667)
XLA Ops:
  0.6 1.3 %collective-permute-start.2 = (bf16[32,4096]{1,0:T(8,128)(2,1)}, bf16[32,4096]{1,0:T(8,128)(2,1)S(1)}, u32[]{:S(2)}, u32[]{:S(2)}) collective-permute-start(bf16[32,4096]{1,0:T(8,128)(2,1)} %refs_2_.1), channel_id=1, source_target_pairs={{0,6},{1,7},{2,4},{3,5},{4,2},{5,3},{6,0},{7,1},{8,14},{9,15},{10,... | collective-permute-start | bytes 786440 | tf_op jit(solution)/shard_map/ppermute | solution.py:160
  1.9 0.2 collective-permute-start.1
  2.1 1.2 %collective-permute-start = (bf16[32,4096]{1,0:T(8,128)(2,1)}, bf16[32,4096]{1,0:T(8,128)(2,1)S(1)}, u32[]{:S(2)}, u32[]{:S(2)}) collective-permute-start(bf16[32,4096]{1,0:T(8,128)(2,1)} %refs_2_.1), channel_id=1, source_target_pairs={{0,2},{1,3},{2,0},{3,1},{4,6},{5,7},{6,4},{7,5},{8,10},{9,11},{10,... | collective-permute-start | bytes 786440 | tf_op jit(solution)/shard_map/ppermute | solution.py:160
  3.4 1.5 %collective-permute-start.3 = (bf16[32,4096]{1,0:T(8,128)(2,1)}, bf16[32,4096]{1,0:T(8,128)(2,1)S(1)}, u32[]{:S(2)}, u32[]{:S(2)}) collective-permute-start(bf16[32,4096]{1,0:T(8,128)(2,1)} %refs_2_.1), channel_id=1, source_target_pairs={{0,1},{1,0},{2,3},{3,2},{4,5},{5,4},{6,7},{7,6},{8,9},{9,8},{10,11... | collective-permute-start | bytes 786440 | tf_op jit(solution)/shard_map/ppermute | solution.py:163
  4.9 2.3 %collective-permute-start.7 = (bf16[64,3584]{1,0:T(8,128)(2,1)}, bf16[64,3584]{1,0:T(8,128)(2,1)S(1)}, u32[]{:S(2)}, u32[]{:S(2)}) collective-permute-start(bf16[64,3584]{1,0:T(8,128)(2,1)} %refs_1_.3), channel_id=1, source_target_pairs={{16,0},{24,8},{0,16},{8,24},{17,1},{25,9},{1,17},{9,25},{18,2},{26... | collective-permute-start | bytes 1376264 | tf_op jit(solution)/shard_map/ppermute | solution.py:174
  7.2 0.7 xor_multiply_fusion
  7.8 0.1 iota_add_fusion
  7.9 0.8 reshape.24
  8.7 0.3 collective-permute-done.2.refs_5_
  9.0 2.7 %collective-permute-start.6 = (bf16[32,4096]{1,0:T(8,128)(2,1)S(1)}, bf16[32,4096]{1,0:T(8,128)(2,1)S(1)}, u32[]{:S(2)}, u32[]{:S(2)}) collective-permute-start(bf16[32,4096]{1,0:T(8,128)(2,1)S(1)} %collective-permute-done.2.refs_5_), channel_id=1, source_target_pairs={{0,1},{1,0},{2,3},{3,2},{4,5},{5,4},{6,7},{7,6},{8,9},{9,8},{10,11... | collective-permute-start | bytes 786440 | tf_op jit(solution)/shard_map/ppermute | solution.py:163
  11.7 3.9 %collective-permute-done.1.refs_4_ = bf16[32,4096]{1,0:T(8,128)(2,1)S(1)} collective-permute-done((bf16[32,4096]{1,0:T(8,128)(2,1)}, bf16[32,4096]{1,0:T(8,128)(2,1)S(1)}, u32[]{:S(2)}, u32[]{:S(2)}) %collective-permute-start.1) | collective-permute-done | bytes 262176 | tf_op jit(solution)/shard_map/ppermute | solution.py:160
  15.7 0.5 collective-permute-start.5
  16.2 0.1 collective-permute-start.4
  16.3 0.1 eq.24
  16.3 0.1 add.35
  16.4 0.1 compare_convert_fusion.refs_0_
  16.5 2.1 %collective-permute-start.9 = (bf16[64,3584]{1,0:T(8,128)(2,1)}, bf16[64,3584]{1,0:T(8,128)(2,1)S(1)}, u32[]{:S(2)}, u32[]{:S(2)}) collective-permute-start(bf16[64,3584]{1,0:T(8,128)(2,1)} %refs_1_.3), channel_id=1, source_target_pairs={{8,0},{16,8},{24,16},{9,1},{17,9},{25,17},{10,2},{18,10},{26,18},{... | collective-permute-start | bytes 1376264 | tf_op jit(solution)/shard_map/ppermute | solution.py:174
  18.6 8.9 %collective-permute-done.7.refs_3_ = bf16[64,3584]{1,0:T(8,128)(2,1)S(1)} collective-permute-done((bf16[64,3584]{1,0:T(8,128)(2,1)}, bf16[64,3584]{1,0:T(8,128)(2,1)S(1)}, u32[]{:S(2)}, u32[]{:S(2)}) %collective-permute-start.7) | collective-permute-done | bytes 458784 | tf_op jit(solution)/shard_map/ppermute | solution.py:174
  27.5 1.9 %collective-permute-start.10 = (bf16[64,3584]{1,0:T(8,128)(2,1)}, bf16[64,3584]{1,0:T(8,128)(2,1)S(1)}, u32[]{:S(2)}, u32[]{:S(2)}) collective-permute-start(bf16[64,3584]{1,0:T(8,128)(2,1)} %refs_1_.3), channel_id=1, source_target_pairs={{0,8},{8,16},{16,24},{1,9},{9,17},{17,25},{2,10},{10,18},{18,26},{... | collective-permute-start | bytes 1376264 | tf_op jit(solution)/shard_map/ppermute | solution.py:174
  29.4 3.4 %collective-permute-start.8 = (bf16[64,3584]{1,0:T(8,128)(2,1)S(1)}, bf16[64,3584]{1,0:T(8,128)(2,1)S(1)}, u32[]{:S(2)}, u32[]{:S(2)}) collective-permute-start(bf16[64,3584]{1,0:T(8,128)(2,1)S(1)} %collective-permute-done.7.refs_3_), channel_id=1, source_target_pairs={{8,0},{16,24},{9,1},{17,25},{10,2},{18,26},{11,3},{19,27},{12,4},{... | collective-permute-start | bytes 1376264 | tf_op jit(solution)/shard_map/ppermute | solution.py:178
  32.9 0.0 copy-start.3
  32.9 0.9 copy-done.3
  33.8 21.0 %partial_sums.1 = (bf16[256,4096]{1,0:T(8,128)(2,1)}, f32[64,3584]{1,0:T(8,128)}, s16[64,3712]{1,0:T(8,128)(2,1)S(1)}, s16[64,3712]{1,0:T(8,128)(2,1)S(1)}, s16[64,3712]{1,0:T(8,128)(2,1)S(1)}) custom-call(bf16[256,256]{1,0:T(8,128)(2,1)S(1)} %compare_convert_fusion.refs_0_, bf16[3584,4096]{1,0:T(8,128)(2,1)} %refs_1_.2, bf16[32,4096]{1,0:T(8,128)(2,1)S(1)} %copy-done.3, ...), custom_call_target="tpu_custom_call" | custom-call | flops 7516192768 | bytes 35651584 | tf_op jit(solution)/shard_map/partial_sums/pallas_call | solution.py:81
  54.8 1.2 %collective-permute-start.11 = (s16[64,3712]{1,0:T(8,128)(2,1)S(1)}, s16[64,3712]{1,0:T(8,128)(2,1)S(1)}, u32[]{:S(2)}, u32[]{:S(2)}) collective-permute-start(s16[64,3712]{1,0:T(8,128)(2,1)S(1)} %get-tuple-element.9), channel_id=1, source_target_pairs={{0,8},{8,16},{16,24},{24,0},{1,9},{9,17},{17,25},{25,1},{2,10},{10... | collective-permute-start | bytes 1425416 | tf_op jit(solution)/shard_map/ppermute | solution.py:200
  56.0 0.3 collective-permute-start.12
  56.3 1.0 collective-permute-start.13
  57.3 0.1 broadcast_select_fusion
  57.4 1.6 %copy-done = bf16[256,4096]{1,0:T(8,128)(2,1)S(1)} copy-done((bf16[256,4096]{1,0:T(8,128)(2,1)S(1)}, bf16[256,4096]{1,0:T(8,128)(2,1)}, u32[]{:S(2)}) %copy-start) | copy-done | bytes 2097176
  58.9 15.2 %weight_grads.1 = bf16[3584,4096]{1,0:T(8,128)(2,1)} custom-call(bf16[256,4096]{1,0:T(8,128)(2,1)S(1)} %copy-done, bf16[64,3584]{1,0:T(8,128)(2,1)S(1)} %copy-done.2, bf16[64,3584]{1,0:T(8,128)(2,1)S(1)} %get-tuple-element.13.refs_2_, bf16[64,3584]{1,0:T(8,128)(2,1)S(1)} %collective-permute-done.7.refs_3_, bf16[64,3584]{1,0:T(8,128)(2,1)S(1)} %get-tuple-element.12.refs_4_), custom_call_target="tpu_custom_call" | custom-call | flops 7516192768 | bytes 33292288 | tf_op jit(solution)/shard_map/weight_grads/pallas_call | solution.py:120
  74.2 21.9 %collective-permute-done.12.refs_1_ = s16[64,3712]{1,0:T(8,128)(2,1)S(1)} collective-permute-done((s16[64,3712]{1,0:T(8,128)(2,1)S(1)}, s16[64,3712]{1,0:T(8,128)(2,1)S(1)}, u32[]{:S(2)}, u32[]{:S(2)}) %collective-permute-start.12) | collective-permute-done | bytes 475168 | tf_op jit(solution)/shard_map/ppermute | solution.py:200
  96.0 2.2 %collective-permute-done.13.refs_2_ = s16[64,3712]{1,0:T(8,128)(2,1)S(1)} collective-permute-done((s16[64,3712]{1,0:T(8,128)(2,1)S(1)}, s16[64,3712]{1,0:T(8,128)(2,1)S(1)}, u32[]{:S(2)}, u32[]{:S(2)}) %collective-permute-start.13) | collective-permute-done | bytes 475168 | tf_op jit(solution)/shard_map/ppermute | solution.py:200
  98.2 1.3 %totals.1 = bf16[64,3584]{1,0:T(8,128)(2,1)} custom-call(f32[64,3584]{1,0:T(8,128)S(1)} %copy-done.1, s16[64,3712]{1,0:T(8,128)(2,1)S(1)} %collective-permute-done.11.refs_0_, s16[64,3712]{1,0:T(8,128)(2,1)S(1)} %collective-permute-done.12.refs_1_, s16[64,3712]{1,0:T(8,128)(2,1)S(1)} %collective-permute-done.13.refs_2_), custom_call_target="tpu_custom_call" | custom-call | flops 1835008 | bytes 2752512 | tf_op jit(solution)/shard_map/totals/pallas_call | solution.py:147
  (16 shorter events, 0.1 us)
Async XLA Ops:
  0.6 56.7 %copy-start.2 = (bf16[64,3584]{1,0:T(8,128)(2,1)S(1)}, bf16[64,3584]{1,0:T(8,128)(2,1)}, u32[]{:S(2)}) copy-start(bf16[64,3584]{1,0:T(8,128)(2,1)} %refs_1_.3) | copy-start | bytes 1376260
  0.6 8.4 %collective-permute-start.2 = (bf16[32,4096]{1,0:T(8,128)(2,1)}, bf16[32,4096]{1,0:T(8,128)(2,1)S(1)}, u32[]{:S(2)}, u32[]{:S(2)}) collective-permute-start(bf16[32,4096]{1,0:T(8,128)(2,1)} %refs_2_.1), channel_id=1, source_target_pairs={{0,6},{1,7},{2,4},{3,5},{4,2},{5,3},{6,0},{7,1},{8,14},{9,15},{10,... | collective-permute-start | bytes 786440 | tf_op jit(solution)/shard_map/ppermute | solution.py:160
  1.9 13.7 %collective-permute-start.1 = (bf16[32,4096]{1,0:T(8,128)(2,1)}, bf16[32,4096]{1,0:T(8,128)(2,1)S(1)}, u32[]{:S(2)}, u32[]{:S(2)}) collective-permute-start(bf16[32,4096]{1,0:T(8,128)(2,1)} %refs_2_.1), channel_id=1, source_target_pairs={{0,4},{1,5},{2,6},{3,7},{4,0},{5,1},{6,2},{7,3},{8,12},{9,13},{10,... | collective-permute-start | bytes 786440 | tf_op jit(solution)/shard_map/ppermute | solution.py:160
  2.1 14.0 %collective-permute-start = (bf16[32,4096]{1,0:T(8,128)(2,1)}, bf16[32,4096]{1,0:T(8,128)(2,1)S(1)}, u32[]{:S(2)}, u32[]{:S(2)}) collective-permute-start(bf16[32,4096]{1,0:T(8,128)(2,1)} %refs_2_.1), channel_id=1, source_target_pairs={{0,2},{1,3},{2,0},{3,1},{4,6},{5,7},{6,4},{7,5},{8,10},{9,11},{10,... | collective-permute-start | bytes 786440 | tf_op jit(solution)/shard_map/ppermute | solution.py:160
  3.4 13.2 %collective-permute-start.3 = (bf16[32,4096]{1,0:T(8,128)(2,1)}, bf16[32,4096]{1,0:T(8,128)(2,1)S(1)}, u32[]{:S(2)}, u32[]{:S(2)}) collective-permute-start(bf16[32,4096]{1,0:T(8,128)(2,1)} %refs_2_.1), channel_id=1, source_target_pairs={{0,1},{1,0},{2,3},{3,2},{4,5},{5,4},{6,7},{7,6},{8,9},{9,8},{10,11... | collective-permute-start | bytes 786440 | tf_op jit(solution)/shard_map/ppermute | solution.py:163
  4.9 22.6 %collective-permute-start.7 = (bf16[64,3584]{1,0:T(8,128)(2,1)}, bf16[64,3584]{1,0:T(8,128)(2,1)S(1)}, u32[]{:S(2)}, u32[]{:S(2)}) collective-permute-start(bf16[64,3584]{1,0:T(8,128)(2,1)} %refs_1_.3), channel_id=1, source_target_pairs={{16,0},{24,8},{0,16},{8,24},{17,1},{25,9},{1,17},{9,25},{18,2},{26... | collective-permute-start | bytes 1376264 | tf_op jit(solution)/shard_map/ppermute | solution.py:174
  9.0 20.4 %collective-permute-start.6 = (bf16[32,4096]{1,0:T(8,128)(2,1)S(1)}, bf16[32,4096]{1,0:T(8,128)(2,1)S(1)}, u32[]{:S(2)}, u32[]{:S(2)}) collective-permute-start(bf16[32,4096]{1,0:T(8,128)(2,1)S(1)} %collective-permute-done.2.refs_5_), channel_id=1, source_target_pairs={{0,1},{1,0},{2,3},{3,2},{4,5},{5,4},{6,7},{7,6},{8,9},{9,8},{10,11... | collective-permute-start | bytes 786440 | tf_op jit(solution)/shard_map/ppermute | solution.py:163
  15.7 17.2 %collective-permute-start.5 = (bf16[32,4096]{1,0:T(8,128)(2,1)S(1)}, bf16[32,4096]{1,0:T(8,128)(2,1)S(1)}, u32[]{:S(2)}, u32[]{:S(2)}) collective-permute-start(bf16[32,4096]{1,0:T(8,128)(2,1)S(1)} %collective-permute-done.1.refs_4_), channel_id=1, source_target_pairs={{0,1},{1,0},{2,3},{3,2},{4,5},{5,4},{6,7},{7,6},{8,9},{9,8},{10,11... | collective-permute-start | bytes 786440 | tf_op jit(solution)/shard_map/ppermute | solution.py:163
  16.2 16.7 %collective-permute-start.4 = (bf16[32,4096]{1,0:T(8,128)(2,1)S(1)}, bf16[32,4096]{1,0:T(8,128)(2,1)S(1)}, u32[]{:S(2)}, u32[]{:S(2)}) collective-permute-start(bf16[32,4096]{1,0:T(8,128)(2,1)S(1)} %collective-permute-done.refs_3_), channel_id=1, source_target_pairs={{0,1},{1,0},{2,3},{3,2},{4,5},{5,4},{6,7},{7,6},{8,9},{9,8},{10,11... | collective-permute-start | bytes 786440 | tf_op jit(solution)/shard_map/ppermute | solution.py:163
  16.5 39.7 %collective-permute-start.9 = (bf16[64,3584]{1,0:T(8,128)(2,1)}, bf16[64,3584]{1,0:T(8,128)(2,1)S(1)}, u32[]{:S(2)}, u32[]{:S(2)}) collective-permute-start(bf16[64,3584]{1,0:T(8,128)(2,1)} %refs_1_.3), channel_id=1, source_target_pairs={{8,0},{16,8},{24,16},{9,1},{17,9},{25,17},{10,2},{18,10},{26,18},{... | collective-permute-start | bytes 1376264 | tf_op jit(solution)/shard_map/ppermute | solution.py:174
  27.5 29.7 %collective-permute-start.10 = (bf16[64,3584]{1,0:T(8,128)(2,1)}, bf16[64,3584]{1,0:T(8,128)(2,1)S(1)}, u32[]{:S(2)}, u32[]{:S(2)}) collective-permute-start(bf16[64,3584]{1,0:T(8,128)(2,1)} %refs_1_.3), channel_id=1, source_target_pairs={{0,8},{8,16},{16,24},{1,9},{9,17},{17,25},{2,10},{10,18},{18,26},{... | collective-permute-start | bytes 1376264 | tf_op jit(solution)/shard_map/ppermute | solution.py:174
  29.4 27.8 %collective-permute-start.8 = (bf16[64,3584]{1,0:T(8,128)(2,1)S(1)}, bf16[64,3584]{1,0:T(8,128)(2,1)S(1)}, u32[]{:S(2)}, u32[]{:S(2)}) collective-permute-start(bf16[64,3584]{1,0:T(8,128)(2,1)S(1)} %collective-permute-done.7.refs_3_), channel_id=1, source_target_pairs={{8,0},{16,24},{9,1},{17,25},{10,2},{18,26},{11,3},{19,27},{12,4},{... | collective-permute-start | bytes 1376264 | tf_op jit(solution)/shard_map/ppermute | solution.py:178
  32.9 1.0 copy-start.3
  54.8 43.4 %copy-start.1 = (f32[64,3584]{1,0:T(8,128)S(1)}, f32[64,3584]{1,0:T(8,128)}, u32[]{:S(2)}) copy-start(f32[64,3584]{1,0:T(8,128)} %get-tuple-element.8.own_ref) | copy-start | bytes 2752516
  54.8 19.4 %collective-permute-start.11 = (s16[64,3712]{1,0:T(8,128)(2,1)S(1)}, s16[64,3712]{1,0:T(8,128)(2,1)S(1)}, u32[]{:S(2)}, u32[]{:S(2)}) collective-permute-start(s16[64,3712]{1,0:T(8,128)(2,1)S(1)} %get-tuple-element.9), channel_id=1, source_target_pairs={{0,8},{8,16},{16,24},{24,0},{1,9},{9,17},{17,25},{25,1},{2,10},{10... | collective-permute-start | bytes 1425416 | tf_op jit(solution)/shard_map/ppermute | solution.py:200
  56.0 40.0 %collective-permute-start.12 = (s16[64,3712]{1,0:T(8,128)(2,1)S(1)}, s16[64,3712]{1,0:T(8,128)(2,1)S(1)}, u32[]{:S(2)}, u32[]{:S(2)}) collective-permute-start(s16[64,3712]{1,0:T(8,128)(2,1)S(1)} %get-tuple-element.10), channel_id=1, source_target_pairs={{0,16},{8,24},{16,0},{24,8},{1,17},{9,25},{17,1},{25,9},{2,18},{10... | collective-permute-start | bytes 1425416 | tf_op jit(solution)/shard_map/ppermute | solution.py:200
  56.3 41.9 %collective-permute-start.13 = (s16[64,3712]{1,0:T(8,128)(2,1)S(1)}, s16[64,3712]{1,0:T(8,128)(2,1)S(1)}, u32[]{:S(2)}, u32[]{:S(2)}) collective-permute-start(s16[64,3712]{1,0:T(8,128)(2,1)S(1)} %get-tuple-element.11), channel_id=1, source_target_pairs={{0,24},{8,0},{16,8},{24,16},{1,25},{9,1},{17,9},{25,17},{2,26},{10... | collective-permute-start | bytes 1425416 | tf_op jit(solution)/shard_map/ppermute | solution.py:200
  57.3 1.6 %copy-start = (bf16[256,4096]{1,0:T(8,128)(2,1)S(1)}, bf16[256,4096]{1,0:T(8,128)(2,1)}, u32[]{:S(2)}) copy-start(bf16[256,4096]{1,0:T(8,128)(2,1)} %get-tuple-element.7.refs_0_) | copy-start | bytes 6291460

commit v2 on v0

v2 whole, which is shorter than its diff:
```python
import functools

import jax
import jax.numpy as jnp
from jax import lax
from jax.experimental import pallas as pl
from jax.experimental.pallas import tpu as pltpu
from jax.sharding import PartitionSpec as P

LANES = 128
STEPS_PER_OCTAVE = 128.0
TOP = 32766.0
LEAST = 2.0 ** -120
VMEM_LIMIT = 48 * 1024 * 1024
SUB = 256
LINE_GROUPS = ((0, 3, 1, 2), (1, 2, 0, 3), (2, 3, 1, 0), (3, 2, 0, 1))


def tile_of(size, largest):
    tile = largest
    while size % tile:
        tile //= 2
    return tile


def dot(left, right, dims):
    return lax.dot_general(left, right, (dims, ((), ())), preferred_element_type=jnp.float32)


def encode(values):
    most = jnp.maximum(jnp.max(jnp.abs(values), axis=1, keepdims=True), LEAST)
    level = jnp.ceil(jnp.log2(most) * STEPS_PER_OCTAVE) + 1.0
    codes = jnp.round(values * jnp.exp2(level * (-1.0 / STEPS_PER_OCTAVE)) * TOP)
    return codes.astype(jnp.int32).astype(jnp.int16), level


def decode(codes, levels):
    scale = jnp.exp2(levels.astype(jnp.int32).astype(jnp.float32) * (1.0 / STEPS_PER_OCTAVE)) * (1.0 / TOP)
    return codes.astype(jnp.int32).astype(jnp.float32) * scale


def to_levels(levels):
    return levels.astype(jnp.int32).astype(jnp.int16)


def params():
    return pltpu.CompilerParams(vmem_limit_bytes=VMEM_LIMIT)


def cost(flops, moved):
    return pl.CostEstimate(flops=flops, bytes_accessed=moved, transcendentals=0)


def align_rows(pick_ref, pieces, aligned_ref):
    depth = aligned_ref.shape[1]
    chunk = tile_of(depth, 512)
    for at in range(0, depth, chunk):
        cols = slice(at, at + chunk)
        gathered = jnp.concatenate([piece[:, cols] for piece in pieces], axis=0)
        aligned_ref[:, cols] = dot(pick_ref[...], gathered, ((1,), (0,))).astype(jnp.bfloat16)


def sums_kernel(n_pieces, n_groups, keeps, turned, tile, *refs):
    refs = list(refs)
    if n_pieces:
        pick_ref = refs.pop(0)
        pieces = [refs.pop(0) for _ in range(n_pieces)]
        weight_ref = refs.pop(0)
        aligned_ref = refs.pop(0)
    else:
        aligned_ref, weight_ref = refs.pop(0), refs.pop(0)
    kept = [refs.pop(0) for _ in keeps]
    sent = [refs.pop(0) for _ in range(n_groups - len(keeps))]
    sends = [at for at in range(n_groups) if at not in keeps]
    levels_ref = refs.pop(0)
    step = pl.program_id(0)
    rows = kept[0].shape[0]
    width = sent[0].shape[1] - LANES

    @pl.when(step == 0)
    def _():
        if n_pieces:
            align_rows(pick_ref, pieces, aligned_ref)
        if turned:
            refs[0][...] = aligned_ref[...].T
        levels_ref[...] = jnp.zeros_like(levels_ref)

    sub = tile_of(tile, SUB)
    spans = [slice(at, at + sub) for at in range(0, tile, sub)]
    if turned:
        products = dot(weight_ref[...], refs[0][...], ((1,), (0,)))
        sums = [products[span].T for span in spans]
    else:
        sums = [dot(aligned_ref[...], weight_ref[span], ((1,), (1,))) for span in spans]
    lane = lax.broadcasted_iota(jnp.int32, levels_ref.shape, 1)
    levels = levels_ref[...]
    for part, (span, values) in enumerate(zip(spans, sums)):
        for at, ref in zip(keeps, kept):
            ref[:, span] = values[at * rows:(at + 1) * rows]
        outgoing = jnp.concatenate([values[at * rows:(at + 1) * rows] for at in sends], axis=0)
        codes, level = encode(outgoing)
        levels = jnp.where(lane == step * len(spans) + part, level, levels)
        cols = pl.ds(pl.multiple_of(step * tile + span.start, sub), sub)
        for at, ref in enumerate(sent):
            ref[:, cols] = codes[at * rows:(at + 1) * rows]
    levels_ref[...] = levels

    @pl.when(step == pl.num_programs(0) - 1)
    def _():
        for at, ref in enumerate(sent):
            ref[:, width:] = to_levels(levels[at * rows:(at + 1) * rows])


def partial_sums(aligned, align, weight, tile, first, count, n_groups, keeps, turned, name):
    depth = weight.shape[1]
    width = count * tile
    whole = lambda i: (0, 0)
    operands = [align[0], *align[1]] if aligned is None else [aligned]
    total = operands[0].shape[0]
    rows = total // n_groups
    n_sent = n_groups - len(keeps)
    in_specs = [pl.BlockSpec(operand.shape, whole) for operand in operands]
    in_specs.append(pl.BlockSpec((tile, depth), lambda i: (i + first, 0)))
    out_specs = [pl.BlockSpec((rows, tile), lambda i: (0, i))] * len(keeps)
    out_specs += [pl.BlockSpec((rows, width + LANES), whole)] * n_sent
    out_shape = [jax.ShapeDtypeStruct((rows, width), jnp.float32)] * len(keeps)
    out_shape += [jax.ShapeDtypeStruct((rows, width + LANES), jnp.int16)] * n_sent
    if aligned is None:
        out_specs.insert(0, pl.BlockSpec((total, depth), whole))
        out_shape.insert(0, jax.ShapeDtypeStruct((total, depth), jnp.bfloat16))
    scratch = [pltpu.VMEM((n_sent * rows, LANES), jnp.float32)]
    if turned:
        scratch.append(pltpu.VMEM((depth, total), jnp.bfloat16))
    outs = pl.pallas_call(
        functools.partial(sums_kernel, 0 if aligned is not None else len(align[1]), n_groups, keeps, turned, tile),
        grid=(count,), in_specs=in_specs, out_specs=out_specs, out_shape=out_shape, scratch_shapes=scratch,
        compiler_params=params(), cost_estimate=cost(2 * total * width * depth, 2 * width * depth), name=name,
    )(*operands, weight)
    if aligned is None:
        aligned, *outs = outs
    return aligned, outs[:len(keeps)], outs[len(keeps):]


def weight_kernel(n_pieces, choose, me_ref, aligned_ref, *refs):
    out_ref = refs[-1]
    left = jnp.concatenate(choose(me_ref[0], [ref[...] for ref in refs[:n_pieces]]), axis=0)
    depth = out_ref.shape[1]
    chunk = tile_of(depth, 1024)
    for at in range(0, depth, chunk):
        cols = slice(at, at + chunk)
        out_ref[:, cols] = dot(left, aligned_ref[:, cols], ((0,), (0,))).astype(jnp.bfloat16)


def weight_grads(me, aligned, pieces, choose, later_than=()):
    total, depth = aligned.shape
    rows, hidden = pieces[0].shape
    tile = tile_of(hidden, 512)
    return pl.pallas_call(
        functools.partial(weight_kernel, len(pieces), choose),
        grid=(hidden // tile,),
        in_specs=[pl.BlockSpec(memory_space=pltpu.SMEM), pl.BlockSpec((total, depth), lambda i: (0, 0))]
        + [pl.BlockSpec((rows, tile), lambda i: (0, i))] * len(pieces)
        + [pl.BlockSpec(memory_space=pl.ANY)] * len(later_than),
        out_specs=pl.BlockSpec((tile, depth), lambda i: (i, 0)),
        out_shape=jax.ShapeDtypeStruct((hidden, depth), jnp.bfloat16),
        compiler_params=params(), cost_estimate=cost(2 * total * hidden * depth, 2 * hidden * depth), name="weight_grads",
    )(me, aligned, *pieces, *later_than)


def line_choose(me, pieces):
    own, left, right, two, far = pieces
    first = jnp.where(me == 0, far, jnp.where(me == 3, left, right))
    second = jnp.where(me == 0, right, jnp.where(me == 3, far, left))
    return [own, first, second, two]


def merge_kernel(me_ref, left_ref, right_ref, kept_ref, first_ref, second_ref, *refs):
    me = me_ref[0]
    two_ref, last_ref = refs[(len(refs) - 2) // 2:][:2]
    width = kept_ref.shape[1]
    last_ref[...] = jnp.where(me == 0, second_ref[...], first_ref[...])
    sub = tile_of(width, SUB)
    lane = lax.broadcasted_iota(jnp.int32, (kept_ref.shape[0], LANES), 1)
    levels = jnp.zeros(lane.shape, jnp.float32)
    inner = jnp.where((me == 1) | (me == 2), 1.0, 0.0)
    for at in range(width // sub):
        cols = slice(at * sub, (at + 1) * sub)
        codes = jnp.where(me == 1, left_ref[:, cols], right_ref[:, cols])
        level = jnp.where(me == 1, left_ref[:, width:], right_ref[:, width:])[:, at:at + 1]
        codes, level = encode(kept_ref[:, cols] + inner * decode(codes, level))
        two_ref[:, cols] = codes
        levels = jnp.where(lane == at, level, levels)
    two_ref[:, width:] = to_levels(levels)


def merged(me, left, right, kept, first, second, passed):
    vmem, anywhere = pl.BlockSpec(memory_space=pltpu.VMEM), pl.BlockSpec(memory_space=pl.ANY)
    like = jax.ShapeDtypeStruct(left.shape, left.dtype)
    onward, last, *passed = pl.pallas_call(
        merge_kernel,
        in_specs=[pl.BlockSpec(memory_space=pltpu.SMEM)] + [vmem] * 5 + [anywhere] * len(passed),
        out_specs=[vmem] * 2 + [anywhere] * len(passed),
        out_shape=[like, like] + [jax.ShapeDtypeStruct(array.shape, array.dtype) for array in passed],
        input_output_aliases={6 + at: 2 + at for at in range(len(passed))},
        compiler_params=params(), cost_estimate=cost(left.size * 20, left.size * 16), name="merged",
    )(me, left, right, kept, first, second, *passed)
    return onward, last, passed


def total_kernel(counts, choose, me_ref, *refs):
    refs = list(refs)
    out_ref = refs.pop()
    base = 0
    for count in counts:
        own_ref, received, refs = refs[0], refs[1:count], refs[count:]
        width = own_ref.shape[1]
        sub = tile_of(width, SUB)
        for at in range(width // sub):
            cols = slice(at * sub, (at + 1) * sub)
            total = own_ref[:, cols]
            codes = choose(me_ref[0], [ref[:, cols] for ref in received])
            levels = choose(me_ref[0], [ref[:, width:] for ref in received])
            for code, level in zip(codes, levels):
                total = total + decode(code, level[:, at:at + 1])
            out_ref[:, base + at * sub:base + (at + 1) * sub] = total.astype(jnp.bfloat16)
        base += width


def line_received(me, messages):
    left, right, two, last = messages
    return [jnp.where(me < 2, right, left), two, last]


def totals(me, parts, choose, later_than=()):
    rows = parts[0][0].shape[0]
    hidden = sum(part[0].shape[1] for part in parts)
    flat = [array for part in parts for array in part]
    return pl.pallas_call(
        functools.partial(total_kernel, [len(part) for part in parts], choose),
        in_specs=[pl.BlockSpec(memory_space=pltpu.SMEM)] + [pl.BlockSpec(memory_space=pltpu.VMEM)] * len(flat)
        + [pl.BlockSpec(memory_space=pl.ANY)] * len(later_than),
        out_shape=jax.ShapeDtypeStruct((rows, hidden), jnp.bfloat16),
        compiler_params=params(), cost_estimate=cost(rows * hidden * 40, rows * hidden * 14), name="totals",
    )(me, *flat, *later_than)


def send(value, axis, pairs):
    return lax.ppermute(value, axis, pairs)


def gather_cotangent(cotangent, n_col):
    pieces = [send(cotangent, "col", [(i, i ^ flip) for i in range(n_col)]) for flip in range(2, n_col, 2)]
    swap = [(i, i ^ 1) for i in range(n_col)]
    swapped = [send(piece, "col", swap) for piece in [cotangent] + pieces]
    flips = list(range(0, n_col, 2))
    return [cotangent] + pieces + swapped, flips + [flip ^ 1 for flip in flips]


def body(n_row, n_col, activations, cotangent, down_weight, row_order):
    rows, hidden = activations.shape
    shard = cotangent.shape[0]
    mine_row, mine_col = lax.axis_index("row"), lax.axis_index("col")
    me = mine_row.astype(jnp.int32).reshape(1)
    on_line = n_row == 4

    pieces, flips = gather_cotangent(cotangent, n_col)
    if on_line:
        groups = [sum(jnp.where(mine_row == row, LINE_GROUPS[row][at], 0) for row in range(n_row)) for at in range(n_row)]
        from_left = send(activations, "row", [(0, 1), (1, 2), (2, 3)])
        from_right = send(activations, "row", [(3, 2), (2, 1), (1, 0)])
    else:
        groups = [(mine_row + o) % n_row for o in range(n_row)]

    order = row_order.reshape(n_row, rows)
    order = jnp.concatenate([lax.dynamic_index_in_dim(order, group, 0, keepdims=False) for group in groups])
    owner = mine_col ^ jnp.asarray(flips, jnp.int32)
    named = (owner[:, None] * shard + jnp.arange(shard, dtype=jnp.int32)[None, :]).reshape(-1)
    pick = (order[:, None] == named[None, :]).astype(jnp.bfloat16)

    tile = tile_of(hidden, 512)
    tiles = hidden // tile
    cut = tiles // 2
    keeps = (0, 3) if on_line else (0,)

    if not on_line:
        aligned, kept, sent = partial_sums(None, (pick, pieces), down_weight, tile, 0, tiles, n_row, keeps, False, "partial_sums")
        shift = lambda o: [(i, (i + o) % n_row) for i in range(n_row)]
        received = [send(message, "row", shift(o)) for o, message in enumerate(sent, 1)]
        act_pieces = [activations] + [send(activations, "row", shift(n_row - o)) for o in range(1, n_row)]
        same = lambda _, values: values
        weight_grad = weight_grads(me, aligned, act_pieces, same)
        return weight_grad, totals(me, [kept + received], same)

    two_left = send(from_left, "row", [(1, 2), (2, 3)])
    two_right = send(from_right, "row", [(2, 1), (1, 0)])

    aligned, kept_a, sent_a = partial_sums(None, (pick, pieces), down_weight, tile, 0, cut, n_row, keeps, False, "sums_a")
    rights, lefts = [(0, 1), (1, 2), (2, 3)], [(3, 2), (2, 1), (1, 0)]
    got_a = [send(sent_a[0], "row", rights), send(sent_a[1], "row", lefts)]
    two = jnp.where(mine_row < 2, two_right, two_left)
    far = send(two, "row", [(2, 3), (1, 0)])

    _, kept_b, sent_b = partial_sums(aligned, None, down_weight, tile, cut, tiles - cut, n_row, keeps, True, "sums_b")
    def carry(onward, last):
        return [send(onward, "row", [(0, 2), (1, 3), (2, 0), (3, 1)]), send(last, "row", [(0, 1), (3, 2)])]

    onward_a, last_a, sent_b = merged(me, *got_a, kept_a[1], *sent_a, sent_b)
    got_b = [send(sent_b[0], "row", rights), send(sent_b[1], "row", lefts)]
    crossed_a = carry(onward_a, last_a)
    onward_b, last_b, _ = merged(me, *got_b, kept_b[1], *sent_b, [])
    crossed_b = carry(onward_b, last_b)
    parts = [[kept_a[0], *got_a, *crossed_a], [kept_b[0], *got_b, *crossed_b]]

    act_pieces = [activations, from_left, from_right, two, far]
    weight_grad = weight_grads(me, aligned, act_pieces, line_choose, [onward_b])
    return weight_grad, totals(me, parts, line_received, [weight_grad])


def solution(mesh):
    in_specs = (P("row", "col"), P("col", "row"), P("col", "row"), P())
    out_specs = (P("col", "row"), P("row", "col"))
    fn = functools.partial(body, mesh.shape["row"], mesh.shape["col"])
    return jax.shard_map(fn, mesh=mesh, in_specs=in_specs, out_specs=out_specs, check_vma=False)
```

time: 163 us -> 92.9 us (0.57)
  waiting for transfers between devices: 69 us -> 10.8 us
  starting transfers between devices: 0.11 us -> 44.2 us
  local copies, waits for them, and re-layouts: 45.4 us -> 1.84 us
  Pallas kernels: 0 us -> 33.7 us
  matrix products: 30.1 us -> 0 us
  between operations: 13.8 us -> 0.89 us
  other arithmetic: 3.37 us -> 0.96 us
    all_gather x2 -> x0, waiting for transfers between devices: 51.9 us -> none  [the longest x1 30.4 us: body(): gathered = lax.all_gather(cotangent, 'col', axis=0, tiled=True)]
    ppermute x0 -> x20, starting transfers between devices: none -> 44.2 us  [send(): return lax.ppermute(value, axis, pairs)]
    unnamed x1 -> x4, local copies, waits for them, and re-layouts: 39.6 us -> 1 us
    pallas_call x0 -> x6, Pallas kernels: none -> 33.7 us  [the longest x2 17.8 us: partial_sums(): pl.pallas_call(functools.partial(sums_kernel, 0 if aligned is not None el...]
    dot_general x2 -> x0, matrix products: 30.1 us -> none  [the longest x1 15.8 us: contract_cols(): lax.dot_general(left, right, (((1,), (1,)), ((), ())), preferred_element_...]
    reduce_scatter x1 -> x0, waiting for transfers between devices: 15.7 us -> none  [body(): lax.psum_scatter(partial_sums, 'row', scatter_dimension=0, tiled=True)]
    ppermute x0 -> x20, waiting for transfers between devices: none -> 10.8 us  [send(): return lax.ppermute(value, axis, pairs)]
    gather x1 -> x0, local copies, waits for them, and re-layouts: 5.74 us -> none  [body(): aligned = jnp.take(gathered, row_order, axis=0)]
  transfers between devices with their start and end apart: 3 -> 20, of which waited for: 3 -> 4; matrix products, arithmetic and copies ran while one was open for 48% -> 2% of each run, Pallas kernels for 0% -> 35%
where the time goes in v2:
time: 92.9 us; the launch traced here: 92.5 us
  starting transfers between devices  44.2 us (48%)
  Pallas kernels  33.7 us (36%)
  waiting for transfers between devices  10.8 us (12%)
  local copies, waits for them, and re-layouts  1.84 us (2%)
  other arithmetic  0.96 us (1%)
    ppermute x20, starting transfers between devices, send(): return lax.ppermute(value, axis, pairs)  44.2 us
    pallas_call x2, Pallas kernels, partial_sums(): pl.pallas_call(functools.partial(sums_kernel, 0 if aligned is not None el...  17.8 us
    pallas_call x1, Pallas kernels, weight_grads(): pl.pallas_call(functools.partial(weight_kernel, len(pieces), choose), gri...  13.4 us
    ppermute x20, waiting for transfers between devices, send(): return lax.ppermute(value, axis, pairs)  10.8 us
  transfers between devices with their start and end apart: 20, of which 4 were waited for; matrix products, arithmetic and copies ran while one was open for 2% of the time, Pallas kernels for 35%

profile of v2, /device:TPU:0, one launch (start us, length us, event | category | flops | bytes accessed | tf_op | source)
XLA Modules:
  0.0 92.5 jit_solution(15614393520546973733)
XLA Ops:
  0.6 3.0 %collective-permute-start = (bf16[32,4096]{1,0:T(8,128)(2,1)}, bf16[32,4096]{1,0:T(8,128)(2,1)S(1)}, u32[]{:S(2)}, u32[]{:S(2)}) collective-permute-start(bf16[32,4096]{1,0:T(8,128)(2,1)} %refs_1_.2), channel_id=1, source_target_pairs={{0,2},{1,3},{2,0},{3,1},{4,6},{5,7},{6,4},{7,5},{8,10},{9,11},{10,... | collective-permute-start | bytes 786440 | tf_op jit(solution)/shard_map/ppermute | solution.py:248
  3.6 1.5 %collective-permute-start.1 = (bf16[32,4096]{1,0:T(8,128)(2,1)}, bf16[32,4096]{1,0:T(8,128)(2,1)S(1)}, u32[]{:S(2)}, u32[]{:S(2)}) collective-permute-start(bf16[32,4096]{1,0:T(8,128)(2,1)} %refs_1_.2), channel_id=1, source_target_pairs={{0,4},{1,5},{2,6},{3,7},{4,0},{5,1},{6,2},{7,3},{8,12},{9,13},{10,... | collective-permute-start | bytes 786440 | tf_op jit(solution)/shard_map/ppermute | solution.py:248
  5.2 4.0 %collective-permute-start.7 = (bf16[64,3584]{1,0:T(8,128)(2,1)}, bf16[64,3584]{1,0:T(8,128)(2,1)S(1)}, u32[]{:S(2)}, u32[]{:S(2)}) collective-permute-start(bf16[64,3584]{1,0:T(8,128)(2,1)} %refs_0_.1), channel_id=1, source_target_pairs={{0,8},{8,16},{16,24},{1,9},{9,17},{17,25},{2,10},{10,18},{18,26},{... | collective-permute-start | bytes 1376264 | tf_op jit(solution)/shard_map/ppermute | solution.py:248
  9.1 1.3 %collective-permute-start.8 = (bf16[64,3584]{1,0:T(8,128)(2,1)}, bf16[64,3584]{1,0:T(8,128)(2,1)S(1)}, u32[]{:S(2)}, u32[]{:S(2)}) collective-permute-start(bf16[64,3584]{1,0:T(8,128)(2,1)} %refs_0_.1), channel_id=1, source_target_pairs={{24,16},{16,8},{8,0},{25,17},{17,9},{9,1},{26,18},{18,10},{10,2},{... | collective-permute-start | bytes 1376264 | tf_op jit(solution)/shard_map/ppermute | solution.py:248
  10.4 0.7 xor_multiply_fusion
  11.1 0.8 reshape.28
  12.0 5.3 %collective-permute-done.1.refs_3_ = bf16[32,4096]{1,0:T(8,128)(2,1)S(1)} collective-permute-done((bf16[32,4096]{1,0:T(8,128)(2,1)}, bf16[32,4096]{1,0:T(8,128)(2,1)S(1)}, u32[]{:S(2)}, u32[]{:S(2)}) %collective-permute-start.1) | collective-permute-done | bytes 262176 | tf_op jit(solution)/shard_map/ppermute | solution.py:248
  17.2 0.5 collective-permute-start.5
  17.8 0.1 pad_add_fusion
  17.9 0.1 add.76
  18.0 0.4 collective-permute-done.7.refs_1_
  18.3 0.7 collective-permute-start.10
  19.0 3.4 %collective-permute-done.8.refs_2_ = bf16[64,3584]{1,0:T(8,128)(2,1)S(1)} collective-permute-done((bf16[64,3584]{1,0:T(8,128)(2,1)}, bf16[64,3584]{1,0:T(8,128)(2,1)S(1)}, u32[]{:S(2)}, u32[]{:S(2)}) %collective-permute-start.8) | collective-permute-done | bytes 458784 | tf_op jit(solution)/shard_map/ppermute | solution.py:248
  22.4 1.3 %collective-permute-start.9 = (bf16[64,3584]{1,0:T(8,128)(2,1)S(1)}, bf16[64,3584]{1,0:T(8,128)(2,1)S(1)}, u32[]{:S(2)}, u32[]{:S(2)}) collective-permute-start(bf16[64,3584]{1,0:T(8,128)(2,1)S(1)} %collective-permute-done.8.refs_2_), channel_id=1, source_target_pairs={{16,8},{8,0},{17,9},{9,1},{18,10},{10,2},{19,11},{11,3},{20,12},{1... | collective-permute-start | bytes 1376264 | tf_op jit(solution)/shard_map/ppermute | solution.py:248
  23.7 0.1 compare_convert_fusion.refs_0_
  23.8 1.0 %copy-done.1 = bf16[32,4096]{1,0:T(8,128)(2,1)S(1)} copy-done((bf16[32,4096]{1,0:T(8,128)(2,1)S(1)}, bf16[32,4096]{1,0:T(8,128)(2,1)}, u32[]{:S(2)}) %copy-start.1) | copy-done | bytes 262168
  24.8 8.0 %sums_a.1 = (bf16[256,4096]{1,0:T(8,128)(2,1)S(1)}, f32[64,1536]{1,0:T(8,128)S(1)}, f32[64,1536]{1,0:T(8,128)S(1)}, s16[64,1664]{1,0:T(8,128)(2,1)S(1)}, s16[64,1664]{1,0:T(8,128)(2,1)S(1)}) custom-call(bf16[256,256]{1,0:T(8,128)(2,1)S(1)} %compare_convert_fusion.refs_0_, bf16[32,4096]{1,0:T(8,128)(2,1)S(1)} %copy-done.1, ...), custom_call_target="tpu_custom_call" | custom-call | flops 3221225472 | bytes 12582912 | tf_op jit(solution)/shard_map/sums_a/pallas_call | solution.py:134
  32.8 4.6 %collective-permute-start.12 = (s16[64,1664]{1,0:T(8,128)(2,1)S(1)}, s16[64,1664]{1,0:T(8,128)(2,1)S(1)}, u32[]{:S(2)}, u32[]{:S(2)}) collective-permute-start(s16[64,1664]{1,0:T(8,128)(2,1)S(1)} %get-tuple-element.18.first_ref), channel_id=1, source_target_pairs={{0,8},{8,16},{16,24},{1,9},{9,17},{17,25},{2,10},{10,18},{18,26},{... | collective-permute-start | bytes 638984 | tf_op jit(solution)/shard_map/ppermute | solution.py:248
  37.4 1.3 %collective-permute-start.13 = (s16[64,1664]{1,0:T(8,128)(2,1)S(1)}, s16[64,1664]{1,0:T(8,128)(2,1)S(1)}, u32[]{:S(2)}, u32[]{:S(2)}) collective-permute-start(s16[64,1664]{1,0:T(8,128)(2,1)S(1)} %get-tuple-element.19.second_ref), channel_id=1, source_target_pairs={{24,16},{16,8},{8,0},{25,17},{17,9},{9,1},{26,18},{18,10},{10,2},{... | collective-permute-start | bytes 638984 | tf_op jit(solution)/shard_map/ppermute | solution.py:248
  38.7 1.3 %collective-permute-start.11 = (bf16[64,3584]{1,0:T(8,128)(2,1)S(1)}, bf16[64,3584]{1,0:T(8,128)(2,1)S(1)}, u32[]{:S(2)}, u32[]{:S(2)}) collective-permute-start(bf16[64,3584]{1,0:T(8,128)(2,1)S(1)} %broadcast_select_fusion.refs_3_), channel_id=1, source_target_pairs={{16,24},{8,0},{17,25},{9,1},{18,26},{10,2},{19,27},{11,3},{20,28},... | collective-permute-start | bytes 1376264 | tf_op jit(solution)/shard_map/ppermute | solution.py:248
  40.0 9.9 %sums_b.1 = (f32[64,2048]{1,0:T(8,128)S(1)}, f32[64,2048]{1,0:T(8,128)S(1)}, s16[64,2176]{1,0:T(8,128)(2,1)S(1)}, s16[64,2176]{1,0:T(8,128)(2,1)S(1)}) custom-call(bf16[256,4096]{1,0:T(8,128)(2,1)S(1)} %get-tuple-element.17.refs_0_.aligned_ref, bf16[3584,4096]{1,0:T(8,128)(2,1)} %refs_1_.3), custom_call_target="tpu_custom_call" | custom-call | flops 4294967296 | bytes 16777216 | tf_op jit(solution)/shard_map/sums_b/pallas_call | solution.py:134
  49.9 0.5 merged.2
  50.4 4.6 %collective-permute-start.14 = (s16[64,2176]{1,0:T(8,128)(2,1)S(1)}, s16[64,2176]{1,0:T(8,128)(2,1)S(1)}, u32[]{:S(2)}, u32[]{:S(2)}) collective-permute-start(s16[64,2176]{1,0:T(8,128)(2,1)S(1)} %get-tuple-element.23.first_ref), channel_id=1, source_target_pairs={{0,8},{8,16},{16,24},{1,9},{9,17},{17,25},{2,10},{10,18},{18,26},{... | collective-permute-start | bytes 835592 | tf_op jit(solution)/shard_map/ppermute | solution.py:248
  55.0 1.3 %collective-permute-start.15 = (s16[64,2176]{1,0:T(8,128)(2,1)S(1)}, s16[64,2176]{1,0:T(8,128)(2,1)S(1)}, u32[]{:S(2)}, u32[]{:S(2)}) collective-permute-start(s16[64,2176]{1,0:T(8,128)(2,1)S(1)} %get-tuple-element.24.second_ref), channel_id=1, source_target_pairs={{24,16},{16,8},{8,0},{25,17},{17,9},{9,1},{26,18},{18,10},{10,2},{... | collective-permute-start | bytes 835592 | tf_op jit(solution)/shard_map/ppermute | solution.py:248
  56.3 4.6 %collective-permute-start.16 = (s16[64,1664]{1,0:T(8,128)(2,1)S(1)}, s16[64,1664]{1,0:T(8,128)(2,1)S(1)}, u32[]{:S(2)}, u32[]{:S(2)}) collective-permute-start(s16[64,1664]{1,0:T(8,128)(2,1)S(1)} %get-tuple-element.28), channel_id=1, source_target_pairs={{0,16},{8,24},{16,0},{24,8},{1,17},{9,25},{17,1},{25,9},{2,18},{10... | collective-permute-start | bytes 638984 | tf_op jit(solution)/shard_map/ppermute | solution.py:248
  61.0 1.9 %collective-permute-start.17 = (s16[64,1664]{1,0:T(8,128)(2,1)S(1)}, s16[64,1664]{1,0:T(8,128)(2,1)S(1)}, u32[]{:S(2)}, u32[]{:S(2)}) collective-permute-start(s16[64,1664]{1,0:T(8,128)(2,1)S(1)} %get-tuple-element.29), channel_id=1, source_target_pairs={{0,8},{24,16},{1,9},{25,17},{2,10},{26,18},{3,11},{27,19},{4,12},{... | collective-permute-start | bytes 638984 | tf_op jit(solution)/shard_map/ppermute | solution.py:248
  62.9 1.8 %collective-permute-done.15.right_ref.refs_7_ = s16[64,2176]{1,0:T(8,128)(2,1)S(1)} collective-permute-done((s16[64,2176]{1,0:T(8,128)(2,1)S(1)}, s16[64,2176]{1,0:T(8,128)(2,1)S(1)}, u32[]{:S(2)}, u32[]{:S(2)}) %collective-permute-start.15) | collective-permute-done | bytes 278560 | tf_op jit(solution)/shard_map/ppermute | solution.py:248
  64.7 0.7 merged.3
  65.4 8.9 %collective-permute-start.18 = (s16[64,2176]{1,0:T(8,128)(2,1)S(1)}, s16[64,2176]{1,0:T(8,128)(2,1)S(1)}, u32[]{:S(2)}, u32[]{:S(2)}) collective-permute-start(s16[64,2176]{1,0:T(8,128)(2,1)S(1)} %get-tuple-element.26.refs_5_), channel_id=1, source_target_pairs={{0,16},{8,24},{16,0},{24,8},{1,17},{9,25},{17,1},{25,9},{2,18},{10... | collective-permute-start | bytes 835592 | tf_op jit(solution)/shard_map/ppermute | solution.py:248
  74.2 3.4 %collective-permute-start.19 = (s16[64,2176]{1,0:T(8,128)(2,1)S(1)}, s16[64,2176]{1,0:T(8,128)(2,1)S(1)}, u32[]{:S(2)}, u32[]{:S(2)}) collective-permute-start(s16[64,2176]{1,0:T(8,128)(2,1)S(1)} %get-tuple-element.31), channel_id=1, source_target_pairs={{0,8},{24,16},{1,9},{25,17},{2,10},{26,18},{3,11},{27,19},{4,12},{... | collective-permute-start | bytes 835592 | tf_op jit(solution)/shard_map/ppermute | solution.py:248
  77.7 13.4 %weight_grads.1.refs_10_ = bf16[3584,4096]{1,0:T(8,128)(2,1)} custom-call(s32[1]{0:T(128)} %bitcast.me_ref, bf16[256,4096]{1,0:T(8,128)(2,1)S(1)} %get-tuple-element.17.refs_0_.aligned_ref, bf16[64,3584]{1,0:T(8,128)(2,1)S(1)} %copy-done, bf16[64,3584]{1,0:T(8,128)(2,1)S(1)} %collective-permute-done.7.refs_1_, ...), custom_call_target="tpu_custom_call" | custom-call | flops 7516192768 | bytes 29360128 | tf_op jit(solution)/shard_map/weight_grads/pallas_call | solution.py:158
  91.1 1.4 %totals.1 = bf16[64,3584]{1,0:T(8,128)(2,1)} custom-call(s32[1]{0:T(128)} %bitcast.me_ref, f32[64,1536]{1,0:T(8,128)S(1)} %get-tuple-element.27.refs_0_, s16[64,1664]{1,0:T(8,128)(2,1)S(1)} %collective-permute-done.12.left_ref.refs_1_, s16[64,1664]{1,0:T(8,128)(2,1)S(1)} %collective-permute-done.13.right_ref.refs_2_, ...), custom_call_target="tpu_custom_call" | custom-call | flops 9175040 | bytes 3211264 | tf_op jit(solution)/shard_map/totals/pallas_call | solution.py:238
  (26 shorter events, 0.3 us)
Async XLA Ops:
  0.6 11.2 %collective-permute-start = (bf16[32,4096]{1,0:T(8,128)(2,1)}, bf16[32,4096]{1,0:T(8,128)(2,1)S(1)}, u32[]{:S(2)}, u32[]{:S(2)}) collective-permute-start(bf16[32,4096]{1,0:T(8,128)(2,1)} %refs_1_.2), channel_id=1, source_target_pairs={{0,2},{1,3},{2,0},{3,1},{4,6},{5,7},{6,4},{7,5},{8,10},{9,11},{10,... | collective-permute-start | bytes 786440 | tf_op jit(solution)/shard_map/ppermute | solution.py:248
  3.6 13.6 %collective-permute-start.1 = (bf16[32,4096]{1,0:T(8,128)(2,1)}, bf16[32,4096]{1,0:T(8,128)(2,1)S(1)}, u32[]{:S(2)}, u32[]{:S(2)}) collective-permute-start(bf16[32,4096]{1,0:T(8,128)(2,1)} %refs_1_.2), channel_id=1, source_target_pairs={{0,4},{1,5},{2,6},{3,7},{4,0},{5,1},{6,2},{7,3},{8,12},{9,13},{10,... | collective-permute-start | bytes 786440 | tf_op jit(solution)/shard_map/ppermute | solution.py:248
  5.2 12.1 %collective-permute-start.2 = (bf16[32,4096]{1,0:T(8,128)(2,1)}, bf16[32,4096]{1,0:T(8,128)(2,1)S(1)}, u32[]{:S(2)}, u32[]{:S(2)}) collective-permute-start(bf16[32,4096]{1,0:T(8,128)(2,1)} %refs_1_.2), channel_id=1, source_target_pairs={{0,6},{1,7},{2,4},{3,5},{4,2},{5,3},{6,0},{7,1},{8,14},{9,15},{10,... | collective-permute-start | bytes 786440 | tf_op jit(solution)/shard_map/ppermute | solution.py:248
  5.2 13.2 %collective-permute-start.7 = (bf16[64,3584]{1,0:T(8,128)(2,1)}, bf16[64,3584]{1,0:T(8,128)(2,1)S(1)}, u32[]{:S(2)}, u32[]{:S(2)}) collective-permute-start(bf16[64,3584]{1,0:T(8,128)(2,1)} %refs_0_.1), channel_id=1, source_target_pairs={{0,8},{8,16},{16,24},{1,9},{9,17},{17,25},{2,10},{10,18},{18,26},{... | collective-permute-start | bytes 1376264 | tf_op jit(solution)/shard_map/ppermute | solution.py:248
  9.1 13.2 %collective-permute-start.8 = (bf16[64,3584]{1,0:T(8,128)(2,1)}, bf16[64,3584]{1,0:T(8,128)(2,1)S(1)}, u32[]{:S(2)}, u32[]{:S(2)}) collective-permute-start(bf16[64,3584]{1,0:T(8,128)(2,1)} %refs_0_.1), channel_id=1, source_target_pairs={{24,16},{16,8},{8,0},{25,17},{17,9},{9,1},{26,18},{18,10},{10,2},{... | collective-permute-start | bytes 1376264 | tf_op jit(solution)/shard_map/ppermute | solution.py:248
  11.9 5.9 %collective-permute-start.3 = (bf16[32,4096]{1,0:T(8,128)(2,1)}, bf16[32,4096]{1,0:T(8,128)(2,1)S(1)}, u32[]{:S(2)}, u32[]{:S(2)}) collective-permute-start(bf16[32,4096]{1,0:T(8,128)(2,1)} %refs_1_.2), channel_id=1, source_target_pairs={{0,1},{1,0},{2,3},{3,2},{4,5},{5,4},{6,7},{7,6},{8,9},{9,8},{10,11... | collective-permute-start | bytes 786440 | tf_op jit(solution)/shard_map/ppermute | solution.py:248
  17.2 6.6 %collective-permute-start.4 = (bf16[32,4096]{1,0:T(8,128)(2,1)S(1)}, bf16[32,4096]{1,0:T(8,128)(2,1)S(1)}, u32[]{:S(2)}, u32[]{:S(2)}) collective-permute-start(bf16[32,4096]{1,0:T(8,128)(2,1)S(1)} %collective-permute-done.refs_2_), channel_id=1, source_target_pairs={{0,1},{1,0},{2,3},{3,2},{4,5},{5,4},{6,7},{7,6},{8,9},{9,8},{10,11... | collective-permute-start | bytes 786440 | tf_op jit(solution)/shard_map/ppermute | solution.py:248
  17.2 6.6 %collective-permute-start.5 = (bf16[32,4096]{1,0:T(8,128)(2,1)S(1)}, bf16[32,4096]{1,0:T(8,128)(2,1)S(1)}, u32[]{:S(2)}, u32[]{:S(2)}) collective-permute-start(bf16[32,4096]{1,0:T(8,128)(2,1)S(1)} %collective-permute-done.1.refs_3_), channel_id=1, source_target_pairs={{0,1},{1,0},{2,3},{3,2},{4,5},{5,4},{6,7},{7,6},{8,9},{9,8},{10,11... | collective-permute-start | bytes 786440 | tf_op jit(solution)/shard_map/ppermute | solution.py:248
  17.7 6.1 %collective-permute-start.6 = (bf16[32,4096]{1,0:T(8,128)(2,1)S(1)}, bf16[32,4096]{1,0:T(8,128)(2,1)S(1)}, u32[]{:S(2)}, u32[]{:S(2)}) collective-permute-start(bf16[32,4096]{1,0:T(8,128)(2,1)S(1)} %collective-permute-done.2.refs_4_), channel_id=1, source_target_pairs={{0,1},{1,0},{2,3},{3,2},{4,5},{5,4},{6,7},{7,6},{8,9},{9,8},{10,11... | collective-permute-start | bytes 786440 | tf_op jit(solution)/shard_map/ppermute | solution.py:248
  18.3 20.3 %collective-permute-start.10 = (bf16[64,3584]{1,0:T(8,128)(2,1)S(1)}, bf16[64,3584]{1,0:T(8,128)(2,1)S(1)}, u32[]{:S(2)}, u32[]{:S(2)}) collective-permute-start(bf16[64,3584]{1,0:T(8,128)(2,1)S(1)} %collective-permute-done.7.refs_1_), channel_id=1, source_target_pairs={{8,16},{16,24},{9,17},{17,25},{10,18},{18,26},{11,19},{19,27},{12,... | collective-permute-start | bytes 1376264 | tf_op jit(solution)/shard_map/ppermute | solution.py:248
  22.4 16.3 %collective-permute-start.9 = (bf16[64,3584]{1,0:T(8,128)(2,1)S(1)}, bf16[64,3584]{1,0:T(8,128)(2,1)S(1)}, u32[]{:S(2)}, u32[]{:S(2)}) collective-permute-start(bf16[64,3584]{1,0:T(8,128)(2,1)S(1)} %collective-permute-done.8.refs_2_), channel_id=1, source_target_pairs={{16,8},{8,0},{17,9},{9,1},{18,10},{10,2},{19,11},{11,3},{20,12},{1... | collective-permute-start | bytes 1376264 | tf_op jit(solution)/shard_map/ppermute | solution.py:248
  23.8 53.9 %copy-start = (bf16[64,3584]{1,0:T(8,128)(2,1)S(1)}, bf16[64,3584]{1,0:T(8,128)(2,1)}, u32[]{:S(2)}) copy-start(bf16[64,3584]{1,0:T(8,128)(2,1)} %refs_0_.1) | copy-start | bytes 1376260
  23.8 1.0 %copy-start.1 = (bf16[32,4096]{1,0:T(8,128)(2,1)S(1)}, bf16[32,4096]{1,0:T(8,128)(2,1)}, u32[]{:S(2)}) copy-start(bf16[32,4096]{1,0:T(8,128)(2,1)} %refs_1_.2) | copy-start | bytes 786436
  32.8 17.1 %collective-permute-start.12 = (s16[64,1664]{1,0:T(8,128)(2,1)S(1)}, s16[64,1664]{1,0:T(8,128)(2,1)S(1)}, u32[]{:S(2)}, u32[]{:S(2)}) collective-permute-start(s16[64,1664]{1,0:T(8,128)(2,1)S(1)} %get-tuple-element.18.first_ref), channel_id=1, source_target_pairs={{0,8},{8,16},{16,24},{1,9},{9,17},{17,25},{2,10},{10,18},{18,26},{... | collective-permute-start | bytes 638984 | tf_op jit(solution)/shard_map/ppermute | solution.py:248
  37.4 12.6 %collective-permute-start.13 = (s16[64,1664]{1,0:T(8,128)(2,1)S(1)}, s16[64,1664]{1,0:T(8,128)(2,1)S(1)}, u32[]{:S(2)}, u32[]{:S(2)}) collective-permute-start(s16[64,1664]{1,0:T(8,128)(2,1)S(1)} %get-tuple-element.19.second_ref), channel_id=1, source_target_pairs={{24,16},{16,8},{8,0},{25,17},{17,9},{9,1},{26,18},{18,10},{10,2},{... | collective-permute-start | bytes 638984 | tf_op jit(solution)/shard_map/ppermute | solution.py:248
  38.7 38.9 %collective-permute-start.11 = (bf16[64,3584]{1,0:T(8,128)(2,1)S(1)}, bf16[64,3584]{1,0:T(8,128)(2,1)S(1)}, u32[]{:S(2)}, u32[]{:S(2)}) collective-permute-start(bf16[64,3584]{1,0:T(8,128)(2,1)S(1)} %broadcast_select_fusion.refs_3_), channel_id=1, source_target_pairs={{16,24},{8,0},{17,25},{9,1},{18,26},{10,2},{19,27},{11,3},{20,28},... | collective-permute-start | bytes 1376264 | tf_op jit(solution)/shard_map/ppermute | solution.py:248
  50.4 12.5 %collective-permute-start.14 = (s16[64,2176]{1,0:T(8,128)(2,1)S(1)}, s16[64,2176]{1,0:T(8,128)(2,1)S(1)}, u32[]{:S(2)}, u32[]{:S(2)}) collective-permute-start(s16[64,2176]{1,0:T(8,128)(2,1)S(1)} %get-tuple-element.23.first_ref), channel_id=1, source_target_pairs={{0,8},{8,16},{16,24},{1,9},{9,17},{17,25},{2,10},{10,18},{18,26},{... | collective-permute-start | bytes 835592 | tf_op jit(solution)/shard_map/ppermute | solution.py:248
  55.0 9.7 %collective-permute-start.15 = (s16[64,2176]{1,0:T(8,128)(2,1)S(1)}, s16[64,2176]{1,0:T(8,128)(2,1)S(1)}, u32[]{:S(2)}, u32[]{:S(2)}) collective-permute-start(s16[64,2176]{1,0:T(8,128)(2,1)S(1)} %get-tuple-element.24.second_ref), channel_id=1, source_target_pairs={{24,16},{16,8},{8,0},{25,17},{17,9},{9,1},{26,18},{18,10},{10,2},{... | collective-permute-start | bytes 835592 | tf_op jit(solution)/shard_map/ppermute | solution.py:248
  56.3 34.7 %collective-permute-start.16 = (s16[64,1664]{1,0:T(8,128)(2,1)S(1)}, s16[64,1664]{1,0:T(8,128)(2,1)S(1)}, u32[]{:S(2)}, u32[]{:S(2)}) collective-permute-start(s16[64,1664]{1,0:T(8,128)(2,1)S(1)} %get-tuple-element.28), channel_id=1, source_target_pairs={{0,16},{8,24},{16,0},{24,8},{1,17},{9,25},{17,1},{25,9},{2,18},{10... | collective-permute-start | bytes 638984 | tf_op jit(solution)/shard_map/ppermute | solution.py:248
  61.0 30.1 %collective-permute-start.17 = (s16[64,1664]{1,0:T(8,128)(2,1)S(1)}, s16[64,1664]{1,0:T(8,128)(2,1)S(1)}, u32[]{:S(2)}, u32[]{:S(2)}) collective-permute-start(s16[64,1664]{1,0:T(8,128)(2,1)S(1)} %get-tuple-element.29), channel_id=1, source_target_pairs={{0,8},{24,16},{1,9},{25,17},{2,10},{26,18},{3,11},{27,19},{4,12},{... | collective-permute-start | bytes 638984 | tf_op jit(solution)/shard_map/ppermute | solution.py:248
  65.4 25.7 %collective-permute-start.18 = (s16[64,2176]{1,0:T(8,128)(2,1)S(1)}, s16[64,2176]{1,0:T(8,128)(2,1)S(1)}, u32[]{:S(2)}, u32[]{:S(2)}) collective-permute-start(s16[64,2176]{1,0:T(8,128)(2,1)S(1)} %get-tuple-element.26.refs_5_), channel_id=1, source_target_pairs={{0,16},{8,24},{16,0},{24,8},{1,17},{9,25},{17,1},{25,9},{2,18},{10... | collective-permute-start | bytes 835592 | tf_op jit(solution)/shard_map/ppermute | solution.py:248
  74.2 16.9 %collective-permute-start.19 = (s16[64,2176]{1,0:T(8,128)(2,1)S(1)}, s16[64,2176]{1,0:T(8,128)(2,1)S(1)}, u32[]{:S(2)}, u32[]{:S(2)}) collective-permute-start(s16[64,2176]{1,0:T(8,128)(2,1)S(1)} %get-tuple-element.31), channel_id=1, source_target_pairs={{0,8},{24,16},{1,9},{25,17},{2,10},{26,18},{3,11},{27,19},{4,12},{... | collective-permute-start | bytes 835592 | tf_op jit(solution)/shard_map/ppermute | solution.py:248

commit v3 on v2

v3 whole, which is shorter than its diff:
```python
import functools

import jax
import jax.numpy as jnp
from jax import lax
from jax.experimental import pallas as pl
from jax.experimental.pallas import tpu as pltpu
from jax.sharding import PartitionSpec as P

LANES = 128
STEPS_PER_OCTAVE = 128.0
TOP = 32766.0
LEAST = 2.0 ** -120
VMEM_LIMIT = 48 * 1024 * 1024
SUB = 256


def tile_of(size, largest):
    tile = largest
    while size % tile:
        tile //= 2
    return tile


def dot(left, right, dims):
    return lax.dot_general(left, right, (dims, ((), ())), preferred_element_type=jnp.float32)


def encode(values):
    most = jnp.maximum(jnp.max(jnp.abs(values), axis=1, keepdims=True), LEAST)
    level = jnp.ceil(jnp.log2(most) * STEPS_PER_OCTAVE) + 1.0
    codes = jnp.round(values * jnp.exp2(level * (-1.0 / STEPS_PER_OCTAVE)) * TOP)
    return codes.astype(jnp.int32).astype(jnp.int16), level


def decode(codes, levels):
    scale = jnp.exp2(levels.astype(jnp.int32).astype(jnp.float32) * (1.0 / STEPS_PER_OCTAVE)) * (1.0 / TOP)
    return codes.astype(jnp.int32).astype(jnp.float32) * scale


def to_levels(levels):
    return levels.astype(jnp.int32).astype(jnp.int16)


def params():
    return pltpu.CompilerParams(vmem_limit_bytes=VMEM_LIMIT)


def cost(flops, moved):
    return pl.CostEstimate(flops=flops, bytes_accessed=moved, transcendentals=0)


def align_rows(pick_ref, pieces, aligned_ref):
    depth = aligned_ref.shape[1]
    chunk = tile_of(depth, 512)
    for at in range(0, depth, chunk):
        cols = slice(at, at + chunk)
        gathered = jnp.concatenate([piece[:, cols] for piece in pieces], axis=0)
        aligned_ref[:, cols] = dot(pick_ref[...], gathered, ((1,), (0,))).astype(jnp.bfloat16)


def sums_kernel(n_pieces, n_groups, n_blocks, tile, *refs):
    refs = list(refs)
    if n_pieces:
        pick_ref = refs.pop(0)
        pieces = [refs.pop(0) for _ in range(n_pieces)]
        blocks = [refs.pop(0) for _ in range(n_blocks)]
        aligned_ref = refs.pop(0)
    else:
        aligned_ref = refs.pop(0)
        blocks = [refs.pop(0) for _ in range(n_blocks)]
    own_ref, *sent, levels_ref = refs
    step = pl.program_id(0)
    rows = own_ref.shape[0]
    width = sent[0].shape[1] - LANES

    @pl.when(step == 0)
    def _():
        if n_pieces:
            align_rows(pick_ref, pieces, aligned_ref)
        levels_ref[...] = jnp.zeros_like(levels_ref)

    lane = lax.broadcasted_iota(jnp.int32, levels_ref.shape, 1)
    levels = levels_ref[...]
    for part, block in enumerate(blocks):
        values = dot(aligned_ref[...], block[...], ((1,), (1,)))
        own_ref[:, part * tile:(part + 1) * tile] = values[:rows]
        codes, level = encode(values[rows:])
        levels = jnp.where(lane == step * n_blocks + part, level, levels)
        cols = pl.ds(pl.multiple_of((step * n_blocks + part) * tile, tile), tile)
        for at, ref in enumerate(sent):
            ref[:, cols] = codes[at * rows:(at + 1) * rows]
    levels_ref[...] = levels

    @pl.when(step == pl.num_programs(0) - 1)
    def _():
        for at, ref in enumerate(sent):
            ref[:, width:] = to_levels(levels[at * rows:(at + 1) * rows])


def partial_sums(aligned, align, weight, tile, first, count, n_groups, name):
    depth = weight.shape[1]
    width = count * tile
    whole = lambda i: (0, 0)
    operands = [align[0], *align[1]] if aligned is None else [aligned]
    total = operands[0].shape[0]
    rows = total // n_groups
    n_sent = n_groups - 1
    n_blocks = 2 if count % 2 == 0 and first % 2 == 0 else 1
    block_at = lambda part: (lambda i: (i * n_blocks + first + part, 0))
    in_specs = [pl.BlockSpec(operand.shape, whole) for operand in operands]
    in_specs += [pl.BlockSpec((tile, depth), block_at(part)) for part in range(n_blocks)]
    out_specs = [pl.BlockSpec((rows, n_blocks * tile), lambda i: (0, i))]
    out_specs += [pl.BlockSpec((rows, width + LANES), whole)] * n_sent
    out_shape = [jax.ShapeDtypeStruct((rows, width), jnp.float32)]
    out_shape += [jax.ShapeDtypeStruct((rows, width + LANES), jnp.int16)] * n_sent
    if aligned is None:
        out_specs.insert(0, pl.BlockSpec((total, depth), whole))
        out_shape.insert(0, jax.ShapeDtypeStruct((total, depth), jnp.bfloat16))
    outs = pl.pallas_call(
        functools.partial(sums_kernel, 0 if aligned is not None else len(align[1]), n_groups, n_blocks, tile),
        grid=(count // n_blocks,), in_specs=in_specs, out_specs=out_specs, out_shape=out_shape,
        scratch_shapes=[pltpu.VMEM((n_sent * rows, LANES), jnp.float32)],
        compiler_params=params(), cost_estimate=cost(2 * total * width * depth, 2 * width * depth), name=name,
    )(*operands, *[weight] * n_blocks)
    if aligned is None:
        aligned, *outs = outs
    return aligned, outs[0], outs[1:]


def weight_kernel(aligned_ref, *refs):
    out_ref = refs[-1]
    left = jnp.concatenate([ref[...] for ref in refs[:-1]], axis=0)
    depth = out_ref.shape[1]
    chunk = tile_of(depth, 1024)
    for at in range(0, depth, chunk):
        cols = slice(at, at + chunk)
        out_ref[:, cols] = dot(left, aligned_ref[:, cols], ((0,), (0,))).astype(jnp.bfloat16)


def weight_grads(aligned, pieces):
    total, depth = aligned.shape
    rows, hidden = pieces[0].shape
    tile = tile_of(hidden, 512)
    return pl.pallas_call(
        weight_kernel,
        grid=(hidden // tile,),
        in_specs=[pl.BlockSpec((total, depth), lambda i: (0, 0))]
        + [pl.BlockSpec((rows, tile), lambda i: (0, i))] * len(pieces),
        out_specs=pl.BlockSpec((tile, depth), lambda i: (i, 0)),
        out_shape=jax.ShapeDtypeStruct((hidden, depth), jnp.bfloat16),
        compiler_params=params(), cost_estimate=cost(2 * total * hidden * depth, 2 * hidden * depth), name="weight_grads",
    )(aligned, *pieces)


def total_kernel(counts, *refs):
    refs = list(refs)
    out_ref = refs.pop()
    base = 0
    for count in counts:
        own_ref, received, refs = refs[0], refs[1:count], refs[count:]
        width = own_ref.shape[1]
        sub = tile_of(width, SUB)
        for at in range(width // sub):
            cols = slice(at * sub, (at + 1) * sub)
            total = own_ref[:, cols]
            for ref in received:
                total = total + decode(ref[:, cols], ref[:, width:][:, at:at + 1])
            out_ref[:, base + at * sub:base + (at + 1) * sub] = total.astype(jnp.bfloat16)
        base += width


def totals(parts, later_than):
    rows = parts[0][0].shape[0]
    hidden = sum(part[0].shape[1] for part in parts)
    flat = [array for part in parts for array in part]
    return pl.pallas_call(
        functools.partial(totals_with_order, len(later_than), [len(part) for part in parts]),
        in_specs=[pl.BlockSpec(memory_space=pltpu.VMEM)] * len(flat) + [pl.BlockSpec(memory_space=pl.ANY)] * len(later_than),
        out_shape=jax.ShapeDtypeStruct((rows, hidden), jnp.bfloat16),
        compiler_params=params(), cost_estimate=cost(rows * hidden * 40, rows * hidden * 14), name="totals",
    )(*flat, *later_than)


def totals_with_order(n_later, counts, *refs):
    total_kernel(counts, *refs[:len(refs) - 1 - n_later], refs[-1])


def send(value, axis, flip, size):
    return lax.ppermute(value, axis, [(i, i ^ flip) for i in range(size)])


def copy_kernel(value_ref, later_ref, out_ref):
    out_ref[...] = value_ref[...]


def copied(value, later_than):
    return pl.pallas_call(
        copy_kernel,
        in_specs=[pl.BlockSpec(memory_space=pltpu.VMEM), pl.BlockSpec(memory_space=pl.ANY)],
        out_shape=jax.ShapeDtypeStruct(value.shape, value.dtype),
        compiler_params=params(), cost_estimate=cost(value.size, value.size * 4), name="copied",
    )(value, later_than)


def same_kernel(*refs):
    pass


def handed_on(values, later_than):
    anywhere = pl.BlockSpec(memory_space=pl.ANY)
    return pl.pallas_call(
        same_kernel,
        in_specs=[anywhere] * (len(values) + len(later_than)), out_specs=[anywhere] * len(values),
        out_shape=[jax.ShapeDtypeStruct(value.shape, value.dtype) for value in values],
        input_output_aliases={at: at for at in range(len(values))},
        compiler_params=params(), cost_estimate=cost(0, 0), name="handed_on",
    )(*values, *later_than)


def gather_cotangent(cotangent, n_col):
    flips = list(range(0, n_col, 2))
    pieces = [send(cotangent, "col", flip, n_col) for flip in flips[1:]]
    pieces = [copied(cotangent, pieces[0])] + pieces
    pieces += [send(piece, "col", 1, n_col) for piece in pieces]
    return pieces, flips + [flip ^ 1 for flip in flips]


def body(n_row, n_col, activations, cotangent, down_weight, row_order):
    rows, hidden = activations.shape
    shard = cotangent.shape[0]
    mine_row, mine_col = lax.axis_index("row"), lax.axis_index("col")

    pieces, flips = gather_cotangent(cotangent, n_col)
    act_pieces = {o: send(activations, "row", o, n_row) for o in [*range(2, n_row, 2), 1]}
    act_pieces[0] = activations

    order = row_order.reshape(n_row, rows)
    order = jnp.concatenate([lax.dynamic_index_in_dim(order, mine_row ^ o, 0, keepdims=False) for o in range(n_row)])
    owner = mine_col ^ jnp.asarray(flips, jnp.int32)
    named = (owner[:, None] * shard + jnp.arange(shard, dtype=jnp.int32)[None, :]).reshape(-1)
    pick = (order[:, None] == named[None, :]).astype(jnp.bfloat16)

    tile = tile_of(hidden, 256)
    tiles = hidden // tile
    cut = tiles * 2 // 7
    aligned, own_a, sent_a = partial_sums(None, (pick, pieces), down_weight, tile, 0, cut, n_row, "sums_a")
    evens = range(2, n_row, 2)
    for o, piece in zip(evens, handed_on([act_pieces[o] for o in evens], [aligned])):
        act_pieces[o], act_pieces[o + 1] = piece, send(piece, "row", 1, n_row)
    got_a = [send(message, "row", o, n_row) for o, message in enumerate(sent_a, 1)]
    _, own_b, sent_b = partial_sums(aligned, None, down_weight, tile, cut, tiles - cut, n_row, "sums_b")
    sent_b = handed_on(sent_b, got_a)
    got_b = [send(message, "row", o, n_row) for o, message in enumerate(sent_b, 1)]
    weight_grad = weight_grads(aligned, [act_pieces[o] for o in range(n_row)])
    return weight_grad, totals([[own_a, *got_a], [own_b, *got_b]], [weight_grad])


def solution(mesh):
    in_specs = (P("row", "col"), P("col", "row"), P("col", "row"), P())
    out_specs = (P("col", "row"), P("row", "col"))
    fn = functools.partial(body, mesh.shape["row"], mesh.shape["col"])
    return jax.shard_map(fn, mesh=mesh, in_specs=in_specs, out_specs=out_specs, check_vma=False)
```

time: 92.9 us -> 90.4 us (0.973)
  the two profiles are of different devices: /device:TPU:0 before, /device:TPU:10 now
where the time goes in v3:
time: 90.4 us; the launch traced here: 90.3 us
  waiting for transfers between devices  37.5 us (41%)
  Pallas kernels  31.7 us (35%)
  starting transfers between devices  17.7 us (20%)
  local copies, waits for them, and re-layouts  1.8 us (2%)
  other arithmetic  0.91 us (1%)
    ppermute x16, waiting for transfers between devices, send(): return lax.ppermute(value, axis, [(i, i ^ flip) for i in range(size)])  37.5 us
    ppermute x16, starting transfers between devices, send(): return lax.ppermute(value, axis, [(i, i ^ flip) for i in range(size)])  17.7 us
    pallas_call x2, Pallas kernels, partial_sums(): pl.pallas_call(functools.partial(sums_kernel, 0 if aligned is not None el...  17.1 us
    pallas_call x1, Pallas kernels, weight_grads(): pl.pallas_call(weight_kernel, grid=(hidden // tile,), in_specs=[pl.BlockS...  13.3 us
  transfers between devices with their start and end apart: 16, of which 8 were waited for; matrix products, arithmetic and copies ran while one was open for 2% of the time, Pallas kernels for 34%

profile of v3, /device:TPU:10, one launch (start us, length us, event | category | flops | bytes accessed | tf_op | source)
XLA Modules:
  0.0 90.3 jit_solution(5130971469680515021)
XLA Ops:
  0.6 0.6 collective-permute-start
  1.2 1.5 %collective-permute-start.1 = (bf16[32,4096]{1,0:T(8,128)(2,1)}, bf16[32,4096]{1,0:T(8,128)(2,1)S(1)}, u32[]{:S(2)}, u32[]{:S(2)}) collective-permute-start(bf16[32,4096]{1,0:T(8,128)(2,1)} %value_ref.1), channel_id=1, source_target_pairs={{0,4},{1,5},{2,6},{3,7},{4,0},{5,1},{6,2},{7,3},{8,12},{9,13},{10,... | collective-permute-start | bytes 786440 | tf_op jit(solution)/shard_map/ppermute | solution.py:190
  2.7 1.4 %collective-permute-start.2 = (bf16[32,4096]{1,0:T(8,128)(2,1)}, bf16[32,4096]{1,0:T(8,128)(2,1)S(1)}, u32[]{:S(2)}, u32[]{:S(2)}) collective-permute-start(bf16[32,4096]{1,0:T(8,128)(2,1)} %value_ref.1), channel_id=1, source_target_pairs={{0,6},{1,7},{2,4},{3,5},{4,2},{5,3},{6,0},{7,1},{8,14},{9,15},{10,... | collective-permute-start | bytes 786440 | tf_op jit(solution)/shard_map/ppermute | solution.py:190
  4.2 2.6 %collective-permute-start.8 = (bf16[64,3584]{1,0:T(8,128)(2,1)}, bf16[64,3584]{1,0:T(8,128)(2,1)S(1)}, u32[]{:S(2)}, u32[]{:S(2)}) collective-permute-start(bf16[64,3584]{1,0:T(8,128)(2,1)} %refs_0_.1), channel_id=1, source_target_pairs={{0,16},{8,24},{16,0},{24,8},{1,17},{9,25},{17,1},{25,9},{2,18},{10... | collective-permute-start | bytes 1376264 | tf_op jit(solution)/shard_map/ppermute | solution.py:190
  6.8 0.8 reshape.24
  7.5 0.7 xor_multiply_fusion
  8.2 0.1 iota_add_fusion
  8.3 1.8 %collective-permute-done.later_ref.refs_2_ = bf16[32,4096]{1,0:T(8,128)(2,1)S(1)} collective-permute-done((bf16[32,4096]{1,0:T(8,128)(2,1)}, bf16[32,4096]{1,0:T(8,128)(2,1)S(1)}, u32[]{:S(2)}, u32[]{:S(2)}) %collective-permute-start) | collective-permute-done | bytes 262176 | tf_op jit(solution)/shard_map/ppermute | solution.py:190
  10.1 0.9 %copy-done.1 = bf16[32,4096]{1,0:T(8,128)(2,1)S(1)} copy-done((bf16[32,4096]{1,0:T(8,128)(2,1)S(1)}, bf16[32,4096]{1,0:T(8,128)(2,1)}, u32[]{:S(2)}) %copy-start.1) | copy-done | bytes 262168
  11.1 0.1 collective-permute-start.3
  11.1 0.5 collective-permute-start.4
  11.6 2.4 %collective-permute-done.1.refs_3_ = bf16[32,4096]{1,0:T(8,128)(2,1)S(1)} collective-permute-done((bf16[32,4096]{1,0:T(8,128)(2,1)}, bf16[32,4096]{1,0:T(8,128)(2,1)S(1)}, u32[]{:S(2)}, u32[]{:S(2)}) %collective-permute-start.1) | collective-permute-done | bytes 262176 | tf_op jit(solution)/shard_map/ppermute | solution.py:190
  14.0 1.5 %collective-permute-done.2.refs_4_ = bf16[32,4096]{1,0:T(8,128)(2,1)S(1)} collective-permute-done((bf16[32,4096]{1,0:T(8,128)(2,1)}, bf16[32,4096]{1,0:T(8,128)(2,1)S(1)}, u32[]{:S(2)}, u32[]{:S(2)}) %collective-permute-start.2) | collective-permute-done | bytes 262176 | tf_op jit(solution)/shard_map/ppermute | solution.py:190
  15.5 0.1 pad_add_fusion
  15.6 0.1 add.40
  15.7 0.1 compare_convert_fusion.refs_0_
  15.8 0.5 collective-permute-start.7
  16.3 0.7 collective-permute-done.6.refs_8_
  17.1 5.9 %sums_a.1 = (bf16[256,4096]{1,0:T(8,128)(2,1)S(1)}, f32[64,1024]{1,0:T(8,128)S(1)}, s16[64,1152]{1,0:T(8,128)(2,1)S(1)}, s16[64,1152]{1,0:T(8,128)(2,1)S(1)}, s16[64,1152]{1,0:T(8,128)(2,1)S(1)}) custom-call(bf16[256,256]{1,0:T(8,128)(2,1)S(1)} %compare_convert_fusion.refs_0_, bf16[32,4096]{1,0:T(8,128)(2,1)S(1)} %copied.1.refs_1_, ...), custom_call_target="tpu_custom_call" | custom-call | flops 2147483648 | bytes 8388608 | tf_op jit(solution)/shard_map/sums_a/pallas_call | solution.py:120
  23.0 2.8 %collective-permute-done.8.refs_0_ = bf16[64,3584]{1,0:T(8,128)(2,1)S(1)} collective-permute-done((bf16[64,3584]{1,0:T(8,128)(2,1)}, bf16[64,3584]{1,0:T(8,128)(2,1)S(1)}, u32[]{:S(2)}, u32[]{:S(2)}) %collective-permute-start.8) | collective-permute-done | bytes 458784 | tf_op jit(solution)/shard_map/ppermute | solution.py:190
  25.8 1.3 %collective-permute-start.9 = (bf16[64,3584]{1,0:T(8,128)(2,1)S(1)}, bf16[64,3584]{1,0:T(8,128)(2,1)S(1)}, u32[]{:S(2)}, u32[]{:S(2)}) collective-permute-start(bf16[64,3584]{1,0:T(8,128)(2,1)S(1)} %handed_on.2.refs_2_), channel_id=1, source_target_pairs={{0,8},{8,0},{16,24},{24,16},{1,9},{9,1},{17,25},{25,17},{2,10},{10... | collective-permute-start | bytes 1376264 | tf_op jit(solution)/shard_map/ppermute | solution.py:190
  27.1 0.7 collective-permute-start.10
  27.8 3.3 %collective-permute-start.11 = (s16[64,1152]{1,0:T(8,128)(2,1)S(1)}, s16[64,1152]{1,0:T(8,128)(2,1)S(1)}, u32[]{:S(2)}, u32[]{:S(2)}) collective-permute-start(s16[64,1152]{1,0:T(8,128)(2,1)S(1)} %get-tuple-element.17), channel_id=1, source_target_pairs={{0,16},{8,24},{16,0},{24,8},{1,17},{9,25},{17,1},{25,9},{2,18},{10... | collective-permute-start | bytes 442376 | tf_op jit(solution)/shard_map/ppermute | solution.py:190
  31.2 11.2 %sums_b.1 = (f32[64,2560]{1,0:T(8,128)S(1)}, s16[64,2688]{1,0:T(8,128)(2,1)S(1)}, s16[64,2688]{1,0:T(8,128)(2,1)S(1)}, s16[64,2688]{1,0:T(8,128)(2,1)S(1)}) custom-call(bf16[256,4096]{1,0:T(8,128)(2,1)S(1)} %get-tuple-element.14.refs_1_.aligned_ref.refs_0_, bf16[3584,4096]{1,0:T(8,128)(2,1)} %refs_2_.1, bf16[3584,4096]{1,0:T(8,128)(2,1)} %refs_2_.1), custom_call_target="tpu_custom_call" | custom-call | flops 5368709120 | bytes 20971520 | tf_op jit(solution)/shard_map/sums_b/pallas_call | solution.py:120
  42.3 11.3 %collective-permute-done.10.refs_3_.refs_1_ = s16[64,1152]{1,0:T(8,128)(2,1)S(1)} collective-permute-done((s16[64,1152]{1,0:T(8,128)(2,1)S(1)}, s16[64,1152]{1,0:T(8,128)(2,1)S(1)}, u32[]{:S(2)}, u32[]{:S(2)}) %collective-permute-start.10) | collective-permute-done | bytes 147488 | tf_op jit(solution)/shard_map/ppermute | solution.py:190
  53.7 2.5 %collective-permute-start.13 = (s16[64,2688]{1,0:T(8,128)(2,1)S(1)}, s16[64,2688]{1,0:T(8,128)(2,1)S(1)}, u32[]{:S(2)}, u32[]{:S(2)}) collective-permute-start(s16[64,2688]{1,0:T(8,128)(2,1)S(1)} %get-tuple-element.23), channel_id=1, source_target_pairs={{0,8},{8,0},{16,24},{24,16},{1,9},{9,1},{17,25},{25,17},{2,10},{10... | collective-permute-start | bytes 1032200 | tf_op jit(solution)/shard_map/ppermute | solution.py:190
  56.2 2.1 %collective-permute-start.14 = (s16[64,2688]{1,0:T(8,128)(2,1)S(1)}, s16[64,2688]{1,0:T(8,128)(2,1)S(1)}, u32[]{:S(2)}, u32[]{:S(2)}) collective-permute-start(s16[64,2688]{1,0:T(8,128)(2,1)S(1)} %get-tuple-element.24), channel_id=1, source_target_pairs={{0,16},{8,24},{16,0},{24,8},{1,17},{9,25},{17,1},{25,9},{2,18},{10... | collective-permute-start | bytes 1032200 | tf_op jit(solution)/shard_map/ppermute | solution.py:190
  58.3 0.5 collective-permute-start.15
  58.8 13.3 %weight_grads.1.refs_8_ = bf16[3584,4096]{1,0:T(8,128)(2,1)} custom-call(bf16[256,4096]{1,0:T(8,128)(2,1)S(1)} %get-tuple-element.14.refs_1_.aligned_ref.refs_0_, bf16[64,3584]{1,0:T(8,128)(2,1)S(1)} %copy-done, bf16[64,3584]{1,0:T(8,128)(2,1)S(1)} %collective-permute-done.7.refs_1_, bf16[64,3584]{1,0:T(8,128)(2,1)S(1)} %handed_on.2.refs_2_, ...), custom_call_target="tpu_custom_call" | custom-call | flops 7516192768 | bytes 29360128 | tf_op jit(solution)/shard_map/weight_grads/pallas_call | solution.py:145
  72.1 9.4 %collective-permute-done.14.refs_6_ = s16[64,2688]{1,0:T(8,128)(2,1)S(1)} collective-permute-done((s16[64,2688]{1,0:T(8,128)(2,1)S(1)}, s16[64,2688]{1,0:T(8,128)(2,1)S(1)}, u32[]{:S(2)}, u32[]{:S(2)}) %collective-permute-start.14) | collective-permute-done | bytes 344096 | tf_op jit(solution)/shard_map/ppermute | solution.py:190
  81.5 7.4 %collective-permute-done.15.refs_7_ = s16[64,2688]{1,0:T(8,128)(2,1)S(1)} collective-permute-done((s16[64,2688]{1,0:T(8,128)(2,1)S(1)}, s16[64,2688]{1,0:T(8,128)(2,1)S(1)}, u32[]{:S(2)}, u32[]{:S(2)}) %collective-permute-start.15) | collective-permute-done | bytes 344096 | tf_op jit(solution)/shard_map/ppermute | solution.py:190
  89.0 1.3 %totals.1 = bf16[64,3584]{1,0:T(8,128)(2,1)} custom-call(f32[64,1024]{1,0:T(8,128)S(1)} %get-tuple-element.15.refs_0_, s16[64,1152]{1,0:T(8,128)(2,1)S(1)} %collective-permute-done.10.refs_3_.refs_1_, s16[64,1152]{1,0:T(8,128)(2,1)S(1)} %collective-permute-done.11.refs_4_.refs_2_, s16[64,1152]{1,0:T(8,128)(2,1)S(1)} %collective-permute-done.12.refs_5_.refs_3_, ...), custom_call_target="tpu_custom_call" | custom-call | flops 9175040 | bytes 3211264 | tf_op jit(solution)/shard_map/totals/pallas_call | solution.py:177
  (18 shorter events, 0.1 us)
Async XLA Ops:
  0.6 9.5 %collective-permute-start = (bf16[32,4096]{1,0:T(8,128)(2,1)}, bf16[32,4096]{1,0:T(8,128)(2,1)S(1)}, u32[]{:S(2)}, u32[]{:S(2)}) collective-permute-start(bf16[32,4096]{1,0:T(8,128)(2,1)} %value_ref.1), channel_id=1, source_target_pairs={{0,2},{1,3},{2,0},{3,1},{4,6},{5,7},{6,4},{7,5},{8,10},{9,11},{10,... | collective-permute-start | bytes 786440 | tf_op jit(solution)/shard_map/ppermute | solution.py:190
  1.2 12.8 %collective-permute-start.1 = (bf16[32,4096]{1,0:T(8,128)(2,1)}, bf16[32,4096]{1,0:T(8,128)(2,1)S(1)}, u32[]{:S(2)}, u32[]{:S(2)}) collective-permute-start(bf16[32,4096]{1,0:T(8,128)(2,1)} %value_ref.1), channel_id=1, source_target_pairs={{0,4},{1,5},{2,6},{3,7},{4,0},{5,1},{6,2},{7,3},{8,12},{9,13},{10,... | collective-permute-start | bytes 786440 | tf_op jit(solution)/shard_map/ppermute | solution.py:190
  2.7 12.8 %collective-permute-start.2 = (bf16[32,4096]{1,0:T(8,128)(2,1)}, bf16[32,4096]{1,0:T(8,128)(2,1)S(1)}, u32[]{:S(2)}, u32[]{:S(2)}) collective-permute-start(bf16[32,4096]{1,0:T(8,128)(2,1)} %value_ref.1), channel_id=1, source_target_pairs={{0,6},{1,7},{2,4},{3,5},{4,2},{5,3},{6,0},{7,1},{8,14},{9,15},{10,... | collective-permute-start | bytes 786440 | tf_op jit(solution)/shard_map/ppermute | solution.py:190
  4.2 21.6 %collective-permute-start.8 = (bf16[64,3584]{1,0:T(8,128)(2,1)}, bf16[64,3584]{1,0:T(8,128)(2,1)S(1)}, u32[]{:S(2)}, u32[]{:S(2)}) collective-permute-start(bf16[64,3584]{1,0:T(8,128)(2,1)} %refs_0_.1), channel_id=1, source_target_pairs={{0,16},{8,24},{16,0},{24,8},{1,17},{9,25},{17,1},{25,9},{2,18},{10... | collective-permute-start | bytes 1376264 | tf_op jit(solution)/shard_map/ppermute | solution.py:190
  10.1 1.0 %copy-start.1 = (bf16[32,4096]{1,0:T(8,128)(2,1)S(1)}, bf16[32,4096]{1,0:T(8,128)(2,1)}, u32[]{:S(2)}) copy-start(bf16[32,4096]{1,0:T(8,128)(2,1)} %value_ref.1) | copy-start | bytes 786436
  11.1 4.7 %collective-permute-start.3 = (bf16[32,4096]{1,0:T(8,128)(2,1)S(1)}, bf16[32,4096]{1,0:T(8,128)(2,1)S(1)}, u32[]{:S(2)}, u32[]{:S(2)}) collective-permute-start(bf16[32,4096]{1,0:T(8,128)(2,1)S(1)} %copied.1.refs_1_), channel_id=1, source_target_pairs={{0,1},{1,0},{2,3},{3,2},{4,5},{5,4},{6,7},{7,6},{8,9},{9,8},{10,11... | collective-permute-start | bytes 786440 | tf_op jit(solution)/shard_map/ppermute | solution.py:190
  11.1 5.2 %collective-permute-start.4 = (bf16[32,4096]{1,0:T(8,128)(2,1)S(1)}, bf16[32,4096]{1,0:T(8,128)(2,1)S(1)}, u32[]{:S(2)}, u32[]{:S(2)}) collective-permute-start(bf16[32,4096]{1,0:T(8,128)(2,1)S(1)} %collective-permute-done.later_ref.refs_2_), channel_id=1, source_target_pairs={{0,1},{1,0},{2,3},{3,2},{4,5},{5,4},{6,7},{7,6},{8,9},{9,8},{10,11... | collective-permute-start | bytes 786440 | tf_op jit(solution)/shard_map/ppermute | solution.py:190
  14.0 2.3 %collective-permute-start.5 = (bf16[32,4096]{1,0:T(8,128)(2,1)S(1)}, bf16[32,4096]{1,0:T(8,128)(2,1)S(1)}, u32[]{:S(2)}, u32[]{:S(2)}) collective-permute-start(bf16[32,4096]{1,0:T(8,128)(2,1)S(1)} %collective-permute-done.1.refs_3_), channel_id=1, source_target_pairs={{0,1},{1,0},{2,3},{3,2},{4,5},{5,4},{6,7},{7,6},{8,9},{9,8},{10,11... | collective-permute-start | bytes 786440 | tf_op jit(solution)/shard_map/ppermute | solution.py:190
  15.5 1.5 %collective-permute-start.6 = (bf16[32,4096]{1,0:T(8,128)(2,1)S(1)}, bf16[32,4096]{1,0:T(8,128)(2,1)S(1)}, u32[]{:S(2)}, u32[]{:S(2)}) collective-permute-start(bf16[32,4096]{1,0:T(8,128)(2,1)S(1)} %collective-permute-done.2.refs_4_), channel_id=1, source_target_pairs={{0,1},{1,0},{2,3},{3,2},{4,5},{5,4},{6,7},{7,6},{8,9},{9,8},{10,11... | collective-permute-start | bytes 786440 | tf_op jit(solution)/shard_map/ppermute | solution.py:190
  15.8 43.0 %collective-permute-start.7 = (bf16[64,3584]{1,0:T(8,128)(2,1)}, bf16[64,3584]{1,0:T(8,128)(2,1)S(1)}, u32[]{:S(2)}, u32[]{:S(2)}) collective-permute-start(bf16[64,3584]{1,0:T(8,128)(2,1)} %refs_0_.1), channel_id=1, source_target_pairs={{0,8},{8,0},{16,24},{24,16},{1,9},{9,1},{17,25},{25,17},{2,10},{10... | collective-permute-start | bytes 1376264 | tf_op jit(solution)/shard_map/ppermute | solution.py:190
  25.8 33.0 %collective-permute-start.9 = (bf16[64,3584]{1,0:T(8,128)(2,1)S(1)}, bf16[64,3584]{1,0:T(8,128)(2,1)S(1)}, u32[]{:S(2)}, u32[]{:S(2)}) collective-permute-start(bf16[64,3584]{1,0:T(8,128)(2,1)S(1)} %handed_on.2.refs_2_), channel_id=1, source_target_pairs={{0,8},{8,0},{16,24},{24,16},{1,9},{9,1},{17,25},{25,17},{2,10},{10... | collective-permute-start | bytes 1376264 | tf_op jit(solution)/shard_map/ppermute | solution.py:190
  27.1 26.6 %collective-permute-start.10 = (s16[64,1152]{1,0:T(8,128)(2,1)S(1)}, s16[64,1152]{1,0:T(8,128)(2,1)S(1)}, u32[]{:S(2)}, u32[]{:S(2)}) collective-permute-start(s16[64,1152]{1,0:T(8,128)(2,1)S(1)} %get-tuple-element.16), channel_id=1, source_target_pairs={{0,8},{8,0},{16,24},{24,16},{1,9},{9,1},{17,25},{25,17},{2,10},{10... | collective-permute-start | bytes 442376 | tf_op jit(solution)/shard_map/ppermute | solution.py:190
  27.8 25.9 %collective-permute-start.11 = (s16[64,1152]{1,0:T(8,128)(2,1)S(1)}, s16[64,1152]{1,0:T(8,128)(2,1)S(1)}, u32[]{:S(2)}, u32[]{:S(2)}) collective-permute-start(s16[64,1152]{1,0:T(8,128)(2,1)S(1)} %get-tuple-element.17), channel_id=1, source_target_pairs={{0,16},{8,24},{16,0},{24,8},{1,17},{9,25},{17,1},{25,9},{2,18},{10... | collective-permute-start | bytes 442376 | tf_op jit(solution)/shard_map/ppermute | solution.py:190
  31.2 27.7 %copy-start = (bf16[64,3584]{1,0:T(8,128)(2,1)S(1)}, bf16[64,3584]{1,0:T(8,128)(2,1)}, u32[]{:S(2)}) copy-start(bf16[64,3584]{1,0:T(8,128)(2,1)} %refs_0_.1) | copy-start | bytes 1376260
  31.2 22.5 %collective-permute-start.12 = (s16[64,1152]{1,0:T(8,128)(2,1)S(1)}, s16[64,1152]{1,0:T(8,128)(2,1)S(1)}, u32[]{:S(2)}, u32[]{:S(2)}) collective-permute-start(s16[64,1152]{1,0:T(8,128)(2,1)S(1)} %get-tuple-element.18), channel_id=1, source_target_pairs={{0,24},{8,16},{16,8},{24,0},{1,25},{9,17},{17,9},{25,1},{2,26},{10... | collective-permute-start | bytes 442376 | tf_op jit(solution)/shard_map/ppermute | solution.py:190
  53.7 18.4 %collective-permute-start.13 = (s16[64,2688]{1,0:T(8,128)(2,1)S(1)}, s16[64,2688]{1,0:T(8,128)(2,1)S(1)}, u32[]{:S(2)}, u32[]{:S(2)}) collective-permute-start(s16[64,2688]{1,0:T(8,128)(2,1)S(1)} %get-tuple-element.23), channel_id=1, source_target_pairs={{0,8},{8,0},{16,24},{24,16},{1,9},{9,1},{17,25},{25,17},{2,10},{10... | collective-permute-start | bytes 1032200 | tf_op jit(solution)/shard_map/ppermute | solution.py:190
  56.2 25.3 %collective-permute-start.14 = (s16[64,2688]{1,0:T(8,128)(2,1)S(1)}, s16[64,2688]{1,0:T(8,128)(2,1)S(1)}, u32[]{:S(2)}, u32[]{:S(2)}) collective-permute-start(s16[64,2688]{1,0:T(8,128)(2,1)S(1)} %get-tuple-element.24), channel_id=1, source_target_pairs={{0,16},{8,24},{16,0},{24,8},{1,17},{9,25},{17,1},{25,9},{2,18},{10... | collective-permute-start | bytes 1032200 | tf_op jit(solution)/shard_map/ppermute | solution.py:190
  58.3 30.7 %collective-permute-start.15 = (s16[64,2688]{1,0:T(8,128)(2,1)S(1)}, s16[64,2688]{1,0:T(8,128)(2,1)S(1)}, u32[]{:S(2)}, u32[]{:S(2)}) collective-permute-start(s16[64,2688]{1,0:T(8,128)(2,1)S(1)} %get-tuple-element.25), channel_id=1, source_target_pairs={{0,24},{8,16},{16,8},{24,0},{1,25},{9,17},{17,9},{25,1},{2,26},{10... | collective-permute-start | bytes 1032200 | tf_op jit(solution)/shard_map/ppermute | solution.py:190

commit v4 on v3

v4 whole, which is shorter than its diff:
```python
import functools

import jax
import jax.numpy as jnp
from jax import lax
from jax.experimental import pallas as pl
from jax.experimental.pallas import tpu as pltpu
from jax.sharding import PartitionSpec as P

LANES = 128
STEPS_PER_OCTAVE = 128.0
TOP = 32766.0
LEAST = 2.0 ** -120
VMEM_LIMIT = 48 * 1024 * 1024
SUB = 256


def tile_of(size, largest):
    tile = largest
    while size % tile:
        tile //= 2
    return tile


def dot(left, right, dims):
    return lax.dot_general(left, right, (dims, ((), ())), preferred_element_type=jnp.float32)


def encode(values):
    most = jnp.maximum(jnp.max(jnp.abs(values), axis=1, keepdims=True), LEAST)
    level = jnp.ceil(jnp.log2(most) * STEPS_PER_OCTAVE) + 1.0
    codes = jnp.round(values * jnp.exp2(level * (-1.0 / STEPS_PER_OCTAVE)) * TOP)
    return codes.astype(jnp.int32).astype(jnp.int16), level


def decode(codes, levels):
    scale = jnp.exp2(levels.astype(jnp.int32).astype(jnp.float32) * (1.0 / STEPS_PER_OCTAVE)) * (1.0 / TOP)
    return codes.astype(jnp.int32).astype(jnp.float32) * scale


def to_levels(levels):
    return levels.astype(jnp.int32).astype(jnp.int16)


def params():
    return pltpu.CompilerParams(vmem_limit_bytes=VMEM_LIMIT)


def cost(flops, moved):
    return pl.CostEstimate(flops=flops, bytes_accessed=moved, transcendentals=0)


def align_rows(pick_ref, pieces, aligned_ref):
    depth = aligned_ref.shape[1]
    chunk = tile_of(depth, 512)
    for at in range(0, depth, chunk):
        cols = slice(at, at + chunk)
        gathered = jnp.concatenate([piece[:, cols] for piece in pieces], axis=0)
        aligned_ref[:, cols] = dot(pick_ref[...], gathered, ((1,), (0,))).astype(jnp.bfloat16)


def sums_kernel(n_pieces, n_blocks, n_later, tile, *refs):
    refs = list(refs)
    if n_pieces:
        pick_ref = refs.pop(0)
        pieces = [refs.pop(0) for _ in range(n_pieces)]
        blocks = [refs.pop(0) for _ in range(n_blocks)]
        del refs[:n_later]
        aligned_ref = refs.pop(0)
    else:
        aligned_ref = refs.pop(0)
        blocks = [refs.pop(0) for _ in range(n_blocks)]
        del refs[:n_later]
    kept_ref, sent_ref, levels_ref = refs
    step = pl.program_id(0)
    rows = kept_ref.shape[0]
    width = sent_ref.shape[1] - LANES

    @pl.when(step == 0)
    def _():
        if n_pieces:
            align_rows(pick_ref, pieces, aligned_ref)
        levels_ref[...] = jnp.zeros_like(levels_ref)

    lane = lax.broadcasted_iota(jnp.int32, levels_ref.shape, 1)
    levels = levels_ref[...]
    for part, block in enumerate(blocks):
        values = dot(aligned_ref[...], block[...], ((1,), (1,)))
        kept_ref[:, part * tile:(part + 1) * tile] = values[:rows]
        codes, level = encode(values[rows:])
        levels = jnp.where(lane == step * n_blocks + part, level, levels)
        cols = pl.ds(pl.multiple_of((step * n_blocks + part) * tile, tile), tile)
        sent_ref[:, cols] = codes
    levels_ref[...] = levels

    @pl.when(step == pl.num_programs(0) - 1)
    def _():
        sent_ref[:, width:] = to_levels(levels)


def partial_sums(aligned, align, weight, tile, first, count, later_than, name):
    depth = weight.shape[1]
    width = count * tile
    whole = lambda i: (0, 0)
    operands = [align[0], *align[1]] if aligned is None else [aligned]
    total = operands[0].shape[0]
    half = total // 2
    n_blocks = 2 if count % 2 == 0 and first % 2 == 0 else 1
    block_at = lambda part: (lambda i: (i * n_blocks + first + part, 0))
    in_specs = [pl.BlockSpec(operand.shape, whole) for operand in operands]
    in_specs += [pl.BlockSpec((tile, depth), block_at(part)) for part in range(n_blocks)]
    in_specs += [pl.BlockSpec(memory_space=pl.ANY)] * len(later_than)
    out_specs = [pl.BlockSpec((half, n_blocks * tile), lambda i: (0, i)), pl.BlockSpec((half, width + LANES), whole)]
    out_shape = [jax.ShapeDtypeStruct((half, width), jnp.float32), jax.ShapeDtypeStruct((half, width + LANES), jnp.int16)]
    if aligned is None:
        out_specs.insert(0, pl.BlockSpec((total, depth), whole))
        out_shape.insert(0, jax.ShapeDtypeStruct((total, depth), jnp.bfloat16))
    outs = pl.pallas_call(
        functools.partial(sums_kernel, 0 if aligned is not None else len(align[1]), n_blocks, len(later_than), tile),
        grid=(count // n_blocks,), in_specs=in_specs, out_specs=out_specs, out_shape=out_shape,
        scratch_shapes=[pltpu.VMEM((half, LANES), jnp.float32)],
        compiler_params=params(), cost_estimate=cost(2 * total * width * depth, 2 * width * depth), name=name,
    )(*operands, *[weight] * n_blocks, *later_than)
    return outs if aligned is None else (aligned, *outs)


def weight_kernel(n_pieces, n_later, aligned_ref, *refs):
    refs = list(refs)
    pieces = [refs.pop(0) for _ in range(n_pieces)]
    out_ref, left_ref = refs[n_later:]

    @pl.when(pl.program_id(0) == 0)
    def _():
        if n_pieces == 1:
            left_ref[...] = pieces[0][...]
        else:
            left_ref[...] = jnp.concatenate([piece[...] for piece in pieces], axis=0).T

    out_ref[...] = dot(left_ref[...], aligned_ref[...], ((1,), (0,))).astype(jnp.bfloat16)


def weight_grads(aligned, pieces, part, parts, filled, later_than):
    total, depth = aligned.shape
    hidden = pieces[0].size * len(pieces) // total
    tile = tile_of(depth // parts, 512)
    count = depth // parts // tile
    whole = lambda i: (0, 0)
    here = lambda i: (0, i + part * count)
    later = ([] if filled is None else [filled]) + list(later_than)
    return pl.pallas_call(
        functools.partial(weight_kernel, len(pieces), len(later)),
        grid=(count,),
        in_specs=[pl.BlockSpec((total, tile), here)] + [pl.BlockSpec(piece.shape, whole) for piece in pieces]
        + [pl.BlockSpec(memory_space=pl.ANY)] * len(later),
        out_specs=[pl.BlockSpec((hidden, tile), here), pl.BlockSpec((hidden, total), whole)],
        out_shape=[jax.ShapeDtypeStruct((hidden, depth), jnp.bfloat16), jax.ShapeDtypeStruct((hidden, total), jnp.bfloat16)],
        input_output_aliases={} if filled is None else {1 + len(pieces): 0},
        compiler_params=params(), cost_estimate=cost(2 * total * hidden * depth // parts, 2 * hidden * depth // parts),
        name="weight_grads",
    )(aligned, *pieces, *later)


def fold_kernel(kept_ref, got_ref, *refs):
    n_passed = (len(refs) - 2) // 2
    next_ref, sent_ref = refs[n_passed:n_passed + 2]
    width = kept_ref.shape[1]
    half = next_ref.shape[0]
    sub = tile_of(width, SUB)
    lane = lax.broadcasted_iota(jnp.int32, (half, LANES), 1)
    levels = jnp.zeros(lane.shape, jnp.float32)
    got_levels = got_ref[:, width:]
    for at in range(width // sub):
        cols = slice(at * sub, (at + 1) * sub)
        total = kept_ref[:, cols] + decode(got_ref[:, cols], got_levels[:, at:at + 1])
        next_ref[:, cols] = total[:half]
        codes, level = encode(total[half:])
        sent_ref[:, cols] = codes
        levels = jnp.where(lane == at, level, levels)
    sent_ref[:, width:] = to_levels(levels)


def fold(kept, got, passed):
    vmem, anywhere = pl.BlockSpec(memory_space=pltpu.VMEM), pl.BlockSpec(memory_space=pl.ANY)
    rows, width = kept.shape
    kept, sent, *passed = pl.pallas_call(
        fold_kernel,
        in_specs=[vmem] * 2 + [anywhere] * len(passed),
        out_specs=[vmem] * 2 + [anywhere] * len(passed),
        out_shape=[jax.ShapeDtypeStruct((rows // 2, width), kept.dtype), jax.ShapeDtypeStruct((rows // 2, got.shape[1]), got.dtype)]
        + [jax.ShapeDtypeStruct(array.shape, array.dtype) for array in passed],
        input_output_aliases={2 + at: 2 + at for at in range(len(passed))},
        compiler_params=params(), cost_estimate=cost(kept.size * 20, kept.size * 12), name="fold",
    )(kept, got, *passed)
    return kept, sent, passed


def total_kernel(n_parts, *refs):
    out_ref = refs[-1]
    base = 0
    for kept_ref, got_ref in zip(refs[:2 * n_parts:2], refs[1:2 * n_parts:2]):
        width = kept_ref.shape[1]
        sub = tile_of(width, SUB)
        got_levels = got_ref[:, width:]
        for at in range(width // sub):
            cols = slice(at * sub, (at + 1) * sub)
            total = kept_ref[:, cols] + decode(got_ref[:, cols], got_levels[:, at:at + 1])
            out_ref[:, base + at * sub:base + (at + 1) * sub] = total.astype(jnp.bfloat16)
        base += width


def totals(parts, later_than):
    rows = parts[0][0].shape[0]
    hidden = sum(part[0].shape[1] for part in parts)
    flat = [array for part in parts for array in part]
    return pl.pallas_call(
        functools.partial(total_kernel, len(parts)),
        in_specs=[pl.BlockSpec(memory_space=pltpu.VMEM)] * len(flat) + [pl.BlockSpec(memory_space=pl.ANY)] * len(later_than),
        out_shape=jax.ShapeDtypeStruct((rows, hidden), jnp.bfloat16),
        compiler_params=params(), cost_estimate=cost(rows * hidden * 20, rows * hidden * 8), name="totals",
    )(*flat, *later_than)


def send(value, axis, flip, size):
    return lax.ppermute(value, axis, [(i, i ^ flip) for i in range(size)])


def stack_kernel(n_values, *refs):
    out_ref = refs[-1]
    rows = refs[0].shape[0]
    for at, ref in enumerate(refs[:n_values]):
        out_ref[at * rows:(at + 1) * rows] = ref[...]


def stacked(values, later_than=()):
    rows, width = values[0].shape
    return pl.pallas_call(
        functools.partial(stack_kernel, len(values)),
        in_specs=[pl.BlockSpec(memory_space=pltpu.VMEM)] * len(values) + [pl.BlockSpec(memory_space=pl.ANY)] * len(later_than),
        out_shape=jax.ShapeDtypeStruct((len(values) * rows, width), values[0].dtype),
        compiler_params=params(), cost_estimate=cost(0, 4 * len(values) * rows * width), name="stacked",
    )(*values, *later_than)


def same_kernel(*refs):
    pass


def handed_on(values, later_than):
    anywhere = pl.BlockSpec(memory_space=pl.ANY)
    return pl.pallas_call(
        same_kernel,
        in_specs=[anywhere] * (len(values) + len(later_than)), out_specs=[anywhere] * len(values),
        out_shape=[jax.ShapeDtypeStruct(value.shape, value.dtype) for value in values],
        input_output_aliases={at: at for at in range(len(values))},
        compiler_params=params(), cost_estimate=cost(0, 0), name="handed_on",
    )(*values, *later_than)


def gather_cotangent(cotangent, n_col):
    flips = list(range(0, n_col, 2))
    pieces = [cotangent] + [send(cotangent, "col", flip, n_col) for flip in flips[1:]]
    stacks = [stacked(pieces[:2])]
    stacks.append(stacked(pieces[2:], stacks))
    stacks += [send(stack, "col", 1, n_col) for stack in stacks]
    return stacks, flips + [flip ^ 1 for flip in flips]


def halving_order(size):
    order = [0]
    while len(order) < size:
        order = [2 * o for o in order] + [2 * o + 1 for o in order]
    return order


def body(n_row, n_col, activations, cotangent, down_weight, row_order):
    rows, hidden = activations.shape
    shard = cotangent.shape[0]
    mine_row, mine_col = lax.axis_index("row"), lax.axis_index("col")
    offsets = halving_order(n_row)

    pieces, flips = gather_cotangent(cotangent, n_col)
    act_pieces = {o: send(activations, "row", o, n_row) for o in [1, *range(2, n_row, 2)]}
    act_pieces[0] = activations

    order = row_order.reshape(n_row, rows)
    order = jnp.concatenate([lax.dynamic_index_in_dim(order, mine_row ^ o, 0, keepdims=False) for o in offsets])
    owner = mine_col ^ jnp.asarray(flips, jnp.int32)
    named = (owner[:, None] * shard + jnp.arange(shard, dtype=jnp.int32)[None, :]).reshape(-1)
    pick = (order[:, None] == named[None, :]).astype(jnp.bfloat16)

    tile = tile_of(hidden, 256)
    tiles = hidden // tile
    cut = tiles * 3 // 7
    aligned, kept_a, sent_a = partial_sums(None, (pick, pieces), down_weight, tile, 0, cut, [act_pieces[1]], "sums_a")
    got_a = send(sent_a, "row", 1, n_row)
    evens = range(2, n_row, 2)
    for o, piece in zip(evens, handed_on([act_pieces[o] for o in evens], [aligned])):
        act_pieces[o], act_pieces[o + 1] = piece, send(piece, "row", 1, n_row)
    _, kept_b, sent_b = partial_sums(aligned, None, down_weight, tile, cut, tiles - cut, [], "sums_b")

    passed = [sent_b]
    step = 2
    while step < n_row:
        kept_a, sent_a, passed = fold(kept_a, got_a, passed)
        got_a = send(sent_a, "row", step, n_row)
        step *= 2
    got_b = send(passed[0], "row", 1, n_row)
    act_pieces = [act_pieces[o] for o in offsets]
    grad, turned = weight_grads(aligned, act_pieces, 0, 2, None, [sent_a])
    step = 2
    while step < n_row:
        kept_b, sent_b, _ = fold(kept_b, got_b, [])
        got_b = send(sent_b, "row", step, n_row)
        step *= 2
    weight_grad, _ = weight_grads(aligned, [turned], 1, 2, grad, [sent_b])
    return weight_grad, totals([[kept_a, got_a], [kept_b, got_b]], [weight_grad])


def solution(mesh):
    in_specs = (P("row", "col"), P("col", "row"), P("col", "row"), P())
    out_specs = (P("col", "row"), P("row", "col"))
    fn = functools.partial(body, mesh.shape["row"], mesh.shape["col"])
    return jax.shard_map(fn, mesh=mesh, in_specs=in_specs, out_specs=out_specs, check_vma=False)
```

time: 90.4 us -> 86.2 us (0.954)
  the two profiles are of different devices: /device:TPU:10 before, /device:TPU:0 now
where the time goes in v4:
time: 86.2 us; the launch traced here: 86 us
  Pallas kernels  34.9 us (40%)
  waiting for transfers between devices  31.7 us (37%)
  starting transfers between devices  16 us (19%)
  local copies, waits for them, and re-layouts  1.8 us (2%)
  other arithmetic  0.91 us (1%)
    ppermute x12, waiting for transfers between devices, send(): return lax.ppermute(value, axis, [(i, i ^ flip) for i in range(size)])  31.7 us
    pallas_call x2, Pallas kernels, partial_sums(): pl.pallas_call(functools.partial(sums_kernel, 0 if aligned is not None el...  17.1 us
    ppermute x12, starting transfers between devices, send(): return lax.ppermute(value, axis, [(i, i ^ flip) for i in range(size)])  16 us
    pallas_call x2, Pallas kernels, weight_grads(): pl.pallas_call(functools.partial(weight_kernel, len(pieces), len(later)),...  15.4 us
  transfers between devices with their start and end apart: 12, of which 7 were waited for; matrix products, arithmetic and copies ran while one was open for 2% of the time, Pallas kernels for 39%

profile of v4, /device:TPU:0, one launch (start us, length us, event | category | flops | bytes accessed | tf_op | source)
XLA Modules:
  0.0 86.0 jit_solution(2690493829215123166)
XLA Ops:
  0.6 3.0 %collective-permute-start = (bf16[32,4096]{1,0:T(8,128)(2,1)}, bf16[32,4096]{1,0:T(8,128)(2,1)S(1)}, u32[]{:S(2)}, u32[]{:S(2)}) collective-permute-start(bf16[32,4096]{1,0:T(8,128)(2,1)} %refs_0_.2), channel_id=1, source_target_pairs={{0,2},{1,3},{2,0},{3,1},{4,6},{5,7},{6,4},{7,5},{8,10},{9,11},{10,... | collective-permute-start | bytes 786440 | tf_op jit(solution)/shard_map/ppermute | solution.py:224
  3.6 1.5 %collective-permute-start.1 = (bf16[32,4096]{1,0:T(8,128)(2,1)}, bf16[32,4096]{1,0:T(8,128)(2,1)S(1)}, u32[]{:S(2)}, u32[]{:S(2)}) collective-permute-start(bf16[32,4096]{1,0:T(8,128)(2,1)} %refs_0_.2), channel_id=1, source_target_pairs={{0,4},{1,5},{2,6},{3,7},{4,0},{5,1},{6,2},{7,3},{8,12},{9,13},{10,... | collective-permute-start | bytes 786440 | tf_op jit(solution)/shard_map/ppermute | solution.py:224
  5.2 2.0 %collective-permute-start.5 = (bf16[64,3584]{1,0:T(8,128)(2,1)}, bf16[64,3584]{1,0:T(8,128)(2,1)S(1)}, u32[]{:S(2)}, u32[]{:S(2)}) collective-permute-start(bf16[64,3584]{1,0:T(8,128)(2,1)} %refs_0_.3), channel_id=1, source_target_pairs={{0,8},{8,0},{16,24},{24,16},{1,9},{9,1},{17,25},{25,17},{2,10},{10... | collective-permute-start | bytes 1376264 | tf_op jit(solution)/shard_map/ppermute | solution.py:224
  7.2 2.6 %collective-permute-start.6 = (bf16[64,3584]{1,0:T(8,128)(2,1)}, bf16[64,3584]{1,0:T(8,128)(2,1)S(1)}, u32[]{:S(2)}, u32[]{:S(2)}) collective-permute-start(bf16[64,3584]{1,0:T(8,128)(2,1)} %refs_0_.3), channel_id=1, source_target_pairs={{0,16},{8,24},{16,0},{24,8},{1,17},{9,25},{17,1},{25,9},{2,18},{10... | collective-permute-start | bytes 1376264 | tf_op jit(solution)/shard_map/ppermute | solution.py:224
  9.8 0.7 xor_multiply_fusion
  10.5 0.5 collective-permute-done.refs_1_
  11.0 0.9 %copy-done = bf16[32,4096]{1,0:T(8,128)(2,1)S(1)} copy-done((bf16[32,4096]{1,0:T(8,128)(2,1)S(1)}, bf16[32,4096]{1,0:T(8,128)(2,1)}, u32[]{:S(2)}) %copy-start) | copy-done | bytes 262168
  12.0 0.1 collective-permute-start.3
  12.0 5.2 %collective-permute-done.1.refs_0_ = bf16[32,4096]{1,0:T(8,128)(2,1)S(1)} collective-permute-done((bf16[32,4096]{1,0:T(8,128)(2,1)}, bf16[32,4096]{1,0:T(8,128)(2,1)S(1)}, u32[]{:S(2)}, u32[]{:S(2)}) %collective-permute-start.1) | collective-permute-done | bytes 262176 | tf_op jit(solution)/shard_map/ppermute | solution.py:224
  17.3 0.1 collective-permute-start.4
  17.3 0.1 iota_add_fusion
  17.4 0.8 reshape.24
  18.2 0.1 add.40
  18.3 0.1 pad_add_fusion
  18.3 0.1 compare_convert_fusion.refs_0_
  18.5 8.3 %collective-permute-done.5.refs_7_.refs_2_ = bf16[64,3584]{1,0:T(8,128)(2,1)S(1)} collective-permute-done((bf16[64,3584]{1,0:T(8,128)(2,1)}, bf16[64,3584]{1,0:T(8,128)(2,1)S(1)}, u32[]{:S(2)}, u32[]{:S(2)}) %collective-permute-start.5) | collective-permute-done | bytes 458784 | tf_op jit(solution)/shard_map/ppermute | solution.py:224
  26.8 8.1 %sums_a.1 = (bf16[256,4096]{1,0:T(8,128)(2,1)S(1)}, f32[128,1536]{1,0:T(8,128)S(1)}, s16[128,1664]{1,0:T(8,128)(2,1)S(1)}) custom-call(bf16[256,256]{1,0:T(8,128)(2,1)S(1)} %compare_convert_fusion.refs_0_, bf16[64,4096]{1,0:T(8,128)(2,1)S(1)} %stacked.2.refs_2_.refs_1_, bf16[64,4096]{1,0:T(8,128)(2,1)S(1)} %stacked.3.refs_2_, ...), custom_call_target="tpu_custom_call" | custom-call | flops 3221225472 | bytes 12582912 | tf_op jit(solution)/shard_map/sums_a/pallas_call | solution.py:118
  34.9 0.1 collective-permute-start.8
  35.0 2.0 %collective-permute-start.7 = (bf16[64,3584]{1,0:T(8,128)(2,1)S(1)}, bf16[64,3584]{1,0:T(8,128)(2,1)S(1)}, u32[]{:S(2)}, u32[]{:S(2)}) collective-permute-start(bf16[64,3584]{1,0:T(8,128)(2,1)S(1)} %handed_on.1.refs_1_), channel_id=1, source_target_pairs={{0,8},{8,0},{16,24},{24,16},{1,9},{9,1},{17,25},{25,17},{2,10},{10... | collective-permute-start | bytes 1376264 | tf_op jit(solution)/shard_map/ppermute | solution.py:224
  37.0 9.0 %sums_b.1 = (f32[128,2048]{1,0:T(8,128)S(1)}, s16[128,2176]{1,0:T(8,128)(2,1)S(1)}) custom-call(bf16[256,4096]{1,0:T(8,128)(2,1)S(1)} %get-tuple-element.15.refs_1_.refs_0_.aligned_ref, bf16[3584,4096]{1,0:T(8,128)(2,1)} %refs_2_.1, bf16[3584,4096]{1,0:T(8,128)(2,1)} %refs_2_.1), custom_call_target="tpu_custom_call" | custom-call | flops 4294967296 | bytes 16777216 | tf_op jit(solution)/shard_map/sums_b/pallas_call | solution.py:118
  46.0 1.7 %collective-permute-done.8.got_ref = s16[128,1664]{1,0:T(8,128)(2,1)S(1)} collective-permute-done((s16[128,1664]{1,0:T(8,128)(2,1)S(1)}, s16[128,1664]{1,0:T(8,128)(2,1)S(1)}, u32[]{:S(2)}, u32[]{:S(2)}) %collective-permute-start.8) | collective-permute-done | bytes 426016 | tf_op jit(solution)/shard_map/ppermute | solution.py:224
  47.7 0.6 fold.2
  48.3 0.1 collective-permute-start.9
  48.4 3.2 %collective-permute-start.10 = (s16[64,1664]{1,0:T(8,128)(2,1)S(1)}, s16[64,1664]{1,0:T(8,128)(2,1)S(1)}, u32[]{:S(2)}, u32[]{:S(2)}) collective-permute-start(s16[64,1664]{1,0:T(8,128)(2,1)S(1)} %get-tuple-element.19.refs_4_), channel_id=1, source_target_pairs={{0,16},{8,24},{16,0},{24,8},{1,17},{9,25},{17,1},{25,9},{2,18},{10... | collective-permute-start | bytes 638984 | tf_op jit(solution)/shard_map/ppermute | solution.py:224
  51.6 10.5 %collective-permute-done.7.refs_3_ = bf16[64,3584]{1,0:T(8,128)(2,1)S(1)} collective-permute-done((bf16[64,3584]{1,0:T(8,128)(2,1)S(1)}, bf16[64,3584]{1,0:T(8,128)(2,1)S(1)}, u32[]{:S(2)}, u32[]{:S(2)}) %collective-permute-start.7) | collective-permute-done | bytes 458784 | tf_op jit(solution)/shard_map/ppermute | solution.py:224
  62.1 7.7 %weight_grads.2 = (bf16[3584,4096]{1,0:T(8,128)(2,1)}, bf16[3584,256]{1,0:T(8,128)(2,1)S(1)}) custom-call(bf16[256,4096]{1,0:T(8,128)(2,1)S(1)} %get-tuple-element.15.refs_1_.refs_0_.aligned_ref, bf16[64,3584]{1,0:T(8,128)(2,1)S(1)} %copy-done.1, bf16[64,3584]{1,0:T(8,128)(2,1)S(1)} %handed_on.1.refs_1_, ...), custom_call_target="tpu_custom_call" | custom-call | flops 3758096384 | bytes 14680064 | tf_op jit(solution)/shard_map/weight_grads/pallas_call | solution.py:150
  69.8 1.6 %collective-permute-done.9.got_ref = s16[128,2176]{1,0:T(8,128)(2,1)S(1)} collective-permute-done((s16[128,2176]{1,0:T(8,128)(2,1)S(1)}, s16[128,2176]{1,0:T(8,128)(2,1)S(1)}, u32[]{:S(2)}, u32[]{:S(2)}) %collective-permute-start.9) | collective-permute-done | bytes 557088 | tf_op jit(solution)/shard_map/ppermute | solution.py:224
  71.4 0.8 fold.3
  72.1 1.3 %collective-permute-start.11 = (s16[64,2176]{1,0:T(8,128)(2,1)S(1)}, s16[64,2176]{1,0:T(8,128)(2,1)S(1)}, u32[]{:S(2)}, u32[]{:S(2)}) collective-permute-start(s16[64,2176]{1,0:T(8,128)(2,1)S(1)} %get-tuple-element.24.refs_2_), channel_id=1, source_target_pairs={{0,16},{8,24},{16,0},{24,8},{1,17},{9,25},{17,1},{25,9},{2,18},{10... | collective-permute-start | bytes 835592 | tf_op jit(solution)/shard_map/ppermute | solution.py:224
  73.5 7.7 %weight_grads.3 = (bf16[3584,4096]{1,0:T(8,128)(2,1)}, bf16[3584,256]{1,0:T(8,128)(2,1)}) custom-call(bf16[256,4096]{1,0:T(8,128)(2,1)S(1)} %get-tuple-element.15.refs_1_.refs_0_.aligned_ref, bf16[3584,256]{1,0:T(8,128)(2,1)S(1)} %get-tuple-element.20.refs_0_, bf16[3584,4096]{1,0:T(8,128)(2,1)} %get-tuple-element.21.refs_1_, ...), custom_call_target="tpu_custom_call", output_to_operand_aliasing={{0}: (2, {})} | custom-call | flops 3758096384 | bytes 14680064 | tf_op jit(solution)/shard_map/weight_grads/pallas_call | solution.py:150
  81.2 3.8 %collective-permute-done.11.refs_3_ = s16[64,2176]{1,0:T(8,128)(2,1)S(1)} collective-permute-done((s16[64,2176]{1,0:T(8,128)(2,1)S(1)}, s16[64,2176]{1,0:T(8,128)(2,1)S(1)}, u32[]{:S(2)}, u32[]{:S(2)}) %collective-permute-start.11) | collective-permute-done | bytes 278560 | tf_op jit(solution)/shard_map/ppermute | solution.py:224
  85.1 1.0 %totals.1 = bf16[64,3584]{1,0:T(8,128)(2,1)} custom-call(f32[64,1536]{1,0:T(8,128)S(1)} %get-tuple-element.26.refs_0_, s16[64,1664]{1,0:T(8,128)(2,1)S(1)} %collective-permute-done.10.refs_1_, f32[64,2048]{1,0:T(8,128)S(1)} %get-tuple-element.27.refs_2_, s16[64,2176]{1,0:T(8,128)(2,1)S(1)} %collective-permute-done.11.refs_3_, ...), custom_call_target="tpu_custom_call" | custom-call | flops 4587520 | bytes 1835008 | tf_op jit(solution)/shard_map/totals/pallas_call | solution.py:215
  (13 shorter events, 0.1 us)
Async XLA Ops:
  0.6 10.4 %collective-permute-start = (bf16[32,4096]{1,0:T(8,128)(2,1)}, bf16[32,4096]{1,0:T(8,128)(2,1)S(1)}, u32[]{:S(2)}, u32[]{:S(2)}) collective-permute-start(bf16[32,4096]{1,0:T(8,128)(2,1)} %refs_0_.2), channel_id=1, source_target_pairs={{0,2},{1,3},{2,0},{3,1},{4,6},{5,7},{6,4},{7,5},{8,10},{9,11},{10,... | collective-permute-start | bytes 786440 | tf_op jit(solution)/shard_map/ppermute | solution.py:224
  3.6 13.6 %collective-permute-start.1 = (bf16[32,4096]{1,0:T(8,128)(2,1)}, bf16[32,4096]{1,0:T(8,128)(2,1)S(1)}, u32[]{:S(2)}, u32[]{:S(2)}) collective-permute-start(bf16[32,4096]{1,0:T(8,128)(2,1)} %refs_0_.2), channel_id=1, source_target_pairs={{0,4},{1,5},{2,6},{3,7},{4,0},{5,1},{6,2},{7,3},{8,12},{9,13},{10,... | collective-permute-start | bytes 786440 | tf_op jit(solution)/shard_map/ppermute | solution.py:224
  5.2 12.1 %collective-permute-start.2 = (bf16[32,4096]{1,0:T(8,128)(2,1)}, bf16[32,4096]{1,0:T(8,128)(2,1)S(1)}, u32[]{:S(2)}, u32[]{:S(2)}) collective-permute-start(bf16[32,4096]{1,0:T(8,128)(2,1)} %refs_0_.2), channel_id=1, source_target_pairs={{0,6},{1,7},{2,4},{3,5},{4,2},{5,3},{6,0},{7,1},{8,14},{9,15},{10,... | collective-permute-start | bytes 786440 | tf_op jit(solution)/shard_map/ppermute | solution.py:224
  5.2 21.6 %collective-permute-start.5 = (bf16[64,3584]{1,0:T(8,128)(2,1)}, bf16[64,3584]{1,0:T(8,128)(2,1)S(1)}, u32[]{:S(2)}, u32[]{:S(2)}) collective-permute-start(bf16[64,3584]{1,0:T(8,128)(2,1)} %refs_0_.3), channel_id=1, source_target_pairs={{0,8},{8,0},{16,24},{24,16},{1,9},{9,1},{17,25},{25,17},{2,10},{10... | collective-permute-start | bytes 1376264 | tf_op jit(solution)/shard_map/ppermute | solution.py:224
  7.2 27.8 %collective-permute-start.6 = (bf16[64,3584]{1,0:T(8,128)(2,1)}, bf16[64,3584]{1,0:T(8,128)(2,1)S(1)}, u32[]{:S(2)}, u32[]{:S(2)}) collective-permute-start(bf16[64,3584]{1,0:T(8,128)(2,1)} %refs_0_.3), channel_id=1, source_target_pairs={{0,16},{8,24},{16,0},{24,8},{1,17},{9,25},{17,1},{25,9},{2,18},{10... | collective-permute-start | bytes 1376264 | tf_op jit(solution)/shard_map/ppermute | solution.py:224
  11.0 1.0 %copy-start = (bf16[32,4096]{1,0:T(8,128)(2,1)S(1)}, bf16[32,4096]{1,0:T(8,128)(2,1)}, u32[]{:S(2)}) copy-start(bf16[32,4096]{1,0:T(8,128)(2,1)} %refs_0_.2) | copy-start | bytes 786436
  12.0 14.8 %collective-permute-start.3 = (bf16[64,4096]{1,0:T(8,128)(2,1)S(1)}, bf16[64,4096]{1,0:T(8,128)(2,1)S(1)}, u32[]{:S(2)}, u32[]{:S(2)}) collective-permute-start(bf16[64,4096]{1,0:T(8,128)(2,1)S(1)} %stacked.2.refs_2_.refs_1_), channel_id=1, source_target_pairs={{0,1},{1,0},{2,3},{3,2},{4,5},{5,4},{6,7},{7,6},{8,9},{9,8},{10,11... | collective-permute-start | bytes 1572872 | tf_op jit(solution)/shard_map/ppermute | solution.py:224
  17.3 9.5 %collective-permute-start.4 = (bf16[64,4096]{1,0:T(8,128)(2,1)S(1)}, bf16[64,4096]{1,0:T(8,128)(2,1)S(1)}, u32[]{:S(2)}, u32[]{:S(2)}) collective-permute-start(bf16[64,4096]{1,0:T(8,128)(2,1)S(1)} %stacked.3.refs_2_), channel_id=1, source_target_pairs={{0,1},{1,0},{2,3},{3,2},{4,5},{5,4},{6,7},{7,6},{8,9},{9,8},{10,11... | collective-permute-start | bytes 1572872 | tf_op jit(solution)/shard_map/ppermute | solution.py:224
  34.9 12.8 %collective-permute-start.8 = (s16[128,1664]{1,0:T(8,128)(2,1)S(1)}, s16[128,1664]{1,0:T(8,128)(2,1)S(1)}, u32[]{:S(2)}, u32[]{:S(2)}) collective-permute-start(s16[128,1664]{1,0:T(8,128)(2,1)S(1)} %get-tuple-element.17), channel_id=1, source_target_pairs={{0,8},{8,0},{16,24},{24,16},{1,9},{9,1},{17,25},{25,17},{2,10},{10... | collective-permute-start | bytes 1277960 | tf_op jit(solution)/shard_map/ppermute | solution.py:224
  35.0 27.1 %copy-start.1 = (bf16[64,3584]{1,0:T(8,128)(2,1)S(1)}, bf16[64,3584]{1,0:T(8,128)(2,1)}, u32[]{:S(2)}) copy-start(bf16[64,3584]{1,0:T(8,128)(2,1)} %refs_0_.3) | copy-start | bytes 1376260
  35.0 27.1 %collective-permute-start.7 = (bf16[64,3584]{1,0:T(8,128)(2,1)S(1)}, bf16[64,3584]{1,0:T(8,128)(2,1)S(1)}, u32[]{:S(2)}, u32[]{:S(2)}) collective-permute-start(bf16[64,3584]{1,0:T(8,128)(2,1)S(1)} %handed_on.1.refs_1_), channel_id=1, source_target_pairs={{0,8},{8,0},{16,24},{24,16},{1,9},{9,1},{17,25},{25,17},{2,10},{10... | collective-permute-start | bytes 1376264 | tf_op jit(solution)/shard_map/ppermute | solution.py:224
  48.3 23.1 %collective-permute-start.9 = (s16[128,2176]{1,0:T(8,128)(2,1)S(1)}, s16[128,2176]{1,0:T(8,128)(2,1)S(1)}, u32[]{:S(2)}, u32[]{:S(2)}) collective-permute-start(s16[128,2176]{1,0:T(8,128)(2,1)S(1)} %get-tuple-element.23), channel_id=1, source_target_pairs={{0,8},{8,0},{16,24},{24,16},{1,9},{9,1},{17,25},{25,17},{2,10},{10... | collective-permute-start | bytes 1671176 | tf_op jit(solution)/shard_map/ppermute | solution.py:224
  48.4 32.9 %collective-permute-start.10 = (s16[64,1664]{1,0:T(8,128)(2,1)S(1)}, s16[64,1664]{1,0:T(8,128)(2,1)S(1)}, u32[]{:S(2)}, u32[]{:S(2)}) collective-permute-start(s16[64,1664]{1,0:T(8,128)(2,1)S(1)} %get-tuple-element.19.refs_4_), channel_id=1, source_target_pairs={{0,16},{8,24},{16,0},{24,8},{1,17},{9,25},{17,1},{25,9},{2,18},{10... | collective-permute-start | bytes 638984 | tf_op jit(solution)/shard_map/ppermute | solution.py:224
  72.1 12.9 %collective-permute-start.11 = (s16[64,2176]{1,0:T(8,128)(2,1)S(1)}, s16[64,2176]{1,0:T(8,128)(2,1)S(1)}, u32[]{:S(2)}, u32[]{:S(2)}) collective-permute-start(s16[64,2176]{1,0:T(8,128)(2,1)S(1)} %get-tuple-element.24.refs_2_), channel_id=1, source_target_pairs={{0,16},{8,24},{16,0},{24,8},{1,17},{9,25},{17,1},{25,9},{2,18},{10... | collective-permute-start | bytes 835592 | tf_op jit(solution)/shard_map/ppermute | solution.py:224

commit v5 on v4

--- a/solution.py
+++ b/solution.py
@@ -12,6 +12,9 @@
 TOP = 32766.0
 LEAST = 2.0 ** -120
 VMEM_LIMIT = 48 * 1024 * 1024
+SUMS_LIMIT = 24 * 1024 * 1024
+SMALL_LIMIT = 8 * 1024 * 1024
+WIDE_LIMIT = 40 * 1024 * 1024
 SUB = 256
 
 
@@ -42,8 +45,8 @@
     return levels.astype(jnp.int32).astype(jnp.int16)
 
 
-def params():
-    return pltpu.CompilerParams(vmem_limit_bytes=VMEM_LIMIT)
+def params(limit=VMEM_LIMIT):
+    return pltpu.CompilerParams(vmem_limit_bytes=limit)
 
 
 def cost(flops, moved):
@@ -59,17 +62,17 @@
         aligned_ref[:, cols] = dot(pick_ref[...], gathered, ((1,), (0,))).astype(jnp.bfloat16)
 
 
-def sums_kernel(n_pieces, n_blocks, n_later, tile, *refs):
+def sums_kernel(n_pieces, n_blocks, n_later, resident, tile, *refs):
     refs = list(refs)
     if n_pieces:
         pick_ref = refs.pop(0)
         pieces = [refs.pop(0) for _ in range(n_pieces)]
-        blocks = [refs.pop(0) for _ in range(n_blocks)]
+        blocks = [refs.pop(0) for _ in range(1 if resident else n_blocks)]
         del refs[:n_later]
         aligned_ref = refs.pop(0)
     else:
         aligned_ref = refs.pop(0)
-        blocks = [refs.pop(0) for _ in range(n_blocks)]
+        blocks = [refs.pop(0) for _ in range(1 if resident else n_blocks)]
         del refs[:n_later]
     kept_ref, sent_ref, levels_ref = refs
     step = pl.program_id(0)
@@ -84,8 +87,12 @@
 
     lane = lax.broadcasted_iota(jnp.int32, levels_ref.shape, 1)
     levels = levels_ref[...]
-    for part, block in enumerate(blocks):
-        values = dot(aligned_ref[...], block[...], ((1,), (1,)))
+    for part in range(n_blocks):
+        if resident:
+            block = blocks[0][pl.ds(pl.multiple_of((step * n_blocks + part) * tile, tile), tile)]
+        else:
+            block = blocks[part][...]
+        values = dot(aligned_ref[...], block, ((1,), (1,)))
         kept_ref[:, part * tile:(part + 1) * tile] = values[:rows]
         codes, level = encode(values[rows:])
         levels = jnp.where(lane == step * n_blocks + part, level, levels)
@@ -98,7 +105,30 @@
         sent_ref[:, width:] = to_levels(levels)
 
 
-def partial_sums(aligned, align, weight, tile, first, count, later_than, name):
+def fetch_kernel(weight_ref, out_ref, arrived):
+    count = arrived.shape[0]
+    rows = out_ref.shape[0] // count
+    parts = [pl.ds(at * rows, rows) for at in range(count)]
+    copies = [pltpu.make_async_copy(weight_ref.at[part], out_ref.at[part], arrived.at[at]) for at, part in enumerate(parts)]
+    for copy in copies:
+        copy.start()
+    for copy in copies:
+        copy.wait()
+
+
+def fetched(weight, tile, count):
+    shape = (count * tile, weight.shape[1])
+    return pl.pallas_call(
+        fetch_kernel,
+        in_specs=[pl.BlockSpec(memory_space=pl.ANY)],
+        out_specs=pl.BlockSpec(memory_space=pltpu.VMEM),
+        out_shape=jax.ShapeDtypeStruct(shape, weight.dtype),
+        scratch_shapes=[pltpu.SemaphoreType.DMA((count,))],
+        compiler_params=params(WIDE_LIMIT), cost_estimate=cost(0, 2 * shape[0] * shape[1]), name="fetched",
+    )(weight)
+
+
+def partial_sums(aligned, align, weight, resident, tile, first, count, later_than, name):
     depth = weight.shape[1]
     width = count * tile
     whole = lambda i: (0, 0)
@@ -108,7 +138,10 @@
     n_blocks = 2 if count % 2 == 0 and first % 2 == 0 else 1
     block_at = lambda part: (lambda i: (i * n_blocks + first + part, 0))
     in_specs = [pl.BlockSpec(operand.shape, whole) for operand in operands]
-    in_specs += [pl.BlockSpec((tile, depth), block_at(part)) for part in range(n_blocks)]
+    if resident:
+        in_specs.append(pl.BlockSpec(memory_space=pltpu.VMEM))
+    else:
+        in_specs += [pl.BlockSpec((tile, depth), block_at(part)) for part in range(n_blocks)]
     in_specs += [pl.BlockSpec(memory_space=pl.ANY)] * len(later_than)
     out_specs = [pl.BlockSpec((half, n_blocks * tile), lambda i: (0, i)), pl.BlockSpec((half, width + LANES), whole)]
     out_shape = [jax.ShapeDtypeStruct((half, width), jnp.float32), jax.ShapeDtypeStruct((half, width + LANES), jnp.int16)]
@@ -116,46 +149,38 @@
         out_specs.insert(0, pl.BlockSpec((total, depth), whole))
         out_shape.insert(0, jax.ShapeDtypeStruct((total, depth), jnp.bfloat16))
     outs = pl.pallas_call(
-        functools.partial(sums_kernel, 0 if aligned is not None else len(align[1]), n_blocks, len(later_than), tile),
+        functools.partial(sums_kernel, 0 if aligned is not None else len(align[1]), n_blocks, len(later_than), resident, tile),
         grid=(count // n_blocks,), in_specs=in_specs, out_specs=out_specs, out_shape=out_shape,
         scratch_shapes=[pltpu.VMEM((half, LANES), jnp.float32)],
-        compiler_params=params(), cost_estimate=cost(2 * total * width * depth, 2 * width * depth), name=name,
-    )(*operands, *[weight] * n_blocks, *later_than)
+        compiler_params=params(SUMS_LIMIT if resident else WIDE_LIMIT), cost_estimate=cost(2 * total * width * depth, 2 * width * depth), name=name,
+    )(*operands, *[weight] * (1 if resident else n_blocks), *later_than)
     return outs if aligned is None else (aligned, *outs)
 
 
-def weight_kernel(n_pieces, n_later, aligned_ref, *refs):
-    refs = list(refs)
-    pieces = [refs.pop(0) for _ in range(n_pieces)]
-    out_ref, left_ref = refs[n_later:]
-
-    @pl.when(pl.program_id(0) == 0)
-    def _():
-        if n_pieces == 1:
-            left_ref[...] = pieces[0][...]
-        else:
-            left_ref[...] = jnp.concatenate([piece[...] for piece in pieces], axis=0).T
-
-    out_ref[...] = dot(left_ref[...], aligned_ref[...], ((1,), (0,))).astype(jnp.bfloat16)
-
-
-def weight_grads(aligned, pieces, part, parts, filled, later_than):
+def weight_kernel(n_pieces, aligned_ref, *refs):
+    out_ref = refs[-1]
+    left = jnp.concatenate([piece[...] for piece in refs[:n_pieces]], axis=0)
+    depth = out_ref.shape[1]
+    chunk = tile_of(depth, 1024)
+    for at in range(0, depth, chunk):
+        cols = slice(at, at + chunk)
+        out_ref[:, cols] = dot(left, aligned_ref[:, cols], ((0,), (0,))).astype(jnp.bfloat16)
+
+
+def weight_grads(aligned, pieces, tile, first, count, filled, later_than):
     total, depth = aligned.shape
-    hidden = pieces[0].size * len(pieces) // total
-    tile = tile_of(depth // parts, 512)
-    count = depth // parts // tile
-    whole = lambda i: (0, 0)
-    here = lambda i: (0, i + part * count)
+    rows, hidden = pieces[0].shape
     later = ([] if filled is None else [filled]) + list(later_than)
     return pl.pallas_call(
-        functools.partial(weight_kernel, len(pieces), len(later)),
+        functools.partial(weight_kernel, len(pieces)),
         grid=(count,),
-        in_specs=[pl.BlockSpec((total, tile), here)] + [pl.BlockSpec(piece.shape, whole) for piece in pieces]
+        in_specs=[pl.BlockSpec((total, depth), lambda i: (0, 0))]
+        + [pl.BlockSpec((rows, tile), lambda i: (0, i + first))] * len(pieces)
         + [pl.BlockSpec(memory_space=pl.ANY)] * len(later),
-        out_specs=[pl.BlockSpec((hidden, tile), here), pl.BlockSpec((hidden, total), whole)],
-        out_shape=[jax.ShapeDtypeStruct((hidden, depth), jnp.bfloat16), jax.ShapeDtypeStruct((hidden, total), jnp.bfloat16)],
+        out_specs=pl.BlockSpec((tile, depth), lambda i: (i + first, 0)),
+        out_shape=jax.ShapeDtypeStruct((hidden, depth), jnp.bfloat16),
         input_output_aliases={} if filled is None else {1 + len(pieces): 0},
-        compiler_params=params(), cost_estimate=cost(2 * total * hidden * depth // parts, 2 * hidden * depth // parts),
+        compiler_params=params(), cost_estimate=cost(2 * total * count * tile * depth, 2 * count * tile * depth),
         name="weight_grads",
     )(aligned, *pieces, *later)
 
@@ -237,7 +262,7 @@
         functools.partial(stack_kernel, len(values)),
         in_specs=[pl.BlockSpec(memory_space=pltpu.VMEM)] * len(values) + [pl.BlockSpec(memory_space=pl.ANY)] * len(later_than),
         out_shape=jax.ShapeDtypeStruct((len(values) * rows, width), values[0].dtype),
-        compiler_params=params(), cost_estimate=cost(0, 4 * len(values) * rows * width), name="stacked",
+        compiler_params=params(SMALL_LIMIT), cost_estimate=cost(0, 4 * len(values) * rows * width), name="stacked",
     )(*values, *later_than)
 
 
@@ -252,14 +277,14 @@
         in_specs=[anywhere] * (len(values) + len(later_than)), out_specs=[anywhere] * len(values),
         out_shape=[jax.ShapeDtypeStruct(value.shape, value.dtype) for value in values],
         input_output_aliases={at: at for at in range(len(values))},
-        compiler_params=params(), cost_estimate=cost(0, 0), name="handed_on",
+        compiler_params=params(SMALL_LIMIT), cost_estimate=cost(0, 0), name="handed_on",
     )(*values, *later_than)
 
 
-def gather_cotangent(cotangent, n_col):
+def gather_cotangent(cotangent, n_col, later_than):
     flips = list(range(0, n_col, 2))
     pieces = [cotangent] + [send(cotangent, "col", flip, n_col) for flip in flips[1:]]
-    stacks = [stacked(pieces[:2])]
+    stacks = [stacked(pieces[:2], later_than)]
     stacks.append(stacked(pieces[2:], stacks))
     stacks += [send(stack, "col", 1, n_col) for stack in stacks]
     return stacks, flips + [flip ^ 1 for flip in flips]
@@ -278,7 +303,11 @@
     mine_row, mine_col = lax.axis_index("row"), lax.axis_index("col")
     offsets = halving_order(n_row)
 
-    pieces, flips = gather_cotangent(cotangent, n_col)
+    tile = tile_of(hidden, 256)
+    tiles = hidden // tile
+    cut = tiles * 3 // 7
+    weight_a = fetched(down_weight, tile, cut)
+    pieces, flips = gather_cotangent(cotangent, n_col, [weight_a])
     act_pieces = {o: send(activations, "row", o, n_row) for o in [1, *range(2, n_row, 2)]}
     act_pieces[0] = activations
 
@@ -288,15 +317,12 @@
     named = (owner[:, None] * shard + jnp.arange(shard, dtype=jnp.int32)[None, :]).reshape(-1)
     pick = (order[:, None] == named[None, :]).astype(jnp.bfloat16)
 
-    tile = tile_of(hidden, 256)
-    tiles = hidden // tile
-    cut = tiles * 3 // 7
-    aligned, kept_a, sent_a = partial_sums(None, (pick, pieces), down_weight, tile, 0, cut, [act_pieces[1]], "sums_a")
+    aligned, kept_a, sent_a = partial_sums(None, (pick, pieces), weight_a, True, tile, 0, cut, [], "sums_a")
     got_a = send(sent_a, "row", 1, n_row)
     evens = range(2, n_row, 2)
     for o, piece in zip(evens, handed_on([act_pieces[o] for o in evens], [aligned])):
         act_pieces[o], act_pieces[o + 1] = piece, send(piece, "row", 1, n_row)
-    _, kept_b, sent_b = partial_sums(aligned, None, down_weight, tile, cut, tiles - cut, [], "sums_b")
+    _, kept_b, sent_b = partial_sums(aligned, None, down_weight, False, tile, cut, tiles - cut, [act_pieces[1]], "sums_b")
 
     passed = [sent_b]
     step = 2
@@ -306,13 +332,16 @@
         step *= 2
     got_b = send(passed[0], "row", 1, n_row)
     act_pieces = [act_pieces[o] for o in offsets]
-    grad, turned = weight_grads(aligned, act_pieces, 0, 2, None, [sent_a])
+    grad_tile = tile_of(hidden, 512)
+    grad_tiles = hidden // grad_tile
+    grad_cut = grad_tiles * 4 // 7
+    grad = weight_grads(aligned, act_pieces, grad_tile, 0, grad_cut, None, [sent_a])
     step = 2
     while step < n_row:
         kept_b, sent_b, _ = fold(kept_b, got_b, [])
         got_b = send(sent_b, "row", step, n_row)
         step *= 2
-    weight_grad, _ = weight_grads(aligned, [turned], 1, 2, grad, [sent_b])
+    weight_grad = weight_grads(aligned, act_pieces, grad_tile, grad_cut, grad_tiles - grad_cut, grad, [sent_b])
     return weight_grad, totals([[kept_a, got_a], [kept_b, got_b]], [weight_grad])
 
 

time: 86.2 us -> 85.7 us (level)
  local copies, waits for them, and re-layouts: 1.8 us -> 9.54 us
  waiting for transfers between devices: 31.7 us -> 25.8 us
  starting transfers between devices: 16 us -> 13.3 us
  Pallas kernels: 34.9 us -> 35.8 us
    unnamed x4 -> x12, local copies, waits for them, and re-layouts: 0.96 us -> 9.37 us
    ppermute x12, waiting for transfers between devices: 31.7 us -> 25.8 us  [send(): return lax.ppermute(value, axis, [(i, i ^ flip) for i in range(size)])]
    pallas_call x2 -> x3, Pallas kernels: 15.4 us -> 19.4 us  [the longest x2 14.7 us: weight_grads(): pl.pallas_call(functools.partial(weight_kernel, len(pieces)), grid=(count...]
    pallas_call x2, Pallas kernels: 17.1 us -> 14 us  [partial_sums(): pl.pallas_call(functools.partial(sums_kernel, 0 if aligned is not None el...]
    ppermute x12, starting transfers between devices: 16 us -> 13.3 us  [send(): return lax.ppermute(value, axis, [(i, i ^ flip) for i in range(size)])]
  transfers between devices with their start and end apart: 12 -> 12, of which waited for: 7 -> 5; matrix products, arithmetic and copies ran while one was open for 2% -> 1% of each run, Pallas kernels for 39% -> 41%
where the time goes in v5:
time: 85.7 us; the launch traced here: 85.5 us
  Pallas kernels  35.8 us (42%)
  waiting for transfers between devices  25.8 us (30%)
  starting transfers between devices  13.3 us (16%)
  local copies, waits for them, and re-layouts  9.54 us (11%)
    ppermute x12, waiting for transfers between devices, send(): return lax.ppermute(value, axis, [(i, i ^ flip) for i in range(size)])  25.8 us
    pallas_call x2, Pallas kernels, weight_grads(): pl.pallas_call(functools.partial(weight_kernel, len(pieces)), grid=(count...  14.7 us
    pallas_call x2, Pallas kernels, partial_sums(): pl.pallas_call(functools.partial(sums_kernel, 0 if aligned is not None el...  14 us
    ppermute x12, starting transfers between devices, send(): return lax.ppermute(value, axis, [(i, i ^ flip) for i in range(size)])  13.3 us
    unnamed x12, local copies, waits for them, and re-layouts  9.37 us
    pallas_call x1, Pallas kernels, fetched(): pl.pallas_call(fetch_kernel, in_specs=[pl.BlockSpec(memory_space=pl.ANY)]...  4.71 us
  transfers between devices with their start and end apart: 12, of which 5 were waited for; matrix products, arithmetic and copies ran while one was open for 1% of the time, Pallas kernels for 41%

profile of v5, /device:TPU:0, one launch (start us, length us, event | category | flops | bytes accessed | tf_op | source)
XLA Modules:
  0.0 85.5 jit_solution(1582010253183603849)
XLA Ops:
  0.6 0.0 copy-start.5
  0.7 3.0 %collective-permute-start = (bf16[32,4096]{1,0:T(8,128)(2,1)}, bf16[32,4096]{1,0:T(8,128)(2,1)S(1)}, u32[]{:S(2)}, u32[]{:S(2)}) collective-permute-start(bf16[32,4096]{1,0:T(8,128)(2,1)} %refs_0_.3), channel_id=1, source_target_pairs={{0,2},{1,3},{2,0},{3,1},{4,6},{5,7},{6,4},{7,5},{8,10},{9,11},{10,... | collective-permute-start | bytes 786440 | tf_op jit(solution)/shard_map/ppermute | solution.py:249
  3.7 1.5 %collective-permute-start.1 = (bf16[32,4096]{1,0:T(8,128)(2,1)}, bf16[32,4096]{1,0:T(8,128)(2,1)S(1)}, u32[]{:S(2)}, u32[]{:S(2)}) collective-permute-start(bf16[32,4096]{1,0:T(8,128)(2,1)} %refs_0_.3), channel_id=1, source_target_pairs={{0,4},{1,5},{2,6},{3,7},{4,0},{5,1},{6,2},{7,3},{8,12},{9,13},{10,... | collective-permute-start | bytes 786440 | tf_op jit(solution)/shard_map/ppermute | solution.py:249
  5.2 0.0 collective-permute-start.2
  5.2 2.0 %collective-permute-start.6 = (bf16[64,3584]{1,0:T(8,128)(2,1)}, bf16[64,3584]{1,0:T(8,128)(2,1)S(1)}, u32[]{:S(2)}, u32[]{:S(2)}) collective-permute-start(bf16[64,3584]{1,0:T(8,128)(2,1)} %refs_0_.5), channel_id=1, source_target_pairs={{0,8},{8,0},{16,24},{24,16},{1,9},{9,1},{17,25},{25,17},{2,10},{10... | collective-permute-start | bytes 1376264 | tf_op jit(solution)/shard_map/ppermute | solution.py:249
  7.2 2.6 %collective-permute-start.5 = (bf16[64,3584]{1,0:T(8,128)(2,1)}, bf16[64,3584]{1,0:T(8,128)(2,1)S(1)}, u32[]{:S(2)}, u32[]{:S(2)}) collective-permute-start(bf16[64,3584]{1,0:T(8,128)(2,1)} %refs_0_.5), channel_id=1, source_target_pairs={{0,16},{8,24},{16,0},{24,8},{1,17},{9,25},{17,1},{25,9},{2,18},{10... | collective-permute-start | bytes 1376264 | tf_op jit(solution)/shard_map/ppermute | solution.py:249
  9.8 4.7 %fetched.1.refs_2_.refs_5_ = bf16[1536,4096]{1,0:T(8,128)(2,1)S(1)} custom-call(bf16[3584,4096]{1,0:T(8,128)(2,1)} %refs_2_.1), custom_call_target="tpu_custom_call" | custom-call | bytes 12582912 | tf_op jit(solution)/shard_map/fetched/pallas_call | solution.py:121
  14.7 4.8 %copy-done = bf16[1536,4096]{1,0:T(8,128)(2,1)} copy-done((bf16[1536,4096]{1,0:T(8,128)(2,1)}, bf16[1536,4096]{1,0:T(8,128)(2,1)S(1)}, u32[]{:S(2)}) %copy-start) | copy-done | bytes 12582936
  19.5 0.6 collective-permute-start.4
  20.0 0.1 iota_add_fusion
  20.1 0.1 reshape.24
  20.2 0.1 add.40
  20.3 0.1 pad_add_fusion
  20.4 0.1 compare_convert_fusion.refs_0_
  20.5 1.6 %collective-permute-done.4.refs_4_ = bf16[64,4096]{1,0:T(8,128)(2,1)S(1)} collective-permute-done((bf16[64,4096]{1,0:T(8,128)(2,1)S(1)}, bf16[64,4096]{1,0:T(8,128)(2,1)S(1)}, u32[]{:S(2)}, u32[]{:S(2)}) %collective-permute-start.4) | collective-permute-done | bytes 524320 | tf_op jit(solution)/shard_map/ppermute | solution.py:249
  22.1 4.6 %copy-done.1 = bf16[1536,4096]{1,0:T(8,128)(2,1)S(1)} copy-done((bf16[1536,4096]{1,0:T(8,128)(2,1)S(1)}, bf16[1536,4096]{1,0:T(8,128)(2,1)}, u32[]{:S(2)}) %copy-start.1) | copy-done | bytes 12582936
  26.7 5.0 %sums_a.1 = (bf16[256,4096]{1,0:T(8,128)(2,1)S(1)}, f32[128,1536]{1,0:T(8,128)S(1)}, s16[128,1664]{1,0:T(8,128)(2,1)S(1)}) custom-call(bf16[256,256]{1,0:T(8,128)(2,1)S(1)} %compare_convert_fusion.refs_0_, bf16[64,4096]{1,0:T(8,128)(2,1)S(1)} %stacked.2.refs_2_.refs_1_, bf16[64,4096]{1,0:T(8,128)(2,1)S(1)} %stacked.3.refs_2_, ...), custom_call_target="tpu_custom_call" | custom-call | flops 3221225472 | bytes 12582912 | tf_op jit(solution)/shard_map/sums_a/pallas_call | solution.py:151
  31.7 0.5 collective-permute-start.8
  32.2 1.6 %collective-permute-start.7 = (bf16[64,3584]{1,0:T(8,128)(2,1)S(1)}, bf16[64,3584]{1,0:T(8,128)(2,1)S(1)}, u32[]{:S(2)}, u32[]{:S(2)}) collective-permute-start(bf16[64,3584]{1,0:T(8,128)(2,1)S(1)} %handed_on.1.refs_1_), channel_id=1, source_target_pairs={{0,8},{8,0},{16,24},{24,16},{1,9},{9,1},{17,25},{25,17},{2,10},{10... | collective-permute-start | bytes 1376264 | tf_op jit(solution)/shard_map/ppermute | solution.py:249
  33.8 9.0 %sums_b.1 = (f32[128,2048]{1,0:T(8,128)S(1)}, s16[128,2176]{1,0:T(8,128)(2,1)S(1)}) custom-call(bf16[256,4096]{1,0:T(8,128)(2,1)S(1)} %get-tuple-element.12.refs_1_.refs_0_.aligned_ref, bf16[3584,4096]{1,0:T(8,128)(2,1)} %refs_2_.1, bf16[3584,4096]{1,0:T(8,128)(2,1)} %refs_2_.1, bf16[64,3584]{1,0:T(8,128)(2,1)S(1)} %collective-permute-done.6.refs_3_.refs_2_), custom_call_target="tpu_custom_call" | custom-call | flops 4294967296 | bytes 16777216 | tf_op jit(solution)/shard_map/sums_b/pallas_call | solution.py:151
  42.8 1.6 %collective-permute-done.8.got_ref = s16[128,1664]{1,0:T(8,128)(2,1)S(1)} collective-permute-done((s16[128,1664]{1,0:T(8,128)(2,1)S(1)}, s16[128,1664]{1,0:T(8,128)(2,1)S(1)}, u32[]{:S(2)}, u32[]{:S(2)}) %collective-permute-start.8) | collective-permute-done | bytes 426016 | tf_op jit(solution)/shard_map/ppermute | solution.py:249
  44.4 0.6 fold.2
  45.0 0.5 collective-permute-start.9
  45.5 0.9 %collective-permute-start.10 = (s16[64,1664]{1,0:T(8,128)(2,1)S(1)}, s16[64,1664]{1,0:T(8,128)(2,1)S(1)}, u32[]{:S(2)}, u32[]{:S(2)}) collective-permute-start(s16[64,1664]{1,0:T(8,128)(2,1)S(1)} %get-tuple-element.16.refs_4_), channel_id=1, source_target_pairs={{0,16},{8,24},{16,0},{24,8},{1,17},{9,25},{17,1},{25,9},{2,18},{10... | collective-permute-start | bytes 638984 | tf_op jit(solution)/shard_map/ppermute | solution.py:249
  46.4 12.4 %collective-permute-done.7.refs_3_ = bf16[64,3584]{1,0:T(8,128)(2,1)S(1)} collective-permute-done((bf16[64,3584]{1,0:T(8,128)(2,1)S(1)}, bf16[64,3584]{1,0:T(8,128)(2,1)S(1)}, u32[]{:S(2)}, u32[]{:S(2)}) %collective-permute-start.7) | collective-permute-done | bytes 458784 | tf_op jit(solution)/shard_map/ppermute | solution.py:249
  58.8 8.0 %weight_grads.2.refs_4_ = bf16[3584,4096]{1,0:T(8,128)(2,1)} custom-call(bf16[256,4096]{1,0:T(8,128)(2,1)S(1)} %get-tuple-element.12.refs_1_.refs_0_.aligned_ref, bf16[64,3584]{1,0:T(8,128)(2,1)S(1)} %copy-done.2, bf16[64,3584]{1,0:T(8,128)(2,1)S(1)} %handed_on.1.refs_1_, bf16[64,3584]{1,0:T(8,128)(2,1)S(1)} %collective-permute-done.6.refs_3_.refs_2_, ...), custom_call_target="tpu_custom_call" | custom-call | flops 4294967296 | bytes 16777216 | tf_op jit(solution)/shard_map/weight_grads/pallas_call | solution.py:174
  66.9 3.1 %collective-permute-done.9.got_ref = s16[128,2176]{1,0:T(8,128)(2,1)S(1)} collective-permute-done((s16[128,2176]{1,0:T(8,128)(2,1)S(1)}, s16[128,2176]{1,0:T(8,128)(2,1)S(1)}, u32[]{:S(2)}, u32[]{:S(2)}) %collective-permute-start.9) | collective-permute-done | bytes 557088 | tf_op jit(solution)/shard_map/ppermute | solution.py:249
  70.0 0.8 fold.3
  70.7 0.1 collective-permute-start.11
  70.8 6.7 %weight_grads.3.refs_4_ = bf16[3584,4096]{1,0:T(8,128)(2,1)} custom-call(bf16[256,4096]{1,0:T(8,128)(2,1)S(1)} %get-tuple-element.12.refs_1_.refs_0_.aligned_ref, bf16[64,3584]{1,0:T(8,128)(2,1)S(1)} %copy-done.2, bf16[64,3584]{1,0:T(8,128)(2,1)S(1)} %handed_on.1.refs_1_, ...), custom_call_target="tpu_custom_call", output_to_operand_aliasing={{}: (5, {})} | custom-call | flops 3221225472 | bytes 12582912 | tf_op jit(solution)/shard_map/weight_grads/pallas_call | solution.py:174
  77.5 7.0 %collective-permute-done.11.refs_3_ = s16[64,2176]{1,0:T(8,128)(2,1)S(1)} collective-permute-done((s16[64,2176]{1,0:T(8,128)(2,1)S(1)}, s16[64,2176]{1,0:T(8,128)(2,1)S(1)}, u32[]{:S(2)}, u32[]{:S(2)}) %collective-permute-start.11) | collective-permute-done | bytes 278560 | tf_op jit(solution)/shard_map/ppermute | solution.py:249
  84.5 1.0 %totals.1 = bf16[64,3584]{1,0:T(8,128)(2,1)} custom-call(f32[64,1536]{1,0:T(8,128)S(1)} %get-tuple-element.20.refs_0_, s16[64,1664]{1,0:T(8,128)(2,1)S(1)} %collective-permute-done.10.refs_1_, f32[64,2048]{1,0:T(8,128)S(1)} %get-tuple-element.21.refs_2_, s16[64,2176]{1,0:T(8,128)(2,1)S(1)} %collective-permute-done.11.refs_3_, ...), custom_call_target="tpu_custom_call" | custom-call | flops 4587520 | bytes 1835008 | tf_op jit(solution)/shard_map/totals/pallas_call | solution.py:240
  (22 shorter events, 0.1 us)
Async XLA Ops:
  0.6 13.9 %copy-start.5 = (s32[8]{0:T(128)S(1)}, s32[8]{0:T(128)}, u32[]{:S(2)}) copy-start(s32[8]{0:T(128)} %constant.30.clone) | copy-start | bytes 100
  0.6 13.9 %copy-start.3 = (bf16[32,4096]{1,0:T(8,128)(2,1)S(1)}, bf16[32,4096]{1,0:T(8,128)(2,1)}, u32[]{:S(2)}) copy-start(bf16[32,4096]{1,0:T(8,128)(2,1)} %refs_0_.3) | copy-start | bytes 786436
  0.7 19.5 %copy-start.4 = (s32[256]{0:T(256)S(1)}, s32[256]{0:T(256)}, u32[]{:S(2)}) copy-start(s32[256]{0:T(256)} %param.8) | copy-start | bytes 3076
  0.7 13.9 %collective-permute-start = (bf16[32,4096]{1,0:T(8,128)(2,1)}, bf16[32,4096]{1,0:T(8,128)(2,1)S(1)}, u32[]{:S(2)}, u32[]{:S(2)}) collective-permute-start(bf16[32,4096]{1,0:T(8,128)(2,1)} %refs_0_.3), channel_id=1, source_target_pairs={{0,2},{1,3},{2,0},{3,1},{4,6},{5,7},{6,4},{7,5},{8,10},{9,11},{10,... | collective-permute-start | bytes 786440 | tf_op jit(solution)/shard_map/ppermute | solution.py:249
  3.7 15.8 %collective-permute-start.1 = (bf16[32,4096]{1,0:T(8,128)(2,1)}, bf16[32,4096]{1,0:T(8,128)(2,1)S(1)}, u32[]{:S(2)}, u32[]{:S(2)}) collective-permute-start(bf16[32,4096]{1,0:T(8,128)(2,1)} %refs_0_.3), channel_id=1, source_target_pairs={{0,4},{1,5},{2,6},{3,7},{4,0},{5,1},{6,2},{7,3},{8,12},{9,13},{10,... | collective-permute-start | bytes 786440 | tf_op jit(solution)/shard_map/ppermute | solution.py:249
  5.2 14.2 %collective-permute-start.2 = (bf16[32,4096]{1,0:T(8,128)(2,1)}, bf16[32,4096]{1,0:T(8,128)(2,1)S(1)}, u32[]{:S(2)}, u32[]{:S(2)}) collective-permute-start(bf16[32,4096]{1,0:T(8,128)(2,1)} %refs_0_.3), channel_id=1, source_target_pairs={{0,6},{1,7},{2,4},{3,5},{4,2},{5,3},{6,0},{7,1},{8,14},{9,15},{10,... | collective-permute-start | bytes 786440 | tf_op jit(solution)/shard_map/ppermute | solution.py:249
  5.2 28.6 %collective-permute-start.6 = (bf16[64,3584]{1,0:T(8,128)(2,1)}, bf16[64,3584]{1,0:T(8,128)(2,1)S(1)}, u32[]{:S(2)}, u32[]{:S(2)}) collective-permute-start(bf16[64,3584]{1,0:T(8,128)(2,1)} %refs_0_.5), channel_id=1, source_target_pairs={{0,8},{8,0},{16,24},{24,16},{1,9},{9,1},{17,25},{25,17},{2,10},{10... | collective-permute-start | bytes 1376264 | tf_op jit(solution)/shard_map/ppermute | solution.py:249
  7.2 25.0 %collective-permute-start.5 = (bf16[64,3584]{1,0:T(8,128)(2,1)}, bf16[64,3584]{1,0:T(8,128)(2,1)S(1)}, u32[]{:S(2)}, u32[]{:S(2)}) collective-permute-start(bf16[64,3584]{1,0:T(8,128)(2,1)} %refs_0_.5), channel_id=1, source_target_pairs={{0,16},{8,24},{16,0},{24,8},{1,17},{9,25},{17,1},{25,9},{2,18},{10... | collective-permute-start | bytes 1376264 | tf_op jit(solution)/shard_map/ppermute | solution.py:249
  14.6 4.8 %copy-start = (bf16[1536,4096]{1,0:T(8,128)(2,1)}, bf16[1536,4096]{1,0:T(8,128)(2,1)S(1)}, u32[]{:S(2)}) copy-start(bf16[1536,4096]{1,0:T(8,128)(2,1)S(1)} %fetched.1.refs_2_.refs_5_) | copy-start | bytes 37748740
  19.4 2.7 %collective-permute-start.3 = (bf16[64,4096]{1,0:T(8,128)(2,1)S(1)}, bf16[64,4096]{1,0:T(8,128)(2,1)S(1)}, u32[]{:S(2)}, u32[]{:S(2)}) collective-permute-start(bf16[64,4096]{1,0:T(8,128)(2,1)S(1)} %stacked.2.refs_2_.refs_1_), channel_id=1, source_target_pairs={{0,1},{1,0},{2,3},{3,2},{4,5},{5,4},{6,7},{7,6},{8,9},{9,8},{10,11... | collective-permute-start | bytes 1572872 | tf_op jit(solution)/shard_map/ppermute | solution.py:249
  19.5 2.6 %collective-permute-start.4 = (bf16[64,4096]{1,0:T(8,128)(2,1)S(1)}, bf16[64,4096]{1,0:T(8,128)(2,1)S(1)}, u32[]{:S(2)}, u32[]{:S(2)}) collective-permute-start(bf16[64,4096]{1,0:T(8,128)(2,1)S(1)} %stacked.3.refs_2_), channel_id=1, source_target_pairs={{0,1},{1,0},{2,3},{3,2},{4,5},{5,4},{6,7},{7,6},{8,9},{9,8},{10,11... | collective-permute-start | bytes 1572872 | tf_op jit(solution)/shard_map/ppermute | solution.py:249
  22.1 4.6 %copy-start.1 = (bf16[1536,4096]{1,0:T(8,128)(2,1)S(1)}, bf16[1536,4096]{1,0:T(8,128)(2,1)}, u32[]{:S(2)}) copy-start(bf16[1536,4096]{1,0:T(8,128)(2,1)} %copy-done) | copy-start | bytes 37748740
  31.7 12.7 %collective-permute-start.8 = (s16[128,1664]{1,0:T(8,128)(2,1)S(1)}, s16[128,1664]{1,0:T(8,128)(2,1)S(1)}, u32[]{:S(2)}, u32[]{:S(2)}) collective-permute-start(s16[128,1664]{1,0:T(8,128)(2,1)S(1)} %get-tuple-element.14), channel_id=1, source_target_pairs={{0,8},{8,0},{16,24},{24,16},{1,9},{9,1},{17,25},{25,17},{2,10},{10... | collective-permute-start | bytes 1277960 | tf_op jit(solution)/shard_map/ppermute | solution.py:249
  32.2 26.6 %copy-start.2 = (bf16[64,3584]{1,0:T(8,128)(2,1)S(1)}, bf16[64,3584]{1,0:T(8,128)(2,1)}, u32[]{:S(2)}) copy-start(bf16[64,3584]{1,0:T(8,128)(2,1)} %refs_0_.5) | copy-start | bytes 1376260
  32.2 26.6 %collective-permute-start.7 = (bf16[64,3584]{1,0:T(8,128)(2,1)S(1)}, bf16[64,3584]{1,0:T(8,128)(2,1)S(1)}, u32[]{:S(2)}, u32[]{:S(2)}) collective-permute-start(bf16[64,3584]{1,0:T(8,128)(2,1)S(1)} %handed_on.1.refs_1_), channel_id=1, source_target_pairs={{0,8},{8,0},{16,24},{24,16},{1,9},{9,1},{17,25},{25,17},{2,10},{10... | collective-permute-start | bytes 1376264 | tf_op jit(solution)/shard_map/ppermute | solution.py:249
  45.0 25.0 %collective-permute-start.9 = (s16[128,2176]{1,0:T(8,128)(2,1)S(1)}, s16[128,2176]{1,0:T(8,128)(2,1)S(1)}, u32[]{:S(2)}, u32[]{:S(2)}) collective-permute-start(s16[128,2176]{1,0:T(8,128)(2,1)S(1)} %get-tuple-element.18), channel_id=1, source_target_pairs={{0,8},{8,0},{16,24},{24,16},{1,9},{9,1},{17,25},{25,17},{2,10},{10... | collective-permute-start | bytes 1671176 | tf_op jit(solution)/shard_map/ppermute | solution.py:249
  45.5 32.0 %collective-permute-start.10 = (s16[64,1664]{1,0:T(8,128)(2,1)S(1)}, s16[64,1664]{1,0:T(8,128)(2,1)S(1)}, u32[]{:S(2)}, u32[]{:S(2)}) collective-permute-start(s16[64,1664]{1,0:T(8,128)(2,1)S(1)} %get-tuple-element.16.refs_4_), channel_id=1, source_target_pairs={{0,16},{8,24},{16,0},{24,8},{1,17},{9,25},{17,1},{25,9},{2,18},{10... | collective-permute-start | bytes 638984 | tf_op jit(solution)/shard_map/ppermute | solution.py:249
  70.7 13.8 %collective-permute-start.11 = (s16[64,2176]{1,0:T(8,128)(2,1)S(1)}, s16[64,2176]{1,0:T(8,128)(2,1)S(1)}, u32[]{:S(2)}, u32[]{:S(2)}) collective-permute-start(s16[64,2176]{1,0:T(8,128)(2,1)S(1)} %get-tuple-element.19.refs_5_), channel_id=1, source_target_pairs={{0,16},{8,24},{16,0},{24,8},{1,17},{9,25},{17,1},{25,9},{2,18},{10... | collective-permute-start | bytes 835592 | tf_op jit(solution)/shard_map/ppermute | solution.py:249

commit v6 on v4

v6 whole, which is shorter than its diff:
```python
import functools

import jax
import jax.numpy as jnp
from jax import lax
from jax.experimental import pallas as pl
from jax.experimental.pallas import tpu as pltpu
from jax.sharding import PartitionSpec as P

LANES = 128
STEPS_PER_OCTAVE = 128.0
TOP = 32766.0
LEAST = 2.0 ** -120
VMEM_LIMIT = 48 * 1024 * 1024
SUMS_LIMIT = 36 * 1024 * 1024
SLOTS = 4
SUB = 256


def tile_of(size, largest):
    tile = largest
    while size % tile:
        tile //= 2
    return tile


def dot(left, right, dims):
    return lax.dot_general(left, right, (dims, ((), ())), preferred_element_type=jnp.float32)


def encode(values):
    most = jnp.maximum(jnp.max(jnp.abs(values), axis=1, keepdims=True), LEAST)
    level = jnp.ceil(jnp.log2(most) * STEPS_PER_OCTAVE) + 1.0
    codes = jnp.round(values * jnp.exp2(level * (-1.0 / STEPS_PER_OCTAVE)) * TOP)
    return codes.astype(jnp.int32).astype(jnp.int16), level


def decode(codes, levels):
    scale = jnp.exp2(levels.astype(jnp.int32).astype(jnp.float32) * (1.0 / STEPS_PER_OCTAVE)) * (1.0 / TOP)
    return codes.astype(jnp.int32).astype(jnp.float32) * scale


def to_levels(levels):
    return levels.astype(jnp.int32).astype(jnp.int16)


def params(limit=VMEM_LIMIT):
    return pltpu.CompilerParams(vmem_limit_bytes=limit)


def cost(flops, moved):
    return pl.CostEstimate(flops=flops, bytes_accessed=moved, transcendentals=0)


def align_rows(pick_ref, pieces, aligned_ref):
    depth = aligned_ref.shape[1]
    chunk = tile_of(depth, 512)
    for at in range(0, depth, chunk):
        cols = slice(at, at + chunk)
        gathered = jnp.concatenate([piece[:, cols] for piece in pieces], axis=0)
        aligned_ref[:, cols] = dot(pick_ref[...], gathered, ((1,), (0,))).astype(jnp.bfloat16)


def sums_kernel(n_pieces, n_blocks, n_later, first, coded, kept_rows, sent_rows, tile, *refs):
    refs = list(refs)
    if n_pieces:
        pick_ref = refs.pop(0)
        pieces = [refs.pop(0) for _ in range(n_pieces)]
        weight_ref = refs.pop(0)
        del refs[:n_later]
        aligned_ref = refs.pop(0)
    else:
        aligned_ref = refs.pop(0)
        weight_ref = refs.pop(0)
        del refs[:n_later]
    kept = [refs.pop(0) for _ in kept_rows]
    sent = [refs.pop(0) for _ in sent_rows]
    levels_ref, held_ref, arrived = refs
    step = pl.program_id(0)
    width = sent[0].shape[1] - LANES

    def fetch(at):
        rows = pl.ds(pl.multiple_of((first + at) * tile, tile), tile)
        return pltpu.make_async_copy(weight_ref.at[rows], held_ref.at[at], arrived.at[at])

    @pl.when(step == 0)
    def _():
        for at in range(held_ref.shape[0]):
            fetch(at).start()
        if n_pieces:
            align_rows(pick_ref, pieces, aligned_ref)
        levels_ref[...] = jnp.zeros_like(levels_ref)

    lane = lax.broadcasted_iota(jnp.int32, levels_ref.shape, 1)
    levels = levels_ref[...]
    for part in range(n_blocks):
        at = step * n_blocks + part
        fetch(at).wait()
        values = dot(aligned_ref[...], held_ref[at], ((1,), (1,)))
        for ref, rows in zip(kept, kept_rows):
            ref[:, part * tile:(part + 1) * tile] = values[rows]
        codes, level = encode(values[coded:])
        levels = jnp.where(lane == at, level, levels)
        cols = pl.ds(pl.multiple_of(at * tile, tile), tile)
        for ref, rows in zip(sent, sent_rows):
            ref[:, cols] = codes[rows.start - coded:rows.stop - coded]
    levels_ref[...] = levels

    @pl.when(step == pl.num_programs(0) - 1)
    def _():
        for ref, rows in zip(sent, sent_rows):
            ref[:, width:] = to_levels(levels[rows.start - coded:rows.stop - coded])


def partial_sums(aligned, align, weight, tile, first, count, kept_rows, sent_rows, later_than, name):
    depth = weight.shape[1]
    width = count * tile
    whole = lambda i: (0, 0)
    operands = [align[0], *align[1]] if aligned is None else [aligned]
    total = operands[0].shape[0]
    coded = min(rows.start for rows in sent_rows)
    n_blocks = 2 if count % 2 == 0 else 1
    heights = lambda spans: [span.stop - span.start for span in spans]
    anywhere = pl.BlockSpec(memory_space=pl.ANY)
    in_specs = [pl.BlockSpec(operand.shape, whole) for operand in operands] + [anywhere] * (1 + len(later_than))
    out_specs = [pl.BlockSpec((height, n_blocks * tile), lambda i: (0, i)) for height in heights(kept_rows)]
    out_specs += [pl.BlockSpec((height, width + LANES), whole) for height in heights(sent_rows)]
    out_shape = [jax.ShapeDtypeStruct((height, width), jnp.float32) for height in heights(kept_rows)]
    out_shape += [jax.ShapeDtypeStruct((height, width + LANES), jnp.int16) for height in heights(sent_rows)]
    if aligned is None:
        out_specs.insert(0, pl.BlockSpec((total, depth), whole))
        out_shape.insert(0, jax.ShapeDtypeStruct((total, depth), jnp.bfloat16))
    outs = pl.pallas_call(
        functools.partial(
            sums_kernel, 0 if aligned is not None else len(align[1]), n_blocks, len(later_than), first, coded, kept_rows, sent_rows, tile),
        grid=(count // n_blocks,), in_specs=in_specs, out_specs=out_specs, out_shape=out_shape,
        scratch_shapes=[
            pltpu.VMEM((total - coded, LANES), jnp.float32),
            pltpu.VMEM((count, tile, depth), weight.dtype),
            pltpu.SemaphoreType.DMA((count,)),
        ],
        compiler_params=params(SUMS_LIMIT), cost_estimate=cost(2 * total * width * depth, 2 * width * depth), name=name,
    )(*operands, weight, *later_than)
    if aligned is None:
        aligned, *outs = outs
    return aligned, outs[:len(kept_rows)], outs[len(kept_rows):]


def weight_kernel(places, first, n_later, tile, aligned_ref, *refs):
    n_pieces = sum(len(place) for place in places)
    pieces = [ref[...] for ref in refs[:n_pieces]]
    out_ref, held_ref, left_sem = refs[n_pieces + n_later:]
    step = pl.program_id(0)
    last = pl.num_programs(0) - 1
    slots = held_ref.shape[0]

    def leave(at):
        rows = pl.ds(pl.multiple_of((first + at) * tile, tile), tile)
        slot = lax.rem(at, slots)
        return pltpu.make_async_copy(held_ref.at[slot], out_ref.at[rows], left_sem.at[slot])

    @pl.when(step >= slots)
    def _():
        leave(step - slots).wait()

    blocks = [functools.reduce(lambda x, y: x + y, [pieces[at] for at in place]) for place in places]
    left = jnp.concatenate(blocks, axis=0)
    depth = aligned_ref.shape[1]
    chunk = tile_of(depth, 1024)
    block = held_ref.at[lax.rem(step, slots)]
    for at in range(0, depth, chunk):
        cols = slice(at, at + chunk)
        block[:, cols] = dot(left, aligned_ref[:, cols], ((0,), (0,))).astype(jnp.bfloat16)
    leave(step).start()

    @pl.when(step == last)
    def _():
        for back in range(slots - 1, -1, -1):
            @pl.when(last >= back)
            def _():
                leave(last - back).wait()


def weight_grads(aligned, pieces, places, tile, first, count, filled, later_than):
    total, depth = aligned.shape
    rows, hidden = pieces[0].shape
    later = ([] if filled is None else [filled]) + list(later_than)
    return pl.pallas_call(
        functools.partial(weight_kernel, places, first, len(later), tile),
        grid=(count,),
        in_specs=[pl.BlockSpec((total, depth), lambda i: (0, 0))]
        + [pl.BlockSpec((rows, tile), lambda i: (0, i + first))] * len(pieces)
        + [pl.BlockSpec(memory_space=pl.ANY)] * len(later),
        out_specs=pl.BlockSpec(memory_space=pl.ANY),
        out_shape=jax.ShapeDtypeStruct((hidden, depth), jnp.bfloat16),
        scratch_shapes=[pltpu.VMEM((SLOTS, tile, depth), jnp.bfloat16), pltpu.SemaphoreType.DMA((SLOTS,))],
        input_output_aliases={} if filled is None else {1 + len(pieces): 0},
        compiler_params=params(), cost_estimate=cost(2 * total * count * tile * depth, 2 * count * tile * depth),
        name="weight_grads",
    )(aligned, *pieces, *later)


def fold_kernel(kept_ref, got_ref, *refs):
    n_passed = (len(refs) - 2) // 2
    next_ref, sent_ref = refs[n_passed:n_passed + 2]
    width = kept_ref.shape[1]
    half = next_ref.shape[0]
    sub = tile_of(width, SUB)
    lane = lax.broadcasted_iota(jnp.int32, (half, LANES), 1)
    levels = jnp.zeros(lane.shape, jnp.float32)
    got_levels = got_ref[:, width:]
    for at in range(width // sub):
        cols = slice(at * sub, (at + 1) * sub)
        total = kept_ref[:, cols] + decode(got_ref[:, cols], got_levels[:, at:at + 1])
        next_ref[:, cols] = total[:half]
        codes, level = encode(total[half:])
        sent_ref[:, cols] = codes
        levels = jnp.where(lane == at, level, levels)
    sent_ref[:, width:] = to_levels(levels)


def fold(kept, got, passed):
    vmem, anywhere = pl.BlockSpec(memory_space=pltpu.VMEM), pl.BlockSpec(memory_space=pl.ANY)
    rows, width = kept.shape
    kept, sent, *passed = pl.pallas_call(
        fold_kernel,
        in_specs=[vmem] * 2 + [anywhere] * len(passed),
        out_specs=[vmem] * 2 + [anywhere] * len(passed),
        out_shape=[jax.ShapeDtypeStruct((rows // 2, width), kept.dtype), jax.ShapeDtypeStruct((rows // 2, got.shape[1]), got.dtype)]
        + [jax.ShapeDtypeStruct(array.shape, array.dtype) for array in passed],
        input_output_aliases={2 + at: 2 + at for at in range(len(passed))},
        compiler_params=params(), cost_estimate=cost(kept.size * 20, kept.size * 12), name="fold",
    )(kept, got, *passed)
    return kept, sent, passed


def line_fold_kernel(kept_ref, got_ref, two_ref, three_ref):
    width = kept_ref.shape[1]
    rows = two_ref.shape[0]
    sub = tile_of(width, SUB)
    lane = lax.broadcasted_iota(jnp.int32, (2 * rows, LANES), 1)
    levels = jnp.zeros(lane.shape, jnp.float32)
    got_levels = got_ref[rows:, width:]
    for at in range(width // sub):
        cols = slice(at * sub, (at + 1) * sub)
        came = decode(got_ref[rows:, cols], got_levels[:, at:at + 1])
        came = jnp.concatenate([came[rows:], came[:rows]], axis=0)
        codes, level = encode(kept_ref[:, cols] + came)
        two_ref[:, cols] = codes[:rows]
        three_ref[:, cols] = codes[rows:]
        levels = jnp.where(lane == at, level, levels)
    two_ref[:, width:] = to_levels(levels[:rows])
    three_ref[:, width:] = to_levels(levels[rows:])


def line_fold(kept, got):
    rows = kept.shape[0] // 2
    like = jax.ShapeDtypeStruct((rows, got.shape[1]), got.dtype)
    return pl.pallas_call(
        line_fold_kernel, out_shape=[like, like], compiler_params=params(),
        cost_estimate=cost(kept.size * 20, kept.size * 12), name="line_fold",
    )(kept, got)


def total_kernel(counts, *refs):
    refs = list(refs)
    out_ref = refs.pop()
    base = 0
    for count in counts:
        kept_ref, got, refs = refs[0], refs[1:count], refs[count:]
        rows, width = kept_ref.shape
        sub = tile_of(width, SUB)
        for at in range(width // sub):
            cols = slice(at * sub, (at + 1) * sub)
            total = kept_ref[:, cols]
            for ref in got:
                total = total + decode(ref[:rows, cols], ref[:rows, width:][:, at:at + 1])
            out_ref[:, base + at * sub:base + (at + 1) * sub] = total.astype(jnp.bfloat16)
        base += width


def totals(parts, later_than):
    rows = parts[0][0].shape[0]
    hidden = sum(part[0].shape[1] for part in parts)
    flat = [array for part in parts for array in part]
    return pl.pallas_call(
        functools.partial(total_kernel, [len(part) for part in parts]),
        in_specs=[pl.BlockSpec(memory_space=pltpu.VMEM)] * len(flat) + [pl.BlockSpec(memory_space=pl.ANY)] * len(later_than),
        out_shape=jax.ShapeDtypeStruct((rows, hidden), jnp.bfloat16),
        compiler_params=params(), cost_estimate=cost(rows * hidden * 40, rows * hidden * 14), name="totals",
    )(*flat, *later_than)


def send(value, axis, flip, size):
    return lax.ppermute(value, axis, [(i, i ^ flip) for i in range(size)])


def stack_kernel(n_values, *refs):
    out_ref = refs[-1]
    rows = refs[0].shape[0]
    for at, ref in enumerate(refs[:n_values]):
        out_ref[at * rows:(at + 1) * rows] = ref[...]


def stacked(values, later_than=()):
    rows, width = values[0].shape
    return pl.pallas_call(
        functools.partial(stack_kernel, len(values)),
        in_specs=[pl.BlockSpec(memory_space=pltpu.VMEM)] * len(values) + [pl.BlockSpec(memory_space=pl.ANY)] * len(later_than),
        out_shape=jax.ShapeDtypeStruct((len(values) * rows, width), values[0].dtype),
        compiler_params=params(), cost_estimate=cost(0, 4 * len(values) * rows * width), name="stacked",
    )(*values, *later_than)


def same_kernel(*refs):
    pass


def handed_on(values, later_than):
    anywhere = pl.BlockSpec(memory_space=pl.ANY)
    return pl.pallas_call(
        same_kernel,
        in_specs=[anywhere] * (len(values) + len(later_than)), out_specs=[anywhere] * len(values),
        out_shape=[jax.ShapeDtypeStruct(value.shape, value.dtype) for value in values],
        input_output_aliases={at: at for at in range(len(values))},
        compiler_params=params(), cost_estimate=cost(0, 0), name="handed_on",
    )(*values, *later_than)


def gather_cotangent(cotangent, n_col):
    flips = list(range(0, n_col, 2))
    pieces = [cotangent] + [send(cotangent, "col", flip, n_col) for flip in flips[1:]]
    stacks = [stacked(pieces[:2])]
    stacks.append(stacked(pieces[2:], stacks))
    stacks += [send(stack, "col", 1, n_col) for stack in stacks]
    return stacks, flips + [flip ^ 1 for flip in flips]


def halving_order(size):
    order = [0]
    while len(order) < size:
        order = [2 * o for o in order] + [2 * o + 1 for o in order]
    return order


def part_slices(tiles, shares):
    ends = [tiles * sum(shares[:at]) // 7 for at in range(len(shares) + 1)]
    return [(first, last - first) for first, last in zip(ends, ends[1:])]


def halving_sums(align, weight, act_pieces, n_row, offsets, tile):
    total = align[0].shape[0]
    kept_rows, sent_rows = [slice(0, total // 2)], [slice(total // 2, total)]
    count = weight.shape[0] // tile
    aligned, [kept], [sent] = partial_sums(None, align, weight, tile, 0, count, kept_rows, sent_rows, [], "sums")
    got = send(sent, "row", 1, n_row)
    evens = range(2, n_row, 2)
    for o, piece in zip(evens, handed_on([act_pieces[o] for o in evens], [aligned])):
        act_pieces[o], act_pieces[o + 1] = piece, send(piece, "row", 1, n_row)
    step = 2
    while step < n_row:
        kept, sent, _ = fold(kept, got, [])
        got = send(sent, "row", step, n_row)
        step *= 2
    places = [[at] for at in range(n_row)]
    weight_grad = weight_grads(aligned, [act_pieces[o] for o in offsets], places, tile, 0, count, None, [sent])
    return weight_grad, totals([[kept, got]], [weight_grad])


def line_sums(align, weight, activations, act_pieces, tile):
    total = align[0].shape[0]
    rows = total // 4
    kept_rows = [slice(0, rows), slice(2 * rows, total)]
    sent_rows = [slice(rows, total), slice(rows, 2 * rows)]
    tiles = weight.shape[0] // tile
    first_part, second_part = part_slices(tiles, (3, 4))
    inwards, outwards, middle = [(0, 1), (3, 2)], [(1, 0), (2, 3)], [(1, 2), (2, 1)]

    def spread(sent):
        return lax.ppermute(sent[0], "row", inwards), lax.ppermute(sent[1], "row", outwards)

    def cross(kept, got):
        two, three = line_fold(kept, got)
        return two, lax.ppermute(three, "row", middle), lax.ppermute(two, "row", [(1, 3), (2, 0)])

    aligned, kept_a, sent_a = partial_sums(None, align, weight, tile, *first_part, kept_rows, sent_rows, [], "sums_a")
    got_a = spread(sent_a)
    act_pieces[2], activations = handed_on([act_pieces[2], stacked([activations], align[1][:1])], [aligned])
    across = lax.ppermute(act_pieces[2], "row", outwards)
    near = lax.ppermute(activations, "row", middle)
    _, kept_b, sent_b = partial_sums(aligned, None, weight, tile, *second_part, kept_rows, sent_rows, [act_pieces[1]], "sums_b")
    sent_b = handed_on(sent_b, [got_a[1]])
    got_b = spread(sent_b)
    two_a, *crossed_a = cross(kept_a[1], got_a[0])
    pieces = [activations, act_pieces[1], act_pieces[2], across, near]
    places = [[0], [1], [2], [3, 4]]
    (first_a, count_a), (first_b, count_b) = part_slices(tiles, (4, 3))
    grad = weight_grads(aligned, pieces, places, tile, first_a, count_a, None, [two_a])
    two_b, *crossed_b = cross(kept_b[1], got_b[0])
    weight_grad = weight_grads(aligned, pieces, places, tile, first_b, count_b, grad, [two_b])
    return weight_grad, totals([[kept_a[0], *got_a, *crossed_a], [kept_b[0], *got_b, *crossed_b]], [weight_grad])


def body(n_row, n_col, activations, cotangent, down_weight, row_order):
    rows, hidden = activations.shape
    shard = cotangent.shape[0]
    mine_row, mine_col = lax.axis_index("row"), lax.axis_index("col")
    offsets = list(range(4)) if n_row == 4 else halving_order(n_row)

    pieces, flips = gather_cotangent(cotangent, n_col)
    act_pieces = {o: send(activations, "row", o, n_row) for o in [1, *range(2, n_row, 2)]}
    act_pieces[0] = activations

    order = row_order.reshape(n_row, rows)
    order = jnp.concatenate([lax.dynamic_index_in_dim(order, mine_row ^ o, 0, keepdims=False) for o in offsets])
    owner = mine_col ^ jnp.asarray(flips, jnp.int32)
    named = (owner[:, None] * shard + jnp.arange(shard, dtype=jnp.int32)[None, :]).reshape(-1)
    pick = (order[:, None] == named[None, :]).astype(jnp.bfloat16)

    tile = tile_of(hidden, 256)
    if n_row == 4:
        return line_sums((pick, pieces), down_weight, activations, act_pieces, tile)
    return halving_sums((pick, pieces), down_weight, act_pieces, n_row, offsets, tile)


def solution(mesh):
    in_specs = (P("row", "col"), P("col", "row"), P("col", "row"), P())
    out_specs = (P("col", "row"), P("row", "col"))
    fn = functools.partial(body, mesh.shape["row"], mesh.shape["col"])
    return jax.shard_map(fn, mesh=mesh, in_specs=in_specs, out_specs=out_specs, check_vma=False)
```

time: 86.2 us -> 95.7 us (1.11)
  starting transfers between devices: 16 us -> 31 us
  waiting for transfers between devices: 31.7 us -> 20.3 us
  Pallas kernels: 34.9 us -> 39.5 us
  local copies, waits for them, and re-layouts: 1.8 us -> 2.81 us
    ppermute x12 -> x7, waiting for transfers between devices: 31.7 us -> 5.72 us  [send(): return lax.ppermute(value, axis, [(i, i ^ flip) for i in range(size)])]
    ppermute x0 -> x10, starting transfers between devices: none -> 21.6 us  [the longest x2 13.1 us: spread(): lax.ppermute(sent[0], 'row', inwards)]
    ppermute x0 -> x10, waiting for transfers between devices: none -> 14.6 us  [the longest x2 8.76 us: cross(): lax.ppermute(two, 'row', [(1, 3), (2, 0)])]
    ppermute x12 -> x7, starting transfers between devices: 16 us -> 9.31 us  [send(): return lax.ppermute(value, axis, [(i, i ^ flip) for i in range(size)])]
    pallas_call x2, Pallas kernels: 17.1 us -> 22.7 us  [partial_sums(): pl.pallas_call(functools.partial(sums_kernel, 0 if aligned is not None el...]
    pallas_call x5, Pallas kernels: 17.8 us -> 16.6 us  [the longest x2 13.5 us: weight_grads(): pl.pallas_call(functools.partial(weight_kernel, places, first, len(later)...]
    unnamed x4, local copies, waits for them, and re-layouts: 0.96 us -> 1.96 us
  transfers between devices with their start and end apart: 12 -> 17, of which waited for: 7 -> 4; matrix products, arithmetic and copies ran while one was open for 2% -> 2% of each run, Pallas kernels for 39% -> 40%
where the time goes in v6:
time: 95.7 us; the launch traced here: 95.3 us
  Pallas kernels  39.5 us (41%)
  starting transfers between devices  31 us (32%)
  waiting for transfers between devices  20.3 us (21%)
  local copies, waits for them, and re-layouts  2.81 us (3%)
    pallas_call x2, Pallas kernels, partial_sums(): pl.pallas_call(functools.partial(sums_kernel, 0 if aligned is not None el...  22.7 us
    pallas_call x2, Pallas kernels, weight_grads(): pl.pallas_call(functools.partial(weight_kernel, places, first, len(later)...  13.5 us
    ppermute x2, starting transfers between devices, spread(): lax.ppermute(sent[0], 'row', inwards)  13.1 us
    ppermute x7, starting transfers between devices, send(): return lax.ppermute(value, axis, [(i, i ^ flip) for i in range(size)])  9.31 us
    ppermute x2, waiting for transfers between devices, cross(): lax.ppermute(two, 'row', [(1, 3), (2, 0)])  8.76 us
    ppermute x2, waiting for transfers between devices, spread(): lax.ppermute(sent[0], 'row', inwards)  5.78 us
    ppermute x7, waiting for transfers between devices, send(): return lax.ppermute(value, axis, [(i, i ^ flip) for i in range(size)])  5.72 us
    ppermute x2, starting transfers between devices, spread(): lax.ppermute(sent[1], 'row', outwards)  2.58 us
  transfers between devices with their start and end apart: 17, of which 4 were waited for; matrix products, arithmetic and copies ran while one was open for 2% of the time, Pallas kernels for 40%

profile of v6, /device:TPU:0, one launch (start us, length us, event | category | flops | bytes accessed | tf_op | source)
XLA Modules:
  0.0 95.3 jit_solution(9636554957413766902)
XLA Ops:
  0.6 3.0 %collective-permute-start = (bf16[32,4096]{1,0:T(8,128)(2,1)}, bf16[32,4096]{1,0:T(8,128)(2,1)S(1)}, u32[]{:S(2)}, u32[]{:S(2)}) collective-permute-start(bf16[32,4096]{1,0:T(8,128)(2,1)} %refs_0_.2), channel_id=1, source_target_pairs={{0,2},{1,3},{2,0},{3,1},{4,6},{5,7},{6,4},{7,5},{8,10},{9,11},{10,... | collective-permute-start | bytes 786440 | tf_op jit(solution)/shard_map/ppermute | solution.py:295
  3.6 1.5 %collective-permute-start.1 = (bf16[32,4096]{1,0:T(8,128)(2,1)}, bf16[32,4096]{1,0:T(8,128)(2,1)S(1)}, u32[]{:S(2)}, u32[]{:S(2)}) collective-permute-start(bf16[32,4096]{1,0:T(8,128)(2,1)} %refs_0_.2), channel_id=1, source_target_pairs={{0,4},{1,5},{2,6},{3,7},{4,0},{5,1},{6,2},{7,3},{8,12},{9,13},{10,... | collective-permute-start | bytes 786440 | tf_op jit(solution)/shard_map/ppermute | solution.py:295
  5.2 2.0 %collective-permute-start.6 = (bf16[64,3584]{1,0:T(8,128)(2,1)}, bf16[64,3584]{1,0:T(8,128)(2,1)S(1)}, u32[]{:S(2)}, u32[]{:S(2)}) collective-permute-start(bf16[64,3584]{1,0:T(8,128)(2,1)} %refs_0_.3), channel_id=1, source_target_pairs={{0,8},{8,0},{16,24},{24,16},{1,9},{9,1},{17,25},{25,17},{2,10},{10... | collective-permute-start | bytes 1376264 | tf_op jit(solution)/shard_map/ppermute | solution.py:295
  7.2 2.6 %collective-permute-start.5 = (bf16[64,3584]{1,0:T(8,128)(2,1)}, bf16[64,3584]{1,0:T(8,128)(2,1)S(1)}, u32[]{:S(2)}, u32[]{:S(2)}) collective-permute-start(bf16[64,3584]{1,0:T(8,128)(2,1)} %refs_0_.3), channel_id=1, source_target_pairs={{0,16},{8,24},{16,0},{24,8},{1,17},{9,25},{17,1},{25,9},{2,18},{10... | collective-permute-start | bytes 1376264 | tf_op jit(solution)/shard_map/ppermute | solution.py:295
  9.8 0.7 xor_multiply_fusion
  10.5 0.5 collective-permute-done.refs_1_
  11.0 0.9 copy-done.1
  12.0 5.2 %collective-permute-done.1.refs_0_ = bf16[32,4096]{1,0:T(8,128)(2,1)S(1)} collective-permute-done((bf16[32,4096]{1,0:T(8,128)(2,1)}, bf16[32,4096]{1,0:T(8,128)(2,1)S(1)}, u32[]{:S(2)}, u32[]{:S(2)}) %collective-permute-start.1) | collective-permute-done | bytes 262176 | tf_op jit(solution)/shard_map/ppermute | solution.py:295
  17.4 0.8 reshape.24
  18.2 0.1 add.40
  18.3 0.1 pad_add_fusion
  18.3 0.1 compare_convert_fusion.refs_0_
  18.5 1.0 %copy-done = bf16[64,3584]{1,0:T(8,128)(2,1)S(1)} copy-done((bf16[64,3584]{1,0:T(8,128)(2,1)S(1)}, bf16[64,3584]{1,0:T(8,128)(2,1)}, u32[]{:S(2)}) %copy-start) | copy-done | bytes 458776
  19.5 10.0 %sums_a.1 = (bf16[256,4096]{1,0:T(8,128)(2,1)S(1)}, f32[64,1536]{1,0:T(8,128)S(1)}, f32[128,1536]{1,0:T(8,128)S(1)}, s16[192,1664]{1,0:T(8,128)(2,1)S(1)}, s16[64,1664]{1,0:T(8,128)(2,1)S(1)}) custom-call(bf16[256,256]{1,0:T(8,128)(2,1)S(1)} %compare_convert_fusion.refs_0_, bf16[64,4096]{1,0:T(8,128)(2,1)S(1)} %stacked.3.refs_2_.refs_1_, ...), custom_call_target="tpu_custom_call" | custom-call | flops 3221225472 | bytes 12582912 | tf_op jit(solution)/shard_map/sums_a/pallas_call | solution.py:133
  29.5 1.3 %collective-permute-start.10 = (s16[64,1664]{1,0:T(8,128)(2,1)S(1)}, s16[64,1664]{1,0:T(8,128)(2,1)S(1)}, u32[]{:S(2)}, u32[]{:S(2)}) collective-permute-start(s16[64,1664]{1,0:T(8,128)(2,1)S(1)} %get-tuple-element.28), channel_id=1, source_target_pairs={{8,0},{16,24},{9,1},{17,25},{10,2},{18,26},{11,3},{19,27},{12,4},{... | collective-permute-start | bytes 638984 | tf_op jit(solution)/shard_map/ppermute | solution.py:380
  30.8 4.6 %collective-permute-start.9 = (s16[192,1664]{1,0:T(8,128)(2,1)S(1)}, s16[192,1664]{1,0:T(8,128)(2,1)S(1)}, u32[]{:S(2)}, u32[]{:S(2)}) collective-permute-start(s16[192,1664]{1,0:T(8,128)(2,1)S(1)} %get-tuple-element.23), channel_id=1, source_target_pairs={{0,8},{24,16},{1,9},{25,17},{2,10},{26,18},{3,11},{27,19},{4,12},{... | collective-permute-start | bytes 1916936 | tf_op jit(solution)/shard_map/ppermute | solution.py:380
  35.4 1.3 %collective-permute-start.7 = (bf16[64,3584]{1,0:T(8,128)(2,1)S(1)}, bf16[64,3584]{1,0:T(8,128)(2,1)S(1)}, u32[]{:S(2)}, u32[]{:S(2)}) collective-permute-start(bf16[64,3584]{1,0:T(8,128)(2,1)S(1)} %get-tuple-element.21.refs_2_), channel_id=1, source_target_pairs={{8,0},{16,24},{9,1},{17,25},{10,2},{18,26},{11,3},{19,27},{12,4},{... | collective-permute-start | bytes 1376264 | tf_op jit(solution)/shard_map/ppermute | solution.py:389
  36.7 0.7 collective-permute-start.8
  37.4 12.7 %sums_b.1 = (f32[64,2048]{1,0:T(8,128)S(1)}, f32[128,2048]{1,0:T(8,128)S(1)}, s16[192,2176]{1,0:T(8,128)(2,1)S(1)}, s16[64,2176]{1,0:T(8,128)(2,1)S(1)}) custom-call(bf16[256,4096]{1,0:T(8,128)(2,1)S(1)} %get-tuple-element.19.refs_2_.aligned_ref.refs_0_, bf16[3584,4096]{1,0:T(8,128)(2,1)} %refs_1_.1, bf16[64,3584]{1,0:T(8,128)(2,1)S(1)} %collective-permute-done.6.refs_1_.refs_2_), custom_call_target="tpu_custom_call" | custom-call | flops 4294967296 | bytes 16777216 | tf_op jit(solution)/shard_map/sums_b/pallas_call | solution.py:133
  50.2 8.5 %collective-permute-start.11 = (s16[192,2176]{1,0:T(8,128)(2,1)S(1)}, s16[192,2176]{1,0:T(8,128)(2,1)S(1)}, u32[]{:S(2)}, u32[]{:S(2)}) collective-permute-start(s16[192,2176]{1,0:T(8,128)(2,1)S(1)} %get-tuple-element.29), channel_id=1, source_target_pairs={{0,8},{24,16},{1,9},{25,17},{2,10},{26,18},{3,11},{27,19},{4,12},{... | collective-permute-start | bytes 2506760 | tf_op jit(solution)/shard_map/ppermute | solution.py:380
  58.8 1.3 %collective-permute-start.14 = (s16[64,2176]{1,0:T(8,128)(2,1)S(1)}, s16[64,2176]{1,0:T(8,128)(2,1)S(1)}, u32[]{:S(2)}, u32[]{:S(2)}) collective-permute-start(s16[64,2176]{1,0:T(8,128)(2,1)S(1)} %get-tuple-element.34), channel_id=1, source_target_pairs={{8,0},{16,24},{9,1},{17,25},{10,2},{18,26},{11,3},{19,27},{12,4},{... | collective-permute-start | bytes 835592 | tf_op jit(solution)/shard_map/ppermute | solution.py:380
  60.1 0.7 line_fold.2
  60.8 0.7 collective-permute-start.12
  61.5 1.3 %collective-permute-start.13 = (s16[64,1664]{1,0:T(8,128)(2,1)S(1)}, s16[64,1664]{1,0:T(8,128)(2,1)S(1)}, u32[]{:S(2)}, u32[]{:S(2)}) collective-permute-start(s16[64,1664]{1,0:T(8,128)(2,1)S(1)} %get-tuple-element.24.refs_5_), channel_id=1, source_target_pairs={{8,24},{16,0},{9,25},{17,1},{10,26},{18,2},{11,27},{19,3},{12,28},... | collective-permute-start | bytes 638984 | tf_op jit(solution)/shard_map/ppermute | solution.py:384
  62.8 7.5 %weight_grads.2.refs_5_ = bf16[3584,4096]{1,0:T(8,128)(2,1)} custom-call(bf16[256,4096]{1,0:T(8,128)(2,1)S(1)} %get-tuple-element.19.refs_2_.aligned_ref.refs_0_, bf16[64,3584]{1,0:T(8,128)(2,1)S(1)} %get-tuple-element.20.refs_0_, bf16[64,3584]{1,0:T(8,128)(2,1)S(1)} %collective-permute-done.6.refs_1_.refs_2_, ...), custom_call_target="tpu_custom_call" | custom-call | flops 4294967296 | bytes 16777216 | tf_op jit(solution)/shard_map/weight_grads/pallas_call | solution.py:188
  70.3 5.8 %collective-permute-done.11.got_ref.refs_6_ = s16[192,2176]{1,0:T(8,128)(2,1)S(1)} collective-permute-done((s16[192,2176]{1,0:T(8,128)(2,1)S(1)}, s16[192,2176]{1,0:T(8,128)(2,1)S(1)}, u32[]{:S(2)}, u32[]{:S(2)}) %collective-permute-start.11) | collective-permute-done | bytes 835616 | tf_op jit(solution)/shard_map/ppermute | solution.py:380
  76.1 0.9 line_fold.3
  77.0 0.7 collective-permute-start.15
  77.7 1.3 %collective-permute-start.16 = (s16[64,2176]{1,0:T(8,128)(2,1)S(1)}, s16[64,2176]{1,0:T(8,128)(2,1)S(1)}, u32[]{:S(2)}, u32[]{:S(2)}) collective-permute-start(s16[64,2176]{1,0:T(8,128)(2,1)S(1)} %get-tuple-element.30.refs_6_), channel_id=1, source_target_pairs={{8,24},{16,0},{9,25},{17,1},{10,26},{18,2},{11,27},{19,3},{12,28},... | collective-permute-start | bytes 835592 | tf_op jit(solution)/shard_map/ppermute | solution.py:384
  79.0 6.0 %weight_grads.3.refs_10_ = bf16[3584,4096]{1,0:T(8,128)(2,1)} custom-call(bf16[256,4096]{1,0:T(8,128)(2,1)S(1)} %get-tuple-element.19.refs_2_.aligned_ref.refs_0_, bf16[64,3584]{1,0:T(8,128)(2,1)S(1)} %get-tuple-element.20.refs_0_, bf16[64,3584]{1,0:T(8,128)(2,1)S(1)} %collective-permute-done.6.refs_1_.refs_2_, ...), custom_call_target="tpu_custom_call", output_to_operand_aliasing={{}: (6, {})} | custom-call | flops 3221225472 | bytes 12582912 | tf_op jit(solution)/shard_map/weight_grads/pallas_call | solution.py:188
  85.1 8.8 %collective-permute-done.16.refs_9_ = s16[64,2176]{1,0:T(8,128)(2,1)S(1)} collective-permute-done((s16[64,2176]{1,0:T(8,128)(2,1)S(1)}, s16[64,2176]{1,0:T(8,128)(2,1)S(1)}, u32[]{:S(2)}, u32[]{:S(2)}) %collective-permute-start.16) | collective-permute-done | bytes 278560 | tf_op jit(solution)/shard_map/ppermute | solution.py:384
  93.8 1.5 %totals.1 = bf16[64,3584]{1,0:T(8,128)(2,1)} custom-call(f32[64,1536]{1,0:T(8,128)S(1)} %get-tuple-element.31.refs_0_, s16[192,1664]{1,0:T(8,128)(2,1)S(1)} %collective-permute-done.9.got_ref.refs_1_, s16[64,1664]{1,0:T(8,128)(2,1)S(1)} %collective-permute-done.10.refs_2_, s16[64,1664]{1,0:T(8,128)(2,1)S(1)} %collective-permute-done.12.refs_3_, ...), custom_call_target="tpu_custom_call" | custom-call | flops 9175040 | bytes 3211264 | tf_op jit(solution)/shard_map/totals/pallas_call | solution.py:286
  (25 shorter events, 0.4 us)
Async XLA Ops:
  0.6 10.4 %collective-permute-start = (bf16[32,4096]{1,0:T(8,128)(2,1)}, bf16[32,4096]{1,0:T(8,128)(2,1)S(1)}, u32[]{:S(2)}, u32[]{:S(2)}) collective-permute-start(bf16[32,4096]{1,0:T(8,128)(2,1)} %refs_0_.2), channel_id=1, source_target_pairs={{0,2},{1,3},{2,0},{3,1},{4,6},{5,7},{6,4},{7,5},{8,10},{9,11},{10,... | collective-permute-start | bytes 786440 | tf_op jit(solution)/shard_map/ppermute | solution.py:295
  3.6 13.6 %collective-permute-start.1 = (bf16[32,4096]{1,0:T(8,128)(2,1)}, bf16[32,4096]{1,0:T(8,128)(2,1)S(1)}, u32[]{:S(2)}, u32[]{:S(2)}) collective-permute-start(bf16[32,4096]{1,0:T(8,128)(2,1)} %refs_0_.2), channel_id=1, source_target_pairs={{0,4},{1,5},{2,6},{3,7},{4,0},{5,1},{6,2},{7,3},{8,12},{9,13},{10,... | collective-permute-start | bytes 786440 | tf_op jit(solution)/shard_map/ppermute | solution.py:295
  5.2 12.1 %collective-permute-start.2 = (bf16[32,4096]{1,0:T(8,128)(2,1)}, bf16[32,4096]{1,0:T(8,128)(2,1)S(1)}, u32[]{:S(2)}, u32[]{:S(2)}) collective-permute-start(bf16[32,4096]{1,0:T(8,128)(2,1)} %refs_0_.2), channel_id=1, source_target_pairs={{0,6},{1,7},{2,4},{3,5},{4,2},{5,3},{6,0},{7,1},{8,14},{9,15},{10,... | collective-permute-start | bytes 786440 | tf_op jit(solution)/shard_map/ppermute | solution.py:295
  5.2 32.3 %collective-permute-start.6 = (bf16[64,3584]{1,0:T(8,128)(2,1)}, bf16[64,3584]{1,0:T(8,128)(2,1)S(1)}, u32[]{:S(2)}, u32[]{:S(2)}) collective-permute-start(bf16[64,3584]{1,0:T(8,128)(2,1)} %refs_0_.3), channel_id=1, source_target_pairs={{0,8},{8,0},{16,24},{24,16},{1,9},{9,1},{17,25},{25,17},{2,10},{10... | collective-permute-start | bytes 1376264 | tf_op jit(solution)/shard_map/ppermute | solution.py:295
  7.2 28.2 %collective-permute-start.5 = (bf16[64,3584]{1,0:T(8,128)(2,1)}, bf16[64,3584]{1,0:T(8,128)(2,1)S(1)}, u32[]{:S(2)}, u32[]{:S(2)}) collective-permute-start(bf16[64,3584]{1,0:T(8,128)(2,1)} %refs_0_.3), channel_id=1, source_target_pairs={{0,16},{8,24},{16,0},{24,8},{1,17},{9,25},{17,1},{25,9},{2,18},{10... | collective-permute-start | bytes 1376264 | tf_op jit(solution)/shard_map/ppermute | solution.py:295
  11.0 1.0 copy-start.1
  12.0 7.6 %collective-permute-start.3 = (bf16[64,4096]{1,0:T(8,128)(2,1)S(1)}, bf16[64,4096]{1,0:T(8,128)(2,1)S(1)}, u32[]{:S(2)}, u32[]{:S(2)}) collective-permute-start(bf16[64,4096]{1,0:T(8,128)(2,1)S(1)} %stacked.3.refs_2_.refs_1_), channel_id=1, source_target_pairs={{0,1},{1,0},{2,3},{3,2},{4,5},{5,4},{6,7},{7,6},{8,9},{9,8},{10,11... | collective-permute-start | bytes 1572872 | tf_op jit(solution)/shard_map/ppermute | solution.py:295
  17.3 2.2 %collective-permute-start.4 = (bf16[64,4096]{1,0:T(8,128)(2,1)S(1)}, bf16[64,4096]{1,0:T(8,128)(2,1)S(1)}, u32[]{:S(2)}, u32[]{:S(2)}) collective-permute-start(bf16[64,4096]{1,0:T(8,128)(2,1)S(1)} %stacked.4.refs_2_), channel_id=1, source_target_pairs={{0,1},{1,0},{2,3},{3,2},{4,5},{5,4},{6,7},{7,6},{8,9},{9,8},{10,11... | collective-permute-start | bytes 1572872 | tf_op jit(solution)/shard_map/ppermute | solution.py:295
  18.5 1.0 %copy-start = (bf16[64,3584]{1,0:T(8,128)(2,1)S(1)}, bf16[64,3584]{1,0:T(8,128)(2,1)}, u32[]{:S(2)}) copy-start(bf16[64,3584]{1,0:T(8,128)(2,1)} %refs_0_.3) | copy-start | bytes 1376260
  29.5 20.7 %collective-permute-start.10 = (s16[64,1664]{1,0:T(8,128)(2,1)S(1)}, s16[64,1664]{1,0:T(8,128)(2,1)S(1)}, u32[]{:S(2)}, u32[]{:S(2)}) collective-permute-start(s16[64,1664]{1,0:T(8,128)(2,1)S(1)} %get-tuple-element.28), channel_id=1, source_target_pairs={{8,0},{16,24},{9,1},{17,25},{10,2},{18,26},{11,3},{19,27},{12,4},{... | collective-permute-start | bytes 638984 | tf_op jit(solution)/shard_map/ppermute | solution.py:380
  30.8 29.3 %collective-permute-start.9 = (s16[192,1664]{1,0:T(8,128)(2,1)S(1)}, s16[192,1664]{1,0:T(8,128)(2,1)S(1)}, u32[]{:S(2)}, u32[]{:S(2)}) collective-permute-start(s16[192,1664]{1,0:T(8,128)(2,1)S(1)} %get-tuple-element.23), channel_id=1, source_target_pairs={{0,8},{24,16},{1,9},{25,17},{2,10},{26,18},{3,11},{27,19},{4,12},{... | collective-permute-start | bytes 1916936 | tf_op jit(solution)/shard_map/ppermute | solution.py:380
  35.4 26.0 %collective-permute-start.7 = (bf16[64,3584]{1,0:T(8,128)(2,1)S(1)}, bf16[64,3584]{1,0:T(8,128)(2,1)S(1)}, u32[]{:S(2)}, u32[]{:S(2)}) collective-permute-start(bf16[64,3584]{1,0:T(8,128)(2,1)S(1)} %get-tuple-element.21.refs_2_), channel_id=1, source_target_pairs={{8,0},{16,24},{9,1},{17,25},{10,2},{18,26},{11,3},{19,27},{12,4},{... | collective-permute-start | bytes 1376264 | tf_op jit(solution)/shard_map/ppermute | solution.py:389
  36.7 26.0 %collective-permute-start.8 = (bf16[64,3584]{1,0:T(8,128)(2,1)S(1)}, bf16[64,3584]{1,0:T(8,128)(2,1)S(1)}, u32[]{:S(2)}, u32[]{:S(2)}) collective-permute-start(bf16[64,3584]{1,0:T(8,128)(2,1)S(1)} %get-tuple-element.20.refs_0_), channel_id=1, source_target_pairs={{8,16},{16,8},{9,17},{17,9},{10,18},{18,10},{11,19},{19,11},{12,20... | collective-permute-start | bytes 1376264 | tf_op jit(solution)/shard_map/ppermute | solution.py:390
  50.2 25.9 %collective-permute-start.11 = (s16[192,2176]{1,0:T(8,128)(2,1)S(1)}, s16[192,2176]{1,0:T(8,128)(2,1)S(1)}, u32[]{:S(2)}, u32[]{:S(2)}) collective-permute-start(s16[192,2176]{1,0:T(8,128)(2,1)S(1)} %get-tuple-element.29), channel_id=1, source_target_pairs={{0,8},{24,16},{1,9},{25,17},{2,10},{26,18},{3,11},{27,19},{4,12},{... | collective-permute-start | bytes 2506760 | tf_op jit(solution)/shard_map/ppermute | solution.py:380
  58.8 26.2 %collective-permute-start.14 = (s16[64,2176]{1,0:T(8,128)(2,1)S(1)}, s16[64,2176]{1,0:T(8,128)(2,1)S(1)}, u32[]{:S(2)}, u32[]{:S(2)}) collective-permute-start(s16[64,2176]{1,0:T(8,128)(2,1)S(1)} %get-tuple-element.34), channel_id=1, source_target_pairs={{8,0},{16,24},{9,1},{17,25},{10,2},{18,26},{11,3},{19,27},{12,4},{... | collective-permute-start | bytes 835592 | tf_op jit(solution)/shard_map/ppermute | solution.py:380
  60.8 24.3 %collective-permute-start.12 = (s16[64,1664]{1,0:T(8,128)(2,1)S(1)}, s16[64,1664]{1,0:T(8,128)(2,1)S(1)}, u32[]{:S(2)}, u32[]{:S(2)}) collective-permute-start(s16[64,1664]{1,0:T(8,128)(2,1)S(1)} %get-tuple-element.32), channel_id=1, source_target_pairs={{8,16},{16,8},{9,17},{17,9},{10,18},{18,10},{11,19},{19,11},{12,20... | collective-permute-start | bytes 638984 | tf_op jit(solution)/shard_map/ppermute | solution.py:384
  61.5 23.6 %collective-permute-start.13 = (s16[64,1664]{1,0:T(8,128)(2,1)S(1)}, s16[64,1664]{1,0:T(8,128)(2,1)S(1)}, u32[]{:S(2)}, u32[]{:S(2)}) collective-permute-start(s16[64,1664]{1,0:T(8,128)(2,1)S(1)} %get-tuple-element.24.refs_5_), channel_id=1, source_target_pairs={{8,24},{16,0},{9,25},{17,1},{10,26},{18,2},{11,27},{19,3},{12,28},... | collective-permute-start | bytes 638984 | tf_op jit(solution)/shard_map/ppermute | solution.py:384
  77.0 8.0 %collective-permute-start.15 = (s16[64,2176]{1,0:T(8,128)(2,1)S(1)}, s16[64,2176]{1,0:T(8,128)(2,1)S(1)}, u32[]{:S(2)}, u32[]{:S(2)}) collective-permute-start(s16[64,2176]{1,0:T(8,128)(2,1)S(1)} %get-tuple-element.35), channel_id=1, source_target_pairs={{8,16},{16,8},{9,17},{17,9},{10,18},{18,10},{11,19},{19,11},{12,20... | collective-permute-start | bytes 835592 | tf_op jit(solution)/shard_map/ppermute | solution.py:384
  77.7 16.1 %collective-permute-start.16 = (s16[64,2176]{1,0:T(8,128)(2,1)S(1)}, s16[64,2176]{1,0:T(8,128)(2,1)S(1)}, u32[]{:S(2)}, u32[]{:S(2)}) collective-permute-start(s16[64,2176]{1,0:T(8,128)(2,1)S(1)} %get-tuple-element.30.refs_6_), channel_id=1, source_target_pairs={{8,24},{16,0},{9,25},{17,1},{10,26},{18,2},{11,27},{19,3},{12,28},... | collective-permute-start | bytes 835592 | tf_op jit(solution)/shard_map/ppermute | solution.py:384

commit v7 on v6

--- a/solution.py
+++ b/solution.py
@@ -12,7 +12,8 @@
 TOP = 32766.0
 LEAST = 2.0 ** -120
 VMEM_LIMIT = 48 * 1024 * 1024
-SUMS_LIMIT = 36 * 1024 * 1024
+FETCH_LIMIT = 32 * 1024 * 1024
+SMALL_LIMIT = 8 * 1024 * 1024
 SLOTS = 4
 SUB = 256
 
@@ -61,32 +62,49 @@
         aligned_ref[:, cols] = dot(pick_ref[...], gathered, ((1,), (0,))).astype(jnp.bfloat16)
 
 
-def sums_kernel(n_pieces, n_blocks, n_later, first, coded, kept_rows, sent_rows, tile, *refs):
+def fetch_kernel(weight_ref, *refs):
+    out_ref, arrived = refs[-2:]
+    count = arrived.shape[0]
+    rows = out_ref.shape[0] // count
+    parts = [pl.ds(at * rows, rows) for at in range(count)]
+    copies = [pltpu.make_async_copy(weight_ref.at[part], out_ref.at[part], arrived.at[at]) for at, part in enumerate(parts)]
+    for copy in copies:
+        copy.start()
+    for copy in copies:
+        copy.wait()
+
+
+def fetched(weight, tile, count, later_than):
+    shape = (count * tile, weight.shape[1])
+    return pl.pallas_call(
+        fetch_kernel,
+        in_specs=[pl.BlockSpec(memory_space=pl.ANY)] * (1 + len(later_than)),
+        out_specs=pl.BlockSpec(memory_space=pltpu.VMEM),
+        out_shape=jax.ShapeDtypeStruct(shape, weight.dtype),
+        scratch_shapes=[pltpu.SemaphoreType.DMA((count,))],
+        compiler_params=params(FETCH_LIMIT), cost_estimate=cost(0, 2 * shape[0] * shape[1]), name="fetched",
+    )(weight, *later_than)
+
+
+def sums_kernel(n_pieces, n_blocks, n_later, resident, coded, kept_rows, sent_rows, tile, *refs):
     refs = list(refs)
     if n_pieces:
         pick_ref = refs.pop(0)
         pieces = [refs.pop(0) for _ in range(n_pieces)]
-        weight_ref = refs.pop(0)
-        del refs[:n_later]
-        aligned_ref = refs.pop(0)
     else:
         aligned_ref = refs.pop(0)
-        weight_ref = refs.pop(0)
-        del refs[:n_later]
+    weights = [refs.pop(0) for _ in range(1 if resident else n_blocks)]
+    del refs[:n_later]
+    if n_pieces:
+        aligned_ref = refs.pop(0)
     kept = [refs.pop(0) for _ in kept_rows]
     sent = [refs.pop(0) for _ in sent_rows]
-    levels_ref, held_ref, arrived = refs
+    levels_ref, = refs
     step = pl.program_id(0)
     width = sent[0].shape[1] - LANES
 
-    def fetch(at):
-        rows = pl.ds(pl.multiple_of((first + at) * tile, tile), tile)
-        return pltpu.make_async_copy(weight_ref.at[rows], held_ref.at[at], arrived.at[at])
-
     @pl.when(step == 0)
     def _():
-        for at in range(held_ref.shape[0]):
-            fetch(at).start()
         if n_pieces:
             align_rows(pick_ref, pieces, aligned_ref)
         levels_ref[...] = jnp.zeros_like(levels_ref)
@@ -95,13 +113,13 @@
     levels = levels_ref[...]
     for part in range(n_blocks):
         at = step * n_blocks + part
-        fetch(at).wait()
-        values = dot(aligned_ref[...], held_ref[at], ((1,), (1,)))
+        cols = pl.ds(pl.multiple_of(at * tile, tile), tile)
+        block = weights[0][cols] if resident else weights[part][...]
+        values = dot(aligned_ref[...], block, ((1,), (1,)))
         for ref, rows in zip(kept, kept_rows):
             ref[:, part * tile:(part + 1) * tile] = values[rows]
         codes, level = encode(values[coded:])
         levels = jnp.where(lane == at, level, levels)
-        cols = pl.ds(pl.multiple_of(at * tile, tile), tile)
         for ref, rows in zip(sent, sent_rows):
             ref[:, cols] = codes[rows.start - coded:rows.stop - coded]
     levels_ref[...] = levels
@@ -112,17 +130,22 @@
             ref[:, width:] = to_levels(levels[rows.start - coded:rows.stop - coded])
 
 
-def partial_sums(aligned, align, weight, tile, first, count, kept_rows, sent_rows, later_than, name):
+def partial_sums(aligned, align, weight, resident, tile, first, count, kept_rows, sent_rows, later_than, name):
     depth = weight.shape[1]
     width = count * tile
     whole = lambda i: (0, 0)
     operands = [align[0], *align[1]] if aligned is None else [aligned]
     total = operands[0].shape[0]
     coded = min(rows.start for rows in sent_rows)
-    n_blocks = 2 if count % 2 == 0 else 1
+    n_blocks = 2 if count % 2 == 0 and first % 2 == 0 else 1
+    block_at = lambda part: (lambda i: (i * n_blocks + first + part, 0))
     heights = lambda spans: [span.stop - span.start for span in spans]
-    anywhere = pl.BlockSpec(memory_space=pl.ANY)
-    in_specs = [pl.BlockSpec(operand.shape, whole) for operand in operands] + [anywhere] * (1 + len(later_than))
+    in_specs = [pl.BlockSpec(operand.shape, whole) for operand in operands]
+    if resident:
+        in_specs.append(pl.BlockSpec(memory_space=pltpu.VMEM))
+    else:
+        in_specs += [pl.BlockSpec((tile, depth), block_at(part)) for part in range(n_blocks)]
+    in_specs += [pl.BlockSpec(memory_space=pl.ANY)] * len(later_than)
     out_specs = [pl.BlockSpec((height, n_blocks * tile), lambda i: (0, i)) for height in heights(kept_rows)]
     out_specs += [pl.BlockSpec((height, width + LANES), whole) for height in heights(sent_rows)]
     out_shape = [jax.ShapeDtypeStruct((height, width), jnp.float32) for height in heights(kept_rows)]
@@ -132,22 +155,24 @@
         out_shape.insert(0, jax.ShapeDtypeStruct((total, depth), jnp.bfloat16))
     outs = pl.pallas_call(
         functools.partial(
-            sums_kernel, 0 if aligned is not None else len(align[1]), n_blocks, len(later_than), first, coded, kept_rows, sent_rows, tile),
+            sums_kernel, 0 if aligned is not None else len(align[1]), n_blocks, len(later_than), resident, coded, kept_rows, sent_rows, tile),
         grid=(count // n_blocks,), in_specs=in_specs, out_specs=out_specs, out_shape=out_shape,
-        scratch_shapes=[
-            pltpu.VMEM((total - coded, LANES), jnp.float32),
-            pltpu.VMEM((count, tile, depth), weight.dtype),
-            pltpu.SemaphoreType.DMA((count,)),
-        ],
-        compiler_params=params(SUMS_LIMIT), cost_estimate=cost(2 * total * width * depth, 2 * width * depth), name=name,
-    )(*operands, weight, *later_than)
+        scratch_shapes=[pltpu.VMEM((total - coded, LANES), jnp.float32)],
+        compiler_params=params(2 * SMALL_LIMIT if resident else VMEM_LIMIT),
+        cost_estimate=cost(2 * total * width * depth, 2 * width * depth), name=name,
+    )(*operands, *[weight] * (1 if resident else n_blocks), *later_than)
     if aligned is None:
         aligned, *outs = outs
     return aligned, outs[:len(kept_rows)], outs[len(kept_rows):]
 
 
-def weight_kernel(places, first, n_later, tile, aligned_ref, *refs):
-    n_pieces = sum(len(place) for place in places)
+def line_places(pieces):
+    own, left, right, two, far = pieces
+    even = lax.rem(lax.axis_index("row"), 2) == 0
+    return [own, jnp.where(even, right, left), two, far + jnp.where(even, left, right)]
+
+
+def weight_kernel(n_pieces, place, first, n_later, tile, aligned_ref, *refs):
     pieces = [ref[...] for ref in refs[:n_pieces]]
     out_ref, held_ref, left_sem = refs[n_pieces + n_later:]
     step = pl.program_id(0)
@@ -163,8 +188,7 @@
     def _():
         leave(step - slots).wait()
 
-    blocks = [functools.reduce(lambda x, y: x + y, [pieces[at] for at in place]) for place in places]
-    left = jnp.concatenate(blocks, axis=0)
+    left = jnp.concatenate(place(pieces), axis=0)
     depth = aligned_ref.shape[1]
     chunk = tile_of(depth, 1024)
     block = held_ref.at[lax.rem(step, slots)]
@@ -181,12 +205,12 @@
                 leave(last - back).wait()
 
 
-def weight_grads(aligned, pieces, places, tile, first, count, filled, later_than):
+def weight_grads(aligned, pieces, place, tile, first, count, filled, later_than):
     total, depth = aligned.shape
     rows, hidden = pieces[0].shape
     later = ([] if filled is None else [filled]) + list(later_than)
     return pl.pallas_call(
-        functools.partial(weight_kernel, places, first, len(later), tile),
+        functools.partial(weight_kernel, len(pieces), place, first, len(later), tile),
         grid=(count,),
         in_specs=[pl.BlockSpec((total, depth), lambda i: (0, 0))]
         + [pl.BlockSpec((rows, tile), lambda i: (0, i + first))] * len(pieces)
@@ -308,8 +332,21 @@
         functools.partial(stack_kernel, len(values)),
         in_specs=[pl.BlockSpec(memory_space=pltpu.VMEM)] * len(values) + [pl.BlockSpec(memory_space=pl.ANY)] * len(later_than),
         out_shape=jax.ShapeDtypeStruct((len(values) * rows, width), values[0].dtype),
-        compiler_params=params(), cost_estimate=cost(0, 4 * len(values) * rows * width), name="stacked",
+        compiler_params=params(SMALL_LIMIT), cost_estimate=cost(0, 4 * len(values) * rows * width), name="stacked",
     )(*values, *later_than)
+
+
+def add_kernel(left_ref, right_ref, *refs):
+    refs[-1][...] = left_ref[...] + right_ref[...]
+
+
+def added(left, right, later_than):
+    return pl.pallas_call(
+        add_kernel,
+        in_specs=[pl.BlockSpec(memory_space=pltpu.VMEM)] * 2 + [pl.BlockSpec(memory_space=pl.ANY)] * len(later_than),
+        out_shape=jax.ShapeDtypeStruct(left.shape, left.dtype),
+        compiler_params=params(SMALL_LIMIT), cost_estimate=cost(left.size, left.size * 6), name="added",
+    )(left, right, *later_than)
 
 
 def same_kernel(*refs):
@@ -323,17 +360,15 @@
         in_specs=[anywhere] * (len(values) + len(later_than)), out_specs=[anywhere] * len(values),
         out_shape=[jax.ShapeDtypeStruct(value.shape, value.dtype) for value in values],
         input_output_aliases={at: at for at in range(len(values))},
-        compiler_params=params(), cost_estimate=cost(0, 0), name="handed_on",
+        compiler_params=params(SMALL_LIMIT), cost_estimate=cost(0, 0), name="handed_on",
     )(*values, *later_than)
 
 
-def gather_cotangent(cotangent, n_col):
-    flips = list(range(0, n_col, 2))
-    pieces = [cotangent] + [send(cotangent, "col", flip, n_col) for flip in flips[1:]]
-    stacks = [stacked(pieces[:2])]
-    stacks.append(stacked(pieces[2:], stacks))
-    stacks += [send(stack, "col", 1, n_col) for stack in stacks]
-    return stacks, flips + [flip ^ 1 for flip in flips]
+def gather_cotangent(cotangent, n_col, before_first, before_second):
+    pieces = [cotangent] + [send(cotangent, "col", flip, n_col) for flip in range(2, n_col, 2)]
+    stacks = [stacked(pieces[:2], before_first)]
+    stacks.append(stacked(pieces[2:], stacks + before_second))
+    return stacks + [send(stack, "col", 1, n_col) for stack in stacks]
 
 
 def halving_order(size):
@@ -352,7 +387,7 @@
     total = align[0].shape[0]
     kept_rows, sent_rows = [slice(0, total // 2)], [slice(total // 2, total)]
     count = weight.shape[0] // tile
-    aligned, [kept], [sent] = partial_sums(None, align, weight, tile, 0, count, kept_rows, sent_rows, [], "sums")
+    aligned, [kept], [sent] = partial_sums(None, align, weight, False, tile, 0, count, kept_rows, sent_rows, [], "sums")
     got = send(sent, "row", 1, n_row)
     evens = range(2, n_row, 2)
     for o, piece in zip(evens, handed_on([act_pieces[o] for o in evens], [aligned])):
@@ -362,18 +397,16 @@
         kept, sent, _ = fold(kept, got, [])
         got = send(sent, "row", step, n_row)
         step *= 2
-    places = [[at] for at in range(n_row)]
-    weight_grad = weight_grads(aligned, [act_pieces[o] for o in offsets], places, tile, 0, count, None, [sent])
+    weight_grad = weight_grads(aligned, [act_pieces[o] for o in offsets], lambda values: values, tile, 0, count, None, [sent])
     return weight_grad, totals([[kept, got]], [weight_grad])
 
 
-def line_sums(align, weight, activations, act_pieces, tile):
+def line_sums(align, weight, weight_a, act_pieces, tile):
     total = align[0].shape[0]
     rows = total // 4
     kept_rows = [slice(0, rows), slice(2 * rows, total)]
     sent_rows = [slice(rows, total), slice(rows, 2 * rows)]
-    tiles = weight.shape[0] // tile
-    first_part, second_part = part_slices(tiles, (3, 4))
+    (first_a, count_a), (first_b, count_b) = part_slices(weight.shape[0] // tile, (4, 3))
     inwards, outwards, middle = [(0, 1), (3, 2)], [(1, 0), (2, 3)], [(1, 2), (2, 1)]
 
     def spread(sent):
@@ -383,21 +416,22 @@
         two, three = line_fold(kept, got)
         return two, lax.ppermute(three, "row", middle), lax.ppermute(two, "row", [(1, 3), (2, 0)])
 
-    aligned, kept_a, sent_a = partial_sums(None, align, weight, tile, *first_part, kept_rows, sent_rows, [], "sums_a")
+    own, left, right = act_pieces
+    two_left = lax.ppermute(left, "row", [(1, 2), (2, 3)])
+    two_right = lax.ppermute(right, "row", [(2, 1), (1, 0)])
+    aligned, kept_a, sent_a = partial_sums(None, align, weight_a, True, tile, first_a, count_a, kept_rows, sent_rows, [], "sums_a")
     got_a = spread(sent_a)
-    act_pieces[2], activations = handed_on([act_pieces[2], stacked([activations], align[1][:1])], [aligned])
-    across = lax.ppermute(act_pieces[2], "row", outwards)
-    near = lax.ppermute(activations, "row", middle)
-    _, kept_b, sent_b = partial_sums(aligned, None, weight, tile, *second_part, kept_rows, sent_rows, [act_pieces[1]], "sums_b")
+    _, kept_b, sent_b = partial_sums(
+        aligned, None, weight, False, tile, first_b, count_b, kept_rows, sent_rows, [], "sums_b")
+    two = added(two_left, two_right, kept_b[:1])
+    far = lax.ppermute(two, "row", outwards)
     sent_b = handed_on(sent_b, [got_a[1]])
     got_b = spread(sent_b)
     two_a, *crossed_a = cross(kept_a[1], got_a[0])
-    pieces = [activations, act_pieces[1], act_pieces[2], across, near]
-    places = [[0], [1], [2], [3, 4]]
-    (first_a, count_a), (first_b, count_b) = part_slices(tiles, (4, 3))
-    grad = weight_grads(aligned, pieces, places, tile, first_a, count_a, None, [two_a])
+    pieces = [own, left, right, two, far]
+    grad = weight_grads(aligned, pieces, line_places, tile, first_a, count_a, None, [two_a])
     two_b, *crossed_b = cross(kept_b[1], got_b[0])
-    weight_grad = weight_grads(aligned, pieces, places, tile, first_b, count_b, grad, [two_b])
+    weight_grad = weight_grads(aligned, pieces, line_places, tile, first_b, count_b, grad, [two_b])
     return weight_grad, totals([[kept_a[0], *got_a, *crossed_a], [kept_b[0], *got_b, *crossed_b]], [weight_grad])
 
 
@@ -407,10 +441,8 @@
     mine_row, mine_col = lax.axis_index("row"), lax.axis_index("col")
     offsets = list(range(4)) if n_row == 4 else halving_order(n_row)
 
-    pieces, flips = gather_cotangent(cotangent, n_col)
-    act_pieces = {o: send(activations, "row", o, n_row) for o in [1, *range(2, n_row, 2)]}
-    act_pieces[0] = activations
-
+    flips = list(range(0, n_col, 2))
+    flips += [flip ^ 1 for flip in flips]
     order = row_order.reshape(n_row, rows)
     order = jnp.concatenate([lax.dynamic_index_in_dim(order, mine_row ^ o, 0, keepdims=False) for o in offsets])
     owner = mine_col ^ jnp.asarray(flips, jnp.int32)
@@ -419,7 +451,14 @@
 
     tile = tile_of(hidden, 256)
     if n_row == 4:
-        return line_sums((pick, pieces), down_weight, activations, act_pieces, tile)
+        weight_a = fetched(down_weight, tile, part_slices(hidden // tile, (4, 3))[0][1], [pick])
+        left = lax.ppermute(activations, "row", [(0, 1), (1, 2), (2, 3)])
+        right = lax.ppermute(activations, "row", [(3, 2), (2, 1), (1, 0)])
+        pieces = gather_cotangent(cotangent, n_col, [weight_a], [left, right])
+        return line_sums((pick, pieces), down_weight, weight_a, [activations, left, right], tile)
+    pieces = gather_cotangent(cotangent, n_col, [], [])
+    act_pieces = {o: send(activations, "row", o, n_row) for o in [1, *range(2, n_row, 2)]}
+    act_pieces[0] = activations
     return halving_sums((pick, pieces), down_weight, act_pieces, n_row, offsets, tile)
 
 

time: 95.7 us -> 87.8 us (0.917)
  waiting for transfers between devices: 20.3 us -> 15.7 us
  Pallas kernels: 39.5 us -> 37 us
  local copies, waits for them, and re-layouts: 2.81 us -> 0.86 us
  starting transfers between devices: 31 us -> 32.1 us
    pallas_call x2, Pallas kernels: 22.7 us -> 14.2 us  [partial_sums(): pl.pallas_call(functools.partial(sums_kernel, 0 if aligned is not None el...]
    ppermute x2 -> x5, starting transfers between devices: 1.98 us -> 9.66 us  [the longest x1 5.09 us: body(): left = lax.ppermute(activations, 'row', [(0, 1), (1, 2), (2, 3)])]
    pallas_call x2 -> x4, Pallas kernels: 13.5 us -> 19.6 us  [the longest x2 13.7 us: weight_grads(): pl.pallas_call(functools.partial(weight_kernel, len(pieces), place, first...]
    ppermute x7 -> x5, starting transfers between devices: 9.31 us -> 3.7 us  [send(): return lax.ppermute(value, axis, [(i, i ^ flip) for i in range(size)])]
    ppermute x2, waiting for transfers between devices: 5.78 us -> 2.75 us  [spread(): lax.ppermute(sent[0], 'row', inwards)]
    ppermute x2 -> x5, waiting for transfers between devices: 0.01 us -> 2.42 us  [the longest x1 2.41 us: line_sums(): far = lax.ppermute(two, 'row', outwards)]
    ppermute x7 -> x5, waiting for transfers between devices: 5.72 us -> 3.48 us  [send(): return lax.ppermute(value, axis, [(i, i ^ flip) for i in range(size)])]
    unnamed x4, local copies, waits for them, and re-layouts: 1.96 us -> 0.01 us
  transfers between devices with their start and end apart: 17 -> 18, of which waited for: 4 -> 5; matrix products, arithmetic and copies ran while one was open for 2% -> 2% of each run, Pallas kernels for 40% -> 41%
where the time goes in v7:
time: 87.8 us; the launch traced here: 87.4 us
  Pallas kernels  37 us (42%)
  starting transfers between devices  32.1 us (37%)
  waiting for transfers between devices  15.7 us (18%)
  between operations  0.94 us (1%)
  other arithmetic  0.91 us (1%)
    pallas_call x2, Pallas kernels, partial_sums(): pl.pallas_call(functools.partial(sums_kernel, 0 if aligned is not None el...  14.2 us
    pallas_call x2, Pallas kernels, weight_grads(): pl.pallas_call(functools.partial(weight_kernel, len(pieces), place, first...  13.7 us
    ppermute x2, starting transfers between devices, spread(): lax.ppermute(sent[0], 'row', inwards)  12.2 us
    ppermute x2, waiting for transfers between devices, cross(): lax.ppermute(two, 'row', [(1, 3), (2, 0)])  6.82 us
    pallas_call x1, Pallas kernels, fetched(): pl.pallas_call(fetch_kernel, in_specs=[pl.BlockSpec(memory_space=pl.ANY)]...  5.93 us
    ppermute x1, starting transfers between devices, body(): left = lax.ppermute(activations, 'row', [(0, 1), (1, 2), (2, 3)])  5.09 us
    ppermute x5, starting transfers between devices, send(): return lax.ppermute(value, axis, [(i, i ^ flip) for i in range(size)])  3.7 us
    ppermute x5, waiting for transfers between devices, send(): return lax.ppermute(value, axis, [(i, i ^ flip) for i in range(size)])  3.48 us
  transfers between devices with their start and end apart: 18, of which 5 were waited for; matrix products, arithmetic and copies ran while one was open for 2% of the time, Pallas kernels for 41%

profile of v7, /device:TPU:0, one launch (start us, length us, event | category | flops | bytes accessed | tf_op | source)
XLA Modules:
  0.0 87.4 jit_solution(6608028039620431285)
XLA Ops:
  0.6 5.1 %collective-permute-start.3 = (bf16[64,3584]{1,0:T(8,128)(2,1)}, bf16[64,3584]{1,0:T(8,128)(2,1)S(1)}, u32[]{:S(2)}, u32[]{:S(2)}) collective-permute-start(bf16[64,3584]{1,0:T(8,128)(2,1)} %refs_0_.5), channel_id=1, source_target_pairs={{0,8},{8,16},{16,24},{1,9},{9,17},{17,25},{2,10},{10,18},{18,26},{... | collective-permute-start | bytes 1376264 | tf_op jit(solution)/shard_map/ppermute | solution.py:455
  5.7 1.3 %collective-permute-start.4 = (bf16[64,3584]{1,0:T(8,128)(2,1)}, bf16[64,3584]{1,0:T(8,128)(2,1)S(1)}, u32[]{:S(2)}, u32[]{:S(2)}) collective-permute-start(bf16[64,3584]{1,0:T(8,128)(2,1)} %refs_0_.5), channel_id=1, source_target_pairs={{24,16},{16,8},{8,0},{25,17},{17,9},{9,1},{26,18},{18,10},{10,2},{... | collective-permute-start | bytes 1376264 | tf_op jit(solution)/shard_map/ppermute | solution.py:456
  7.0 1.6 %collective-permute-start = (bf16[32,4096]{1,0:T(8,128)(2,1)}, bf16[32,4096]{1,0:T(8,128)(2,1)S(1)}, u32[]{:S(2)}, u32[]{:S(2)}) collective-permute-start(bf16[32,4096]{1,0:T(8,128)(2,1)} %refs_0_.3), channel_id=1, source_target_pairs={{0,2},{1,3},{2,0},{3,1},{4,6},{5,7},{6,4},{7,5},{8,10},{9,11},{10,... | collective-permute-start | bytes 786440 | tf_op jit(solution)/shard_map/ppermute | solution.py:319
  8.6 1.5 %collective-permute-start.1 = (bf16[32,4096]{1,0:T(8,128)(2,1)}, bf16[32,4096]{1,0:T(8,128)(2,1)S(1)}, u32[]{:S(2)}, u32[]{:S(2)}) collective-permute-start(bf16[32,4096]{1,0:T(8,128)(2,1)} %refs_0_.3), channel_id=1, source_target_pairs={{0,4},{1,5},{2,6},{3,7},{4,0},{5,1},{6,2},{7,3},{8,12},{9,13},{10,... | collective-permute-start | bytes 786440 | tf_op jit(solution)/shard_map/ppermute | solution.py:319
  10.1 0.5 collective-permute-start.2
  10.6 0.7 xor_multiply_fusion
  11.3 0.8 reshape.24
  12.3 0.1 compare_convert_fusion.refs_0_
  12.4 5.9 %fetched.1.refs_2_.refs_5_ = bf16[2048,4096]{1,0:T(8,128)(2,1)S(1)} custom-call(bf16[3584,4096]{1,0:T(8,128)(2,1)} %refs_2_.1, bf16[256,256]{1,0:T(8,128)(2,1)S(1)} %compare_convert_fusion.refs_0_), custom_call_target="tpu_custom_call" | custom-call | bytes 16777216 | tf_op jit(solution)/shard_map/fetched/pallas_call | solution.py:79
  18.4 3.5 %collective-permute-done.1.refs_0_ = bf16[32,4096]{1,0:T(8,128)(2,1)S(1)} collective-permute-done((bf16[32,4096]{1,0:T(8,128)(2,1)}, bf16[32,4096]{1,0:T(8,128)(2,1)S(1)}, u32[]{:S(2)}, u32[]{:S(2)}) %collective-permute-start.1) | collective-permute-done | bytes 262176 | tf_op jit(solution)/shard_map/ppermute | solution.py:319
  22.0 0.7 collective-permute-start.7
  22.7 1.3 %collective-permute-start.8 = (bf16[64,3584]{1,0:T(8,128)(2,1)S(1)}, bf16[64,3584]{1,0:T(8,128)(2,1)S(1)}, u32[]{:S(2)}, u32[]{:S(2)}) collective-permute-start(bf16[64,3584]{1,0:T(8,128)(2,1)S(1)} %collective-permute-done.4.refs_4_.refs_2_), channel_id=1, source_target_pairs={{16,8},{8,0},{17,9},{9,1},{18,10},{10,2},{19,11},{11,3},{20,12},{1... | collective-permute-start | bytes 1376264 | tf_op jit(solution)/shard_map/ppermute | solution.py:421
  24.1 6.7 %sums_a.1 = (bf16[256,4096]{1,0:T(8,128)(2,1)S(1)}, f32[64,2048]{1,0:T(8,128)S(1)}, f32[128,2048]{1,0:T(8,128)S(1)}, s16[192,2176]{1,0:T(8,128)(2,1)S(1)}, s16[64,2176]{1,0:T(8,128)(2,1)S(1)}) custom-call(bf16[256,256]{1,0:T(8,128)(2,1)S(1)} %compare_convert_fusion.refs_0_, bf16[64,4096]{1,0:T(8,128)(2,1)S(1)} %stacked.2.refs_2_.refs_1_, ...), custom_call_target="tpu_custom_call" | custom-call | flops 4294967296 | bytes 16777216 | tf_op jit(solution)/shard_map/sums_a/pallas_call | solution.py:156
  30.7 7.7 %collective-permute-start.10 = (s16[192,2176]{1,0:T(8,128)(2,1)S(1)}, s16[192,2176]{1,0:T(8,128)(2,1)S(1)}, u32[]{:S(2)}, u32[]{:S(2)}) collective-permute-start(s16[192,2176]{1,0:T(8,128)(2,1)S(1)} %get-tuple-element.20), channel_id=1, source_target_pairs={{0,8},{24,16},{1,9},{25,17},{2,10},{26,18},{3,11},{27,19},{4,12},{... | collective-permute-start | bytes 2506760 | tf_op jit(solution)/shard_map/ppermute | solution.py:413
  38.5 1.3 %collective-permute-start.11 = (s16[64,2176]{1,0:T(8,128)(2,1)S(1)}, s16[64,2176]{1,0:T(8,128)(2,1)S(1)}, u32[]{:S(2)}, u32[]{:S(2)}) collective-permute-start(s16[64,2176]{1,0:T(8,128)(2,1)S(1)} %get-tuple-element.25), channel_id=1, source_target_pairs={{8,0},{16,24},{9,1},{17,25},{10,2},{18,26},{11,3},{19,27},{12,4},{... | collective-permute-start | bytes 835592 | tf_op jit(solution)/shard_map/ppermute | solution.py:413
  39.8 7.5 %sums_b.1 = (f32[64,1536]{1,0:T(8,128)S(1)}, f32[128,1536]{1,0:T(8,128)S(1)}, s16[192,1664]{1,0:T(8,128)(2,1)S(1)}, s16[64,1664]{1,0:T(8,128)(2,1)S(1)}) custom-call(bf16[256,4096]{1,0:T(8,128)(2,1)S(1)} %get-tuple-element.17.refs_0_.aligned_ref, bf16[3584,4096]{1,0:T(8,128)(2,1)} %refs_2_.1, bf16[3584,4096]{1,0:T(8,128)(2,1)} %refs_2_.1), custom_call_target="tpu_custom_call" | custom-call | flops 3221225472 | bytes 12582912 | tf_op jit(solution)/shard_map/sums_b/pallas_call | solution.py:156
  47.4 1.3 %collective-permute-start.9 = (bf16[64,3584]{1,0:T(8,128)(2,1)S(1)}, bf16[64,3584]{1,0:T(8,128)(2,1)S(1)}, u32[]{:S(2)}, u32[]{:S(2)}) collective-permute-start(bf16[64,3584]{1,0:T(8,128)(2,1)S(1)} %added.1.refs_3_), channel_id=1, source_target_pairs={{8,0},{16,24},{9,1},{17,25},{10,2},{18,26},{11,3},{19,27},{12,4},{... | collective-permute-start | bytes 1376264 | tf_op jit(solution)/shard_map/ppermute | solution.py:427
  48.7 0.2 collective-permute-done.11.refs_2_
  48.8 4.5 %collective-permute-start.12 = (s16[192,1664]{1,0:T(8,128)(2,1)S(1)}, s16[192,1664]{1,0:T(8,128)(2,1)S(1)}, u32[]{:S(2)}, u32[]{:S(2)}) collective-permute-start(s16[192,1664]{1,0:T(8,128)(2,1)S(1)} %get-tuple-element.26), channel_id=1, source_target_pairs={{0,8},{24,16},{1,9},{25,17},{2,10},{26,18},{3,11},{27,19},{4,12},{... | collective-permute-start | bytes 1916936 | tf_op jit(solution)/shard_map/ppermute | solution.py:413
  53.3 1.3 %collective-permute-start.15 = (s16[64,1664]{1,0:T(8,128)(2,1)S(1)}, s16[64,1664]{1,0:T(8,128)(2,1)S(1)}, u32[]{:S(2)}, u32[]{:S(2)}) collective-permute-start(s16[64,1664]{1,0:T(8,128)(2,1)S(1)} %get-tuple-element.30), channel_id=1, source_target_pairs={{8,0},{16,24},{9,1},{17,25},{10,2},{18,26},{11,3},{19,27},{12,4},{... | collective-permute-start | bytes 638984 | tf_op jit(solution)/shard_map/ppermute | solution.py:413
  54.6 2.7 %collective-permute-done.10.got_ref.refs_1_ = s16[192,2176]{1,0:T(8,128)(2,1)S(1)} collective-permute-done((s16[192,2176]{1,0:T(8,128)(2,1)S(1)}, s16[192,2176]{1,0:T(8,128)(2,1)S(1)}, u32[]{:S(2)}, u32[]{:S(2)}) %collective-permute-start.10) | collective-permute-done | bytes 835616 | tf_op jit(solution)/shard_map/ppermute | solution.py:413
  57.4 0.9 %line_fold.2 = (s16[64,2176]{1,0:T(8,128)(2,1)S(1)}, s16[64,2176]{1,0:T(8,128)(2,1)S(1)}) custom-call(f32[128,2048]{1,0:T(8,128)S(1)} %get-tuple-element.19.kept_ref, s16[192,2176]{1,0:T(8,128)(2,1)S(1)} %collective-permute-done.10.got_ref.refs_1_), custom_call_target="tpu_custom_call" | custom-call | flops 5242880 | bytes 3145728 | tf_op jit(solution)/shard_map/line_fold/pallas_call | solution.py:283
  58.3 0.7 collective-permute-start.13
  59.0 1.3 %collective-permute-start.14 = (s16[64,2176]{1,0:T(8,128)(2,1)S(1)}, s16[64,2176]{1,0:T(8,128)(2,1)S(1)}, u32[]{:S(2)}, u32[]{:S(2)}) collective-permute-start(s16[64,2176]{1,0:T(8,128)(2,1)S(1)} %get-tuple-element.21.refs_5_), channel_id=1, source_target_pairs={{8,24},{16,0},{9,25},{17,1},{10,26},{18,2},{11,27},{19,3},{12,28},... | collective-permute-start | bytes 835592 | tf_op jit(solution)/shard_map/ppermute | solution.py:417
  60.3 2.4 %collective-permute-done.9.refs_4_ = bf16[64,3584]{1,0:T(8,128)(2,1)S(1)} collective-permute-done((bf16[64,3584]{1,0:T(8,128)(2,1)S(1)}, bf16[64,3584]{1,0:T(8,128)(2,1)S(1)}, u32[]{:S(2)}, u32[]{:S(2)}) %collective-permute-start.9) | collective-permute-done | bytes 458784 | tf_op jit(solution)/shard_map/ppermute | solution.py:427
  62.7 7.6 %weight_grads.2.refs_5_ = bf16[3584,4096]{1,0:T(8,128)(2,1)} custom-call(bf16[256,4096]{1,0:T(8,128)(2,1)S(1)} %get-tuple-element.17.refs_0_.aligned_ref, bf16[64,3584]{1,0:T(8,128)(2,1)S(1)} %copy-done, bf16[64,3584]{1,0:T(8,128)(2,1)S(1)} %collective-permute-done.3.refs_3_.refs_1_, bf16[64,3584]{1,0:T(8,128)(2,1)S(1)} %collective-permute-done.4.refs_4_.refs_2_, ...), custom_call_target="tpu_custom_call" | custom-call | flops 4294967296 | bytes 16777216 | tf_op jit(solution)/shard_map/weight_grads/pallas_call | solution.py:212
  70.3 0.7 line_fold.3
  71.0 0.7 collective-permute-start.16
  71.7 1.3 %collective-permute-start.17 = (s16[64,1664]{1,0:T(8,128)(2,1)S(1)}, s16[64,1664]{1,0:T(8,128)(2,1)S(1)}, u32[]{:S(2)}, u32[]{:S(2)}) collective-permute-start(s16[64,1664]{1,0:T(8,128)(2,1)S(1)} %get-tuple-element.27.refs_6_), channel_id=1, source_target_pairs={{8,24},{16,0},{9,25},{17,1},{10,26},{18,2},{11,27},{19,3},{12,28},... | collective-permute-start | bytes 638984 | tf_op jit(solution)/shard_map/ppermute | solution.py:417
  73.0 6.1 %weight_grads.3.refs_10_ = bf16[3584,4096]{1,0:T(8,128)(2,1)} custom-call(bf16[256,4096]{1,0:T(8,128)(2,1)S(1)} %get-tuple-element.17.refs_0_.aligned_ref, bf16[64,3584]{1,0:T(8,128)(2,1)S(1)} %copy-done, bf16[64,3584]{1,0:T(8,128)(2,1)S(1)} %collective-permute-done.3.refs_3_.refs_1_, ...), custom_call_target="tpu_custom_call", output_to_operand_aliasing={{}: (6, {})} | custom-call | flops 3221225472 | bytes 12582912 | tf_op jit(solution)/shard_map/weight_grads/pallas_call | solution.py:212
  79.1 6.8 %collective-permute-done.17.refs_9_ = s16[64,1664]{1,0:T(8,128)(2,1)S(1)} collective-permute-done((s16[64,1664]{1,0:T(8,128)(2,1)S(1)}, s16[64,1664]{1,0:T(8,128)(2,1)S(1)}, u32[]{:S(2)}, u32[]{:S(2)}) %collective-permute-start.17) | collective-permute-done | bytes 213024 | tf_op jit(solution)/shard_map/ppermute | solution.py:417
  85.9 1.5 %totals.1 = bf16[64,3584]{1,0:T(8,128)(2,1)} custom-call(f32[64,2048]{1,0:T(8,128)S(1)} %get-tuple-element.28.refs_0_, s16[192,2176]{1,0:T(8,128)(2,1)S(1)} %collective-permute-done.10.got_ref.refs_1_, s16[64,2176]{1,0:T(8,128)(2,1)S(1)} %collective-permute-done.11.refs_2_, s16[64,2176]{1,0:T(8,128)(2,1)S(1)} %collective-permute-done.13.refs_3_, ...), custom_call_target="tpu_custom_call" | custom-call | flops 9175040 | bytes 3211264 | tf_op jit(solution)/shard_map/totals/pallas_call | solution.py:310
  (27 shorter events, 0.6 us)
Async XLA Ops:
  0.6 17.7 %copy-start.1 = (bf16[32,4096]{1,0:T(8,128)(2,1)S(1)}, bf16[32,4096]{1,0:T(8,128)(2,1)}, u32[]{:S(2)}) copy-start(bf16[32,4096]{1,0:T(8,128)(2,1)} %refs_0_.3) | copy-start | bytes 786436
  0.6 21.3 %collective-permute-start.3 = (bf16[64,3584]{1,0:T(8,128)(2,1)}, bf16[64,3584]{1,0:T(8,128)(2,1)S(1)}, u32[]{:S(2)}, u32[]{:S(2)}) collective-permute-start(bf16[64,3584]{1,0:T(8,128)(2,1)} %refs_0_.5), channel_id=1, source_target_pairs={{0,8},{8,16},{16,24},{1,9},{9,17},{17,25},{2,10},{10,18},{18,26},{... | collective-permute-start | bytes 1376264 | tf_op jit(solution)/shard_map/ppermute | solution.py:455
  5.7 16.2 %collective-permute-start.4 = (bf16[64,3584]{1,0:T(8,128)(2,1)}, bf16[64,3584]{1,0:T(8,128)(2,1)S(1)}, u32[]{:S(2)}, u32[]{:S(2)}) collective-permute-start(bf16[64,3584]{1,0:T(8,128)(2,1)} %refs_0_.5), channel_id=1, source_target_pairs={{24,16},{16,8},{8,0},{25,17},{17,9},{9,1},{26,18},{18,10},{10,2},{... | collective-permute-start | bytes 1376264 | tf_op jit(solution)/shard_map/ppermute | solution.py:456
  7.0 11.3 %collective-permute-start = (bf16[32,4096]{1,0:T(8,128)(2,1)}, bf16[32,4096]{1,0:T(8,128)(2,1)S(1)}, u32[]{:S(2)}, u32[]{:S(2)}) collective-permute-start(bf16[32,4096]{1,0:T(8,128)(2,1)} %refs_0_.3), channel_id=1, source_target_pairs={{0,2},{1,3},{2,0},{3,1},{4,6},{5,7},{6,4},{7,5},{8,10},{9,11},{10,... | collective-permute-start | bytes 786440 | tf_op jit(solution)/shard_map/ppermute | solution.py:319
  8.6 13.3 %collective-permute-start.1 = (bf16[32,4096]{1,0:T(8,128)(2,1)}, bf16[32,4096]{1,0:T(8,128)(2,1)S(1)}, u32[]{:S(2)}, u32[]{:S(2)}) collective-permute-start(bf16[32,4096]{1,0:T(8,128)(2,1)} %refs_0_.3), channel_id=1, source_target_pairs={{0,4},{1,5},{2,6},{3,7},{4,0},{5,1},{6,2},{7,3},{8,12},{9,13},{10,... | collective-permute-start | bytes 786440 | tf_op jit(solution)/shard_map/ppermute | solution.py:319
  10.1 11.8 %collective-permute-start.2 = (bf16[32,4096]{1,0:T(8,128)(2,1)}, bf16[32,4096]{1,0:T(8,128)(2,1)S(1)}, u32[]{:S(2)}, u32[]{:S(2)}) collective-permute-start(bf16[32,4096]{1,0:T(8,128)(2,1)} %refs_0_.3), channel_id=1, source_target_pairs={{0,6},{1,7},{2,4},{3,5},{4,2},{5,3},{6,0},{7,1},{8,14},{9,15},{10,... | collective-permute-start | bytes 786440 | tf_op jit(solution)/shard_map/ppermute | solution.py:319
  18.4 5.7 %collective-permute-start.5 = (bf16[64,4096]{1,0:T(8,128)(2,1)S(1)}, bf16[64,4096]{1,0:T(8,128)(2,1)S(1)}, u32[]{:S(2)}, u32[]{:S(2)}) collective-permute-start(bf16[64,4096]{1,0:T(8,128)(2,1)S(1)} %stacked.2.refs_2_.refs_1_), channel_id=1, source_target_pairs={{0,1},{1,0},{2,3},{3,2},{4,5},{5,4},{6,7},{7,6},{8,9},{9,8},{10,11... | collective-permute-start | bytes 1572872 | tf_op jit(solution)/shard_map/ppermute | solution.py:319
  22.0 2.1 %collective-permute-start.6 = (bf16[64,4096]{1,0:T(8,128)(2,1)S(1)}, bf16[64,4096]{1,0:T(8,128)(2,1)S(1)}, u32[]{:S(2)}, u32[]{:S(2)}) collective-permute-start(bf16[64,4096]{1,0:T(8,128)(2,1)S(1)} %stacked.3.refs_2_), channel_id=1, source_target_pairs={{0,1},{1,0},{2,3},{3,2},{4,5},{5,4},{6,7},{7,6},{8,9},{9,8},{10,11... | collective-permute-start | bytes 1572872 | tf_op jit(solution)/shard_map/ppermute | solution.py:319
  22.0 25.2 %collective-permute-start.7 = (bf16[64,3584]{1,0:T(8,128)(2,1)S(1)}, bf16[64,3584]{1,0:T(8,128)(2,1)S(1)}, u32[]{:S(2)}, u32[]{:S(2)}) collective-permute-start(bf16[64,3584]{1,0:T(8,128)(2,1)S(1)} %collective-permute-done.3.refs_3_.refs_1_), channel_id=1, source_target_pairs={{8,16},{16,24},{9,17},{17,25},{10,18},{18,26},{11,19},{19,27},{12,... | collective-permute-start | bytes 1376264 | tf_op jit(solution)/shard_map/ppermute | solution.py:420
  22.7 24.6 %collective-permute-start.8 = (bf16[64,3584]{1,0:T(8,128)(2,1)S(1)}, bf16[64,3584]{1,0:T(8,128)(2,1)S(1)}, u32[]{:S(2)}, u32[]{:S(2)}) collective-permute-start(bf16[64,3584]{1,0:T(8,128)(2,1)S(1)} %collective-permute-done.4.refs_4_.refs_2_), channel_id=1, source_target_pairs={{16,8},{8,0},{17,9},{9,1},{18,10},{10,2},{19,11},{11,3},{20,12},{1... | collective-permute-start | bytes 1376264 | tf_op jit(solution)/shard_map/ppermute | solution.py:421
  30.7 26.6 %collective-permute-start.10 = (s16[192,2176]{1,0:T(8,128)(2,1)S(1)}, s16[192,2176]{1,0:T(8,128)(2,1)S(1)}, u32[]{:S(2)}, u32[]{:S(2)}) collective-permute-start(s16[192,2176]{1,0:T(8,128)(2,1)S(1)} %get-tuple-element.20), channel_id=1, source_target_pairs={{0,8},{24,16},{1,9},{25,17},{2,10},{26,18},{3,11},{27,19},{4,12},{... | collective-permute-start | bytes 2506760 | tf_op jit(solution)/shard_map/ppermute | solution.py:413
  38.5 10.4 %collective-permute-start.11 = (s16[64,2176]{1,0:T(8,128)(2,1)S(1)}, s16[64,2176]{1,0:T(8,128)(2,1)S(1)}, u32[]{:S(2)}, u32[]{:S(2)}) collective-permute-start(s16[64,2176]{1,0:T(8,128)(2,1)S(1)} %get-tuple-element.25), channel_id=1, source_target_pairs={{8,0},{16,24},{9,1},{17,25},{10,2},{18,26},{11,3},{19,27},{12,4},{... | collective-permute-start | bytes 835592 | tf_op jit(solution)/shard_map/ppermute | solution.py:413
  39.8 22.9 %copy-start = (bf16[64,3584]{1,0:T(8,128)(2,1)S(1)}, bf16[64,3584]{1,0:T(8,128)(2,1)}, u32[]{:S(2)}) copy-start(bf16[64,3584]{1,0:T(8,128)(2,1)} %refs_0_.5) | copy-start | bytes 1376260
  47.4 15.3 %collective-permute-start.9 = (bf16[64,3584]{1,0:T(8,128)(2,1)S(1)}, bf16[64,3584]{1,0:T(8,128)(2,1)S(1)}, u32[]{:S(2)}, u32[]{:S(2)}) collective-permute-start(bf16[64,3584]{1,0:T(8,128)(2,1)S(1)} %added.1.refs_3_), channel_id=1, source_target_pairs={{8,0},{16,24},{9,1},{17,25},{10,2},{18,26},{11,3},{19,27},{12,4},{... | collective-permute-start | bytes 1376264 | tf_op jit(solution)/shard_map/ppermute | solution.py:427
  48.8 21.5 %collective-permute-start.12 = (s16[192,1664]{1,0:T(8,128)(2,1)S(1)}, s16[192,1664]{1,0:T(8,128)(2,1)S(1)}, u32[]{:S(2)}, u32[]{:S(2)}) collective-permute-start(s16[192,1664]{1,0:T(8,128)(2,1)S(1)} %get-tuple-element.26), channel_id=1, source_target_pairs={{0,8},{24,16},{1,9},{25,17},{2,10},{26,18},{3,11},{27,19},{4,12},{... | collective-permute-start | bytes 1916936 | tf_op jit(solution)/shard_map/ppermute | solution.py:413
  53.3 25.7 %collective-permute-start.15 = (s16[64,1664]{1,0:T(8,128)(2,1)S(1)}, s16[64,1664]{1,0:T(8,128)(2,1)S(1)}, u32[]{:S(2)}, u32[]{:S(2)}) collective-permute-start(s16[64,1664]{1,0:T(8,128)(2,1)S(1)} %get-tuple-element.30), channel_id=1, source_target_pairs={{8,0},{16,24},{9,1},{17,25},{10,2},{18,26},{11,3},{19,27},{12,4},{... | collective-permute-start | bytes 638984 | tf_op jit(solution)/shard_map/ppermute | solution.py:413
  58.3 20.8 %collective-permute-start.13 = (s16[64,2176]{1,0:T(8,128)(2,1)S(1)}, s16[64,2176]{1,0:T(8,128)(2,1)S(1)}, u32[]{:S(2)}, u32[]{:S(2)}) collective-permute-start(s16[64,2176]{1,0:T(8,128)(2,1)S(1)} %get-tuple-element.29), channel_id=1, source_target_pairs={{8,16},{16,8},{9,17},{17,9},{10,18},{18,10},{11,19},{19,11},{12,20... | collective-permute-start | bytes 835592 | tf_op jit(solution)/shard_map/ppermute | solution.py:417
  59.0 20.1 %collective-permute-start.14 = (s16[64,2176]{1,0:T(8,128)(2,1)S(1)}, s16[64,2176]{1,0:T(8,128)(2,1)S(1)}, u32[]{:S(2)}, u32[]{:S(2)}) collective-permute-start(s16[64,2176]{1,0:T(8,128)(2,1)S(1)} %get-tuple-element.21.refs_5_), channel_id=1, source_target_pairs={{8,24},{16,0},{9,25},{17,1},{10,26},{18,2},{11,27},{19,3},{12,28},... | collective-permute-start | bytes 835592 | tf_op jit(solution)/shard_map/ppermute | solution.py:417
  71.0 8.1 %collective-permute-start.16 = (s16[64,1664]{1,0:T(8,128)(2,1)S(1)}, s16[64,1664]{1,0:T(8,128)(2,1)S(1)}, u32[]{:S(2)}, u32[]{:S(2)}) collective-permute-start(s16[64,1664]{1,0:T(8,128)(2,1)S(1)} %get-tuple-element.31), channel_id=1, source_target_pairs={{8,16},{16,8},{9,17},{17,9},{10,18},{18,10},{11,19},{19,11},{12,20... | collective-permute-start | bytes 638984 | tf_op jit(solution)/shard_map/ppermute | solution.py:417
  71.7 14.2 %collective-permute-start.17 = (s16[64,1664]{1,0:T(8,128)(2,1)S(1)}, s16[64,1664]{1,0:T(8,128)(2,1)S(1)}, u32[]{:S(2)}, u32[]{:S(2)}) collective-permute-start(s16[64,1664]{1,0:T(8,128)(2,1)S(1)} %get-tuple-element.27.refs_6_), channel_id=1, source_target_pairs={{8,24},{16,0},{9,25},{17,1},{10,26},{18,2},{11,27},{19,3},{12,28},... | collective-permute-start | bytes 638984 | tf_op jit(solution)/shard_map/ppermute | solution.py:417

commit v8 on v7

--- a/solution.py
+++ b/solution.py
@@ -12,9 +12,9 @@
 TOP = 32766.0
 LEAST = 2.0 ** -120
 VMEM_LIMIT = 48 * 1024 * 1024
-FETCH_LIMIT = 32 * 1024 * 1024
 SMALL_LIMIT = 8 * 1024 * 1024
 SLOTS = 4
+SHARES = (2, 3, 2)
 SUB = 256
 
 
@@ -62,38 +62,14 @@
         aligned_ref[:, cols] = dot(pick_ref[...], gathered, ((1,), (0,))).astype(jnp.bfloat16)
 
 
-def fetch_kernel(weight_ref, *refs):
-    out_ref, arrived = refs[-2:]
-    count = arrived.shape[0]
-    rows = out_ref.shape[0] // count
-    parts = [pl.ds(at * rows, rows) for at in range(count)]
-    copies = [pltpu.make_async_copy(weight_ref.at[part], out_ref.at[part], arrived.at[at]) for at, part in enumerate(parts)]
-    for copy in copies:
-        copy.start()
-    for copy in copies:
-        copy.wait()
-
-
-def fetched(weight, tile, count, later_than):
-    shape = (count * tile, weight.shape[1])
-    return pl.pallas_call(
-        fetch_kernel,
-        in_specs=[pl.BlockSpec(memory_space=pl.ANY)] * (1 + len(later_than)),
-        out_specs=pl.BlockSpec(memory_space=pltpu.VMEM),
-        out_shape=jax.ShapeDtypeStruct(shape, weight.dtype),
-        scratch_shapes=[pltpu.SemaphoreType.DMA((count,))],
-        compiler_params=params(FETCH_LIMIT), cost_estimate=cost(0, 2 * shape[0] * shape[1]), name="fetched",
-    )(weight, *later_than)
-
-
-def sums_kernel(n_pieces, n_blocks, n_later, resident, coded, kept_rows, sent_rows, tile, *refs):
+def sums_kernel(n_pieces, n_blocks, n_later, coded, kept_rows, sent_rows, tile, *refs):
     refs = list(refs)
     if n_pieces:
         pick_ref = refs.pop(0)
         pieces = [refs.pop(0) for _ in range(n_pieces)]
     else:
         aligned_ref = refs.pop(0)
-    weights = [refs.pop(0) for _ in range(1 if resident else n_blocks)]
+    weights = [refs.pop(0) for _ in range(n_blocks)]
     del refs[:n_later]
     if n_pieces:
         aligned_ref = refs.pop(0)
@@ -114,8 +90,7 @@
     for part in range(n_blocks):
         at = step * n_blocks + part
         cols = pl.ds(pl.multiple_of(at * tile, tile), tile)
-        block = weights[0][cols] if resident else weights[part][...]
-        values = dot(aligned_ref[...], block, ((1,), (1,)))
+        values = dot(aligned_ref[...], weights[part][...], ((1,), (1,)))
         for ref, rows in zip(kept, kept_rows):
             ref[:, part * tile:(part + 1) * tile] = values[rows]
         codes, level = encode(values[coded:])
@@ -130,7 +105,7 @@
             ref[:, width:] = to_levels(levels[rows.start - coded:rows.stop - coded])
 
 
-def partial_sums(aligned, align, weight, resident, tile, first, count, kept_rows, sent_rows, later_than, name):
+def partial_sums(aligned, align, weight, tile, first, count, kept_rows, sent_rows, later_than, name):
     depth = weight.shape[1]
     width = count * tile
     whole = lambda i: (0, 0)
@@ -141,10 +116,7 @@
     block_at = lambda part: (lambda i: (i * n_blocks + first + part, 0))
     heights = lambda spans: [span.stop - span.start for span in spans]
     in_specs = [pl.BlockSpec(operand.shape, whole) for operand in operands]
-    if resident:
-        in_specs.append(pl.BlockSpec(memory_space=pltpu.VMEM))
-    else:
-        in_specs += [pl.BlockSpec((tile, depth), block_at(part)) for part in range(n_blocks)]
+    in_specs += [pl.BlockSpec((tile, depth), block_at(part)) for part in range(n_blocks)]
     in_specs += [pl.BlockSpec(memory_space=pl.ANY)] * len(later_than)
     out_specs = [pl.BlockSpec((height, n_blocks * tile), lambda i: (0, i)) for height in heights(kept_rows)]
     out_specs += [pl.BlockSpec((height, width + LANES), whole) for height in heights(sent_rows)]
@@ -155,24 +127,18 @@
         out_shape.insert(0, jax.ShapeDtypeStruct((total, depth), jnp.bfloat16))
     outs = pl.pallas_call(
         functools.partial(
-            sums_kernel, 0 if aligned is not None else len(align[1]), n_blocks, len(later_than), resident, coded, kept_rows, sent_rows, tile),
+            sums_kernel, 0 if aligned is not None else len(align[1]), n_blocks, len(later_than), coded, kept_rows, sent_rows, tile),
         grid=(count // n_blocks,), in_specs=in_specs, out_specs=out_specs, out_shape=out_shape,
         scratch_shapes=[pltpu.VMEM((total - coded, LANES), jnp.float32)],
-        compiler_params=params(2 * SMALL_LIMIT if resident else VMEM_LIMIT),
+        compiler_params=params(),
         cost_estimate=cost(2 * total * width * depth, 2 * width * depth), name=name,
-    )(*operands, *[weight] * (1 if resident else n_blocks), *later_than)
+    )(*operands, *[weight] * n_blocks, *later_than)
     if aligned is None:
         aligned, *outs = outs
     return aligned, outs[:len(kept_rows)], outs[len(kept_rows):]
 
 
-def line_places(pieces):
-    own, left, right, two, far = pieces
-    even = lax.rem(lax.axis_index("row"), 2) == 0
-    return [own, jnp.where(even, right, left), two, far + jnp.where(even, left, right)]
-
-
-def weight_kernel(n_pieces, place, first, n_later, tile, aligned_ref, *refs):
+def weight_kernel(n_pieces, first, n_later, tile, aligned_ref, *refs):
     pieces = [ref[...] for ref in refs[:n_pieces]]
     out_ref, held_ref, left_sem = refs[n_pieces + n_later:]
     step = pl.program_id(0)
@@ -188,7 +154,7 @@
     def _():
         leave(step - slots).wait()
 
-    left = jnp.concatenate(place(pieces), axis=0)
+    left = jnp.concatenate(pieces, axis=0)
     depth = aligned_ref.shape[1]
     chunk = tile_of(depth, 1024)
     block = held_ref.at[lax.rem(step, slots)]
@@ -205,12 +171,12 @@
                 leave(last - back).wait()
 
 
-def weight_grads(aligned, pieces, place, tile, first, count, filled, later_than):
+def weight_grads(aligned, pieces, tile, first, count, filled, later_than):
     total, depth = aligned.shape
     rows, hidden = pieces[0].shape
     later = ([] if filled is None else [filled]) + list(later_than)
     return pl.pallas_call(
-        functools.partial(weight_kernel, len(pieces), place, first, len(later), tile),
+        functools.partial(weight_kernel, len(pieces), first, len(later), tile),
         grid=(count,),
         in_specs=[pl.BlockSpec((total, depth), lambda i: (0, 0))]
         + [pl.BlockSpec((rows, tile), lambda i: (0, i + first))] * len(pieces)
@@ -258,34 +224,6 @@
     return kept, sent, passed
 
 
-def line_fold_kernel(kept_ref, got_ref, two_ref, three_ref):
-    width = kept_ref.shape[1]
-    rows = two_ref.shape[0]
-    sub = tile_of(width, SUB)
-    lane = lax.broadcasted_iota(jnp.int32, (2 * rows, LANES), 1)
-    levels = jnp.zeros(lane.shape, jnp.float32)
-    got_levels = got_ref[rows:, width:]
-    for at in range(width // sub):
-        cols = slice(at * sub, (at + 1) * sub)
-        came = decode(got_ref[rows:, cols], got_levels[:, at:at + 1])
-        came = jnp.concatenate([came[rows:], came[:rows]], axis=0)
-        codes, level = encode(kept_ref[:, cols] + came)
-        two_ref[:, cols] = codes[:rows]
-        three_ref[:, cols] = codes[rows:]
-        levels = jnp.where(lane == at, level, levels)
-    two_ref[:, width:] = to_levels(levels[:rows])
-    three_ref[:, width:] = to_levels(levels[rows:])
-
-
-def line_fold(kept, got):
-    rows = kept.shape[0] // 2
-    like = jax.ShapeDtypeStruct((rows, got.shape[1]), got.dtype)
-    return pl.pallas_call(
-        line_fold_kernel, out_shape=[like, like], compiler_params=params(),
-        cost_estimate=cost(kept.size * 20, kept.size * 12), name="line_fold",
-    )(kept, got)
-
-
 def total_kernel(counts, *refs):
     refs = list(refs)
     out_ref = refs.pop()
@@ -336,19 +274,6 @@
     )(*values, *later_than)
 
 
-def add_kernel(left_ref, right_ref, *refs):
-    refs[-1][...] = left_ref[...] + right_ref[...]
-
-
-def added(left, right, later_than):
-    return pl.pallas_call(
-        add_kernel,
-        in_specs=[pl.BlockSpec(memory_space=pltpu.VMEM)] * 2 + [pl.BlockSpec(memory_space=pl.ANY)] * len(later_than),
-        out_shape=jax.ShapeDtypeStruct(left.shape, left.dtype),
-        compiler_params=params(SMALL_LIMIT), cost_estimate=cost(left.size, left.size * 6), name="added",
-    )(left, right, *later_than)
-
-
 def same_kernel(*refs):
     pass
 
@@ -364,10 +289,10 @@
     )(*values, *later_than)
 
 
-def gather_cotangent(cotangent, n_col, before_first, before_second):
+def gather_cotangent(cotangent, n_col):
     pieces = [cotangent] + [send(cotangent, "col", flip, n_col) for flip in range(2, n_col, 2)]
-    stacks = [stacked(pieces[:2], before_first)]
-    stacks.append(stacked(pieces[2:], stacks + before_second))
+    stacks = [stacked(pieces[:2])]
+    stacks.append(stacked(pieces[2:], stacks))
     return stacks + [send(stack, "col", 1, n_col) for stack in stacks]
 
 
@@ -383,63 +308,21 @@
     return [(first, last - first) for first, last in zip(ends, ends[1:])]
 
 
-def halving_sums(align, weight, act_pieces, n_row, offsets, tile):
-    total = align[0].shape[0]
-    kept_rows, sent_rows = [slice(0, total // 2)], [slice(total // 2, total)]
-    count = weight.shape[0] // tile
-    aligned, [kept], [sent] = partial_sums(None, align, weight, False, tile, 0, count, kept_rows, sent_rows, [], "sums")
-    got = send(sent, "row", 1, n_row)
-    evens = range(2, n_row, 2)
-    for o, piece in zip(evens, handed_on([act_pieces[o] for o in evens], [aligned])):
-        act_pieces[o], act_pieces[o + 1] = piece, send(piece, "row", 1, n_row)
-    step = 2
+def halved(kept, got, passed, n_row):
+    step, sent = 2, None
     while step < n_row:
-        kept, sent, _ = fold(kept, got, [])
+        kept, sent, passed = fold(kept, got, passed)
         got = send(sent, "row", step, n_row)
         step *= 2
-    weight_grad = weight_grads(aligned, [act_pieces[o] for o in offsets], lambda values: values, tile, 0, count, None, [sent])
-    return weight_grad, totals([[kept, got]], [weight_grad])
-
-
-def line_sums(align, weight, weight_a, act_pieces, tile):
-    total = align[0].shape[0]
-    rows = total // 4
-    kept_rows = [slice(0, rows), slice(2 * rows, total)]
-    sent_rows = [slice(rows, total), slice(rows, 2 * rows)]
-    (first_a, count_a), (first_b, count_b) = part_slices(weight.shape[0] // tile, (4, 3))
-    inwards, outwards, middle = [(0, 1), (3, 2)], [(1, 0), (2, 3)], [(1, 2), (2, 1)]
-
-    def spread(sent):
-        return lax.ppermute(sent[0], "row", inwards), lax.ppermute(sent[1], "row", outwards)
-
-    def cross(kept, got):
-        two, three = line_fold(kept, got)
-        return two, lax.ppermute(three, "row", middle), lax.ppermute(two, "row", [(1, 3), (2, 0)])
-
-    own, left, right = act_pieces
-    two_left = lax.ppermute(left, "row", [(1, 2), (2, 3)])
-    two_right = lax.ppermute(right, "row", [(2, 1), (1, 0)])
-    aligned, kept_a, sent_a = partial_sums(None, align, weight_a, True, tile, first_a, count_a, kept_rows, sent_rows, [], "sums_a")
-    got_a = spread(sent_a)
-    _, kept_b, sent_b = partial_sums(
-        aligned, None, weight, False, tile, first_b, count_b, kept_rows, sent_rows, [], "sums_b")
-    two = added(two_left, two_right, kept_b[:1])
-    far = lax.ppermute(two, "row", outwards)
-    sent_b = handed_on(sent_b, [got_a[1]])
-    got_b = spread(sent_b)
-    two_a, *crossed_a = cross(kept_a[1], got_a[0])
-    pieces = [own, left, right, two, far]
-    grad = weight_grads(aligned, pieces, line_places, tile, first_a, count_a, None, [two_a])
-    two_b, *crossed_b = cross(kept_b[1], got_b[0])
-    weight_grad = weight_grads(aligned, pieces, line_places, tile, first_b, count_b, grad, [two_b])
-    return weight_grad, totals([[kept_a[0], *got_a, *crossed_a], [kept_b[0], *got_b, *crossed_b]], [weight_grad])
+    return [kept, got], [sent] if sent is not None else [], passed
 
 
 def body(n_row, n_col, activations, cotangent, down_weight, row_order):
     rows, hidden = activations.shape
     shard = cotangent.shape[0]
     mine_row, mine_col = lax.axis_index("row"), lax.axis_index("col")
-    offsets = list(range(4)) if n_row == 4 else halving_order(n_row)
+    offsets = halving_order(n_row)
+    total = n_row * rows
 
     flips = list(range(0, n_col, 2))
     flips += [flip ^ 1 for flip in flips]
@@ -450,16 +333,34 @@
     pick = (order[:, None] == named[None, :]).astype(jnp.bfloat16)
 
     tile = tile_of(hidden, 256)
-    if n_row == 4:
-        weight_a = fetched(down_weight, tile, part_slices(hidden // tile, (4, 3))[0][1], [pick])
-        left = lax.ppermute(activations, "row", [(0, 1), (1, 2), (2, 3)])
-        right = lax.ppermute(activations, "row", [(3, 2), (2, 1), (1, 0)])
-        pieces = gather_cotangent(cotangent, n_col, [weight_a], [left, right])
-        return line_sums((pick, pieces), down_weight, weight_a, [activations, left, right], tile)
-    pieces = gather_cotangent(cotangent, n_col, [], [])
+    parts = part_slices(hidden // tile, SHARES)
+    pieces = gather_cotangent(cotangent, n_col)
     act_pieces = {o: send(activations, "row", o, n_row) for o in [1, *range(2, n_row, 2)]}
     act_pieces[0] = activations
-    return halving_sums((pick, pieces), down_weight, act_pieces, n_row, offsets, tile)
+
+    kept_rows, sent_rows = [slice(0, total // 2)], [slice(total // 2, total)]
+    aligned, [kept], [sent] = partial_sums(
+        None, (pick, pieces), down_weight, tile, *parts[0], kept_rows, sent_rows, [], "sums_first")
+    got = send(sent, "row", 1, n_row)
+    evens = range(2, n_row, 2)
+    for o, piece in zip(evens, handed_on([act_pieces[o] for o in evens], [aligned])):
+        act_pieces[o], act_pieces[o + 1] = piece, send(piece, "row", 1, n_row)
+
+    done, crossed = [], []
+    for at, part in enumerate(parts[1:]):
+        _, [next_kept], [sent] = partial_sums(
+            aligned, None, down_weight, tile, *part, kept_rows, sent_rows, [act_pieces[1]] if at == 0 else [], "sums_next")
+        ended, crossed, [sent] = halved(kept, got, [sent], n_row)
+        done.append(ended)
+        kept, got = next_kept, send(sent, "row", 1, n_row)
+
+    grad_pieces = [act_pieces[o] for o in offsets]
+    (first_a, count_a), (first_b, count_b) = part_slices(hidden // tile, (4, 3))
+    grad = weight_grads(aligned, grad_pieces, tile, first_a, count_a, None, crossed)
+    ended, crossed, _ = halved(kept, got, [], n_row)
+    done.append(ended)
+    weight_grad = weight_grads(aligned, grad_pieces, tile, first_b, count_b, grad, crossed)
+    return weight_grad, totals(done, [weight_grad])
 
 
 def solution(mesh):

time: 87.8 us -> 79.7 us (0.908)
  starting transfers between devices: 32.1 us -> 20.6 us
  waiting for transfers between devices: 15.7 us -> 21.3 us
  Pallas kernels: 37 us -> 34.1 us
  local copies, waits for them, and re-layouts: 0.86 us -> 1.8 us
    ppermute x13 -> x0, starting transfers between devices: 28.4 us -> none  [the longest x2 12.2 us: spread(): lax.ppermute(sent[0], 'row', inwards)]
    ppermute x5 -> x14, waiting for transfers between devices: 3.48 us -> 21.3 us  [send(): return lax.ppermute(value, axis, [(i, i ^ flip) for i in range(size)])]
    ppermute x5 -> x14, starting transfers between devices: 3.7 us -> 20.6 us  [send(): return lax.ppermute(value, axis, [(i, i ^ flip) for i in range(size)])]
    ppermute x13 -> x0, waiting for transfers between devices: 12.2 us -> none  [the longest x2 6.82 us: cross(): lax.ppermute(two, 'row', [(1, 3), (2, 0)])]
    pallas_call x6 -> x5, Pallas kernels: 21.2 us -> 14.7 us  [the longest x2 13.4 us: weight_grads(): pl.pallas_call(functools.partial(weight_kernel, len(pieces), first, len(l...]
    pallas_call x2 -> x3, Pallas kernels: 14.2 us -> 18.4 us  [partial_sums(): pl.pallas_call(functools.partial(sums_kernel, 0 if aligned is not None el...]
    unnamed x4, local copies, waits for them, and re-layouts: 0.01 us -> 0.96 us
  transfers between devices with their start and end apart: 18 -> 14, of which waited for: 5 -> 6; matrix products, arithmetic and copies ran while one was open for 2% -> 2% of each run, Pallas kernels for 41% -> 42%
where the time goes in v8:
time: 79.7 us; the launch traced here: 79.5 us
  Pallas kernels  34.1 us (43%)
  waiting for transfers between devices  21.3 us (27%)
  starting transfers between devices  20.6 us (26%)
  local copies, waits for them, and re-layouts  1.8 us (2%)
  other arithmetic  0.91 us (1%)
    ppermute x14, waiting for transfers between devices, send(): return lax.ppermute(value, axis, [(i, i ^ flip) for i in range(size)])  21.3 us
    ppermute x14, starting transfers between devices, send(): return lax.ppermute(value, axis, [(i, i ^ flip) for i in range(size)])  20.6 us
    pallas_call x3, Pallas kernels, partial_sums(): pl.pallas_call(functools.partial(sums_kernel, 0 if aligned is not None el...  18.4 us
    pallas_call x2, Pallas kernels, weight_grads(): pl.pallas_call(functools.partial(weight_kernel, len(pieces), first, len(l...  13.4 us
  transfers between devices with their start and end apart: 14, of which 6 were waited for; matrix products, arithmetic and copies ran while one was open for 2% of the time, Pallas kernels for 42%

profile of v8, /device:TPU:0, one launch (start us, length us, event | category | flops | bytes accessed | tf_op | source)
XLA Modules:
  0.0 79.5 jit_solution(2269213647380331635)
XLA Ops:
  0.6 3.0 %collective-permute-start = (bf16[32,4096]{1,0:T(8,128)(2,1)}, bf16[32,4096]{1,0:T(8,128)(2,1)S(1)}, u32[]{:S(2)}, u32[]{:S(2)}) collective-permute-start(bf16[32,4096]{1,0:T(8,128)(2,1)} %refs_0_.3), channel_id=1, source_target_pairs={{0,2},{1,3},{2,0},{3,1},{4,6},{5,7},{6,4},{7,5},{8,10},{9,11},{10,... | collective-permute-start | bytes 786440 | tf_op jit(solution)/shard_map/ppermute | solution.py:257
  3.6 1.5 %collective-permute-start.1 = (bf16[32,4096]{1,0:T(8,128)(2,1)}, bf16[32,4096]{1,0:T(8,128)(2,1)S(1)}, u32[]{:S(2)}, u32[]{:S(2)}) collective-permute-start(bf16[32,4096]{1,0:T(8,128)(2,1)} %refs_0_.3), channel_id=1, source_target_pairs={{0,4},{1,5},{2,6},{3,7},{4,0},{5,1},{6,2},{7,3},{8,12},{9,13},{10,... | collective-permute-start | bytes 786440 | tf_op jit(solution)/shard_map/ppermute | solution.py:257
  5.2 2.0 %collective-permute-start.6 = (bf16[64,3584]{1,0:T(8,128)(2,1)}, bf16[64,3584]{1,0:T(8,128)(2,1)S(1)}, u32[]{:S(2)}, u32[]{:S(2)}) collective-permute-start(bf16[64,3584]{1,0:T(8,128)(2,1)} %refs_0_.5), channel_id=1, source_target_pairs={{0,8},{8,0},{16,24},{24,16},{1,9},{9,1},{17,25},{25,17},{2,10},{10... | collective-permute-start | bytes 1376264 | tf_op jit(solution)/shard_map/ppermute | solution.py:257
  7.2 2.6 %collective-permute-start.5 = (bf16[64,3584]{1,0:T(8,128)(2,1)}, bf16[64,3584]{1,0:T(8,128)(2,1)S(1)}, u32[]{:S(2)}, u32[]{:S(2)}) collective-permute-start(bf16[64,3584]{1,0:T(8,128)(2,1)} %refs_0_.5), channel_id=1, source_target_pairs={{0,16},{8,24},{16,0},{24,8},{1,17},{9,25},{17,1},{25,9},{2,18},{10... | collective-permute-start | bytes 1376264 | tf_op jit(solution)/shard_map/ppermute | solution.py:257
  9.8 0.8 reshape.24
  10.6 0.7 xor_multiply_fusion
  11.2 0.9 %copy-done.1 = bf16[32,4096]{1,0:T(8,128)(2,1)S(1)} copy-done((bf16[32,4096]{1,0:T(8,128)(2,1)S(1)}, bf16[32,4096]{1,0:T(8,128)(2,1)}, u32[]{:S(2)}) %copy-start.1) | copy-done | bytes 262168
  12.2 0.1 collective-permute-start.3
  12.3 4.9 %collective-permute-done.1.refs_0_ = bf16[32,4096]{1,0:T(8,128)(2,1)S(1)} collective-permute-done((bf16[32,4096]{1,0:T(8,128)(2,1)}, bf16[32,4096]{1,0:T(8,128)(2,1)S(1)}, u32[]{:S(2)}, u32[]{:S(2)}) %collective-permute-start.1) | collective-permute-done | bytes 262176 | tf_op jit(solution)/shard_map/ppermute | solution.py:257
  17.4 0.1 pad_add_fusion
  17.5 0.1 add.40
  17.6 0.1 compare_convert_fusion.refs_0_
  17.7 1.6 %collective-permute-done.4.refs_4_ = bf16[64,4096]{1,0:T(8,128)(2,1)S(1)} collective-permute-done((bf16[64,4096]{1,0:T(8,128)(2,1)S(1)}, bf16[64,4096]{1,0:T(8,128)(2,1)S(1)}, u32[]{:S(2)}, u32[]{:S(2)}) %collective-permute-start.4) | collective-permute-done | bytes 524320 | tf_op jit(solution)/shard_map/ppermute | solution.py:257
  19.2 5.9 %sums_first.1 = (bf16[256,4096]{1,0:T(8,128)(2,1)S(1)}, f32[128,1024]{1,0:T(8,128)S(1)}, s16[128,1152]{1,0:T(8,128)(2,1)S(1)}) custom-call(bf16[256,256]{1,0:T(8,128)(2,1)S(1)} %compare_convert_fusion.refs_0_, bf16[64,4096]{1,0:T(8,128)(2,1)S(1)} %stacked.2.refs_2_.refs_1_, bf16[64,4096]{1,0:T(8,128)(2,1)S(1)} %stacked.3.refs_2_, ...), custom_call_target="tpu_custom_call" | custom-call | flops 2147483648 | bytes 8388608 | tf_op jit(solution)/shard_map/sums_first/pallas_call | solution.py:128
  25.1 1.6 %collective-permute-start.8 = (s16[128,1152]{1,0:T(8,128)(2,1)S(1)}, s16[128,1152]{1,0:T(8,128)(2,1)S(1)}, u32[]{:S(2)}, u32[]{:S(2)}) collective-permute-start(s16[128,1152]{1,0:T(8,128)(2,1)S(1)} %get-tuple-element.20), channel_id=1, source_target_pairs={{0,8},{8,0},{16,24},{24,16},{1,9},{9,1},{17,25},{25,17},{2,10},{10... | collective-permute-start | bytes 884744 | tf_op jit(solution)/shard_map/ppermute | solution.py:257
  26.8 2.7 %collective-permute-done.5.refs_0_ = bf16[64,3584]{1,0:T(8,128)(2,1)S(1)} collective-permute-done((bf16[64,3584]{1,0:T(8,128)(2,1)}, bf16[64,3584]{1,0:T(8,128)(2,1)S(1)}, u32[]{:S(2)}, u32[]{:S(2)}) %collective-permute-start.5) | collective-permute-done | bytes 458784 | tf_op jit(solution)/shard_map/ppermute | solution.py:257
  29.5 0.3 collective-permute-start.7
  29.8 7.4 %sums_next.2 = (f32[128,1536]{1,0:T(8,128)S(1)}, s16[128,1664]{1,0:T(8,128)(2,1)S(1)}) custom-call(bf16[256,4096]{1,0:T(8,128)(2,1)S(1)} %get-tuple-element.17.refs_1_.refs_0_.aligned_ref, bf16[3584,4096]{1,0:T(8,128)(2,1)} %refs_2_.3, bf16[3584,4096]{1,0:T(8,128)(2,1)} %refs_2_.3, bf16[64,3584]{1,0:T(8,128)(2,1)S(1)} %collective-permute-done.6.refs_3_.refs_2_), custom_call_target="tpu_custom_call" | custom-call | flops 3221225472 | bytes 12582912 | tf_op jit(solution)/shard_map/sums_next/pallas_call | solution.py:128
  37.2 0.3 fold.3
  37.5 1.8 %collective-permute-start.9 = (s16[128,1664]{1,0:T(8,128)(2,1)S(1)}, s16[128,1664]{1,0:T(8,128)(2,1)S(1)}, u32[]{:S(2)}, u32[]{:S(2)}) collective-permute-start(s16[128,1664]{1,0:T(8,128)(2,1)S(1)} %get-tuple-element.22), channel_id=1, source_target_pairs={{0,8},{8,0},{16,24},{24,16},{1,9},{9,1},{17,25},{25,17},{2,10},{10... | collective-permute-start | bytes 1277960 | tf_op jit(solution)/shard_map/ppermute | solution.py:257
  39.3 5.1 %sums_next.3 = (f32[128,1024]{1,0:T(8,128)S(1)}, s16[128,1152]{1,0:T(8,128)(2,1)S(1)}) custom-call(bf16[256,4096]{1,0:T(8,128)(2,1)S(1)} %get-tuple-element.17.refs_1_.refs_0_.aligned_ref, bf16[3584,4096]{1,0:T(8,128)(2,1)} %refs_2_.3, bf16[3584,4096]{1,0:T(8,128)(2,1)} %refs_2_.3), custom_call_target="tpu_custom_call" | custom-call | flops 2147483648 | bytes 8388608 | tf_op jit(solution)/shard_map/sums_next/pallas_call | solution.py:128
  44.5 1.0 %collective-permute-start.11 = (s16[64,1152]{1,0:T(8,128)(2,1)S(1)}, s16[64,1152]{1,0:T(8,128)(2,1)S(1)}, u32[]{:S(2)}, u32[]{:S(2)}) collective-permute-start(s16[64,1152]{1,0:T(8,128)(2,1)S(1)} %get-tuple-element.29), channel_id=1, source_target_pairs={{0,16},{8,24},{16,0},{24,8},{1,17},{9,25},{17,1},{25,9},{2,18},{10... | collective-permute-start | bytes 442376 | tf_op jit(solution)/shard_map/ppermute | solution.py:257
  45.5 11.0 %collective-permute-done.9.got_ref = s16[128,1664]{1,0:T(8,128)(2,1)S(1)} collective-permute-done((s16[128,1664]{1,0:T(8,128)(2,1)S(1)}, s16[128,1664]{1,0:T(8,128)(2,1)S(1)}, u32[]{:S(2)}, u32[]{:S(2)}) %collective-permute-start.9) | collective-permute-done | bytes 426016 | tf_op jit(solution)/shard_map/ppermute | solution.py:257
  56.5 0.6 fold.4
  57.1 4.3 %collective-permute-start.12 = (s16[64,1664]{1,0:T(8,128)(2,1)S(1)}, s16[64,1664]{1,0:T(8,128)(2,1)S(1)}, u32[]{:S(2)}, u32[]{:S(2)}) collective-permute-start(s16[64,1664]{1,0:T(8,128)(2,1)S(1)} %get-tuple-element.24.refs_4_), channel_id=1, source_target_pairs={{0,16},{8,24},{16,0},{24,8},{1,17},{9,25},{17,1},{25,9},{2,18},{10... | collective-permute-start | bytes 638984 | tf_op jit(solution)/shard_map/ppermute | solution.py:257
  61.4 7.5 %weight_grads.2.refs_4_ = bf16[3584,4096]{1,0:T(8,128)(2,1)} custom-call(bf16[256,4096]{1,0:T(8,128)(2,1)S(1)} %get-tuple-element.17.refs_1_.refs_0_.aligned_ref, bf16[64,3584]{1,0:T(8,128)(2,1)S(1)} %copy-done, bf16[64,3584]{1,0:T(8,128)(2,1)S(1)} %handed_on.1.refs_1_, bf16[64,3584]{1,0:T(8,128)(2,1)S(1)} %collective-permute-done.6.refs_3_.refs_2_, ...), custom_call_target="tpu_custom_call" | custom-call | flops 4294967296 | bytes 16777216 | tf_op jit(solution)/shard_map/weight_grads/pallas_call | solution.py:178
  68.9 1.0 %collective-permute-done.10.got_ref = s16[128,1152]{1,0:T(8,128)(2,1)S(1)} collective-permute-done((s16[128,1152]{1,0:T(8,128)(2,1)S(1)}, s16[128,1152]{1,0:T(8,128)(2,1)S(1)}, u32[]{:S(2)}, u32[]{:S(2)}) %collective-permute-start.10) | collective-permute-done | bytes 294944 | tf_op jit(solution)/shard_map/ppermute | solution.py:257
  69.9 0.3 fold.5
  70.3 2.2 %collective-permute-start.13 = (s16[64,1152]{1,0:T(8,128)(2,1)S(1)}, s16[64,1152]{1,0:T(8,128)(2,1)S(1)}, u32[]{:S(2)}, u32[]{:S(2)}) collective-permute-start(s16[64,1152]{1,0:T(8,128)(2,1)S(1)} %get-tuple-element.27.refs_5_), channel_id=1, source_target_pairs={{0,16},{8,24},{16,0},{24,8},{1,17},{9,25},{17,1},{25,9},{2,18},{10... | collective-permute-start | bytes 442376 | tf_op jit(solution)/shard_map/ppermute | solution.py:257
  72.4 5.9 %weight_grads.3.refs_6_ = bf16[3584,4096]{1,0:T(8,128)(2,1)} custom-call(bf16[256,4096]{1,0:T(8,128)(2,1)S(1)} %get-tuple-element.17.refs_1_.refs_0_.aligned_ref, bf16[64,3584]{1,0:T(8,128)(2,1)S(1)} %copy-done, bf16[64,3584]{1,0:T(8,128)(2,1)S(1)} %handed_on.1.refs_1_, ...), custom_call_target="tpu_custom_call", output_to_operand_aliasing={{}: (5, {})} | custom-call | flops 3221225472 | bytes 12582912 | tf_op jit(solution)/shard_map/weight_grads/pallas_call | solution.py:178
  78.4 0.1 collective-permute-done.13.refs_5_
  78.5 1.0 %totals.1 = bf16[64,3584]{1,0:T(8,128)(2,1)} custom-call(f32[64,1024]{1,0:T(8,128)S(1)} %get-tuple-element.28.refs_0_, s16[64,1152]{1,0:T(8,128)(2,1)S(1)} %collective-permute-done.11.refs_1_, f32[64,1536]{1,0:T(8,128)S(1)} %get-tuple-element.30.refs_2_, s16[64,1664]{1,0:T(8,128)(2,1)S(1)} %collective-permute-done.12.refs_3_, ...), custom_call_target="tpu_custom_call" | custom-call | flops 9175040 | bytes 3211264 | tf_op jit(solution)/shard_map/totals/pallas_call | solution.py:248
  (19 shorter events, 0.3 us)
Async XLA Ops:
  0.6 10.6 %collective-permute-start = (bf16[32,4096]{1,0:T(8,128)(2,1)}, bf16[32,4096]{1,0:T(8,128)(2,1)S(1)}, u32[]{:S(2)}, u32[]{:S(2)}) collective-permute-start(bf16[32,4096]{1,0:T(8,128)(2,1)} %refs_0_.3), channel_id=1, source_target_pairs={{0,2},{1,3},{2,0},{3,1},{4,6},{5,7},{6,4},{7,5},{8,10},{9,11},{10,... | collective-permute-start | bytes 786440 | tf_op jit(solution)/shard_map/ppermute | solution.py:257
  3.6 13.6 %collective-permute-start.1 = (bf16[32,4096]{1,0:T(8,128)(2,1)}, bf16[32,4096]{1,0:T(8,128)(2,1)S(1)}, u32[]{:S(2)}, u32[]{:S(2)}) collective-permute-start(bf16[32,4096]{1,0:T(8,128)(2,1)} %refs_0_.3), channel_id=1, source_target_pairs={{0,4},{1,5},{2,6},{3,7},{4,0},{5,1},{6,2},{7,3},{8,12},{9,13},{10,... | collective-permute-start | bytes 786440 | tf_op jit(solution)/shard_map/ppermute | solution.py:257
  5.2 12.1 %collective-permute-start.2 = (bf16[32,4096]{1,0:T(8,128)(2,1)}, bf16[32,4096]{1,0:T(8,128)(2,1)S(1)}, u32[]{:S(2)}, u32[]{:S(2)}) collective-permute-start(bf16[32,4096]{1,0:T(8,128)(2,1)} %refs_0_.3), channel_id=1, source_target_pairs={{0,6},{1,7},{2,4},{3,5},{4,2},{5,3},{6,0},{7,1},{8,14},{9,15},{10,... | collective-permute-start | bytes 786440 | tf_op jit(solution)/shard_map/ppermute | solution.py:257
  5.2 24.6 %collective-permute-start.6 = (bf16[64,3584]{1,0:T(8,128)(2,1)}, bf16[64,3584]{1,0:T(8,128)(2,1)S(1)}, u32[]{:S(2)}, u32[]{:S(2)}) collective-permute-start(bf16[64,3584]{1,0:T(8,128)(2,1)} %refs_0_.5), channel_id=1, source_target_pairs={{0,8},{8,0},{16,24},{24,16},{1,9},{9,1},{17,25},{25,17},{2,10},{10... | collective-permute-start | bytes 1376264 | tf_op jit(solution)/shard_map/ppermute | solution.py:257
  7.2 22.3 %collective-permute-start.5 = (bf16[64,3584]{1,0:T(8,128)(2,1)}, bf16[64,3584]{1,0:T(8,128)(2,1)S(1)}, u32[]{:S(2)}, u32[]{:S(2)}) collective-permute-start(bf16[64,3584]{1,0:T(8,128)(2,1)} %refs_0_.5), channel_id=1, source_target_pairs={{0,16},{8,24},{16,0},{24,8},{1,17},{9,25},{17,1},{25,9},{2,18},{10... | collective-permute-start | bytes 1376264 | tf_op jit(solution)/shard_map/ppermute | solution.py:257
  11.2 1.0 %copy-start.1 = (bf16[32,4096]{1,0:T(8,128)(2,1)S(1)}, bf16[32,4096]{1,0:T(8,128)(2,1)}, u32[]{:S(2)}) copy-start(bf16[32,4096]{1,0:T(8,128)(2,1)} %refs_0_.3) | copy-start | bytes 786436
  12.2 7.0 %collective-permute-start.3 = (bf16[64,4096]{1,0:T(8,128)(2,1)S(1)}, bf16[64,4096]{1,0:T(8,128)(2,1)S(1)}, u32[]{:S(2)}, u32[]{:S(2)}) collective-permute-start(bf16[64,4096]{1,0:T(8,128)(2,1)S(1)} %stacked.2.refs_2_.refs_1_), channel_id=1, source_target_pairs={{0,1},{1,0},{2,3},{3,2},{4,5},{5,4},{6,7},{7,6},{8,9},{9,8},{10,11... | collective-permute-start | bytes 1572872 | tf_op jit(solution)/shard_map/ppermute | solution.py:257
  17.3 2.0 %collective-permute-start.4 = (bf16[64,4096]{1,0:T(8,128)(2,1)S(1)}, bf16[64,4096]{1,0:T(8,128)(2,1)S(1)}, u32[]{:S(2)}, u32[]{:S(2)}) collective-permute-start(bf16[64,4096]{1,0:T(8,128)(2,1)S(1)} %stacked.3.refs_2_), channel_id=1, source_target_pairs={{0,1},{1,0},{2,3},{3,2},{4,5},{5,4},{6,7},{7,6},{8,9},{9,8},{10,11... | collective-permute-start | bytes 1572872 | tf_op jit(solution)/shard_map/ppermute | solution.py:257
  25.1 12.0 %collective-permute-start.8 = (s16[128,1152]{1,0:T(8,128)(2,1)S(1)}, s16[128,1152]{1,0:T(8,128)(2,1)S(1)}, u32[]{:S(2)}, u32[]{:S(2)}) collective-permute-start(s16[128,1152]{1,0:T(8,128)(2,1)S(1)} %get-tuple-element.20), channel_id=1, source_target_pairs={{0,8},{8,0},{16,24},{24,16},{1,9},{9,1},{17,25},{25,17},{2,10},{10... | collective-permute-start | bytes 884744 | tf_op jit(solution)/shard_map/ppermute | solution.py:257
  29.5 32.0 %collective-permute-start.7 = (bf16[64,3584]{1,0:T(8,128)(2,1)S(1)}, bf16[64,3584]{1,0:T(8,128)(2,1)S(1)}, u32[]{:S(2)}, u32[]{:S(2)}) collective-permute-start(bf16[64,3584]{1,0:T(8,128)(2,1)S(1)} %handed_on.1.refs_1_), channel_id=1, source_target_pairs={{0,8},{8,0},{16,24},{24,16},{1,9},{9,1},{17,25},{25,17},{2,10},{10... | collective-permute-start | bytes 1376264 | tf_op jit(solution)/shard_map/ppermute | solution.py:257
  37.5 23.9 %copy-start = (bf16[64,3584]{1,0:T(8,128)(2,1)S(1)}, bf16[64,3584]{1,0:T(8,128)(2,1)}, u32[]{:S(2)}) copy-start(bf16[64,3584]{1,0:T(8,128)(2,1)} %refs_0_.5) | copy-start | bytes 1376260
  37.5 19.0 %collective-permute-start.9 = (s16[128,1664]{1,0:T(8,128)(2,1)S(1)}, s16[128,1664]{1,0:T(8,128)(2,1)S(1)}, u32[]{:S(2)}, u32[]{:S(2)}) collective-permute-start(s16[128,1664]{1,0:T(8,128)(2,1)S(1)} %get-tuple-element.22), channel_id=1, source_target_pairs={{0,8},{8,0},{16,24},{24,16},{1,9},{9,1},{17,25},{25,17},{2,10},{10... | collective-permute-start | bytes 1277960 | tf_op jit(solution)/shard_map/ppermute | solution.py:257
  44.5 33.9 %collective-permute-start.11 = (s16[64,1152]{1,0:T(8,128)(2,1)S(1)}, s16[64,1152]{1,0:T(8,128)(2,1)S(1)}, u32[]{:S(2)}, u32[]{:S(2)}) collective-permute-start(s16[64,1152]{1,0:T(8,128)(2,1)S(1)} %get-tuple-element.29), channel_id=1, source_target_pairs={{0,16},{8,24},{16,0},{24,8},{1,17},{9,25},{17,1},{25,9},{2,18},{10... | collective-permute-start | bytes 442376 | tf_op jit(solution)/shard_map/ppermute | solution.py:257
  57.1 12.8 %collective-permute-start.10 = (s16[128,1152]{1,0:T(8,128)(2,1)S(1)}, s16[128,1152]{1,0:T(8,128)(2,1)S(1)}, u32[]{:S(2)}, u32[]{:S(2)}) collective-permute-start(s16[128,1152]{1,0:T(8,128)(2,1)S(1)} %get-tuple-element.26), channel_id=1, source_target_pairs={{0,8},{8,0},{16,24},{24,16},{1,9},{9,1},{17,25},{25,17},{2,10},{10... | collective-permute-start | bytes 884744 | tf_op jit(solution)/shard_map/ppermute | solution.py:257
  57.1 21.3 %collective-permute-start.12 = (s16[64,1664]{1,0:T(8,128)(2,1)S(1)}, s16[64,1664]{1,0:T(8,128)(2,1)S(1)}, u32[]{:S(2)}, u32[]{:S(2)}) collective-permute-start(s16[64,1664]{1,0:T(8,128)(2,1)S(1)} %get-tuple-element.24.refs_4_), channel_id=1, source_target_pairs={{0,16},{8,24},{16,0},{24,8},{1,17},{9,25},{17,1},{25,9},{2,18},{10... | collective-permute-start | bytes 638984 | tf_op jit(solution)/shard_map/ppermute | solution.py:257
  70.3 8.3 %collective-permute-start.13 = (s16[64,1152]{1,0:T(8,128)(2,1)S(1)}, s16[64,1152]{1,0:T(8,128)(2,1)S(1)}, u32[]{:S(2)}, u32[]{:S(2)}) collective-permute-start(s16[64,1152]{1,0:T(8,128)(2,1)S(1)} %get-tuple-element.27.refs_5_), channel_id=1, source_target_pairs={{0,16},{8,24},{16,0},{24,8},{1,17},{9,25},{17,1},{25,9},{2,18},{10... | collective-permute-start | bytes 442376 | tf_op jit(solution)/shard_map/ppermute | solution.py:257

commit v9 on v8

--- a/solution.py
+++ b/solution.py
@@ -15,7 +15,8 @@
 SMALL_LIMIT = 8 * 1024 * 1024
 SLOTS = 4
 SHARES = (2, 3, 2)
-SUB = 256
+GRAD_SHARES = (4, 3)
+SUB = 512
 
 
 def tile_of(size, largest):
@@ -190,9 +191,8 @@
     )(aligned, *pieces, *later)
 
 
-def fold_kernel(kept_ref, got_ref, *refs):
-    n_passed = (len(refs) - 2) // 2
-    next_ref, sent_ref = refs[n_passed:n_passed + 2]
+def fold_kernel(n_others, kept_ref, got_ref, *refs):
+    next_ref, sent_ref = refs[n_others:n_others + 2]
     width = kept_ref.shape[1]
     half = next_ref.shape[0]
     sub = tile_of(width, SUB)
@@ -209,18 +209,19 @@
     sent_ref[:, width:] = to_levels(levels)
 
 
-def fold(kept, got, passed):
+def fold(kept, got, passed, later_than):
+    others = [*passed, *later_than]
     vmem, anywhere = pl.BlockSpec(memory_space=pltpu.VMEM), pl.BlockSpec(memory_space=pl.ANY)
     rows, width = kept.shape
     kept, sent, *passed = pl.pallas_call(
-        fold_kernel,
-        in_specs=[vmem] * 2 + [anywhere] * len(passed),
+        functools.partial(fold_kernel, len(others)),
+        in_specs=[vmem] * 2 + [anywhere] * len(others),
         out_specs=[vmem] * 2 + [anywhere] * len(passed),
         out_shape=[jax.ShapeDtypeStruct((rows // 2, width), kept.dtype), jax.ShapeDtypeStruct((rows // 2, got.shape[1]), got.dtype)]
         + [jax.ShapeDtypeStruct(array.shape, array.dtype) for array in passed],
         input_output_aliases={2 + at: 2 + at for at in range(len(passed))},
         compiler_params=params(), cost_estimate=cost(kept.size * 20, kept.size * 12), name="fold",
-    )(kept, got, *passed)
+    )(kept, got, *others)
     return kept, sent, passed
 
 
@@ -308,10 +309,10 @@
     return [(first, last - first) for first, last in zip(ends, ends[1:])]
 
 
-def halved(kept, got, passed, n_row):
+def halved(kept, got, passed, later_than, n_row):
     step, sent = 2, None
     while step < n_row:
-        kept, sent, passed = fold(kept, got, passed)
+        kept, sent, passed = fold(kept, got, passed, later_than)
         got = send(sent, "row", step, n_row)
         step *= 2
     return [kept, got], [sent] if sent is not None else [], passed
@@ -332,7 +333,7 @@
     named = (owner[:, None] * shard + jnp.arange(shard, dtype=jnp.int32)[None, :]).reshape(-1)
     pick = (order[:, None] == named[None, :]).astype(jnp.bfloat16)
 
-    tile = tile_of(hidden, 256)
+    tile = tile_of(hidden, SUB)
     parts = part_slices(hidden // tile, SHARES)
     pieces = gather_cotangent(cotangent, n_col)
     act_pieces = {o: send(activations, "row", o, n_row) for o in [1, *range(2, n_row, 2)]}
@@ -346,20 +347,23 @@
     for o, piece in zip(evens, handed_on([act_pieces[o] for o in evens], [aligned])):
         act_pieces[o], act_pieces[o + 1] = piece, send(piece, "row", 1, n_row)
 
-    done, crossed = [], []
-    for at, part in enumerate(parts[1:]):
+    grad_pieces = [act_pieces[o] for o in offsets]
+    grad_tile = tile_of(hidden, 256)
+    grad_parts = part_slices(hidden // grad_tile, GRAD_SHARES)
+    done, crossed, grad = [], [], None
+    for at, part in enumerate(parts[1:], 1):
         _, [next_kept], [sent] = partial_sums(
-            aligned, None, down_weight, tile, *part, kept_rows, sent_rows, [act_pieces[1]] if at == 0 else [], "sums_next")
-        ended, crossed, [sent] = halved(kept, got, [sent], n_row)
+            aligned, None, down_weight, tile, *part, kept_rows, sent_rows, [act_pieces[1]] if at == 1 else [], "sums_next")
+        earlier = [ended[1] for ended in done]
+        if at == len(parts) - 1:
+            grad = weight_grads(aligned, grad_pieces, grad_tile, *grad_parts[0], None, [sent, *crossed])
+            earlier.append(grad)
+        ended, crossed, [sent] = halved(kept, got, [sent], earlier, n_row)
         done.append(ended)
         kept, got = next_kept, send(sent, "row", 1, n_row)
-
-    grad_pieces = [act_pieces[o] for o in offsets]
-    (first_a, count_a), (first_b, count_b) = part_slices(hidden // tile, (4, 3))
-    grad = weight_grads(aligned, grad_pieces, tile, first_a, count_a, None, crossed)
-    ended, crossed, _ = halved(kept, got, [], n_row)
+    ended, crossed, _ = halved(kept, got, [], [], n_row)
     done.append(ended)
-    weight_grad = weight_grads(aligned, grad_pieces, tile, first_b, count_b, grad, crossed)
+    weight_grad = weight_grads(aligned, grad_pieces, grad_tile, *grad_parts[1], grad, crossed)
     return weight_grad, totals(done, [weight_grad])
 
 

time: 79.7 us -> 82.1 us (1.030)
  waiting for transfers between devices: 21.3 us -> 23.9 us
    ppermute x14, waiting for transfers between devices: 21.3 us -> 23.9 us  [send(): return lax.ppermute(value, axis, [(i, i ^ flip) for i in range(size)])]
  transfers between devices with their start and end apart: 14 -> 14, of which waited for: 6 -> 9; matrix products, arithmetic and copies ran while one was open for 2% -> 2% of each run, Pallas kernels for 42% -> 40%
where the time goes in v9:
time: 82.1 us; the launch traced here: 81.9 us
  Pallas kernels  33.9 us (41%)
  waiting for transfers between devices  23.9 us (29%)
  starting transfers between devices  20.6 us (25%)
  local copies, waits for them, and re-layouts  1.8 us (2%)
  other arithmetic  0.91 us (1%)
    ppermute x14, waiting for transfers between devices, send(): return lax.ppermute(value, axis, [(i, i ^ flip) for i in range(size)])  23.9 us
    ppermute x14, starting transfers between devices, send(): return lax.ppermute(value, axis, [(i, i ^ flip) for i in range(size)])  20.6 us
    pallas_call x3, Pallas kernels, partial_sums(): pl.pallas_call(functools.partial(sums_kernel, 0 if aligned is not None el...  18.8 us
    pallas_call x2, Pallas kernels, weight_grads(): pl.pallas_call(functools.partial(weight_kernel, len(pieces), first, len(l...  13.4 us
  transfers between devices with their start and end apart: 14, of which 9 were waited for; matrix products, arithmetic and copies ran while one was open for 2% of the time, Pallas kernels for 40%

profile of v9, /device:TPU:0, one launch (start us, length us, event | category | flops | bytes accessed | tf_op | source)
XLA Modules:
  0.0 81.9 jit_solution(3716839536769575416)
XLA Ops:
  0.6 3.0 %collective-permute-start = (bf16[32,4096]{1,0:T(8,128)(2,1)}, bf16[32,4096]{1,0:T(8,128)(2,1)S(1)}, u32[]{:S(2)}, u32[]{:S(2)}) collective-permute-start(bf16[32,4096]{1,0:T(8,128)(2,1)} %refs_0_.3), channel_id=1, source_target_pairs={{0,2},{1,3},{2,0},{3,1},{4,6},{5,7},{6,4},{7,5},{8,10},{9,11},{10,... | collective-permute-start | bytes 786440 | tf_op jit(solution)/shard_map/ppermute | solution.py:258
  3.6 1.5 %collective-permute-start.2 = (bf16[32,4096]{1,0:T(8,128)(2,1)}, bf16[32,4096]{1,0:T(8,128)(2,1)S(1)}, u32[]{:S(2)}, u32[]{:S(2)}) collective-permute-start(bf16[32,4096]{1,0:T(8,128)(2,1)} %refs_0_.3), channel_id=1, source_target_pairs={{0,6},{1,7},{2,4},{3,5},{4,2},{5,3},{6,0},{7,1},{8,14},{9,15},{10,... | collective-permute-start | bytes 786440 | tf_op jit(solution)/shard_map/ppermute | solution.py:258
  5.2 2.0 %collective-permute-start.6 = (bf16[64,3584]{1,0:T(8,128)(2,1)}, bf16[64,3584]{1,0:T(8,128)(2,1)S(1)}, u32[]{:S(2)}, u32[]{:S(2)}) collective-permute-start(bf16[64,3584]{1,0:T(8,128)(2,1)} %refs_0_.5), channel_id=1, source_target_pairs={{0,8},{8,0},{16,24},{24,16},{1,9},{9,1},{17,25},{25,17},{2,10},{10... | collective-permute-start | bytes 1376264 | tf_op jit(solution)/shard_map/ppermute | solution.py:258
  7.2 2.6 %collective-permute-start.5 = (bf16[64,3584]{1,0:T(8,128)(2,1)}, bf16[64,3584]{1,0:T(8,128)(2,1)S(1)}, u32[]{:S(2)}, u32[]{:S(2)}) collective-permute-start(bf16[64,3584]{1,0:T(8,128)(2,1)} %refs_0_.5), channel_id=1, source_target_pairs={{0,16},{8,24},{16,0},{24,8},{1,17},{9,25},{17,1},{25,9},{2,18},{10... | collective-permute-start | bytes 1376264 | tf_op jit(solution)/shard_map/ppermute | solution.py:258
  9.8 0.8 reshape.24
  10.6 0.7 xor_multiply_fusion
  11.2 0.9 %copy-done.1 = bf16[32,4096]{1,0:T(8,128)(2,1)S(1)} copy-done((bf16[32,4096]{1,0:T(8,128)(2,1)S(1)}, bf16[32,4096]{1,0:T(8,128)(2,1)}, u32[]{:S(2)}) %copy-start.1) | copy-done | bytes 262168
  12.3 4.8 %collective-permute-done.2.refs_1_ = bf16[32,4096]{1,0:T(8,128)(2,1)S(1)} collective-permute-done((bf16[32,4096]{1,0:T(8,128)(2,1)}, bf16[32,4096]{1,0:T(8,128)(2,1)S(1)}, u32[]{:S(2)}, u32[]{:S(2)}) %collective-permute-start.2) | collective-permute-done | bytes 262176 | tf_op jit(solution)/shard_map/ppermute | solution.py:258
  17.1 1.4 %collective-permute-done.1.refs_0_ = bf16[32,4096]{1,0:T(8,128)(2,1)S(1)} collective-permute-done((bf16[32,4096]{1,0:T(8,128)(2,1)}, bf16[32,4096]{1,0:T(8,128)(2,1)S(1)}, u32[]{:S(2)}, u32[]{:S(2)}) %collective-permute-start.1) | collective-permute-done | bytes 262176 | tf_op jit(solution)/shard_map/ppermute | solution.py:258
  18.9 1.6 %collective-permute-done.4.refs_4_ = bf16[64,4096]{1,0:T(8,128)(2,1)S(1)} collective-permute-done((bf16[64,4096]{1,0:T(8,128)(2,1)S(1)}, bf16[64,4096]{1,0:T(8,128)(2,1)S(1)}, u32[]{:S(2)}, u32[]{:S(2)}) %collective-permute-start.4) | collective-permute-done | bytes 524320 | tf_op jit(solution)/shard_map/ppermute | solution.py:258
  20.5 6.5 %sums_first.1 = (bf16[256,4096]{1,0:T(8,128)(2,1)S(1)}, f32[128,1024]{1,0:T(8,128)S(1)}, s16[128,1152]{1,0:T(8,128)(2,1)S(1)}) custom-call(bf16[256,256]{1,0:T(8,128)(2,1)S(1)} %compare_convert_fusion.refs_0_, bf16[64,4096]{1,0:T(8,128)(2,1)S(1)} %stacked.2.refs_2_.refs_1_, bf16[64,4096]{1,0:T(8,128)(2,1)S(1)} %stacked.3.refs_2_, ...), custom_call_target="tpu_custom_call" | custom-call | flops 2147483648 | bytes 8388608 | tf_op jit(solution)/shard_map/sums_first/pallas_call | solution.py:129
  26.9 1.6 %collective-permute-start.8 = (s16[128,1152]{1,0:T(8,128)(2,1)S(1)}, s16[128,1152]{1,0:T(8,128)(2,1)S(1)}, u32[]{:S(2)}, u32[]{:S(2)}) collective-permute-start(s16[128,1152]{1,0:T(8,128)(2,1)S(1)} %get-tuple-element.20), channel_id=1, source_target_pairs={{0,8},{8,0},{16,24},{24,16},{1,9},{9,1},{17,25},{25,17},{2,10},{10... | collective-permute-start | bytes 884744 | tf_op jit(solution)/shard_map/ppermute | solution.py:258
  28.6 0.8 collective-permute-done.5.refs_0_
  29.4 0.4 collective-permute-start.7
  29.8 7.2 %sums_next.3 = (f32[128,1536]{1,0:T(8,128)S(1)}, s16[128,1664]{1,0:T(8,128)(2,1)S(1)}) custom-call(bf16[256,4096]{1,0:T(8,128)(2,1)S(1)} %get-tuple-element.17.refs_1_.refs_0_.aligned_ref, bf16[3584,4096]{1,0:T(8,128)(2,1)} %refs_1_.3, bf16[64,3584]{1,0:T(8,128)(2,1)S(1)} %collective-permute-done.6.refs_2_), custom_call_target="tpu_custom_call" | custom-call | flops 3221225472 | bytes 12582912 | tf_op jit(solution)/shard_map/sums_next/pallas_call | solution.py:129
  37.0 0.2 fold.3
  37.3 1.7 %collective-permute-start.9 = (s16[128,1664]{1,0:T(8,128)(2,1)S(1)}, s16[128,1664]{1,0:T(8,128)(2,1)S(1)}, u32[]{:S(2)}, u32[]{:S(2)}) collective-permute-start(s16[128,1664]{1,0:T(8,128)(2,1)S(1)} %get-tuple-element.25), channel_id=1, source_target_pairs={{0,8},{8,0},{16,24},{24,16},{1,9},{9,1},{17,25},{25,17},{2,10},{10... | collective-permute-start | bytes 1277960 | tf_op jit(solution)/shard_map/ppermute | solution.py:258
  38.9 5.1 %sums_next.2 = (f32[128,1024]{1,0:T(8,128)S(1)}, s16[128,1152]{1,0:T(8,128)(2,1)S(1)}) custom-call(bf16[256,4096]{1,0:T(8,128)(2,1)S(1)} %get-tuple-element.17.refs_1_.refs_0_.aligned_ref, bf16[3584,4096]{1,0:T(8,128)(2,1)} %refs_1_.3), custom_call_target="tpu_custom_call" | custom-call | flops 2147483648 | bytes 8388608 | tf_op jit(solution)/shard_map/sums_next/pallas_call | solution.py:129
  44.0 2.4 %collective-permute-start.10 = (s16[64,1152]{1,0:T(8,128)(2,1)S(1)}, s16[64,1152]{1,0:T(8,128)(2,1)S(1)}, u32[]{:S(2)}, u32[]{:S(2)}) collective-permute-start(s16[64,1152]{1,0:T(8,128)(2,1)S(1)} %get-tuple-element.22.refs_5_), channel_id=1, source_target_pairs={{0,16},{8,24},{16,0},{24,8},{1,17},{9,25},{17,1},{25,9},{2,18},{10... | collective-permute-start | bytes 442376 | tf_op jit(solution)/shard_map/ppermute | solution.py:258
  46.5 1.8 %collective-permute-done.7.refs_3_ = bf16[64,3584]{1,0:T(8,128)(2,1)S(1)} collective-permute-done((bf16[64,3584]{1,0:T(8,128)(2,1)S(1)}, bf16[64,3584]{1,0:T(8,128)(2,1)S(1)}, u32[]{:S(2)}, u32[]{:S(2)}) %collective-permute-start.7) | collective-permute-done | bytes 458784 | tf_op jit(solution)/shard_map/ppermute | solution.py:258
  48.3 7.5 %weight_grads.2.refs_2_.refs_4_ = bf16[3584,4096]{1,0:T(8,128)(2,1)} custom-call(bf16[256,4096]{1,0:T(8,128)(2,1)S(1)} %get-tuple-element.17.refs_1_.refs_0_.aligned_ref, bf16[64,3584]{1,0:T(8,128)(2,1)S(1)} %copy-done, bf16[64,3584]{1,0:T(8,128)(2,1)S(1)} %handed_on.1.refs_1_, bf16[64,3584]{1,0:T(8,128)(2,1)S(1)} %collective-permute-done.6.refs_2_, ...), custom_call_target="tpu_custom_call" | custom-call | flops 4294967296 | bytes 16777216 | tf_op jit(solution)/shard_map/weight_grads/pallas_call | solution.py:179
  55.8 1.5 %collective-permute-done.10.refs_1_ = s16[64,1152]{1,0:T(8,128)(2,1)S(1)} collective-permute-done((s16[64,1152]{1,0:T(8,128)(2,1)S(1)}, s16[64,1152]{1,0:T(8,128)(2,1)S(1)}, u32[]{:S(2)}, u32[]{:S(2)}) %collective-permute-start.10) | collective-permute-done | bytes 147488 | tf_op jit(solution)/shard_map/ppermute | solution.py:258
  57.3 0.9 %collective-permute-done.9.got_ref = s16[128,1664]{1,0:T(8,128)(2,1)S(1)} collective-permute-done((s16[128,1664]{1,0:T(8,128)(2,1)S(1)}, s16[128,1664]{1,0:T(8,128)(2,1)S(1)}, u32[]{:S(2)}, u32[]{:S(2)}) %collective-permute-start.9) | collective-permute-done | bytes 426016 | tf_op jit(solution)/shard_map/ppermute | solution.py:258
  58.2 0.3 fold.4
  58.4 2.7 %collective-permute-start.11 = (s16[128,1152]{1,0:T(8,128)(2,1)S(1)}, s16[128,1152]{1,0:T(8,128)(2,1)S(1)}, u32[]{:S(2)}, u32[]{:S(2)}) collective-permute-start(s16[128,1152]{1,0:T(8,128)(2,1)S(1)} %get-tuple-element.26), channel_id=1, source_target_pairs={{0,8},{8,0},{16,24},{24,16},{1,9},{9,1},{17,25},{25,17},{2,10},{10... | collective-permute-start | bytes 884744 | tf_op jit(solution)/shard_map/ppermute | solution.py:258
  61.1 1.6 %collective-permute-start.12 = (s16[64,1664]{1,0:T(8,128)(2,1)S(1)}, s16[64,1664]{1,0:T(8,128)(2,1)S(1)}, u32[]{:S(2)}, u32[]{:S(2)}) collective-permute-start(s16[64,1664]{1,0:T(8,128)(2,1)S(1)} %get-tuple-element.30), channel_id=1, source_target_pairs={{0,16},{8,24},{16,0},{24,8},{1,17},{9,25},{17,1},{25,9},{2,18},{10... | collective-permute-start | bytes 638984 | tf_op jit(solution)/shard_map/ppermute | solution.py:258
  62.7 9.5 %collective-permute-done.11.got_ref = s16[128,1152]{1,0:T(8,128)(2,1)S(1)} collective-permute-done((s16[128,1152]{1,0:T(8,128)(2,1)S(1)}, s16[128,1152]{1,0:T(8,128)(2,1)S(1)}, u32[]{:S(2)}, u32[]{:S(2)}) %collective-permute-start.11) | collective-permute-done | bytes 294944 | tf_op jit(solution)/shard_map/ppermute | solution.py:258
  72.1 0.2 fold.5
  72.4 0.9 %collective-permute-start.13 = (s16[64,1152]{1,0:T(8,128)(2,1)S(1)}, s16[64,1152]{1,0:T(8,128)(2,1)S(1)}, u32[]{:S(2)}, u32[]{:S(2)}) collective-permute-start(s16[64,1152]{1,0:T(8,128)(2,1)S(1)} %get-tuple-element.27.refs_5_), channel_id=1, source_target_pairs={{0,16},{8,24},{16,0},{24,8},{1,17},{9,25},{17,1},{25,9},{2,18},{10... | collective-permute-start | bytes 442376 | tf_op jit(solution)/shard_map/ppermute | solution.py:258
  73.3 5.9 %weight_grads.3.refs_6_ = bf16[3584,4096]{1,0:T(8,128)(2,1)} custom-call(bf16[256,4096]{1,0:T(8,128)(2,1)S(1)} %get-tuple-element.17.refs_1_.refs_0_.aligned_ref, bf16[64,3584]{1,0:T(8,128)(2,1)S(1)} %copy-done, bf16[64,3584]{1,0:T(8,128)(2,1)S(1)} %handed_on.1.refs_1_, ...), custom_call_target="tpu_custom_call", output_to_operand_aliasing={{}: (5, {})} | custom-call | flops 3221225472 | bytes 12582912 | tf_op jit(solution)/shard_map/weight_grads/pallas_call | solution.py:179
  79.2 1.7 %collective-permute-done.13.refs_5_ = s16[64,1152]{1,0:T(8,128)(2,1)S(1)} collective-permute-done((s16[64,1152]{1,0:T(8,128)(2,1)S(1)}, s16[64,1152]{1,0:T(8,128)(2,1)S(1)}, u32[]{:S(2)}, u32[]{:S(2)}) %collective-permute-start.13) | collective-permute-done | bytes 147488 | tf_op jit(solution)/shard_map/ppermute | solution.py:258
  81.0 0.9 %totals.1 = bf16[64,3584]{1,0:T(8,128)(2,1)} custom-call(f32[64,1024]{1,0:T(8,128)S(1)} %get-tuple-element.28.refs_0_, s16[64,1152]{1,0:T(8,128)(2,1)S(1)} %collective-permute-done.10.refs_1_, f32[64,1536]{1,0:T(8,128)S(1)} %get-tuple-element.29.refs_2_, s16[64,1664]{1,0:T(8,128)(2,1)S(1)} %collective-permute-done.12.refs_3_, ...), custom_call_target="tpu_custom_call" | custom-call | flops 9175040 | bytes 3211264 | tf_op jit(solution)/shard_map/totals/pallas_call | solution.py:249
  (19 shorter events, 0.6 us)
Async XLA Ops:
  0.6 10.6 %collective-permute-start = (bf16[32,4096]{1,0:T(8,128)(2,1)}, bf16[32,4096]{1,0:T(8,128)(2,1)S(1)}, u32[]{:S(2)}, u32[]{:S(2)}) collective-permute-start(bf16[32,4096]{1,0:T(8,128)(2,1)} %refs_0_.3), channel_id=1, source_target_pairs={{0,2},{1,3},{2,0},{3,1},{4,6},{5,7},{6,4},{7,5},{8,10},{9,11},{10,... | collective-permute-start | bytes 786440 | tf_op jit(solution)/shard_map/ppermute | solution.py:258
  3.6 13.4 %collective-permute-start.2 = (bf16[32,4096]{1,0:T(8,128)(2,1)}, bf16[32,4096]{1,0:T(8,128)(2,1)S(1)}, u32[]{:S(2)}, u32[]{:S(2)}) collective-permute-start(bf16[32,4096]{1,0:T(8,128)(2,1)} %refs_0_.3), channel_id=1, source_target_pairs={{0,6},{1,7},{2,4},{3,5},{4,2},{5,3},{6,0},{7,1},{8,14},{9,15},{10,... | collective-permute-start | bytes 786440 | tf_op jit(solution)/shard_map/ppermute | solution.py:258
  5.1 13.3 %collective-permute-start.1 = (bf16[32,4096]{1,0:T(8,128)(2,1)}, bf16[32,4096]{1,0:T(8,128)(2,1)S(1)}, u32[]{:S(2)}, u32[]{:S(2)}) collective-permute-start(bf16[32,4096]{1,0:T(8,128)(2,1)} %refs_0_.3), channel_id=1, source_target_pairs={{0,4},{1,5},{2,6},{3,7},{4,0},{5,1},{6,2},{7,3},{8,12},{9,13},{10,... | collective-permute-start | bytes 786440 | tf_op jit(solution)/shard_map/ppermute | solution.py:258
  5.2 24.6 %collective-permute-start.6 = (bf16[64,3584]{1,0:T(8,128)(2,1)}, bf16[64,3584]{1,0:T(8,128)(2,1)S(1)}, u32[]{:S(2)}, u32[]{:S(2)}) collective-permute-start(bf16[64,3584]{1,0:T(8,128)(2,1)} %refs_0_.5), channel_id=1, source_target_pairs={{0,8},{8,0},{16,24},{24,16},{1,9},{9,1},{17,25},{25,17},{2,10},{10... | collective-permute-start | bytes 1376264 | tf_op jit(solution)/shard_map/ppermute | solution.py:258
  7.2 22.1 %collective-permute-start.5 = (bf16[64,3584]{1,0:T(8,128)(2,1)}, bf16[64,3584]{1,0:T(8,128)(2,1)S(1)}, u32[]{:S(2)}, u32[]{:S(2)}) collective-permute-start(bf16[64,3584]{1,0:T(8,128)(2,1)} %refs_0_.5), channel_id=1, source_target_pairs={{0,16},{8,24},{16,0},{24,8},{1,17},{9,25},{17,1},{25,9},{2,18},{10... | collective-permute-start | bytes 1376264 | tf_op jit(solution)/shard_map/ppermute | solution.py:258
  11.2 1.0 %copy-start.1 = (bf16[32,4096]{1,0:T(8,128)(2,1)S(1)}, bf16[32,4096]{1,0:T(8,128)(2,1)}, u32[]{:S(2)}) copy-start(bf16[32,4096]{1,0:T(8,128)(2,1)} %refs_0_.3) | copy-start | bytes 786436
  12.2 8.2 %collective-permute-start.3 = (bf16[64,4096]{1,0:T(8,128)(2,1)S(1)}, bf16[64,4096]{1,0:T(8,128)(2,1)S(1)}, u32[]{:S(2)}, u32[]{:S(2)}) collective-permute-start(bf16[64,4096]{1,0:T(8,128)(2,1)S(1)} %stacked.2.refs_2_.refs_1_), channel_id=1, source_target_pairs={{0,1},{1,0},{2,3},{3,2},{4,5},{5,4},{6,7},{7,6},{8,9},{9,8},{10,11... | collective-permute-start | bytes 1572872 | tf_op jit(solution)/shard_map/ppermute | solution.py:258
  18.5 2.0 %collective-permute-start.4 = (bf16[64,4096]{1,0:T(8,128)(2,1)S(1)}, bf16[64,4096]{1,0:T(8,128)(2,1)S(1)}, u32[]{:S(2)}, u32[]{:S(2)}) collective-permute-start(bf16[64,4096]{1,0:T(8,128)(2,1)S(1)} %stacked.3.refs_2_), channel_id=1, source_target_pairs={{0,1},{1,0},{2,3},{3,2},{4,5},{5,4},{6,7},{7,6},{8,9},{9,8},{10,11... | collective-permute-start | bytes 1572872 | tf_op jit(solution)/shard_map/ppermute | solution.py:258
  26.9 10.1 %collective-permute-start.8 = (s16[128,1152]{1,0:T(8,128)(2,1)S(1)}, s16[128,1152]{1,0:T(8,128)(2,1)S(1)}, u32[]{:S(2)}, u32[]{:S(2)}) collective-permute-start(s16[128,1152]{1,0:T(8,128)(2,1)S(1)} %get-tuple-element.20), channel_id=1, source_target_pairs={{0,8},{8,0},{16,24},{24,16},{1,9},{9,1},{17,25},{25,17},{2,10},{10... | collective-permute-start | bytes 884744 | tf_op jit(solution)/shard_map/ppermute | solution.py:258
  29.4 18.9 %copy-start = (bf16[64,3584]{1,0:T(8,128)(2,1)S(1)}, bf16[64,3584]{1,0:T(8,128)(2,1)}, u32[]{:S(2)}) copy-start(bf16[64,3584]{1,0:T(8,128)(2,1)} %refs_0_.5) | copy-start | bytes 1376260
  29.4 18.9 %collective-permute-start.7 = (bf16[64,3584]{1,0:T(8,128)(2,1)S(1)}, bf16[64,3584]{1,0:T(8,128)(2,1)S(1)}, u32[]{:S(2)}, u32[]{:S(2)}) collective-permute-start(bf16[64,3584]{1,0:T(8,128)(2,1)S(1)} %handed_on.1.refs_1_), channel_id=1, source_target_pairs={{0,8},{8,0},{16,24},{24,16},{1,9},{9,1},{17,25},{25,17},{2,10},{10... | collective-permute-start | bytes 1376264 | tf_op jit(solution)/shard_map/ppermute | solution.py:258
  37.3 20.9 %collective-permute-start.9 = (s16[128,1664]{1,0:T(8,128)(2,1)S(1)}, s16[128,1664]{1,0:T(8,128)(2,1)S(1)}, u32[]{:S(2)}, u32[]{:S(2)}) collective-permute-start(s16[128,1664]{1,0:T(8,128)(2,1)S(1)} %get-tuple-element.25), channel_id=1, source_target_pairs={{0,8},{8,0},{16,24},{24,16},{1,9},{9,1},{17,25},{25,17},{2,10},{10... | collective-permute-start | bytes 1277960 | tf_op jit(solution)/shard_map/ppermute | solution.py:258
  44.0 13.3 %collective-permute-start.10 = (s16[64,1152]{1,0:T(8,128)(2,1)S(1)}, s16[64,1152]{1,0:T(8,128)(2,1)S(1)}, u32[]{:S(2)}, u32[]{:S(2)}) collective-permute-start(s16[64,1152]{1,0:T(8,128)(2,1)S(1)} %get-tuple-element.22.refs_5_), channel_id=1, source_target_pairs={{0,16},{8,24},{16,0},{24,8},{1,17},{9,25},{17,1},{25,9},{2,18},{10... | collective-permute-start | bytes 442376 | tf_op jit(solution)/shard_map/ppermute | solution.py:258
  58.4 13.7 %collective-permute-start.11 = (s16[128,1152]{1,0:T(8,128)(2,1)S(1)}, s16[128,1152]{1,0:T(8,128)(2,1)S(1)}, u32[]{:S(2)}, u32[]{:S(2)}) collective-permute-start(s16[128,1152]{1,0:T(8,128)(2,1)S(1)} %get-tuple-element.26), channel_id=1, source_target_pairs={{0,8},{8,0},{16,24},{24,16},{1,9},{9,1},{17,25},{25,17},{2,10},{10... | collective-permute-start | bytes 884744 | tf_op jit(solution)/shard_map/ppermute | solution.py:258
  61.1 18.1 %collective-permute-start.12 = (s16[64,1664]{1,0:T(8,128)(2,1)S(1)}, s16[64,1664]{1,0:T(8,128)(2,1)S(1)}, u32[]{:S(2)}, u32[]{:S(2)}) collective-permute-start(s16[64,1664]{1,0:T(8,128)(2,1)S(1)} %get-tuple-element.30), channel_id=1, source_target_pairs={{0,16},{8,24},{16,0},{24,8},{1,17},{9,25},{17,1},{25,9},{2,18},{10... | collective-permute-start | bytes 638984 | tf_op jit(solution)/shard_map/ppermute | solution.py:258
  72.4 8.6 %collective-permute-start.13 = (s16[64,1152]{1,0:T(8,128)(2,1)S(1)}, s16[64,1152]{1,0:T(8,128)(2,1)S(1)}, u32[]{:S(2)}, u32[]{:S(2)}) collective-permute-start(s16[64,1152]{1,0:T(8,128)(2,1)S(1)} %get-tuple-element.27.refs_5_), channel_id=1, source_target_pairs={{0,16},{8,24},{16,0},{24,8},{1,17},{9,25},{17,1},{25,9},{2,18},{10... | collective-permute-start | bytes 442376 | tf_op jit(solution)/shard_map/ppermute | solution.py:258

commit v10 on v9

--- a/solution.py
+++ b/solution.py
@@ -14,9 +14,9 @@
 VMEM_LIMIT = 48 * 1024 * 1024
 SMALL_LIMIT = 8 * 1024 * 1024
 SLOTS = 4
-SHARES = (2, 3, 2)
+SHARES = (2, 4, 1)
 GRAD_SHARES = (4, 3)
-SUB = 512
+SUB = 256
 
 
 def tile_of(size, largest):

time: 82.1 us -> 83 us (1.011)
  transfers between devices with their start and end apart: 14 -> 14, of which waited for: 9 -> 9; matrix products, arithmetic and copies ran while one was open for 2% -> 2% of each run, Pallas kernels for 40% -> 39%
where the time goes in v10:
time: 83 us; the launch traced here: 82.8 us
  Pallas kernels  34.3 us (41%)
  waiting for transfers between devices  24.1 us (29%)
  starting transfers between devices  21 us (25%)
  local copies, waits for them, and re-layouts  1.8 us (2%)
  other arithmetic  0.91 us (1%)
    ppermute x14, waiting for transfers between devices, send(): return lax.ppermute(value, axis, [(i, i ^ flip) for i in range(size)])  24.1 us
    ppermute x14, starting transfers between devices, send(): return lax.ppermute(value, axis, [(i, i ^ flip) for i in range(size)])  21 us
    pallas_call x3, Pallas kernels, partial_sums(): pl.pallas_call(functools.partial(sums_kernel, 0 if aligned is not None el...  18.5 us
    pallas_call x2, Pallas kernels, weight_grads(): pl.pallas_call(functools.partial(weight_kernel, len(pieces), first, len(l...  13.4 us
  transfers between devices with their start and end apart: 14, of which 9 were waited for; matrix products, arithmetic and copies ran while one was open for 2% of the time, Pallas kernels for 39%

profile of v10, /device:TPU:0, one launch (start us, length us, event | category | flops | bytes accessed | tf_op | source)
XLA Modules:
  0.0 82.8 jit_solution(5534268194138871696)
XLA Ops:
  0.6 3.0 %collective-permute-start = (bf16[32,4096]{1,0:T(8,128)(2,1)}, bf16[32,4096]{1,0:T(8,128)(2,1)S(1)}, u32[]{:S(2)}, u32[]{:S(2)}) collective-permute-start(bf16[32,4096]{1,0:T(8,128)(2,1)} %refs_0_.3), channel_id=1, source_target_pairs={{0,2},{1,3},{2,0},{3,1},{4,6},{5,7},{6,4},{7,5},{8,10},{9,11},{10,... | collective-permute-start | bytes 786440 | tf_op jit(solution)/shard_map/ppermute | solution.py:258
  3.6 1.5 %collective-permute-start.2 = (bf16[32,4096]{1,0:T(8,128)(2,1)}, bf16[32,4096]{1,0:T(8,128)(2,1)S(1)}, u32[]{:S(2)}, u32[]{:S(2)}) collective-permute-start(bf16[32,4096]{1,0:T(8,128)(2,1)} %refs_0_.3), channel_id=1, source_target_pairs={{0,6},{1,7},{2,4},{3,5},{4,2},{5,3},{6,0},{7,1},{8,14},{9,15},{10,... | collective-permute-start | bytes 786440 | tf_op jit(solution)/shard_map/ppermute | solution.py:258
  5.2 2.0 %collective-permute-start.6 = (bf16[64,3584]{1,0:T(8,128)(2,1)}, bf16[64,3584]{1,0:T(8,128)(2,1)S(1)}, u32[]{:S(2)}, u32[]{:S(2)}) collective-permute-start(bf16[64,3584]{1,0:T(8,128)(2,1)} %refs_0_.5), channel_id=1, source_target_pairs={{0,8},{8,0},{16,24},{24,16},{1,9},{9,1},{17,25},{25,17},{2,10},{10... | collective-permute-start | bytes 1376264 | tf_op jit(solution)/shard_map/ppermute | solution.py:258
  7.2 2.6 %collective-permute-start.5 = (bf16[64,3584]{1,0:T(8,128)(2,1)}, bf16[64,3584]{1,0:T(8,128)(2,1)S(1)}, u32[]{:S(2)}, u32[]{:S(2)}) collective-permute-start(bf16[64,3584]{1,0:T(8,128)(2,1)} %refs_0_.5), channel_id=1, source_target_pairs={{0,16},{8,24},{16,0},{24,8},{1,17},{9,25},{17,1},{25,9},{2,18},{10... | collective-permute-start | bytes 1376264 | tf_op jit(solution)/shard_map/ppermute | solution.py:258
  9.8 0.8 reshape.24
  10.6 0.7 xor_multiply_fusion
  11.2 0.9 %copy-done.1 = bf16[32,4096]{1,0:T(8,128)(2,1)S(1)} copy-done((bf16[32,4096]{1,0:T(8,128)(2,1)S(1)}, bf16[32,4096]{1,0:T(8,128)(2,1)}, u32[]{:S(2)}) %copy-start.1) | copy-done | bytes 262168
  12.3 4.8 %collective-permute-done.2.refs_1_ = bf16[32,4096]{1,0:T(8,128)(2,1)S(1)} collective-permute-done((bf16[32,4096]{1,0:T(8,128)(2,1)}, bf16[32,4096]{1,0:T(8,128)(2,1)S(1)}, u32[]{:S(2)}, u32[]{:S(2)}) %collective-permute-start.2) | collective-permute-done | bytes 262176 | tf_op jit(solution)/shard_map/ppermute | solution.py:258
  17.1 1.4 %collective-permute-done.1.refs_0_ = bf16[32,4096]{1,0:T(8,128)(2,1)S(1)} collective-permute-done((bf16[32,4096]{1,0:T(8,128)(2,1)}, bf16[32,4096]{1,0:T(8,128)(2,1)S(1)}, u32[]{:S(2)}, u32[]{:S(2)}) %collective-permute-start.1) | collective-permute-done | bytes 262176 | tf_op jit(solution)/shard_map/ppermute | solution.py:258
  18.9 1.6 %collective-permute-done.4.refs_4_ = bf16[64,4096]{1,0:T(8,128)(2,1)S(1)} collective-permute-done((bf16[64,4096]{1,0:T(8,128)(2,1)S(1)}, bf16[64,4096]{1,0:T(8,128)(2,1)S(1)}, u32[]{:S(2)}, u32[]{:S(2)}) %collective-permute-start.4) | collective-permute-done | bytes 524320 | tf_op jit(solution)/shard_map/ppermute | solution.py:258
  20.5 5.9 %sums_first.1 = (bf16[256,4096]{1,0:T(8,128)(2,1)S(1)}, f32[128,1024]{1,0:T(8,128)S(1)}, s16[128,1152]{1,0:T(8,128)(2,1)S(1)}) custom-call(bf16[256,256]{1,0:T(8,128)(2,1)S(1)} %compare_convert_fusion.refs_0_, bf16[64,4096]{1,0:T(8,128)(2,1)S(1)} %stacked.2.refs_2_.refs_1_, bf16[64,4096]{1,0:T(8,128)(2,1)S(1)} %stacked.3.refs_2_, ...), custom_call_target="tpu_custom_call" | custom-call | flops 2147483648 | bytes 8388608 | tf_op jit(solution)/shard_map/sums_first/pallas_call | solution.py:129
  26.3 1.6 %collective-permute-start.8 = (s16[128,1152]{1,0:T(8,128)(2,1)S(1)}, s16[128,1152]{1,0:T(8,128)(2,1)S(1)}, u32[]{:S(2)}, u32[]{:S(2)}) collective-permute-start(s16[128,1152]{1,0:T(8,128)(2,1)S(1)} %get-tuple-element.20), channel_id=1, source_target_pairs={{0,8},{8,0},{16,24},{24,16},{1,9},{9,1},{17,25},{25,17},{2,10},{10... | collective-permute-start | bytes 884744 | tf_op jit(solution)/shard_map/ppermute | solution.py:258
  28.0 1.5 %collective-permute-done.5.refs_0_ = bf16[64,3584]{1,0:T(8,128)(2,1)S(1)} collective-permute-done((bf16[64,3584]{1,0:T(8,128)(2,1)}, bf16[64,3584]{1,0:T(8,128)(2,1)S(1)}, u32[]{:S(2)}, u32[]{:S(2)}) %collective-permute-start.5) | collective-permute-done | bytes 458784 | tf_op jit(solution)/shard_map/ppermute | solution.py:258
  29.5 0.3 collective-permute-start.7
  29.8 9.0 %sums_next.3 = (f32[128,2048]{1,0:T(8,128)S(1)}, s16[128,2176]{1,0:T(8,128)(2,1)S(1)}) custom-call(bf16[256,4096]{1,0:T(8,128)(2,1)S(1)} %get-tuple-element.17.refs_1_.refs_0_.aligned_ref, bf16[3584,4096]{1,0:T(8,128)(2,1)} %refs_2_.3, bf16[3584,4096]{1,0:T(8,128)(2,1)} %refs_2_.3, bf16[64,3584]{1,0:T(8,128)(2,1)S(1)} %collective-permute-done.6.refs_3_.refs_2_), custom_call_target="tpu_custom_call" | custom-call | flops 4294967296 | bytes 16777216 | tf_op jit(solution)/shard_map/sums_next/pallas_call | solution.py:129
  38.8 0.3 fold.3
  39.1 1.8 %collective-permute-start.9 = (s16[128,2176]{1,0:T(8,128)(2,1)S(1)}, s16[128,2176]{1,0:T(8,128)(2,1)S(1)}, u32[]{:S(2)}, u32[]{:S(2)}) collective-permute-start(s16[128,2176]{1,0:T(8,128)(2,1)S(1)} %get-tuple-element.25), channel_id=1, source_target_pairs={{0,8},{8,0},{16,24},{24,16},{1,9},{9,1},{17,25},{25,17},{2,10},{10... | collective-permute-start | bytes 1671176 | tf_op jit(solution)/shard_map/ppermute | solution.py:258
  40.9 3.6 %sums_next.2 = (f32[128,512]{1,0:T(8,128)S(1)}, s16[128,640]{1,0:T(8,128)(2,1)S(1)}) custom-call(bf16[256,4096]{1,0:T(8,128)(2,1)S(1)} %get-tuple-element.17.refs_1_.refs_0_.aligned_ref, bf16[3584,4096]{1,0:T(8,128)(2,1)} %refs_2_.3, bf16[3584,4096]{1,0:T(8,128)(2,1)} %refs_2_.3), custom_call_target="tpu_custom_call" | custom-call | flops 1073741824 | bytes 4194304 | tf_op jit(solution)/shard_map/sums_next/pallas_call | solution.py:129
  44.5 1.2 %collective-permute-start.10 = (s16[64,1152]{1,0:T(8,128)(2,1)S(1)}, s16[64,1152]{1,0:T(8,128)(2,1)S(1)}, u32[]{:S(2)}, u32[]{:S(2)}) collective-permute-start(s16[64,1152]{1,0:T(8,128)(2,1)S(1)} %get-tuple-element.22.refs_5_), channel_id=1, source_target_pairs={{0,16},{8,24},{16,0},{24,8},{1,17},{9,25},{17,1},{25,9},{2,18},{10... | collective-permute-start | bytes 442376 | tf_op jit(solution)/shard_map/ppermute | solution.py:258
  45.7 1.9 %collective-permute-done.7.refs_3_ = bf16[64,3584]{1,0:T(8,128)(2,1)S(1)} collective-permute-done((bf16[64,3584]{1,0:T(8,128)(2,1)S(1)}, bf16[64,3584]{1,0:T(8,128)(2,1)S(1)}, u32[]{:S(2)}, u32[]{:S(2)}) %collective-permute-start.7) | collective-permute-done | bytes 458784 | tf_op jit(solution)/shard_map/ppermute | solution.py:258
  47.7 7.5 %weight_grads.2.refs_2_.refs_4_ = bf16[3584,4096]{1,0:T(8,128)(2,1)} custom-call(bf16[256,4096]{1,0:T(8,128)(2,1)S(1)} %get-tuple-element.17.refs_1_.refs_0_.aligned_ref, bf16[64,3584]{1,0:T(8,128)(2,1)S(1)} %copy-done, bf16[64,3584]{1,0:T(8,128)(2,1)S(1)} %handed_on.1.refs_1_, bf16[64,3584]{1,0:T(8,128)(2,1)S(1)} %collective-permute-done.6.refs_3_.refs_2_, ...), custom_call_target="tpu_custom_call" | custom-call | flops 4294967296 | bytes 16777216 | tf_op jit(solution)/shard_map/weight_grads/pallas_call | solution.py:179
  55.1 4.3 %collective-permute-done.10.refs_1_ = s16[64,1152]{1,0:T(8,128)(2,1)S(1)} collective-permute-done((s16[64,1152]{1,0:T(8,128)(2,1)S(1)}, s16[64,1152]{1,0:T(8,128)(2,1)S(1)}, u32[]{:S(2)}, u32[]{:S(2)}) %collective-permute-start.10) | collective-permute-done | bytes 147488 | tf_op jit(solution)/shard_map/ppermute | solution.py:258
  59.5 1.0 %collective-permute-done.9.got_ref = s16[128,2176]{1,0:T(8,128)(2,1)S(1)} collective-permute-done((s16[128,2176]{1,0:T(8,128)(2,1)S(1)}, s16[128,2176]{1,0:T(8,128)(2,1)S(1)}, u32[]{:S(2)}, u32[]{:S(2)}) %collective-permute-start.9) | collective-permute-done | bytes 557088 | tf_op jit(solution)/shard_map/ppermute | solution.py:258
  60.5 0.8 fold.4
  61.3 2.5 %collective-permute-start.11 = (s16[128,640]{1,0:T(8,128)(2,1)S(1)}, s16[128,640]{1,0:T(8,128)(2,1)S(1)}, u32[]{:S(2)}, u32[]{:S(2)}) collective-permute-start(s16[128,640]{1,0:T(8,128)(2,1)S(1)} %get-tuple-element.26), channel_id=1, source_target_pairs={{0,8},{8,0},{16,24},{24,16},{1,9},{9,1},{17,25},{25,17},{2,10},{10... | collective-permute-start | bytes 491528 | tf_op jit(solution)/shard_map/ppermute | solution.py:258
  63.8 1.6 %collective-permute-start.12 = (s16[64,2176]{1,0:T(8,128)(2,1)S(1)}, s16[64,2176]{1,0:T(8,128)(2,1)S(1)}, u32[]{:S(2)}, u32[]{:S(2)}) collective-permute-start(s16[64,2176]{1,0:T(8,128)(2,1)S(1)} %get-tuple-element.30), channel_id=1, source_target_pairs={{0,16},{8,24},{16,0},{24,8},{1,17},{9,25},{17,1},{25,9},{2,18},{10... | collective-permute-start | bytes 835592 | tf_op jit(solution)/shard_map/ppermute | solution.py:258
  65.4 3.7 %collective-permute-done.11.got_ref = s16[128,640]{1,0:T(8,128)(2,1)S(1)} collective-permute-done((s16[128,640]{1,0:T(8,128)(2,1)S(1)}, s16[128,640]{1,0:T(8,128)(2,1)S(1)}, u32[]{:S(2)}, u32[]{:S(2)}) %collective-permute-start.11) | collective-permute-done | bytes 163872 | tf_op jit(solution)/shard_map/ppermute | solution.py:258
  69.1 0.2 fold.5
  69.3 2.6 %collective-permute-start.13 = (s16[64,640]{1,0:T(8,128)(2,1)S(1)}, s16[64,640]{1,0:T(8,128)(2,1)S(1)}, u32[]{:S(2)}, u32[]{:S(2)}) collective-permute-start(s16[64,640]{1,0:T(8,128)(2,1)S(1)} %get-tuple-element.27.refs_5_), channel_id=1, source_target_pairs={{0,16},{8,24},{16,0},{24,8},{1,17},{9,25},{17,1},{25,9},{2,18},{10... | collective-permute-start | bytes 245768 | tf_op jit(solution)/shard_map/ppermute | solution.py:258
  72.0 5.9 %weight_grads.3.refs_6_ = bf16[3584,4096]{1,0:T(8,128)(2,1)} custom-call(bf16[256,4096]{1,0:T(8,128)(2,1)S(1)} %get-tuple-element.17.refs_1_.refs_0_.aligned_ref, bf16[64,3584]{1,0:T(8,128)(2,1)S(1)} %copy-done, bf16[64,3584]{1,0:T(8,128)(2,1)S(1)} %handed_on.1.refs_1_, ...), custom_call_target="tpu_custom_call", output_to_operand_aliasing={{}: (5, {})} | custom-call | flops 3221225472 | bytes 12582912 | tf_op jit(solution)/shard_map/weight_grads/pallas_call | solution.py:179
  77.9 3.8 %collective-permute-done.13.refs_5_ = s16[64,640]{1,0:T(8,128)(2,1)S(1)} collective-permute-done((s16[64,640]{1,0:T(8,128)(2,1)S(1)}, s16[64,640]{1,0:T(8,128)(2,1)S(1)}, u32[]{:S(2)}, u32[]{:S(2)}) %collective-permute-start.13) | collective-permute-done | bytes 81952 | tf_op jit(solution)/shard_map/ppermute | solution.py:258
  81.8 1.0 %totals.1 = bf16[64,3584]{1,0:T(8,128)(2,1)} custom-call(f32[64,1024]{1,0:T(8,128)S(1)} %get-tuple-element.28.refs_0_, s16[64,1152]{1,0:T(8,128)(2,1)S(1)} %collective-permute-done.10.refs_1_, f32[64,2048]{1,0:T(8,128)S(1)} %get-tuple-element.29.refs_2_, s16[64,2176]{1,0:T(8,128)(2,1)S(1)} %collective-permute-done.12.refs_3_, ...), custom_call_target="tpu_custom_call" | custom-call | flops 9175040 | bytes 3211264 | tf_op jit(solution)/shard_map/totals/pallas_call | solution.py:249
  (19 shorter events, 0.6 us)
Async XLA Ops:
  0.6 10.6 %collective-permute-start = (bf16[32,4096]{1,0:T(8,128)(2,1)}, bf16[32,4096]{1,0:T(8,128)(2,1)S(1)}, u32[]{:S(2)}, u32[]{:S(2)}) collective-permute-start(bf16[32,4096]{1,0:T(8,128)(2,1)} %refs_0_.3), channel_id=1, source_target_pairs={{0,2},{1,3},{2,0},{3,1},{4,6},{5,7},{6,4},{7,5},{8,10},{9,11},{10,... | collective-permute-start | bytes 786440 | tf_op jit(solution)/shard_map/ppermute | solution.py:258
  3.6 13.4 %collective-permute-start.2 = (bf16[32,4096]{1,0:T(8,128)(2,1)}, bf16[32,4096]{1,0:T(8,128)(2,1)S(1)}, u32[]{:S(2)}, u32[]{:S(2)}) collective-permute-start(bf16[32,4096]{1,0:T(8,128)(2,1)} %refs_0_.3), channel_id=1, source_target_pairs={{0,6},{1,7},{2,4},{3,5},{4,2},{5,3},{6,0},{7,1},{8,14},{9,15},{10,... | collective-permute-start | bytes 786440 | tf_op jit(solution)/shard_map/ppermute | solution.py:258
  5.1 13.3 %collective-permute-start.1 = (bf16[32,4096]{1,0:T(8,128)(2,1)}, bf16[32,4096]{1,0:T(8,128)(2,1)S(1)}, u32[]{:S(2)}, u32[]{:S(2)}) collective-permute-start(bf16[32,4096]{1,0:T(8,128)(2,1)} %refs_0_.3), channel_id=1, source_target_pairs={{0,4},{1,5},{2,6},{3,7},{4,0},{5,1},{6,2},{7,3},{8,12},{9,13},{10,... | collective-permute-start | bytes 786440 | tf_op jit(solution)/shard_map/ppermute | solution.py:258
  5.2 24.6 %collective-permute-start.6 = (bf16[64,3584]{1,0:T(8,128)(2,1)}, bf16[64,3584]{1,0:T(8,128)(2,1)S(1)}, u32[]{:S(2)}, u32[]{:S(2)}) collective-permute-start(bf16[64,3584]{1,0:T(8,128)(2,1)} %refs_0_.5), channel_id=1, source_target_pairs={{0,8},{8,0},{16,24},{24,16},{1,9},{9,1},{17,25},{25,17},{2,10},{10... | collective-permute-start | bytes 1376264 | tf_op jit(solution)/shard_map/ppermute | solution.py:258
  7.2 22.2 %collective-permute-start.5 = (bf16[64,3584]{1,0:T(8,128)(2,1)}, bf16[64,3584]{1,0:T(8,128)(2,1)S(1)}, u32[]{:S(2)}, u32[]{:S(2)}) collective-permute-start(bf16[64,3584]{1,0:T(8,128)(2,1)} %refs_0_.5), channel_id=1, source_target_pairs={{0,16},{8,24},{16,0},{24,8},{1,17},{9,25},{17,1},{25,9},{2,18},{10... | collective-permute-start | bytes 1376264 | tf_op jit(solution)/shard_map/ppermute | solution.py:258
  11.2 1.0 %copy-start.1 = (bf16[32,4096]{1,0:T(8,128)(2,1)S(1)}, bf16[32,4096]{1,0:T(8,128)(2,1)}, u32[]{:S(2)}) copy-start(bf16[32,4096]{1,0:T(8,128)(2,1)} %refs_0_.3) | copy-start | bytes 786436
  12.2 8.2 %collective-permute-start.3 = (bf16[64,4096]{1,0:T(8,128)(2,1)S(1)}, bf16[64,4096]{1,0:T(8,128)(2,1)S(1)}, u32[]{:S(2)}, u32[]{:S(2)}) collective-permute-start(bf16[64,4096]{1,0:T(8,128)(2,1)S(1)} %stacked.2.refs_2_.refs_1_), channel_id=1, source_target_pairs={{0,1},{1,0},{2,3},{3,2},{4,5},{5,4},{6,7},{7,6},{8,9},{9,8},{10,11... | collective-permute-start | bytes 1572872 | tf_op jit(solution)/shard_map/ppermute | solution.py:258
  18.5 2.0 %collective-permute-start.4 = (bf16[64,4096]{1,0:T(8,128)(2,1)S(1)}, bf16[64,4096]{1,0:T(8,128)(2,1)S(1)}, u32[]{:S(2)}, u32[]{:S(2)}) collective-permute-start(bf16[64,4096]{1,0:T(8,128)(2,1)S(1)} %stacked.3.refs_2_), channel_id=1, source_target_pairs={{0,1},{1,0},{2,3},{3,2},{4,5},{5,4},{6,7},{7,6},{8,9},{9,8},{10,11... | collective-permute-start | bytes 1572872 | tf_op jit(solution)/shard_map/ppermute | solution.py:258
  26.3 12.4 %collective-permute-start.8 = (s16[128,1152]{1,0:T(8,128)(2,1)S(1)}, s16[128,1152]{1,0:T(8,128)(2,1)S(1)}, u32[]{:S(2)}, u32[]{:S(2)}) collective-permute-start(s16[128,1152]{1,0:T(8,128)(2,1)S(1)} %get-tuple-element.20), channel_id=1, source_target_pairs={{0,8},{8,0},{16,24},{24,16},{1,9},{9,1},{17,25},{25,17},{2,10},{10... | collective-permute-start | bytes 884744 | tf_op jit(solution)/shard_map/ppermute | solution.py:258
  29.5 18.2 %collective-permute-start.7 = (bf16[64,3584]{1,0:T(8,128)(2,1)S(1)}, bf16[64,3584]{1,0:T(8,128)(2,1)S(1)}, u32[]{:S(2)}, u32[]{:S(2)}) collective-permute-start(bf16[64,3584]{1,0:T(8,128)(2,1)S(1)} %handed_on.1.refs_1_), channel_id=1, source_target_pairs={{0,8},{8,0},{16,24},{24,16},{1,9},{9,1},{17,25},{25,17},{2,10},{10... | collective-permute-start | bytes 1376264 | tf_op jit(solution)/shard_map/ppermute | solution.py:258
  39.1 8.5 %copy-start = (bf16[64,3584]{1,0:T(8,128)(2,1)S(1)}, bf16[64,3584]{1,0:T(8,128)(2,1)}, u32[]{:S(2)}) copy-start(bf16[64,3584]{1,0:T(8,128)(2,1)} %refs_0_.5) | copy-start | bytes 1376260
  39.1 21.4 %collective-permute-start.9 = (s16[128,2176]{1,0:T(8,128)(2,1)S(1)}, s16[128,2176]{1,0:T(8,128)(2,1)S(1)}, u32[]{:S(2)}, u32[]{:S(2)}) collective-permute-start(s16[128,2176]{1,0:T(8,128)(2,1)S(1)} %get-tuple-element.25), channel_id=1, source_target_pairs={{0,8},{8,0},{16,24},{24,16},{1,9},{9,1},{17,25},{25,17},{2,10},{10... | collective-permute-start | bytes 1671176 | tf_op jit(solution)/shard_map/ppermute | solution.py:258
  44.5 14.9 %collective-permute-start.10 = (s16[64,1152]{1,0:T(8,128)(2,1)S(1)}, s16[64,1152]{1,0:T(8,128)(2,1)S(1)}, u32[]{:S(2)}, u32[]{:S(2)}) collective-permute-start(s16[64,1152]{1,0:T(8,128)(2,1)S(1)} %get-tuple-element.22.refs_5_), channel_id=1, source_target_pairs={{0,16},{8,24},{16,0},{24,8},{1,17},{9,25},{17,1},{25,9},{2,18},{10... | collective-permute-start | bytes 442376 | tf_op jit(solution)/shard_map/ppermute | solution.py:258
  61.3 7.8 %collective-permute-start.11 = (s16[128,640]{1,0:T(8,128)(2,1)S(1)}, s16[128,640]{1,0:T(8,128)(2,1)S(1)}, u32[]{:S(2)}, u32[]{:S(2)}) collective-permute-start(s16[128,640]{1,0:T(8,128)(2,1)S(1)} %get-tuple-element.26), channel_id=1, source_target_pairs={{0,8},{8,0},{16,24},{24,16},{1,9},{9,1},{17,25},{25,17},{2,10},{10... | collective-permute-start | bytes 491528 | tf_op jit(solution)/shard_map/ppermute | solution.py:258
  63.8 18.0 %collective-permute-start.12 = (s16[64,2176]{1,0:T(8,128)(2,1)S(1)}, s16[64,2176]{1,0:T(8,128)(2,1)S(1)}, u32[]{:S(2)}, u32[]{:S(2)}) collective-permute-start(s16[64,2176]{1,0:T(8,128)(2,1)S(1)} %get-tuple-element.30), channel_id=1, source_target_pairs={{0,16},{8,24},{16,0},{24,8},{1,17},{9,25},{17,1},{25,9},{2,18},{10... | collective-permute-start | bytes 835592 | tf_op jit(solution)/shard_map/ppermute | solution.py:258
  69.3 12.4 %collective-permute-start.13 = (s16[64,640]{1,0:T(8,128)(2,1)S(1)}, s16[64,640]{1,0:T(8,128)(2,1)S(1)}, u32[]{:S(2)}, u32[]{:S(2)}) collective-permute-start(s16[64,640]{1,0:T(8,128)(2,1)S(1)} %get-tuple-element.27.refs_5_), channel_id=1, source_target_pairs={{0,16},{8,24},{16,0},{24,8},{1,17},{9,25},{17,1},{25,9},{2,18},{10... | collective-permute-start | bytes 245768 | tf_op jit(solution)/shard_map/ppermute | solution.py:258

commit v11 on v8

--- a/solution.py
+++ b/solution.py
@@ -342,15 +342,15 @@
     aligned, [kept], [sent] = partial_sums(
         None, (pick, pieces), down_weight, tile, *parts[0], kept_rows, sent_rows, [], "sums_first")
     got = send(sent, "row", 1, n_row)
-    evens = range(2, n_row, 2)
-    for o, piece in zip(evens, handed_on([act_pieces[o] for o in evens], [aligned])):
-        act_pieces[o], act_pieces[o + 1] = piece, send(piece, "row", 1, n_row)
-
     done, crossed = [], []
     for at, part in enumerate(parts[1:]):
         _, [next_kept], [sent] = partial_sums(
             aligned, None, down_weight, tile, *part, kept_rows, sent_rows, [act_pieces[1]] if at == 0 else [], "sums_next")
         ended, crossed, [sent] = halved(kept, got, [sent], n_row)
+        if at == 0:
+            evens = range(2, n_row, 2)
+            for o, piece in zip(evens, handed_on([act_pieces[o] for o in evens], crossed)):
+                act_pieces[o], act_pieces[o + 1] = piece, send(piece, "row", 1, n_row)
         done.append(ended)
         kept, got = next_kept, send(sent, "row", 1, n_row)
 

time: 79.7 us -> 81.5 us (1.023)
  starting transfers between devices: 20.6 us -> 21.7 us
    ppermute x14, starting transfers between devices: 20.6 us -> 21.7 us  [send(): return lax.ppermute(value, axis, [(i, i ^ flip) for i in range(size)])]
  transfers between devices with their start and end apart: 14 -> 14, of which waited for: 6 -> 6; matrix products, arithmetic and copies ran while one was open for 2% -> 2% of each run, Pallas kernels for 42% -> 41%
where the time goes in v11:
time: 81.5 us; the launch traced here: 81.2 us
  Pallas kernels  34.1 us (42%)
  waiting for transfers between devices  21.9 us (27%)
  starting transfers between devices  21.7 us (27%)
  local copies, waits for them, and re-layouts  1.8 us (2%)
  other arithmetic  0.91 us (1%)
    ppermute x14, waiting for transfers between devices, send(): return lax.ppermute(value, axis, [(i, i ^ flip) for i in range(size)])  21.9 us
    ppermute x14, starting transfers between devices, send(): return lax.ppermute(value, axis, [(i, i ^ flip) for i in range(size)])  21.7 us
    pallas_call x3, Pallas kernels, partial_sums(): pl.pallas_call(functools.partial(sums_kernel, 0 if aligned is not None el...  18.4 us
    pallas_call x2, Pallas kernels, weight_grads(): pl.pallas_call(functools.partial(weight_kernel, len(pieces), first, len(l...  13.4 us
  transfers between devices with their start and end apart: 14, of which 6 were waited for; matrix products, arithmetic and copies ran while one was open for 2% of the time, Pallas kernels for 41%

profile of v11, /device:TPU:0, one launch (start us, length us, event | category | flops | bytes accessed | tf_op | source)
XLA Modules:
  0.0 81.2 jit_solution(5215847041719507763)
XLA Ops:
  0.6 3.0 %collective-permute-start = (bf16[32,4096]{1,0:T(8,128)(2,1)}, bf16[32,4096]{1,0:T(8,128)(2,1)S(1)}, u32[]{:S(2)}, u32[]{:S(2)}) collective-permute-start(bf16[32,4096]{1,0:T(8,128)(2,1)} %refs_0_.3), channel_id=1, source_target_pairs={{0,2},{1,3},{2,0},{3,1},{4,6},{5,7},{6,4},{7,5},{8,10},{9,11},{10,... | collective-permute-start | bytes 786440 | tf_op jit(solution)/shard_map/ppermute | solution.py:257
  3.6 1.5 %collective-permute-start.1 = (bf16[32,4096]{1,0:T(8,128)(2,1)}, bf16[32,4096]{1,0:T(8,128)(2,1)S(1)}, u32[]{:S(2)}, u32[]{:S(2)}) collective-permute-start(bf16[32,4096]{1,0:T(8,128)(2,1)} %refs_0_.3), channel_id=1, source_target_pairs={{0,4},{1,5},{2,6},{3,7},{4,0},{5,1},{6,2},{7,3},{8,12},{9,13},{10,... | collective-permute-start | bytes 786440 | tf_op jit(solution)/shard_map/ppermute | solution.py:257
  5.2 2.0 %collective-permute-start.7 = (bf16[64,3584]{1,0:T(8,128)(2,1)}, bf16[64,3584]{1,0:T(8,128)(2,1)S(1)}, u32[]{:S(2)}, u32[]{:S(2)}) collective-permute-start(bf16[64,3584]{1,0:T(8,128)(2,1)} %refs_0_.5), channel_id=1, source_target_pairs={{0,8},{8,0},{16,24},{24,16},{1,9},{9,1},{17,25},{25,17},{2,10},{10... | collective-permute-start | bytes 1376264 | tf_op jit(solution)/shard_map/ppermute | solution.py:257
  7.2 2.6 %collective-permute-start.5 = (bf16[64,3584]{1,0:T(8,128)(2,1)}, bf16[64,3584]{1,0:T(8,128)(2,1)S(1)}, u32[]{:S(2)}, u32[]{:S(2)}) collective-permute-start(bf16[64,3584]{1,0:T(8,128)(2,1)} %refs_0_.5), channel_id=1, source_target_pairs={{0,16},{8,24},{16,0},{24,8},{1,17},{9,25},{17,1},{25,9},{2,18},{10... | collective-permute-start | bytes 1376264 | tf_op jit(solution)/shard_map/ppermute | solution.py:257
  9.8 0.8 reshape.24
  10.6 0.7 xor_multiply_fusion
  11.2 0.9 %copy-done.1 = bf16[32,4096]{1,0:T(8,128)(2,1)S(1)} copy-done((bf16[32,4096]{1,0:T(8,128)(2,1)S(1)}, bf16[32,4096]{1,0:T(8,128)(2,1)}, u32[]{:S(2)}) %copy-start.1) | copy-done | bytes 262168
  12.2 0.1 collective-permute-start.3
  12.3 4.9 %collective-permute-done.1.refs_0_ = bf16[32,4096]{1,0:T(8,128)(2,1)S(1)} collective-permute-done((bf16[32,4096]{1,0:T(8,128)(2,1)}, bf16[32,4096]{1,0:T(8,128)(2,1)S(1)}, u32[]{:S(2)}, u32[]{:S(2)}) %collective-permute-start.1) | collective-permute-done | bytes 262176 | tf_op jit(solution)/shard_map/ppermute | solution.py:257
  17.4 0.1 pad_add_fusion
  17.5 0.1 add.40
  17.6 0.1 compare_convert_fusion.refs_0_
  17.7 1.6 %collective-permute-done.4.refs_4_ = bf16[64,4096]{1,0:T(8,128)(2,1)S(1)} collective-permute-done((bf16[64,4096]{1,0:T(8,128)(2,1)S(1)}, bf16[64,4096]{1,0:T(8,128)(2,1)S(1)}, u32[]{:S(2)}, u32[]{:S(2)}) %collective-permute-start.4) | collective-permute-done | bytes 524320 | tf_op jit(solution)/shard_map/ppermute | solution.py:257
  19.2 5.9 %sums_first.1 = (bf16[256,4096]{1,0:T(8,128)(2,1)S(1)}, f32[128,1024]{1,0:T(8,128)S(1)}, s16[128,1152]{1,0:T(8,128)(2,1)S(1)}) custom-call(bf16[256,256]{1,0:T(8,128)(2,1)S(1)} %compare_convert_fusion.refs_0_, bf16[64,4096]{1,0:T(8,128)(2,1)S(1)} %stacked.2.refs_2_.refs_1_, bf16[64,4096]{1,0:T(8,128)(2,1)S(1)} %stacked.3.refs_2_, ...), custom_call_target="tpu_custom_call" | custom-call | flops 2147483648 | bytes 8388608 | tf_op jit(solution)/shard_map/sums_first/pallas_call | solution.py:128
  25.1 1.6 %collective-permute-start.6 = (s16[128,1152]{1,0:T(8,128)(2,1)S(1)}, s16[128,1152]{1,0:T(8,128)(2,1)S(1)}, u32[]{:S(2)}, u32[]{:S(2)}) collective-permute-start(s16[128,1152]{1,0:T(8,128)(2,1)S(1)} %get-tuple-element.19), channel_id=1, source_target_pairs={{0,8},{8,0},{16,24},{24,16},{1,9},{9,1},{17,25},{25,17},{2,10},{10... | collective-permute-start | bytes 884744 | tf_op jit(solution)/shard_map/ppermute | solution.py:257
  26.8 7.4 %sums_next.2 = (f32[128,1536]{1,0:T(8,128)S(1)}, s16[128,1664]{1,0:T(8,128)(2,1)S(1)}) custom-call(bf16[256,4096]{1,0:T(8,128)(2,1)S(1)} %get-tuple-element.17.refs_0_.aligned_ref, bf16[3584,4096]{1,0:T(8,128)(2,1)} %refs_2_.3, bf16[3584,4096]{1,0:T(8,128)(2,1)} %refs_2_.3, bf16[64,3584]{1,0:T(8,128)(2,1)S(1)} %collective-permute-done.7.refs_3_.refs_2_), custom_call_target="tpu_custom_call" | custom-call | flops 3221225472 | bytes 12582912 | tf_op jit(solution)/shard_map/sums_next/pallas_call | solution.py:128
  34.2 0.2 collective-permute-done.6.got_ref
  34.4 0.3 fold.3
  34.7 1.5 %collective-permute-start.8 = (bf16[64,3584]{1,0:T(8,128)(2,1)S(1)}, bf16[64,3584]{1,0:T(8,128)(2,1)S(1)}, u32[]{:S(2)}, u32[]{:S(2)}) collective-permute-start(bf16[64,3584]{1,0:T(8,128)(2,1)S(1)} %handed_on.1.refs_1_), channel_id=1, source_target_pairs={{0,8},{8,0},{16,24},{24,16},{1,9},{9,1},{17,25},{25,17},{2,10},{10... | collective-permute-start | bytes 1376264 | tf_op jit(solution)/shard_map/ppermute | solution.py:257
  36.3 0.6 collective-permute-start.9
  36.8 5.1 %sums_next.3 = (f32[128,1024]{1,0:T(8,128)S(1)}, s16[128,1152]{1,0:T(8,128)(2,1)S(1)}) custom-call(bf16[256,4096]{1,0:T(8,128)(2,1)S(1)} %get-tuple-element.17.refs_0_.aligned_ref, bf16[3584,4096]{1,0:T(8,128)(2,1)} %refs_2_.3, bf16[3584,4096]{1,0:T(8,128)(2,1)} %refs_2_.3), custom_call_target="tpu_custom_call" | custom-call | flops 2147483648 | bytes 8388608 | tf_op jit(solution)/shard_map/sums_next/pallas_call | solution.py:128
  42.0 2.5 %collective-permute-start.11 = (s16[64,1152]{1,0:T(8,128)(2,1)S(1)}, s16[64,1152]{1,0:T(8,128)(2,1)S(1)}, u32[]{:S(2)}, u32[]{:S(2)}) collective-permute-start(s16[64,1152]{1,0:T(8,128)(2,1)S(1)} %get-tuple-element.21.refs_1_), channel_id=1, source_target_pairs={{0,16},{8,24},{16,0},{24,8},{1,17},{9,25},{17,1},{25,9},{2,18},{10... | collective-permute-start | bytes 442376 | tf_op jit(solution)/shard_map/ppermute | solution.py:257
  44.5 14.6 %collective-permute-done.9.got_ref = s16[128,1664]{1,0:T(8,128)(2,1)S(1)} collective-permute-done((s16[128,1664]{1,0:T(8,128)(2,1)S(1)}, s16[128,1664]{1,0:T(8,128)(2,1)S(1)}, u32[]{:S(2)}, u32[]{:S(2)}) %collective-permute-start.9) | collective-permute-done | bytes 426016 | tf_op jit(solution)/shard_map/ppermute | solution.py:257
  59.2 0.6 fold.4
  59.8 4.3 %collective-permute-start.12 = (s16[64,1664]{1,0:T(8,128)(2,1)S(1)}, s16[64,1664]{1,0:T(8,128)(2,1)S(1)}, u32[]{:S(2)}, u32[]{:S(2)}) collective-permute-start(s16[64,1664]{1,0:T(8,128)(2,1)S(1)} %get-tuple-element.25.refs_4_), channel_id=1, source_target_pairs={{0,16},{8,24},{16,0},{24,8},{1,17},{9,25},{17,1},{25,9},{2,18},{10... | collective-permute-start | bytes 638984 | tf_op jit(solution)/shard_map/ppermute | solution.py:257
  64.1 7.5 %weight_grads.2.refs_4_ = bf16[3584,4096]{1,0:T(8,128)(2,1)} custom-call(bf16[256,4096]{1,0:T(8,128)(2,1)S(1)} %get-tuple-element.17.refs_0_.aligned_ref, bf16[64,3584]{1,0:T(8,128)(2,1)S(1)} %copy-done, bf16[64,3584]{1,0:T(8,128)(2,1)S(1)} %handed_on.1.refs_1_, bf16[64,3584]{1,0:T(8,128)(2,1)S(1)} %collective-permute-done.7.refs_3_.refs_2_, ...), custom_call_target="tpu_custom_call" | custom-call | flops 4294967296 | bytes 16777216 | tf_op jit(solution)/shard_map/weight_grads/pallas_call | solution.py:178
  71.5 0.4 collective-permute-done.10.got_ref
  72.0 0.3 fold.5
  72.3 1.8 %collective-permute-start.13 = (s16[64,1152]{1,0:T(8,128)(2,1)S(1)}, s16[64,1152]{1,0:T(8,128)(2,1)S(1)}, u32[]{:S(2)}, u32[]{:S(2)}) collective-permute-start(s16[64,1152]{1,0:T(8,128)(2,1)S(1)} %get-tuple-element.28.refs_5_), channel_id=1, source_target_pairs={{0,16},{8,24},{16,0},{24,8},{1,17},{9,25},{17,1},{25,9},{2,18},{10... | collective-permute-start | bytes 442376 | tf_op jit(solution)/shard_map/ppermute | solution.py:257
  74.2 5.9 %weight_grads.3.refs_6_ = bf16[3584,4096]{1,0:T(8,128)(2,1)} custom-call(bf16[256,4096]{1,0:T(8,128)(2,1)S(1)} %get-tuple-element.17.refs_0_.aligned_ref, bf16[64,3584]{1,0:T(8,128)(2,1)S(1)} %copy-done, bf16[64,3584]{1,0:T(8,128)(2,1)S(1)} %handed_on.1.refs_1_, ...), custom_call_target="tpu_custom_call", output_to_operand_aliasing={{}: (5, {})} | custom-call | flops 3221225472 | bytes 12582912 | tf_op jit(solution)/shard_map/weight_grads/pallas_call | solution.py:178
  80.1 0.1 collective-permute-done.13.refs_5_
  80.2 1.0 %totals.1 = bf16[64,3584]{1,0:T(8,128)(2,1)} custom-call(f32[64,1024]{1,0:T(8,128)S(1)} %get-tuple-element.29.refs_0_, s16[64,1152]{1,0:T(8,128)(2,1)S(1)} %collective-permute-done.11.refs_1_, f32[64,1536]{1,0:T(8,128)S(1)} %get-tuple-element.30.refs_2_, s16[64,1664]{1,0:T(8,128)(2,1)S(1)} %collective-permute-done.12.refs_3_, ...), custom_call_target="tpu_custom_call" | custom-call | flops 9175040 | bytes 3211264 | tf_op jit(solution)/shard_map/totals/pallas_call | solution.py:248
  (19 shorter events, 0.4 us)
Async XLA Ops:
  0.6 10.6 %collective-permute-start = (bf16[32,4096]{1,0:T(8,128)(2,1)}, bf16[32,4096]{1,0:T(8,128)(2,1)S(1)}, u32[]{:S(2)}, u32[]{:S(2)}) collective-permute-start(bf16[32,4096]{1,0:T(8,128)(2,1)} %refs_0_.3), channel_id=1, source_target_pairs={{0,2},{1,3},{2,0},{3,1},{4,6},{5,7},{6,4},{7,5},{8,10},{9,11},{10,... | collective-permute-start | bytes 786440 | tf_op jit(solution)/shard_map/ppermute | solution.py:257
  3.6 13.6 %collective-permute-start.1 = (bf16[32,4096]{1,0:T(8,128)(2,1)}, bf16[32,4096]{1,0:T(8,128)(2,1)S(1)}, u32[]{:S(2)}, u32[]{:S(2)}) collective-permute-start(bf16[32,4096]{1,0:T(8,128)(2,1)} %refs_0_.3), channel_id=1, source_target_pairs={{0,4},{1,5},{2,6},{3,7},{4,0},{5,1},{6,2},{7,3},{8,12},{9,13},{10,... | collective-permute-start | bytes 786440 | tf_op jit(solution)/shard_map/ppermute | solution.py:257
  5.2 12.1 %collective-permute-start.2 = (bf16[32,4096]{1,0:T(8,128)(2,1)}, bf16[32,4096]{1,0:T(8,128)(2,1)S(1)}, u32[]{:S(2)}, u32[]{:S(2)}) collective-permute-start(bf16[32,4096]{1,0:T(8,128)(2,1)} %refs_0_.3), channel_id=1, source_target_pairs={{0,6},{1,7},{2,4},{3,5},{4,2},{5,3},{6,0},{7,1},{8,14},{9,15},{10,... | collective-permute-start | bytes 786440 | tf_op jit(solution)/shard_map/ppermute | solution.py:257
  5.2 21.6 %collective-permute-start.7 = (bf16[64,3584]{1,0:T(8,128)(2,1)}, bf16[64,3584]{1,0:T(8,128)(2,1)S(1)}, u32[]{:S(2)}, u32[]{:S(2)}) collective-permute-start(bf16[64,3584]{1,0:T(8,128)(2,1)} %refs_0_.5), channel_id=1, source_target_pairs={{0,8},{8,0},{16,24},{24,16},{1,9},{9,1},{17,25},{25,17},{2,10},{10... | collective-permute-start | bytes 1376264 | tf_op jit(solution)/shard_map/ppermute | solution.py:257
  7.2 27.5 %collective-permute-start.5 = (bf16[64,3584]{1,0:T(8,128)(2,1)}, bf16[64,3584]{1,0:T(8,128)(2,1)S(1)}, u32[]{:S(2)}, u32[]{:S(2)}) collective-permute-start(bf16[64,3584]{1,0:T(8,128)(2,1)} %refs_0_.5), channel_id=1, source_target_pairs={{0,16},{8,24},{16,0},{24,8},{1,17},{9,25},{17,1},{25,9},{2,18},{10... | collective-permute-start | bytes 1376264 | tf_op jit(solution)/shard_map/ppermute | solution.py:257
  11.2 1.0 %copy-start.1 = (bf16[32,4096]{1,0:T(8,128)(2,1)S(1)}, bf16[32,4096]{1,0:T(8,128)(2,1)}, u32[]{:S(2)}) copy-start(bf16[32,4096]{1,0:T(8,128)(2,1)} %refs_0_.3) | copy-start | bytes 786436
  12.2 7.0 %collective-permute-start.3 = (bf16[64,4096]{1,0:T(8,128)(2,1)S(1)}, bf16[64,4096]{1,0:T(8,128)(2,1)S(1)}, u32[]{:S(2)}, u32[]{:S(2)}) collective-permute-start(bf16[64,4096]{1,0:T(8,128)(2,1)S(1)} %stacked.2.refs_2_.refs_1_), channel_id=1, source_target_pairs={{0,1},{1,0},{2,3},{3,2},{4,5},{5,4},{6,7},{7,6},{8,9},{9,8},{10,11... | collective-permute-start | bytes 1572872 | tf_op jit(solution)/shard_map/ppermute | solution.py:257
  17.3 2.0 %collective-permute-start.4 = (bf16[64,4096]{1,0:T(8,128)(2,1)S(1)}, bf16[64,4096]{1,0:T(8,128)(2,1)S(1)}, u32[]{:S(2)}, u32[]{:S(2)}) collective-permute-start(bf16[64,4096]{1,0:T(8,128)(2,1)S(1)} %stacked.3.refs_2_), channel_id=1, source_target_pairs={{0,1},{1,0},{2,3},{3,2},{4,5},{5,4},{6,7},{7,6},{8,9},{9,8},{10,11... | collective-permute-start | bytes 1572872 | tf_op jit(solution)/shard_map/ppermute | solution.py:257
  25.1 9.2 %collective-permute-start.6 = (s16[128,1152]{1,0:T(8,128)(2,1)S(1)}, s16[128,1152]{1,0:T(8,128)(2,1)S(1)}, u32[]{:S(2)}, u32[]{:S(2)}) collective-permute-start(s16[128,1152]{1,0:T(8,128)(2,1)S(1)} %get-tuple-element.19), channel_id=1, source_target_pairs={{0,8},{8,0},{16,24},{24,16},{1,9},{9,1},{17,25},{25,17},{2,10},{10... | collective-permute-start | bytes 884744 | tf_op jit(solution)/shard_map/ppermute | solution.py:257
  34.7 29.3 %collective-permute-start.8 = (bf16[64,3584]{1,0:T(8,128)(2,1)S(1)}, bf16[64,3584]{1,0:T(8,128)(2,1)S(1)}, u32[]{:S(2)}, u32[]{:S(2)}) collective-permute-start(bf16[64,3584]{1,0:T(8,128)(2,1)S(1)} %handed_on.1.refs_1_), channel_id=1, source_target_pairs={{0,8},{8,0},{16,24},{24,16},{1,9},{9,1},{17,25},{25,17},{2,10},{10... | collective-permute-start | bytes 1376264 | tf_op jit(solution)/shard_map/ppermute | solution.py:257
  36.3 27.8 %copy-start = (bf16[64,3584]{1,0:T(8,128)(2,1)S(1)}, bf16[64,3584]{1,0:T(8,128)(2,1)}, u32[]{:S(2)}) copy-start(bf16[64,3584]{1,0:T(8,128)(2,1)} %refs_0_.5) | copy-start | bytes 1376260
  36.3 22.9 %collective-permute-start.9 = (s16[128,1664]{1,0:T(8,128)(2,1)S(1)}, s16[128,1664]{1,0:T(8,128)(2,1)S(1)}, u32[]{:S(2)}, u32[]{:S(2)}) collective-permute-start(s16[128,1664]{1,0:T(8,128)(2,1)S(1)} %get-tuple-element.23), channel_id=1, source_target_pairs={{0,8},{8,0},{16,24},{24,16},{1,9},{9,1},{17,25},{25,17},{2,10},{10... | collective-permute-start | bytes 1277960 | tf_op jit(solution)/shard_map/ppermute | solution.py:257
  42.0 38.1 %collective-permute-start.11 = (s16[64,1152]{1,0:T(8,128)(2,1)S(1)}, s16[64,1152]{1,0:T(8,128)(2,1)S(1)}, u32[]{:S(2)}, u32[]{:S(2)}) collective-permute-start(s16[64,1152]{1,0:T(8,128)(2,1)S(1)} %get-tuple-element.21.refs_1_), channel_id=1, source_target_pairs={{0,16},{8,24},{16,0},{24,8},{1,17},{9,25},{17,1},{25,9},{2,18},{10... | collective-permute-start | bytes 442376 | tf_op jit(solution)/shard_map/ppermute | solution.py:257
  59.7 12.3 %collective-permute-start.10 = (s16[128,1152]{1,0:T(8,128)(2,1)S(1)}, s16[128,1152]{1,0:T(8,128)(2,1)S(1)}, u32[]{:S(2)}, u32[]{:S(2)}) collective-permute-start(s16[128,1152]{1,0:T(8,128)(2,1)S(1)} %get-tuple-element.27), channel_id=1, source_target_pairs={{0,8},{8,0},{16,24},{24,16},{1,9},{9,1},{17,25},{25,17},{2,10},{10... | collective-permute-start | bytes 884744 | tf_op jit(solution)/shard_map/ppermute | solution.py:257
  59.8 20.3 %collective-permute-start.12 = (s16[64,1664]{1,0:T(8,128)(2,1)S(1)}, s16[64,1664]{1,0:T(8,128)(2,1)S(1)}, u32[]{:S(2)}, u32[]{:S(2)}) collective-permute-start(s16[64,1664]{1,0:T(8,128)(2,1)S(1)} %get-tuple-element.25.refs_4_), channel_id=1, source_target_pairs={{0,16},{8,24},{16,0},{24,8},{1,17},{9,25},{17,1},{25,9},{2,18},{10... | collective-permute-start | bytes 638984 | tf_op jit(solution)/shard_map/ppermute | solution.py:257
  72.3 7.9 %collective-permute-start.13 = (s16[64,1152]{1,0:T(8,128)(2,1)S(1)}, s16[64,1152]{1,0:T(8,128)(2,1)S(1)}, u32[]{:S(2)}, u32[]{:S(2)}) collective-permute-start(s16[64,1152]{1,0:T(8,128)(2,1)S(1)} %get-tuple-element.28.refs_5_), channel_id=1, source_target_pairs={{0,16},{8,24},{16,0},{24,8},{1,17},{9,25},{17,1},{25,9},{2,18},{10... | collective-permute-start | bytes 442376 | tf_op jit(solution)/shard_map/ppermute | solution.py:257

commit v12 on v10

--- a/solution.py
+++ b/solution.py
@@ -14,8 +14,7 @@
 VMEM_LIMIT = 48 * 1024 * 1024
 SMALL_LIMIT = 8 * 1024 * 1024
 SLOTS = 4
-SHARES = (2, 4, 1)
-GRAD_SHARES = (4, 3)
+SHARES = (2, 2, 3)
 SUB = 256
 
 
@@ -310,12 +309,12 @@
 
 
 def halved(kept, got, passed, later_than, n_row):
-    step, sent = 2, None
+    step = 2
     while step < n_row:
         kept, sent, passed = fold(kept, got, passed, later_than)
         got = send(sent, "row", step, n_row)
         step *= 2
-    return [kept, got], [sent] if sent is not None else [], passed
+    return [kept, got], [sent], passed
 
 
 def body(n_row, n_col, activations, cotangent, down_weight, row_order):
@@ -333,7 +332,7 @@
     named = (owner[:, None] * shard + jnp.arange(shard, dtype=jnp.int32)[None, :]).reshape(-1)
     pick = (order[:, None] == named[None, :]).astype(jnp.bfloat16)
 
-    tile = tile_of(hidden, SUB)
+    tile = tile_of(hidden, 256)
     parts = part_slices(hidden // tile, SHARES)
     pieces = gather_cotangent(cotangent, n_col)
     act_pieces = {o: send(activations, "row", o, n_row) for o in [1, *range(2, n_row, 2)]}
@@ -347,24 +346,23 @@
     for o, piece in zip(evens, handed_on([act_pieces[o] for o in evens], [aligned])):
         act_pieces[o], act_pieces[o + 1] = piece, send(piece, "row", 1, n_row)
 
+    _, [kept_b], [sent_b] = partial_sums(
+        aligned, None, down_weight, tile, *parts[1], kept_rows, sent_rows, [act_pieces[1]], "sums_second")
+    done_a, crossed, [sent_b] = halved(kept, got, [sent_b], [], n_row)
+    got_b = send(sent_b, "row", 1, n_row)
+
+    spans = [slice(at * rows, (at + 1) * rows) for at in range(n_row)]
+    _, [kept_c], sent_c = partial_sums(
+        aligned, None, down_weight, tile, *parts[2], spans[:1], spans[1:], crossed, "sums_last")
+    done_c = [kept_c] + [send(message, "row", o, n_row) for message, o in zip(sent_c, offsets[1:])]
+
     grad_pieces = [act_pieces[o] for o in offsets]
     grad_tile = tile_of(hidden, 256)
-    grad_parts = part_slices(hidden // grad_tile, GRAD_SHARES)
-    done, crossed, grad = [], [], None
-    for at, part in enumerate(parts[1:], 1):
-        _, [next_kept], [sent] = partial_sums(
-            aligned, None, down_weight, tile, *part, kept_rows, sent_rows, [act_pieces[1]] if at == 1 else [], "sums_next")
-        earlier = [ended[1] for ended in done]
-        if at == len(parts) - 1:
-            grad = weight_grads(aligned, grad_pieces, grad_tile, *grad_parts[0], None, [sent, *crossed])
-            earlier.append(grad)
-        ended, crossed, [sent] = halved(kept, got, [sent], earlier, n_row)
-        done.append(ended)
-        kept, got = next_kept, send(sent, "row", 1, n_row)
-    ended, crossed, _ = halved(kept, got, [], [], n_row)
-    done.append(ended)
-    weight_grad = weight_grads(aligned, grad_pieces, grad_tile, *grad_parts[1], grad, crossed)
-    return weight_grad, totals(done, [weight_grad])
+    (first_a, count_a), (first_b, count_b) = part_slices(hidden // grad_tile, (3, 4))
+    grad = weight_grads(aligned, grad_pieces, grad_tile, first_a, count_a, None, sent_c[:1])
+    done_b, crossed_b, _ = halved(kept_b, got_b, [], [grad], n_row)
+    weight_grad = weight_grads(aligned, grad_pieces, grad_tile, first_b, count_b, grad, crossed_b)
+    return weight_grad, totals([done_a, done_b, done_c], [weight_grad])
 
 
 def solution(mesh):

time: 83 us -> 77.8 us (0.937)
  waiting for transfers between devices: 24.1 us -> 15.3 us
  starting transfers between devices: 21 us -> 25.2 us
    ppermute x14 -> x15, waiting for transfers between devices: 24.1 us -> 15.3 us  [send(): return lax.ppermute(value, axis, [(i, i ^ flip) for i in range(size)])]
    ppermute x14 -> x15, starting transfers between devices: 21 us -> 25.2 us  [send(): return lax.ppermute(value, axis, [(i, i ^ flip) for i in range(size)])]
  transfers between devices with their start and end apart: 14 -> 15, of which waited for: 9 -> 8; matrix products, arithmetic and copies ran while one was open for 2% -> 2% of each run, Pallas kernels for 39% -> 42%
where the time goes in v12:
time: 77.8 us; the launch traced here: 77.7 us
  Pallas kernels  33.7 us (43%)
  starting transfers between devices  25.2 us (32%)
  waiting for transfers between devices  15.3 us (20%)
  local copies, waits for them, and re-layouts  1.8 us (2%)
  other arithmetic  0.91 us (1%)
    ppermute x15, starting transfers between devices, send(): return lax.ppermute(value, axis, [(i, i ^ flip) for i in range(size)])  25.2 us
    pallas_call x3, Pallas kernels, partial_sums(): pl.pallas_call(functools.partial(sums_kernel, 0 if aligned is not None el...  18.4 us
    ppermute x15, waiting for transfers between devices, send(): return lax.ppermute(value, axis, [(i, i ^ flip) for i in range(size)])  15.3 us
    pallas_call x2, Pallas kernels, weight_grads(): pl.pallas_call(functools.partial(weight_kernel, len(pieces), first, len(l...  13.4 us
  transfers between devices with their start and end apart: 15, of which 8 were waited for; matrix products, arithmetic and copies ran while one was open for 2% of the time, Pallas kernels for 42%

profile of v12, /device:TPU:0, one launch (start us, length us, event | category | flops | bytes accessed | tf_op | source)
XLA Modules:
  0.0 77.7 jit_solution(17992274190224604538)
XLA Ops:
  0.6 3.0 %collective-permute-start = (bf16[32,4096]{1,0:T(8,128)(2,1)}, bf16[32,4096]{1,0:T(8,128)(2,1)S(1)}, u32[]{:S(2)}, u32[]{:S(2)}) collective-permute-start(bf16[32,4096]{1,0:T(8,128)(2,1)} %refs_0_.3), channel_id=1, source_target_pairs={{0,2},{1,3},{2,0},{3,1},{4,6},{5,7},{6,4},{7,5},{8,10},{9,11},{10,... | collective-permute-start | bytes 786440 | tf_op jit(solution)/shard_map/ppermute | solution.py:257
  3.6 1.5 %collective-permute-start.2 = (bf16[32,4096]{1,0:T(8,128)(2,1)}, bf16[32,4096]{1,0:T(8,128)(2,1)S(1)}, u32[]{:S(2)}, u32[]{:S(2)}) collective-permute-start(bf16[32,4096]{1,0:T(8,128)(2,1)} %refs_0_.3), channel_id=1, source_target_pairs={{0,6},{1,7},{2,4},{3,5},{4,2},{5,3},{6,0},{7,1},{8,14},{9,15},{10,... | collective-permute-start | bytes 786440 | tf_op jit(solution)/shard_map/ppermute | solution.py:257
  5.2 2.0 %collective-permute-start.6 = (bf16[64,3584]{1,0:T(8,128)(2,1)}, bf16[64,3584]{1,0:T(8,128)(2,1)S(1)}, u32[]{:S(2)}, u32[]{:S(2)}) collective-permute-start(bf16[64,3584]{1,0:T(8,128)(2,1)} %refs_0_.5), channel_id=1, source_target_pairs={{0,8},{8,0},{16,24},{24,16},{1,9},{9,1},{17,25},{25,17},{2,10},{10... | collective-permute-start | bytes 1376264 | tf_op jit(solution)/shard_map/ppermute | solution.py:257
  7.2 2.6 %collective-permute-start.5 = (bf16[64,3584]{1,0:T(8,128)(2,1)}, bf16[64,3584]{1,0:T(8,128)(2,1)S(1)}, u32[]{:S(2)}, u32[]{:S(2)}) collective-permute-start(bf16[64,3584]{1,0:T(8,128)(2,1)} %refs_0_.5), channel_id=1, source_target_pairs={{0,16},{8,24},{16,0},{24,8},{1,17},{9,25},{17,1},{25,9},{2,18},{10... | collective-permute-start | bytes 1376264 | tf_op jit(solution)/shard_map/ppermute | solution.py:257
  9.8 0.7 xor_multiply_fusion
  10.5 0.5 collective-permute-done.refs_1_
  11.0 0.9 %copy-done.1 = bf16[32,4096]{1,0:T(8,128)(2,1)S(1)} copy-done((bf16[32,4096]{1,0:T(8,128)(2,1)S(1)}, bf16[32,4096]{1,0:T(8,128)(2,1)}, u32[]{:S(2)}) %copy-start.1) | copy-done | bytes 262168
  12.0 5.0 %collective-permute-done.2.refs_1_ = bf16[32,4096]{1,0:T(8,128)(2,1)S(1)} collective-permute-done((bf16[32,4096]{1,0:T(8,128)(2,1)}, bf16[32,4096]{1,0:T(8,128)(2,1)S(1)}, u32[]{:S(2)}, u32[]{:S(2)}) %collective-permute-start.2) | collective-permute-done | bytes 262176 | tf_op jit(solution)/shard_map/ppermute | solution.py:257
  17.1 1.4 %collective-permute-done.1.refs_0_ = bf16[32,4096]{1,0:T(8,128)(2,1)S(1)} collective-permute-done((bf16[32,4096]{1,0:T(8,128)(2,1)}, bf16[32,4096]{1,0:T(8,128)(2,1)S(1)}, u32[]{:S(2)}, u32[]{:S(2)}) %collective-permute-start.1) | collective-permute-done | bytes 262176 | tf_op jit(solution)/shard_map/ppermute | solution.py:257
  18.6 0.8 reshape.24
  19.6 0.1 compare_convert_fusion.refs_0_
  19.7 0.8 %collective-permute-done.4.refs_4_ = bf16[64,4096]{1,0:T(8,128)(2,1)S(1)} collective-permute-done((bf16[64,4096]{1,0:T(8,128)(2,1)S(1)}, bf16[64,4096]{1,0:T(8,128)(2,1)S(1)}, u32[]{:S(2)}, u32[]{:S(2)}) %collective-permute-start.4) | collective-permute-done | bytes 524320 | tf_op jit(solution)/shard_map/ppermute | solution.py:257
  20.5 5.9 %sums_first.1 = (bf16[256,4096]{1,0:T(8,128)(2,1)S(1)}, f32[128,1024]{1,0:T(8,128)S(1)}, s16[128,1152]{1,0:T(8,128)(2,1)S(1)}) custom-call(bf16[256,256]{1,0:T(8,128)(2,1)S(1)} %compare_convert_fusion.refs_0_, bf16[64,4096]{1,0:T(8,128)(2,1)S(1)} %stacked.2.refs_2_.refs_1_, bf16[64,4096]{1,0:T(8,128)(2,1)S(1)} %stacked.3.refs_2_, ...), custom_call_target="tpu_custom_call" | custom-call | flops 2147483648 | bytes 8388608 | tf_op jit(solution)/shard_map/sums_first/pallas_call | solution.py:128
  26.3 1.6 %collective-permute-start.8 = (s16[128,1152]{1,0:T(8,128)(2,1)S(1)}, s16[128,1152]{1,0:T(8,128)(2,1)S(1)}, u32[]{:S(2)}, u32[]{:S(2)}) collective-permute-start(s16[128,1152]{1,0:T(8,128)(2,1)S(1)} %get-tuple-element.18), channel_id=1, source_target_pairs={{0,8},{8,0},{16,24},{24,16},{1,9},{9,1},{17,25},{25,17},{2,10},{10... | collective-permute-start | bytes 884744 | tf_op jit(solution)/shard_map/ppermute | solution.py:257
  28.0 1.5 %collective-permute-done.5.refs_0_ = bf16[64,3584]{1,0:T(8,128)(2,1)S(1)} collective-permute-done((bf16[64,3584]{1,0:T(8,128)(2,1)}, bf16[64,3584]{1,0:T(8,128)(2,1)S(1)}, u32[]{:S(2)}, u32[]{:S(2)}) %collective-permute-start.5) | collective-permute-done | bytes 458784 | tf_op jit(solution)/shard_map/ppermute | solution.py:257
  29.5 0.3 collective-permute-start.7
  29.8 5.2 %sums_second.1 = (f32[128,1024]{1,0:T(8,128)S(1)}, s16[128,1152]{1,0:T(8,128)(2,1)S(1)}) custom-call(bf16[256,4096]{1,0:T(8,128)(2,1)S(1)} %get-tuple-element.16.refs_1_.refs_0_.aligned_ref, bf16[3584,4096]{1,0:T(8,128)(2,1)} %refs_2_.3, bf16[3584,4096]{1,0:T(8,128)(2,1)} %refs_2_.3, bf16[64,3584]{1,0:T(8,128)(2,1)S(1)} %collective-permute-done.6.refs_3_.refs_2_), custom_call_target="tpu_custom_call" | custom-call | flops 2147483648 | bytes 8388608 | tf_op jit(solution)/shard_map/sums_second/pallas_call | solution.py:128
  34.9 1.3 %collective-permute-done.8.got_ref = s16[128,1152]{1,0:T(8,128)(2,1)S(1)} collective-permute-done((s16[128,1152]{1,0:T(8,128)(2,1)S(1)}, s16[128,1152]{1,0:T(8,128)(2,1)S(1)}, u32[]{:S(2)}, u32[]{:S(2)}) %collective-permute-start.8) | collective-permute-done | bytes 294944 | tf_op jit(solution)/shard_map/ppermute | solution.py:257
  36.3 0.3 fold.2
  36.6 2.7 %collective-permute-start.10 = (s16[64,1152]{1,0:T(8,128)(2,1)S(1)}, s16[64,1152]{1,0:T(8,128)(2,1)S(1)}, u32[]{:S(2)}, u32[]{:S(2)}) collective-permute-start(s16[64,1152]{1,0:T(8,128)(2,1)S(1)} %get-tuple-element.20.refs_3_), channel_id=1, source_target_pairs={{0,16},{8,24},{16,0},{24,8},{1,17},{9,25},{17,1},{25,9},{2,18},{10... | collective-permute-start | bytes 442376 | tf_op jit(solution)/shard_map/ppermute | solution.py:257
  39.3 1.6 %collective-permute-start.9 = (s16[128,1152]{1,0:T(8,128)(2,1)S(1)}, s16[128,1152]{1,0:T(8,128)(2,1)S(1)}, u32[]{:S(2)}, u32[]{:S(2)}) collective-permute-start(s16[128,1152]{1,0:T(8,128)(2,1)S(1)} %get-tuple-element.23), channel_id=1, source_target_pairs={{0,8},{8,0},{16,24},{24,16},{1,9},{9,1},{17,25},{25,17},{2,10},{10... | collective-permute-start | bytes 884744 | tf_op jit(solution)/shard_map/ppermute | solution.py:257
  40.8 7.4 %sums_last.1 = (f32[64,1536]{1,0:T(8,128)S(1)}, s16[64,1664]{1,0:T(8,128)(2,1)S(1)}, s16[64,1664]{1,0:T(8,128)(2,1)S(1)}, s16[64,1664]{1,0:T(8,128)(2,1)S(1)}) custom-call(bf16[256,4096]{1,0:T(8,128)(2,1)S(1)} %get-tuple-element.16.refs_1_.refs_0_.aligned_ref, bf16[3584,4096]{1,0:T(8,128)(2,1)} %refs_2_.3, bf16[3584,4096]{1,0:T(8,128)(2,1)} %refs_2_.3, ...), custom_call_target="tpu_custom_call" | custom-call | flops 3221225472 | bytes 12582912 | tf_op jit(solution)/shard_map/sums_last/pallas_call | solution.py:128
  48.2 0.5 collective-permute-start.13
  48.8 1.4 %collective-permute-start.14 = (s16[64,1664]{1,0:T(8,128)(2,1)S(1)}, s16[64,1664]{1,0:T(8,128)(2,1)S(1)}, u32[]{:S(2)}, u32[]{:S(2)}) collective-permute-start(s16[64,1664]{1,0:T(8,128)(2,1)S(1)} %get-tuple-element.29), channel_id=1, source_target_pairs={{0,24},{8,16},{16,8},{24,0},{1,25},{9,17},{17,9},{25,1},{2,26},{10... | collective-permute-start | bytes 638984 | tf_op jit(solution)/shard_map/ppermute | solution.py:257
  50.1 1.7 %collective-permute-start.12 = (s16[64,1664]{1,0:T(8,128)(2,1)S(1)}, s16[64,1664]{1,0:T(8,128)(2,1)S(1)}, u32[]{:S(2)}, u32[]{:S(2)}) collective-permute-start(s16[64,1664]{1,0:T(8,128)(2,1)S(1)} %get-tuple-element.21.refs_4_), channel_id=1, source_target_pairs={{0,16},{8,24},{16,0},{24,8},{1,17},{9,25},{17,1},{25,9},{2,18},{10... | collective-permute-start | bytes 638984 | tf_op jit(solution)/shard_map/ppermute | solution.py:257
  51.8 5.9 %weight_grads.2.refs_0_.refs_4_ = bf16[3584,4096]{1,0:T(8,128)(2,1)} custom-call(bf16[256,4096]{1,0:T(8,128)(2,1)S(1)} %get-tuple-element.16.refs_1_.refs_0_.aligned_ref, bf16[64,3584]{1,0:T(8,128)(2,1)S(1)} %copy-done, bf16[64,3584]{1,0:T(8,128)(2,1)S(1)} %handed_on.1.refs_1_, bf16[64,3584]{1,0:T(8,128)(2,1)S(1)} %collective-permute-done.6.refs_3_.refs_2_, ...), custom_call_target="tpu_custom_call" | custom-call | flops 3221225472 | bytes 12582912 | tf_op jit(solution)/shard_map/weight_grads/pallas_call | solution.py:178
  57.7 2.4 %collective-permute-done.9.got_ref = s16[128,1152]{1,0:T(8,128)(2,1)S(1)} collective-permute-done((s16[128,1152]{1,0:T(8,128)(2,1)S(1)}, s16[128,1152]{1,0:T(8,128)(2,1)S(1)}, u32[]{:S(2)}, u32[]{:S(2)}) %collective-permute-start.9) | collective-permute-done | bytes 294944 | tf_op jit(solution)/shard_map/ppermute | solution.py:257
  60.1 0.3 fold.3
  60.5 6.1 %collective-permute-start.11 = (s16[64,1152]{1,0:T(8,128)(2,1)S(1)}, s16[64,1152]{1,0:T(8,128)(2,1)S(1)}, u32[]{:S(2)}, u32[]{:S(2)}) collective-permute-start(s16[64,1152]{1,0:T(8,128)(2,1)S(1)} %get-tuple-element.24.refs_5_), channel_id=1, source_target_pairs={{0,16},{8,24},{16,0},{24,8},{1,17},{9,25},{17,1},{25,9},{2,18},{10... | collective-permute-start | bytes 442376 | tf_op jit(solution)/shard_map/ppermute | solution.py:257
  66.6 7.5 %weight_grads.3.refs_8_ = bf16[3584,4096]{1,0:T(8,128)(2,1)} custom-call(bf16[256,4096]{1,0:T(8,128)(2,1)S(1)} %get-tuple-element.16.refs_1_.refs_0_.aligned_ref, bf16[64,3584]{1,0:T(8,128)(2,1)S(1)} %copy-done, bf16[64,3584]{1,0:T(8,128)(2,1)S(1)} %handed_on.1.refs_1_, ...), custom_call_target="tpu_custom_call", output_to_operand_aliasing={{}: (5, {})} | custom-call | flops 4294967296 | bytes 16777216 | tf_op jit(solution)/shard_map/weight_grads/pallas_call | solution.py:178
  74.1 2.4 %collective-permute-done.11.refs_3_ = s16[64,1152]{1,0:T(8,128)(2,1)S(1)} collective-permute-done((s16[64,1152]{1,0:T(8,128)(2,1)S(1)}, s16[64,1152]{1,0:T(8,128)(2,1)S(1)}, u32[]{:S(2)}, u32[]{:S(2)}) %collective-permute-start.11) | collective-permute-done | bytes 147488 | tf_op jit(solution)/shard_map/ppermute | solution.py:257
  76.6 1.1 %totals.1 = bf16[64,3584]{1,0:T(8,128)(2,1)} custom-call(f32[64,1024]{1,0:T(8,128)S(1)} %get-tuple-element.25.refs_0_, s16[64,1152]{1,0:T(8,128)(2,1)S(1)} %collective-permute-done.10.refs_1_, f32[64,1024]{1,0:T(8,128)S(1)} %get-tuple-element.26.refs_2_, s16[64,1152]{1,0:T(8,128)(2,1)S(1)} %collective-permute-done.11.refs_3_, ...), custom_call_target="tpu_custom_call" | custom-call | flops 9175040 | bytes 3211264 | tf_op jit(solution)/shard_map/totals/pallas_call | solution.py:248
  (20 shorter events, 0.5 us)
Async XLA Ops:
  0.6 10.4 %collective-permute-start = (bf16[32,4096]{1,0:T(8,128)(2,1)}, bf16[32,4096]{1,0:T(8,128)(2,1)S(1)}, u32[]{:S(2)}, u32[]{:S(2)}) collective-permute-start(bf16[32,4096]{1,0:T(8,128)(2,1)} %refs_0_.3), channel_id=1, source_target_pairs={{0,2},{1,3},{2,0},{3,1},{4,6},{5,7},{6,4},{7,5},{8,10},{9,11},{10,... | collective-permute-start | bytes 786440 | tf_op jit(solution)/shard_map/ppermute | solution.py:257
  3.6 13.4 %collective-permute-start.2 = (bf16[32,4096]{1,0:T(8,128)(2,1)}, bf16[32,4096]{1,0:T(8,128)(2,1)S(1)}, u32[]{:S(2)}, u32[]{:S(2)}) collective-permute-start(bf16[32,4096]{1,0:T(8,128)(2,1)} %refs_0_.3), channel_id=1, source_target_pairs={{0,6},{1,7},{2,4},{3,5},{4,2},{5,3},{6,0},{7,1},{8,14},{9,15},{10,... | collective-permute-start | bytes 786440 | tf_op jit(solution)/shard_map/ppermute | solution.py:257
  5.1 13.3 %collective-permute-start.1 = (bf16[32,4096]{1,0:T(8,128)(2,1)}, bf16[32,4096]{1,0:T(8,128)(2,1)S(1)}, u32[]{:S(2)}, u32[]{:S(2)}) collective-permute-start(bf16[32,4096]{1,0:T(8,128)(2,1)} %refs_0_.3), channel_id=1, source_target_pairs={{0,4},{1,5},{2,6},{3,7},{4,0},{5,1},{6,2},{7,3},{8,12},{9,13},{10,... | collective-permute-start | bytes 786440 | tf_op jit(solution)/shard_map/ppermute | solution.py:257
  5.2 24.6 %collective-permute-start.6 = (bf16[64,3584]{1,0:T(8,128)(2,1)}, bf16[64,3584]{1,0:T(8,128)(2,1)S(1)}, u32[]{:S(2)}, u32[]{:S(2)}) collective-permute-start(bf16[64,3584]{1,0:T(8,128)(2,1)} %refs_0_.5), channel_id=1, source_target_pairs={{0,8},{8,0},{16,24},{24,16},{1,9},{9,1},{17,25},{25,17},{2,10},{10... | collective-permute-start | bytes 1376264 | tf_op jit(solution)/shard_map/ppermute | solution.py:257
  7.2 22.2 %collective-permute-start.5 = (bf16[64,3584]{1,0:T(8,128)(2,1)}, bf16[64,3584]{1,0:T(8,128)(2,1)S(1)}, u32[]{:S(2)}, u32[]{:S(2)}) collective-permute-start(bf16[64,3584]{1,0:T(8,128)(2,1)} %refs_0_.5), channel_id=1, source_target_pairs={{0,16},{8,24},{16,0},{24,8},{1,17},{9,25},{17,1},{25,9},{2,18},{10... | collective-permute-start | bytes 1376264 | tf_op jit(solution)/shard_map/ppermute | solution.py:257
  11.0 1.0 %copy-start.1 = (bf16[32,4096]{1,0:T(8,128)(2,1)S(1)}, bf16[32,4096]{1,0:T(8,128)(2,1)}, u32[]{:S(2)}) copy-start(bf16[32,4096]{1,0:T(8,128)(2,1)} %refs_0_.3) | copy-start | bytes 786436
  12.0 8.5 %collective-permute-start.3 = (bf16[64,4096]{1,0:T(8,128)(2,1)S(1)}, bf16[64,4096]{1,0:T(8,128)(2,1)S(1)}, u32[]{:S(2)}, u32[]{:S(2)}) collective-permute-start(bf16[64,4096]{1,0:T(8,128)(2,1)S(1)} %stacked.2.refs_2_.refs_1_), channel_id=1, source_target_pairs={{0,1},{1,0},{2,3},{3,2},{4,5},{5,4},{6,7},{7,6},{8,9},{9,8},{10,11... | collective-permute-start | bytes 1572872 | tf_op jit(solution)/shard_map/ppermute | solution.py:257
  18.5 2.0 %collective-permute-start.4 = (bf16[64,4096]{1,0:T(8,128)(2,1)S(1)}, bf16[64,4096]{1,0:T(8,128)(2,1)S(1)}, u32[]{:S(2)}, u32[]{:S(2)}) collective-permute-start(bf16[64,4096]{1,0:T(8,128)(2,1)S(1)} %stacked.3.refs_2_), channel_id=1, source_target_pairs={{0,1},{1,0},{2,3},{3,2},{4,5},{5,4},{6,7},{7,6},{8,9},{9,8},{10,11... | collective-permute-start | bytes 1572872 | tf_op jit(solution)/shard_map/ppermute | solution.py:257
  26.3 9.9 %collective-permute-start.8 = (s16[128,1152]{1,0:T(8,128)(2,1)S(1)}, s16[128,1152]{1,0:T(8,128)(2,1)S(1)}, u32[]{:S(2)}, u32[]{:S(2)}) collective-permute-start(s16[128,1152]{1,0:T(8,128)(2,1)S(1)} %get-tuple-element.18), channel_id=1, source_target_pairs={{0,8},{8,0},{16,24},{24,16},{1,9},{9,1},{17,25},{25,17},{2,10},{10... | collective-permute-start | bytes 884744 | tf_op jit(solution)/shard_map/ppermute | solution.py:257
  29.5 20.7 %collective-permute-start.7 = (bf16[64,3584]{1,0:T(8,128)(2,1)S(1)}, bf16[64,3584]{1,0:T(8,128)(2,1)S(1)}, u32[]{:S(2)}, u32[]{:S(2)}) collective-permute-start(bf16[64,3584]{1,0:T(8,128)(2,1)S(1)} %handed_on.1.refs_1_), channel_id=1, source_target_pairs={{0,8},{8,0},{16,24},{24,16},{1,9},{9,1},{17,25},{25,17},{2,10},{10... | collective-permute-start | bytes 1376264 | tf_op jit(solution)/shard_map/ppermute | solution.py:257
  36.6 37.5 %collective-permute-start.10 = (s16[64,1152]{1,0:T(8,128)(2,1)S(1)}, s16[64,1152]{1,0:T(8,128)(2,1)S(1)}, u32[]{:S(2)}, u32[]{:S(2)}) collective-permute-start(s16[64,1152]{1,0:T(8,128)(2,1)S(1)} %get-tuple-element.20.refs_3_), channel_id=1, source_target_pairs={{0,16},{8,24},{16,0},{24,8},{1,17},{9,25},{17,1},{25,9},{2,18},{10... | collective-permute-start | bytes 442376 | tf_op jit(solution)/shard_map/ppermute | solution.py:257
  39.3 12.5 %copy-start = (bf16[64,3584]{1,0:T(8,128)(2,1)S(1)}, bf16[64,3584]{1,0:T(8,128)(2,1)}, u32[]{:S(2)}) copy-start(bf16[64,3584]{1,0:T(8,128)(2,1)} %refs_0_.5) | copy-start | bytes 1376260
  39.3 20.9 %collective-permute-start.9 = (s16[128,1152]{1,0:T(8,128)(2,1)S(1)}, s16[128,1152]{1,0:T(8,128)(2,1)S(1)}, u32[]{:S(2)}, u32[]{:S(2)}) collective-permute-start(s16[128,1152]{1,0:T(8,128)(2,1)S(1)} %get-tuple-element.23), channel_id=1, source_target_pairs={{0,8},{8,0},{16,24},{24,16},{1,9},{9,1},{17,25},{25,17},{2,10},{10... | collective-permute-start | bytes 884744 | tf_op jit(solution)/shard_map/ppermute | solution.py:257
  48.2 25.8 %collective-permute-start.13 = (s16[64,1664]{1,0:T(8,128)(2,1)S(1)}, s16[64,1664]{1,0:T(8,128)(2,1)S(1)}, u32[]{:S(2)}, u32[]{:S(2)}) collective-permute-start(s16[64,1664]{1,0:T(8,128)(2,1)S(1)} %get-tuple-element.28), channel_id=1, source_target_pairs={{0,8},{8,0},{16,24},{24,16},{1,9},{9,1},{17,25},{25,17},{2,10},{10... | collective-permute-start | bytes 638984 | tf_op jit(solution)/shard_map/ppermute | solution.py:257
  48.8 25.3 %collective-permute-start.14 = (s16[64,1664]{1,0:T(8,128)(2,1)S(1)}, s16[64,1664]{1,0:T(8,128)(2,1)S(1)}, u32[]{:S(2)}, u32[]{:S(2)}) collective-permute-start(s16[64,1664]{1,0:T(8,128)(2,1)S(1)} %get-tuple-element.29), channel_id=1, source_target_pairs={{0,24},{8,16},{16,8},{24,0},{1,25},{9,17},{17,9},{25,1},{2,26},{10... | collective-permute-start | bytes 638984 | tf_op jit(solution)/shard_map/ppermute | solution.py:257
  50.1 24.0 %collective-permute-start.12 = (s16[64,1664]{1,0:T(8,128)(2,1)S(1)}, s16[64,1664]{1,0:T(8,128)(2,1)S(1)}, u32[]{:S(2)}, u32[]{:S(2)}) collective-permute-start(s16[64,1664]{1,0:T(8,128)(2,1)S(1)} %get-tuple-element.21.refs_4_), channel_id=1, source_target_pairs={{0,16},{8,24},{16,0},{24,8},{1,17},{9,25},{17,1},{25,9},{2,18},{10... | collective-permute-start | bytes 638984 | tf_op jit(solution)/shard_map/ppermute | solution.py:257
  60.5 16.1 %collective-permute-start.11 = (s16[64,1152]{1,0:T(8,128)(2,1)S(1)}, s16[64,1152]{1,0:T(8,128)(2,1)S(1)}, u32[]{:S(2)}, u32[]{:S(2)}) collective-permute-start(s16[64,1152]{1,0:T(8,128)(2,1)S(1)} %get-tuple-element.24.refs_5_), channel_id=1, source_target_pairs={{0,16},{8,24},{16,0},{24,8},{1,17},{9,25},{17,1},{25,9},{2,18},{10... | collective-permute-start | bytes 442376 | tf_op jit(solution)/shard_map/ppermute | solution.py:257

commit v13 on v12

--- a/solution.py
+++ b/solution.py
@@ -14,7 +14,7 @@
 VMEM_LIMIT = 48 * 1024 * 1024
 SMALL_LIMIT = 8 * 1024 * 1024
 SLOTS = 4
-SHARES = (2, 2, 3)
+SHARES = (2, 3, 2)
 SUB = 256
 
 
@@ -289,8 +289,12 @@
     )(*values, *later_than)
 
 
+def chip_order(n_col):
+    return [2, *range(n_col - 2, 2, -2)]
+
+
 def gather_cotangent(cotangent, n_col):
-    pieces = [cotangent] + [send(cotangent, "col", flip, n_col) for flip in range(2, n_col, 2)]
+    pieces = [cotangent] + [send(cotangent, "col", flip, n_col) for flip in chip_order(n_col)]
     stacks = [stacked(pieces[:2])]
     stacks.append(stacked(pieces[2:], stacks))
     return stacks + [send(stack, "col", 1, n_col) for stack in stacks]
@@ -324,7 +328,7 @@
     offsets = halving_order(n_row)
     total = n_row * rows
 
-    flips = list(range(0, n_col, 2))
+    flips = [0, *chip_order(n_col)]
     flips += [flip ^ 1 for flip in flips]
     order = row_order.reshape(n_row, rows)
     order = jnp.concatenate([lax.dynamic_index_in_dim(order, mine_row ^ o, 0, keepdims=False) for o in offsets])

time: 77.8 us -> 78.3 us (level)
  waiting for transfers between devices: 15.3 us -> 18 us
  starting transfers between devices: 25.2 us -> 22.7 us
    ppermute x15, waiting for transfers between devices: 15.3 us -> 18 us  [send(): return lax.ppermute(value, axis, [(i, i ^ flip) for i in range(size)])]
    ppermute x15, starting transfers between devices: 25.2 us -> 22.7 us  [send(): return lax.ppermute(value, axis, [(i, i ^ flip) for i in range(size)])]
  transfers between devices with their start and end apart: 15 -> 15, of which waited for: 8 -> 5; matrix products, arithmetic and copies ran while one was open for 2% -> 2% of each run, Pallas kernels for 42% -> 42%
where the time goes in v13:
time: 78.3 us; the launch traced here: 78.1 us
  Pallas kernels  33.9 us (43%)
  starting transfers between devices  22.7 us (29%)
  waiting for transfers between devices  18 us (23%)
  local copies, waits for them, and re-layouts  1.8 us (2%)
  other arithmetic  0.91 us (1%)
    ppermute x15, starting transfers between devices, send(): return lax.ppermute(value, axis, [(i, i ^ flip) for i in range(size)])  22.7 us
    pallas_call x3, Pallas kernels, partial_sums(): pl.pallas_call(functools.partial(sums_kernel, 0 if aligned is not None el...  18.5 us
    ppermute x15, waiting for transfers between devices, send(): return lax.ppermute(value, axis, [(i, i ^ flip) for i in range(size)])  18 us
    pallas_call x2, Pallas kernels, weight_grads(): pl.pallas_call(functools.partial(weight_kernel, len(pieces), first, len(l...  13.4 us
  transfers between devices with their start and end apart: 15, of which 5 were waited for; matrix products, arithmetic and copies ran while one was open for 2% of the time, Pallas kernels for 42%

profile of v13, /device:TPU:0, one launch (start us, length us, event | category | flops | bytes accessed | tf_op | source)
XLA Modules:
  0.0 78.1 jit_solution(14460005350113303139)
XLA Ops:
  0.6 3.0 %collective-permute-start = (bf16[32,4096]{1,0:T(8,128)(2,1)}, bf16[32,4096]{1,0:T(8,128)(2,1)S(1)}, u32[]{:S(2)}, u32[]{:S(2)}) collective-permute-start(bf16[32,4096]{1,0:T(8,128)(2,1)} %refs_0_.3), channel_id=1, source_target_pairs={{0,2},{1,3},{2,0},{3,1},{4,6},{5,7},{6,4},{7,5},{8,10},{9,11},{10,... | collective-permute-start | bytes 786440 | tf_op jit(solution)/shard_map/ppermute | solution.py:257
  3.6 1.5 %collective-permute-start.2 = (bf16[32,4096]{1,0:T(8,128)(2,1)}, bf16[32,4096]{1,0:T(8,128)(2,1)S(1)}, u32[]{:S(2)}, u32[]{:S(2)}) collective-permute-start(bf16[32,4096]{1,0:T(8,128)(2,1)} %refs_0_.3), channel_id=1, source_target_pairs={{0,4},{1,5},{2,6},{3,7},{4,0},{5,1},{6,2},{7,3},{8,12},{9,13},{10,... | collective-permute-start | bytes 786440 | tf_op jit(solution)/shard_map/ppermute | solution.py:257
  5.2 2.0 %collective-permute-start.6 = (bf16[64,3584]{1,0:T(8,128)(2,1)}, bf16[64,3584]{1,0:T(8,128)(2,1)S(1)}, u32[]{:S(2)}, u32[]{:S(2)}) collective-permute-start(bf16[64,3584]{1,0:T(8,128)(2,1)} %refs_0_.5), channel_id=1, source_target_pairs={{0,8},{8,0},{16,24},{24,16},{1,9},{9,1},{17,25},{25,17},{2,10},{10... | collective-permute-start | bytes 1376264 | tf_op jit(solution)/shard_map/ppermute | solution.py:257
  7.2 2.6 %collective-permute-start.5 = (bf16[64,3584]{1,0:T(8,128)(2,1)}, bf16[64,3584]{1,0:T(8,128)(2,1)S(1)}, u32[]{:S(2)}, u32[]{:S(2)}) collective-permute-start(bf16[64,3584]{1,0:T(8,128)(2,1)} %refs_0_.5), channel_id=1, source_target_pairs={{0,16},{8,24},{16,0},{24,8},{1,17},{9,25},{17,1},{25,9},{2,18},{10... | collective-permute-start | bytes 1376264 | tf_op jit(solution)/shard_map/ppermute | solution.py:257
  9.8 0.8 reshape.24
  10.6 0.7 xor_multiply_fusion
  11.2 0.9 %copy-done.1 = bf16[32,4096]{1,0:T(8,128)(2,1)S(1)} copy-done((bf16[32,4096]{1,0:T(8,128)(2,1)S(1)}, bf16[32,4096]{1,0:T(8,128)(2,1)}, u32[]{:S(2)}) %copy-start.1) | copy-done | bytes 262168
  12.2 0.1 collective-permute-start.3
  12.3 4.9 %collective-permute-done.2.refs_1_ = bf16[32,4096]{1,0:T(8,128)(2,1)S(1)} collective-permute-done((bf16[32,4096]{1,0:T(8,128)(2,1)}, bf16[32,4096]{1,0:T(8,128)(2,1)S(1)}, u32[]{:S(2)}, u32[]{:S(2)}) %collective-permute-start.2) | collective-permute-done | bytes 262176 | tf_op jit(solution)/shard_map/ppermute | solution.py:257
  17.3 0.1 collective-permute-start.4
  17.4 0.1 pad_add_fusion
  17.5 0.1 add.40
  17.6 0.1 compare_convert_fusion.refs_0_
  17.7 1.6 %collective-permute-done.4.refs_4_ = bf16[64,4096]{1,0:T(8,128)(2,1)S(1)} collective-permute-done((bf16[64,4096]{1,0:T(8,128)(2,1)S(1)}, bf16[64,4096]{1,0:T(8,128)(2,1)S(1)}, u32[]{:S(2)}, u32[]{:S(2)}) %collective-permute-start.4) | collective-permute-done | bytes 524320 | tf_op jit(solution)/shard_map/ppermute | solution.py:257
  19.2 5.9 %sums_first.1 = (bf16[256,4096]{1,0:T(8,128)(2,1)S(1)}, f32[128,1024]{1,0:T(8,128)S(1)}, s16[128,1152]{1,0:T(8,128)(2,1)S(1)}) custom-call(bf16[256,256]{1,0:T(8,128)(2,1)S(1)} %compare_convert_fusion.refs_0_, bf16[64,4096]{1,0:T(8,128)(2,1)S(1)} %stacked.2.refs_2_.refs_1_, bf16[64,4096]{1,0:T(8,128)(2,1)S(1)} %stacked.3.refs_2_, ...), custom_call_target="tpu_custom_call" | custom-call | flops 2147483648 | bytes 8388608 | tf_op jit(solution)/shard_map/sums_first/pallas_call | solution.py:128
  25.1 1.6 %collective-permute-start.8 = (s16[128,1152]{1,0:T(8,128)(2,1)S(1)}, s16[128,1152]{1,0:T(8,128)(2,1)S(1)}, u32[]{:S(2)}, u32[]{:S(2)}) collective-permute-start(s16[128,1152]{1,0:T(8,128)(2,1)S(1)} %get-tuple-element.18), channel_id=1, source_target_pairs={{0,8},{8,0},{16,24},{24,16},{1,9},{9,1},{17,25},{25,17},{2,10},{10... | collective-permute-start | bytes 884744 | tf_op jit(solution)/shard_map/ppermute | solution.py:257
  26.8 2.7 %collective-permute-done.5.refs_0_ = bf16[64,3584]{1,0:T(8,128)(2,1)S(1)} collective-permute-done((bf16[64,3584]{1,0:T(8,128)(2,1)}, bf16[64,3584]{1,0:T(8,128)(2,1)S(1)}, u32[]{:S(2)}, u32[]{:S(2)}) %collective-permute-start.5) | collective-permute-done | bytes 458784 | tf_op jit(solution)/shard_map/ppermute | solution.py:257
  29.5 0.3 collective-permute-start.7
  29.8 7.4 %sums_second.1 = (f32[128,1536]{1,0:T(8,128)S(1)}, s16[128,1664]{1,0:T(8,128)(2,1)S(1)}) custom-call(bf16[256,4096]{1,0:T(8,128)(2,1)S(1)} %get-tuple-element.16.refs_1_.refs_0_.aligned_ref, bf16[3584,4096]{1,0:T(8,128)(2,1)} %refs_2_.3, bf16[3584,4096]{1,0:T(8,128)(2,1)} %refs_2_.3, bf16[64,3584]{1,0:T(8,128)(2,1)S(1)} %collective-permute-done.6.refs_3_.refs_2_), custom_call_target="tpu_custom_call" | custom-call | flops 3221225472 | bytes 12582912 | tf_op jit(solution)/shard_map/sums_second/pallas_call | solution.py:128
  37.2 0.3 fold.2
  37.5 2.7 %collective-permute-start.10 = (s16[64,1152]{1,0:T(8,128)(2,1)S(1)}, s16[64,1152]{1,0:T(8,128)(2,1)S(1)}, u32[]{:S(2)}, u32[]{:S(2)}) collective-permute-start(s16[64,1152]{1,0:T(8,128)(2,1)S(1)} %get-tuple-element.20.refs_3_), channel_id=1, source_target_pairs={{0,16},{8,24},{16,0},{24,8},{1,17},{9,25},{17,1},{25,9},{2,18},{10... | collective-permute-start | bytes 442376 | tf_op jit(solution)/shard_map/ppermute | solution.py:257
  40.2 5.2 %sums_last.1 = (f32[64,1024]{1,0:T(8,128)S(1)}, s16[64,1152]{1,0:T(8,128)(2,1)S(1)}, s16[64,1152]{1,0:T(8,128)(2,1)S(1)}, s16[64,1152]{1,0:T(8,128)(2,1)S(1)}) custom-call(bf16[256,4096]{1,0:T(8,128)(2,1)S(1)} %get-tuple-element.16.refs_1_.refs_0_.aligned_ref, bf16[3584,4096]{1,0:T(8,128)(2,1)} %refs_2_.3, bf16[3584,4096]{1,0:T(8,128)(2,1)} %refs_2_.3, ...), custom_call_target="tpu_custom_call" | custom-call | flops 2147483648 | bytes 8388608 | tf_op jit(solution)/shard_map/sums_last/pallas_call | solution.py:128
  45.5 2.0 %collective-permute-start.13 = (s16[64,1152]{1,0:T(8,128)(2,1)S(1)}, s16[64,1152]{1,0:T(8,128)(2,1)S(1)}, u32[]{:S(2)}, u32[]{:S(2)}) collective-permute-start(s16[64,1152]{1,0:T(8,128)(2,1)S(1)} %get-tuple-element.28), channel_id=1, source_target_pairs={{0,8},{8,0},{16,24},{24,16},{1,9},{9,1},{17,25},{25,17},{2,10},{10... | collective-permute-start | bytes 442376 | tf_op jit(solution)/shard_map/ppermute | solution.py:257
  47.5 1.5 %collective-permute-start.14 = (s16[64,1152]{1,0:T(8,128)(2,1)S(1)}, s16[64,1152]{1,0:T(8,128)(2,1)S(1)}, u32[]{:S(2)}, u32[]{:S(2)}) collective-permute-start(s16[64,1152]{1,0:T(8,128)(2,1)S(1)} %get-tuple-element.29), channel_id=1, source_target_pairs={{0,24},{8,16},{16,8},{24,0},{1,25},{9,17},{17,9},{25,1},{2,26},{10... | collective-permute-start | bytes 442376 | tf_op jit(solution)/shard_map/ppermute | solution.py:257
  48.9 0.8 %collective-permute-start.12 = (s16[64,1152]{1,0:T(8,128)(2,1)S(1)}, s16[64,1152]{1,0:T(8,128)(2,1)S(1)}, u32[]{:S(2)}, u32[]{:S(2)}) collective-permute-start(s16[64,1152]{1,0:T(8,128)(2,1)S(1)} %get-tuple-element.21.refs_4_), channel_id=1, source_target_pairs={{0,16},{8,24},{16,0},{24,8},{1,17},{9,25},{17,1},{25,9},{2,18},{10... | collective-permute-start | bytes 442376 | tf_op jit(solution)/shard_map/ppermute | solution.py:257
  49.7 5.9 %weight_grads.2.refs_0_.refs_4_ = bf16[3584,4096]{1,0:T(8,128)(2,1)} custom-call(bf16[256,4096]{1,0:T(8,128)(2,1)S(1)} %get-tuple-element.16.refs_1_.refs_0_.aligned_ref, bf16[64,3584]{1,0:T(8,128)(2,1)S(1)} %copy-done, bf16[64,3584]{1,0:T(8,128)(2,1)S(1)} %handed_on.1.refs_1_, bf16[64,3584]{1,0:T(8,128)(2,1)S(1)} %collective-permute-done.6.refs_3_.refs_2_, ...), custom_call_target="tpu_custom_call" | custom-call | flops 3221225472 | bytes 12582912 | tf_op jit(solution)/shard_map/weight_grads/pallas_call | solution.py:178
  55.7 4.8 %collective-permute-done.9.got_ref = s16[128,1664]{1,0:T(8,128)(2,1)S(1)} collective-permute-done((s16[128,1664]{1,0:T(8,128)(2,1)S(1)}, s16[128,1664]{1,0:T(8,128)(2,1)S(1)}, u32[]{:S(2)}, u32[]{:S(2)}) %collective-permute-start.9) | collective-permute-done | bytes 426016 | tf_op jit(solution)/shard_map/ppermute | solution.py:257
  60.5 0.6 fold.3
  61.0 4.5 %collective-permute-start.11 = (s16[64,1664]{1,0:T(8,128)(2,1)S(1)}, s16[64,1664]{1,0:T(8,128)(2,1)S(1)}, u32[]{:S(2)}, u32[]{:S(2)}) collective-permute-start(s16[64,1664]{1,0:T(8,128)(2,1)S(1)} %get-tuple-element.24.refs_5_), channel_id=1, source_target_pairs={{0,16},{8,24},{16,0},{24,8},{1,17},{9,25},{17,1},{25,9},{2,18},{10... | collective-permute-start | bytes 638984 | tf_op jit(solution)/shard_map/ppermute | solution.py:257
  65.5 7.5 %weight_grads.3.refs_8_ = bf16[3584,4096]{1,0:T(8,128)(2,1)} custom-call(bf16[256,4096]{1,0:T(8,128)(2,1)S(1)} %get-tuple-element.16.refs_1_.refs_0_.aligned_ref, bf16[64,3584]{1,0:T(8,128)(2,1)S(1)} %copy-done, bf16[64,3584]{1,0:T(8,128)(2,1)S(1)} %handed_on.1.refs_1_, ...), custom_call_target="tpu_custom_call", output_to_operand_aliasing={{}: (5, {})} | custom-call | flops 4294967296 | bytes 16777216 | tf_op jit(solution)/shard_map/weight_grads/pallas_call | solution.py:178
  73.0 4.0 %collective-permute-done.11.refs_3_ = s16[64,1664]{1,0:T(8,128)(2,1)S(1)} collective-permute-done((s16[64,1664]{1,0:T(8,128)(2,1)S(1)}, s16[64,1664]{1,0:T(8,128)(2,1)S(1)}, u32[]{:S(2)}, u32[]{:S(2)}) %collective-permute-start.11) | collective-permute-done | bytes 213024 | tf_op jit(solution)/shard_map/ppermute | solution.py:257
  77.0 1.1 %totals.1 = bf16[64,3584]{1,0:T(8,128)(2,1)} custom-call(f32[64,1024]{1,0:T(8,128)S(1)} %get-tuple-element.25.refs_0_, s16[64,1152]{1,0:T(8,128)(2,1)S(1)} %collective-permute-done.10.refs_1_, f32[64,1536]{1,0:T(8,128)S(1)} %get-tuple-element.26.refs_2_, s16[64,1664]{1,0:T(8,128)(2,1)S(1)} %collective-permute-done.11.refs_3_, ...), custom_call_target="tpu_custom_call" | custom-call | flops 9175040 | bytes 3211264 | tf_op jit(solution)/shard_map/totals/pallas_call | solution.py:248
  (20 shorter events, 0.2 us)
Async XLA Ops:
  0.6 10.6 %collective-permute-start = (bf16[32,4096]{1,0:T(8,128)(2,1)}, bf16[32,4096]{1,0:T(8,128)(2,1)S(1)}, u32[]{:S(2)}, u32[]{:S(2)}) collective-permute-start(bf16[32,4096]{1,0:T(8,128)(2,1)} %refs_0_.3), channel_id=1, source_target_pairs={{0,2},{1,3},{2,0},{3,1},{4,6},{5,7},{6,4},{7,5},{8,10},{9,11},{10,... | collective-permute-start | bytes 786440 | tf_op jit(solution)/shard_map/ppermute | solution.py:257
  3.6 13.6 %collective-permute-start.2 = (bf16[32,4096]{1,0:T(8,128)(2,1)}, bf16[32,4096]{1,0:T(8,128)(2,1)S(1)}, u32[]{:S(2)}, u32[]{:S(2)}) collective-permute-start(bf16[32,4096]{1,0:T(8,128)(2,1)} %refs_0_.3), channel_id=1, source_target_pairs={{0,4},{1,5},{2,6},{3,7},{4,0},{5,1},{6,2},{7,3},{8,12},{9,13},{10,... | collective-permute-start | bytes 786440 | tf_op jit(solution)/shard_map/ppermute | solution.py:257
  5.2 12.1 %collective-permute-start.1 = (bf16[32,4096]{1,0:T(8,128)(2,1)}, bf16[32,4096]{1,0:T(8,128)(2,1)S(1)}, u32[]{:S(2)}, u32[]{:S(2)}) collective-permute-start(bf16[32,4096]{1,0:T(8,128)(2,1)} %refs_0_.3), channel_id=1, source_target_pairs={{0,6},{1,7},{2,4},{3,5},{4,2},{5,3},{6,0},{7,1},{8,14},{9,15},{10,... | collective-permute-start | bytes 786440 | tf_op jit(solution)/shard_map/ppermute | solution.py:257
  5.2 24.6 %collective-permute-start.6 = (bf16[64,3584]{1,0:T(8,128)(2,1)}, bf16[64,3584]{1,0:T(8,128)(2,1)S(1)}, u32[]{:S(2)}, u32[]{:S(2)}) collective-permute-start(bf16[64,3584]{1,0:T(8,128)(2,1)} %refs_0_.5), channel_id=1, source_target_pairs={{0,8},{8,0},{16,24},{24,16},{1,9},{9,1},{17,25},{25,17},{2,10},{10... | collective-permute-start | bytes 1376264 | tf_op jit(solution)/shard_map/ppermute | solution.py:257
  7.2 22.3 %collective-permute-start.5 = (bf16[64,3584]{1,0:T(8,128)(2,1)}, bf16[64,3584]{1,0:T(8,128)(2,1)S(1)}, u32[]{:S(2)}, u32[]{:S(2)}) collective-permute-start(bf16[64,3584]{1,0:T(8,128)(2,1)} %refs_0_.5), channel_id=1, source_target_pairs={{0,16},{8,24},{16,0},{24,8},{1,17},{9,25},{17,1},{25,9},{2,18},{10... | collective-permute-start | bytes 1376264 | tf_op jit(solution)/shard_map/ppermute | solution.py:257
  11.2 1.0 %copy-start.1 = (bf16[32,4096]{1,0:T(8,128)(2,1)S(1)}, bf16[32,4096]{1,0:T(8,128)(2,1)}, u32[]{:S(2)}) copy-start(bf16[32,4096]{1,0:T(8,128)(2,1)} %refs_0_.3) | copy-start | bytes 786436
  12.2 7.0 %collective-permute-start.3 = (bf16[64,4096]{1,0:T(8,128)(2,1)S(1)}, bf16[64,4096]{1,0:T(8,128)(2,1)S(1)}, u32[]{:S(2)}, u32[]{:S(2)}) collective-permute-start(bf16[64,4096]{1,0:T(8,128)(2,1)S(1)} %stacked.2.refs_2_.refs_1_), channel_id=1, source_target_pairs={{0,1},{1,0},{2,3},{3,2},{4,5},{5,4},{6,7},{7,6},{8,9},{9,8},{10,11... | collective-permute-start | bytes 1572872 | tf_op jit(solution)/shard_map/ppermute | solution.py:257
  17.3 2.0 %collective-permute-start.4 = (bf16[64,4096]{1,0:T(8,128)(2,1)S(1)}, bf16[64,4096]{1,0:T(8,128)(2,1)S(1)}, u32[]{:S(2)}, u32[]{:S(2)}) collective-permute-start(bf16[64,4096]{1,0:T(8,128)(2,1)S(1)} %stacked.3.refs_2_), channel_id=1, source_target_pairs={{0,1},{1,0},{2,3},{3,2},{4,5},{5,4},{6,7},{7,6},{8,9},{9,8},{10,11... | collective-permute-start | bytes 1572872 | tf_op jit(solution)/shard_map/ppermute | solution.py:257
  25.1 12.0 %collective-permute-start.8 = (s16[128,1152]{1,0:T(8,128)(2,1)S(1)}, s16[128,1152]{1,0:T(8,128)(2,1)S(1)}, u32[]{:S(2)}, u32[]{:S(2)}) collective-permute-start(s16[128,1152]{1,0:T(8,128)(2,1)S(1)} %get-tuple-element.18), channel_id=1, source_target_pairs={{0,8},{8,0},{16,24},{24,16},{1,9},{9,1},{17,25},{25,17},{2,10},{10... | collective-permute-start | bytes 884744 | tf_op jit(solution)/shard_map/ppermute | solution.py:257
  29.5 19.5 %collective-permute-start.7 = (bf16[64,3584]{1,0:T(8,128)(2,1)S(1)}, bf16[64,3584]{1,0:T(8,128)(2,1)S(1)}, u32[]{:S(2)}, u32[]{:S(2)}) collective-permute-start(bf16[64,3584]{1,0:T(8,128)(2,1)S(1)} %handed_on.1.refs_1_), channel_id=1, source_target_pairs={{0,8},{8,0},{16,24},{24,16},{1,9},{9,1},{17,25},{25,17},{2,10},{10... | collective-permute-start | bytes 1376264 | tf_op jit(solution)/shard_map/ppermute | solution.py:257
  37.5 35.5 %collective-permute-start.10 = (s16[64,1152]{1,0:T(8,128)(2,1)S(1)}, s16[64,1152]{1,0:T(8,128)(2,1)S(1)}, u32[]{:S(2)}, u32[]{:S(2)}) collective-permute-start(s16[64,1152]{1,0:T(8,128)(2,1)S(1)} %get-tuple-element.20.refs_3_), channel_id=1, source_target_pairs={{0,16},{8,24},{16,0},{24,8},{1,17},{9,25},{17,1},{25,9},{2,18},{10... | collective-permute-start | bytes 442376 | tf_op jit(solution)/shard_map/ppermute | solution.py:257
  40.2 9.5 %copy-start = (bf16[64,3584]{1,0:T(8,128)(2,1)S(1)}, bf16[64,3584]{1,0:T(8,128)(2,1)}, u32[]{:S(2)}) copy-start(bf16[64,3584]{1,0:T(8,128)(2,1)} %refs_0_.5) | copy-start | bytes 1376260
  40.2 20.3 %collective-permute-start.9 = (s16[128,1664]{1,0:T(8,128)(2,1)S(1)}, s16[128,1664]{1,0:T(8,128)(2,1)S(1)}, u32[]{:S(2)}, u32[]{:S(2)}) collective-permute-start(s16[128,1664]{1,0:T(8,128)(2,1)S(1)} %get-tuple-element.23), channel_id=1, source_target_pairs={{0,8},{8,0},{16,24},{24,16},{1,9},{9,1},{17,25},{25,17},{2,10},{10... | collective-permute-start | bytes 1277960 | tf_op jit(solution)/shard_map/ppermute | solution.py:257
  45.5 27.5 %collective-permute-start.13 = (s16[64,1152]{1,0:T(8,128)(2,1)S(1)}, s16[64,1152]{1,0:T(8,128)(2,1)S(1)}, u32[]{:S(2)}, u32[]{:S(2)}) collective-permute-start(s16[64,1152]{1,0:T(8,128)(2,1)S(1)} %get-tuple-element.28), channel_id=1, source_target_pairs={{0,8},{8,0},{16,24},{24,16},{1,9},{9,1},{17,25},{25,17},{2,10},{10... | collective-permute-start | bytes 442376 | tf_op jit(solution)/shard_map/ppermute | solution.py:257
  47.5 25.5 %collective-permute-start.14 = (s16[64,1152]{1,0:T(8,128)(2,1)S(1)}, s16[64,1152]{1,0:T(8,128)(2,1)S(1)}, u32[]{:S(2)}, u32[]{:S(2)}) collective-permute-start(s16[64,1152]{1,0:T(8,128)(2,1)S(1)} %get-tuple-element.29), channel_id=1, source_target_pairs={{0,24},{8,16},{16,8},{24,0},{1,25},{9,17},{17,9},{25,1},{2,26},{10... | collective-permute-start | bytes 442376 | tf_op jit(solution)/shard_map/ppermute | solution.py:257
  48.9 24.1 %collective-permute-start.12 = (s16[64,1152]{1,0:T(8,128)(2,1)S(1)}, s16[64,1152]{1,0:T(8,128)(2,1)S(1)}, u32[]{:S(2)}, u32[]{:S(2)}) collective-permute-start(s16[64,1152]{1,0:T(8,128)(2,1)S(1)} %get-tuple-element.21.refs_4_), channel_id=1, source_target_pairs={{0,16},{8,24},{16,0},{24,8},{1,17},{9,25},{17,1},{25,9},{2,18},{10... | collective-permute-start | bytes 442376 | tf_op jit(solution)/shard_map/ppermute | solution.py:257
  61.0 16.0 %collective-permute-start.11 = (s16[64,1664]{1,0:T(8,128)(2,1)S(1)}, s16[64,1664]{1,0:T(8,128)(2,1)S(1)}, u32[]{:S(2)}, u32[]{:S(2)}) collective-permute-start(s16[64,1664]{1,0:T(8,128)(2,1)S(1)} %get-tuple-element.24.refs_5_), channel_id=1, source_target_pairs={{0,16},{8,24},{16,0},{24,8},{1,17},{9,25},{17,1},{25,9},{2,18},{10... | collective-permute-start | bytes 638984 | tf_op jit(solution)/shard_map/ppermute | solution.py:257

commit v14 on v13

--- a/solution.py
+++ b/solution.py
@@ -14,7 +14,7 @@
 VMEM_LIMIT = 48 * 1024 * 1024
 SMALL_LIMIT = 8 * 1024 * 1024
 SLOTS = 4
-SHARES = (2, 3, 2)
+SHARES = (3, 2, 2)
 SUB = 256
 
 

time: 78.3 us -> 79.1 us (1.010)
  starting transfers between devices: 22.7 us -> 23.7 us
    ppermute x15, starting transfers between devices: 22.7 us -> 23.7 us  [send(): return lax.ppermute(value, axis, [(i, i ^ flip) for i in range(size)])]
  transfers between devices with their start and end apart: 15 -> 15, of which waited for: 5 -> 8; matrix products, arithmetic and copies ran while one was open for 2% -> 2% of each run, Pallas kernels for 42% -> 42%
where the time goes in v14:
time: 79.1 us; the launch traced here: 79 us
  Pallas kernels  33.9 us (43%)
  starting transfers between devices  23.7 us (30%)
  waiting for transfers between devices  17.9 us (23%)
  local copies, waits for them, and re-layouts  1.8 us (2%)
  other arithmetic  0.91 us (1%)
    ppermute x15, starting transfers between devices, send(): return lax.ppermute(value, axis, [(i, i ^ flip) for i in range(size)])  23.7 us
    pallas_call x3, Pallas kernels, partial_sums(): pl.pallas_call(functools.partial(sums_kernel, 0 if aligned is not None el...  18.4 us
    ppermute x15, waiting for transfers between devices, send(): return lax.ppermute(value, axis, [(i, i ^ flip) for i in range(size)])  17.9 us
    pallas_call x2, Pallas kernels, weight_grads(): pl.pallas_call(functools.partial(weight_kernel, len(pieces), first, len(l...  13.4 us
  transfers between devices with their start and end apart: 15, of which 8 were waited for; matrix products, arithmetic and copies ran while one was open for 2% of the time, Pallas kernels for 42%

profile of v14, /device:TPU:0, one launch (start us, length us, event | category | flops | bytes accessed | tf_op | source)
XLA Modules:
  0.0 79.0 jit_solution(12669433489239848342)
XLA Ops:
  0.6 3.0 %collective-permute-start = (bf16[32,4096]{1,0:T(8,128)(2,1)}, bf16[32,4096]{1,0:T(8,128)(2,1)S(1)}, u32[]{:S(2)}, u32[]{:S(2)}) collective-permute-start(bf16[32,4096]{1,0:T(8,128)(2,1)} %refs_0_.3), channel_id=1, source_target_pairs={{0,2},{1,3},{2,0},{3,1},{4,6},{5,7},{6,4},{7,5},{8,10},{9,11},{10,... | collective-permute-start | bytes 786440 | tf_op jit(solution)/shard_map/ppermute | solution.py:257
  3.6 1.5 %collective-permute-start.2 = (bf16[32,4096]{1,0:T(8,128)(2,1)}, bf16[32,4096]{1,0:T(8,128)(2,1)S(1)}, u32[]{:S(2)}, u32[]{:S(2)}) collective-permute-start(bf16[32,4096]{1,0:T(8,128)(2,1)} %refs_0_.3), channel_id=1, source_target_pairs={{0,4},{1,5},{2,6},{3,7},{4,0},{5,1},{6,2},{7,3},{8,12},{9,13},{10,... | collective-permute-start | bytes 786440 | tf_op jit(solution)/shard_map/ppermute | solution.py:257
  5.2 2.0 %collective-permute-start.6 = (bf16[64,3584]{1,0:T(8,128)(2,1)}, bf16[64,3584]{1,0:T(8,128)(2,1)S(1)}, u32[]{:S(2)}, u32[]{:S(2)}) collective-permute-start(bf16[64,3584]{1,0:T(8,128)(2,1)} %refs_0_.5), channel_id=1, source_target_pairs={{0,8},{8,0},{16,24},{24,16},{1,9},{9,1},{17,25},{25,17},{2,10},{10... | collective-permute-start | bytes 1376264 | tf_op jit(solution)/shard_map/ppermute | solution.py:257
  7.2 2.6 %collective-permute-start.5 = (bf16[64,3584]{1,0:T(8,128)(2,1)}, bf16[64,3584]{1,0:T(8,128)(2,1)S(1)}, u32[]{:S(2)}, u32[]{:S(2)}) collective-permute-start(bf16[64,3584]{1,0:T(8,128)(2,1)} %refs_0_.5), channel_id=1, source_target_pairs={{0,16},{8,24},{16,0},{24,8},{1,17},{9,25},{17,1},{25,9},{2,18},{10... | collective-permute-start | bytes 1376264 | tf_op jit(solution)/shard_map/ppermute | solution.py:257
  9.8 0.7 xor_multiply_fusion
  10.5 0.5 collective-permute-done.refs_1_
  11.0 0.9 %copy-done.1 = bf16[32,4096]{1,0:T(8,128)(2,1)S(1)} copy-done((bf16[32,4096]{1,0:T(8,128)(2,1)S(1)}, bf16[32,4096]{1,0:T(8,128)(2,1)}, u32[]{:S(2)}) %copy-start.1) | copy-done | bytes 262168
  12.0 5.2 %collective-permute-done.2.refs_1_ = bf16[32,4096]{1,0:T(8,128)(2,1)S(1)} collective-permute-done((bf16[32,4096]{1,0:T(8,128)(2,1)}, bf16[32,4096]{1,0:T(8,128)(2,1)S(1)}, u32[]{:S(2)}, u32[]{:S(2)}) %collective-permute-start.2) | collective-permute-done | bytes 262176 | tf_op jit(solution)/shard_map/ppermute | solution.py:257
  17.4 0.8 reshape.24
  18.3 0.1 compare_convert_fusion.refs_0_
  18.5 0.8 collective-permute-done.4.refs_4_
  19.2 8.1 %sums_first.1 = (bf16[256,4096]{1,0:T(8,128)(2,1)S(1)}, f32[128,1536]{1,0:T(8,128)S(1)}, s16[128,1664]{1,0:T(8,128)(2,1)S(1)}) custom-call(bf16[256,256]{1,0:T(8,128)(2,1)S(1)} %compare_convert_fusion.refs_0_, bf16[64,4096]{1,0:T(8,128)(2,1)S(1)} %stacked.2.refs_2_.refs_1_, bf16[64,4096]{1,0:T(8,128)(2,1)S(1)} %stacked.3.refs_2_, ...), custom_call_target="tpu_custom_call" | custom-call | flops 3221225472 | bytes 12582912 | tf_op jit(solution)/shard_map/sums_first/pallas_call | solution.py:128
  27.3 1.6 %collective-permute-start.8 = (s16[128,1664]{1,0:T(8,128)(2,1)S(1)}, s16[128,1664]{1,0:T(8,128)(2,1)S(1)}, u32[]{:S(2)}, u32[]{:S(2)}) collective-permute-start(s16[128,1664]{1,0:T(8,128)(2,1)S(1)} %get-tuple-element.18), channel_id=1, source_target_pairs={{0,8},{8,0},{16,24},{24,16},{1,9},{9,1},{17,25},{25,17},{2,10},{10... | collective-permute-start | bytes 1277960 | tf_op jit(solution)/shard_map/ppermute | solution.py:257
  29.0 0.4 collective-permute-done.5.refs_0_
  29.4 0.4 collective-permute-start.7
  29.8 5.2 %sums_second.1 = (f32[128,1024]{1,0:T(8,128)S(1)}, s16[128,1152]{1,0:T(8,128)(2,1)S(1)}) custom-call(bf16[256,4096]{1,0:T(8,128)(2,1)S(1)} %get-tuple-element.16.refs_1_.refs_0_.aligned_ref, bf16[3584,4096]{1,0:T(8,128)(2,1)} %refs_2_.3, bf16[3584,4096]{1,0:T(8,128)(2,1)} %refs_2_.3, bf16[64,3584]{1,0:T(8,128)(2,1)S(1)} %collective-permute-done.6.refs_3_.refs_2_), custom_call_target="tpu_custom_call" | custom-call | flops 2147483648 | bytes 8388608 | tf_op jit(solution)/shard_map/sums_second/pallas_call | solution.py:128
  34.9 5.1 %collective-permute-done.8.got_ref = s16[128,1664]{1,0:T(8,128)(2,1)S(1)} collective-permute-done((s16[128,1664]{1,0:T(8,128)(2,1)S(1)}, s16[128,1664]{1,0:T(8,128)(2,1)S(1)}, u32[]{:S(2)}, u32[]{:S(2)}) %collective-permute-start.8) | collective-permute-done | bytes 426016 | tf_op jit(solution)/shard_map/ppermute | solution.py:257
  40.1 0.6 fold.2
  40.6 2.7 %collective-permute-start.10 = (s16[64,1664]{1,0:T(8,128)(2,1)S(1)}, s16[64,1664]{1,0:T(8,128)(2,1)S(1)}, u32[]{:S(2)}, u32[]{:S(2)}) collective-permute-start(s16[64,1664]{1,0:T(8,128)(2,1)S(1)} %get-tuple-element.20.refs_3_), channel_id=1, source_target_pairs={{0,16},{8,24},{16,0},{24,8},{1,17},{9,25},{17,1},{25,9},{2,18},{10... | collective-permute-start | bytes 638984 | tf_op jit(solution)/shard_map/ppermute | solution.py:257
  43.3 1.6 %collective-permute-start.9 = (s16[128,1152]{1,0:T(8,128)(2,1)S(1)}, s16[128,1152]{1,0:T(8,128)(2,1)S(1)}, u32[]{:S(2)}, u32[]{:S(2)}) collective-permute-start(s16[128,1152]{1,0:T(8,128)(2,1)S(1)} %get-tuple-element.23), channel_id=1, source_target_pairs={{0,8},{8,0},{16,24},{24,16},{1,9},{9,1},{17,25},{25,17},{2,10},{10... | collective-permute-start | bytes 884744 | tf_op jit(solution)/shard_map/ppermute | solution.py:257
  44.9 5.2 %sums_last.1 = (f32[64,1024]{1,0:T(8,128)S(1)}, s16[64,1152]{1,0:T(8,128)(2,1)S(1)}, s16[64,1152]{1,0:T(8,128)(2,1)S(1)}, s16[64,1152]{1,0:T(8,128)(2,1)S(1)}) custom-call(bf16[256,4096]{1,0:T(8,128)(2,1)S(1)} %get-tuple-element.16.refs_1_.refs_0_.aligned_ref, bf16[3584,4096]{1,0:T(8,128)(2,1)} %refs_2_.3, bf16[3584,4096]{1,0:T(8,128)(2,1)} %refs_2_.3, ...), custom_call_target="tpu_custom_call" | custom-call | flops 2147483648 | bytes 8388608 | tf_op jit(solution)/shard_map/sums_last/pallas_call | solution.py:128
  50.0 0.5 collective-permute-start.13
  50.6 1.3 %collective-permute-start.14 = (s16[64,1152]{1,0:T(8,128)(2,1)S(1)}, s16[64,1152]{1,0:T(8,128)(2,1)S(1)}, u32[]{:S(2)}, u32[]{:S(2)}) collective-permute-start(s16[64,1152]{1,0:T(8,128)(2,1)S(1)} %get-tuple-element.29), channel_id=1, source_target_pairs={{0,24},{8,16},{16,8},{24,0},{1,25},{9,17},{17,9},{25,1},{2,26},{10... | collective-permute-start | bytes 442376 | tf_op jit(solution)/shard_map/ppermute | solution.py:257
  51.9 2.5 %collective-permute-done.7.refs_3_ = bf16[64,3584]{1,0:T(8,128)(2,1)S(1)} collective-permute-done((bf16[64,3584]{1,0:T(8,128)(2,1)S(1)}, bf16[64,3584]{1,0:T(8,128)(2,1)S(1)}, u32[]{:S(2)}, u32[]{:S(2)}) %collective-permute-start.7) | collective-permute-done | bytes 458784 | tf_op jit(solution)/shard_map/ppermute | solution.py:257
  54.5 1.7 %collective-permute-start.12 = (s16[64,1152]{1,0:T(8,128)(2,1)S(1)}, s16[64,1152]{1,0:T(8,128)(2,1)S(1)}, u32[]{:S(2)}, u32[]{:S(2)}) collective-permute-start(s16[64,1152]{1,0:T(8,128)(2,1)S(1)} %get-tuple-element.21.refs_4_), channel_id=1, source_target_pairs={{0,16},{8,24},{16,0},{24,8},{1,17},{9,25},{17,1},{25,9},{2,18},{10... | collective-permute-start | bytes 442376 | tf_op jit(solution)/shard_map/ppermute | solution.py:257
  56.1 5.9 %weight_grads.2.refs_0_.refs_4_ = bf16[3584,4096]{1,0:T(8,128)(2,1)} custom-call(bf16[256,4096]{1,0:T(8,128)(2,1)S(1)} %get-tuple-element.16.refs_1_.refs_0_.aligned_ref, bf16[64,3584]{1,0:T(8,128)(2,1)S(1)} %copy-done, bf16[64,3584]{1,0:T(8,128)(2,1)S(1)} %handed_on.1.refs_1_, bf16[64,3584]{1,0:T(8,128)(2,1)S(1)} %collective-permute-done.6.refs_3_.refs_2_, ...), custom_call_target="tpu_custom_call" | custom-call | flops 3221225472 | bytes 12582912 | tf_op jit(solution)/shard_map/weight_grads/pallas_call | solution.py:178
  62.1 1.8 %collective-permute-done.9.got_ref = s16[128,1152]{1,0:T(8,128)(2,1)S(1)} collective-permute-done((s16[128,1152]{1,0:T(8,128)(2,1)S(1)}, s16[128,1152]{1,0:T(8,128)(2,1)S(1)}, u32[]{:S(2)}, u32[]{:S(2)}) %collective-permute-start.9) | collective-permute-done | bytes 294944 | tf_op jit(solution)/shard_map/ppermute | solution.py:257
  63.9 0.3 fold.3
  64.3 4.6 %collective-permute-start.11 = (s16[64,1152]{1,0:T(8,128)(2,1)S(1)}, s16[64,1152]{1,0:T(8,128)(2,1)S(1)}, u32[]{:S(2)}, u32[]{:S(2)}) collective-permute-start(s16[64,1152]{1,0:T(8,128)(2,1)S(1)} %get-tuple-element.24.refs_5_), channel_id=1, source_target_pairs={{0,16},{8,24},{16,0},{24,8},{1,17},{9,25},{17,1},{25,9},{2,18},{10... | collective-permute-start | bytes 442376 | tf_op jit(solution)/shard_map/ppermute | solution.py:257
  68.8 7.5 %weight_grads.3.refs_8_ = bf16[3584,4096]{1,0:T(8,128)(2,1)} custom-call(bf16[256,4096]{1,0:T(8,128)(2,1)S(1)} %get-tuple-element.16.refs_1_.refs_0_.aligned_ref, bf16[64,3584]{1,0:T(8,128)(2,1)S(1)} %copy-done, bf16[64,3584]{1,0:T(8,128)(2,1)S(1)} %handed_on.1.refs_1_, ...), custom_call_target="tpu_custom_call", output_to_operand_aliasing={{}: (5, {})} | custom-call | flops 4294967296 | bytes 16777216 | tf_op jit(solution)/shard_map/weight_grads/pallas_call | solution.py:178
  76.4 1.5 %collective-permute-done.11.refs_3_ = s16[64,1152]{1,0:T(8,128)(2,1)S(1)} collective-permute-done((s16[64,1152]{1,0:T(8,128)(2,1)S(1)}, s16[64,1152]{1,0:T(8,128)(2,1)S(1)}, u32[]{:S(2)}, u32[]{:S(2)}) %collective-permute-start.11) | collective-permute-done | bytes 147488 | tf_op jit(solution)/shard_map/ppermute | solution.py:257
  77.9 1.1 %totals.1 = bf16[64,3584]{1,0:T(8,128)(2,1)} custom-call(f32[64,1536]{1,0:T(8,128)S(1)} %get-tuple-element.25.refs_0_, s16[64,1664]{1,0:T(8,128)(2,1)S(1)} %collective-permute-done.10.refs_1_, f32[64,1024]{1,0:T(8,128)S(1)} %get-tuple-element.26.refs_2_, s16[64,1152]{1,0:T(8,128)(2,1)S(1)} %collective-permute-done.11.refs_3_, ...), custom_call_target="tpu_custom_call" | custom-call | flops 9175040 | bytes 3211264 | tf_op jit(solution)/shard_map/totals/pallas_call | solution.py:248
  (20 shorter events, 0.5 us)
Async XLA Ops:
  0.6 10.4 %collective-permute-start = (bf16[32,4096]{1,0:T(8,128)(2,1)}, bf16[32,4096]{1,0:T(8,128)(2,1)S(1)}, u32[]{:S(2)}, u32[]{:S(2)}) collective-permute-start(bf16[32,4096]{1,0:T(8,128)(2,1)} %refs_0_.3), channel_id=1, source_target_pairs={{0,2},{1,3},{2,0},{3,1},{4,6},{5,7},{6,4},{7,5},{8,10},{9,11},{10,... | collective-permute-start | bytes 786440 | tf_op jit(solution)/shard_map/ppermute | solution.py:257
  3.6 13.6 %collective-permute-start.2 = (bf16[32,4096]{1,0:T(8,128)(2,1)}, bf16[32,4096]{1,0:T(8,128)(2,1)S(1)}, u32[]{:S(2)}, u32[]{:S(2)}) collective-permute-start(bf16[32,4096]{1,0:T(8,128)(2,1)} %refs_0_.3), channel_id=1, source_target_pairs={{0,4},{1,5},{2,6},{3,7},{4,0},{5,1},{6,2},{7,3},{8,12},{9,13},{10,... | collective-permute-start | bytes 786440 | tf_op jit(solution)/shard_map/ppermute | solution.py:257
  5.2 12.1 %collective-permute-start.1 = (bf16[32,4096]{1,0:T(8,128)(2,1)}, bf16[32,4096]{1,0:T(8,128)(2,1)S(1)}, u32[]{:S(2)}, u32[]{:S(2)}) collective-permute-start(bf16[32,4096]{1,0:T(8,128)(2,1)} %refs_0_.3), channel_id=1, source_target_pairs={{0,6},{1,7},{2,4},{3,5},{4,2},{5,3},{6,0},{7,1},{8,14},{9,15},{10,... | collective-permute-start | bytes 786440 | tf_op jit(solution)/shard_map/ppermute | solution.py:257
  5.2 24.6 %collective-permute-start.6 = (bf16[64,3584]{1,0:T(8,128)(2,1)}, bf16[64,3584]{1,0:T(8,128)(2,1)S(1)}, u32[]{:S(2)}, u32[]{:S(2)}) collective-permute-start(bf16[64,3584]{1,0:T(8,128)(2,1)} %refs_0_.5), channel_id=1, source_target_pairs={{0,8},{8,0},{16,24},{24,16},{1,9},{9,1},{17,25},{25,17},{2,10},{10... | collective-permute-start | bytes 1376264 | tf_op jit(solution)/shard_map/ppermute | solution.py:257
  7.2 22.1 %collective-permute-start.5 = (bf16[64,3584]{1,0:T(8,128)(2,1)}, bf16[64,3584]{1,0:T(8,128)(2,1)S(1)}, u32[]{:S(2)}, u32[]{:S(2)}) collective-permute-start(bf16[64,3584]{1,0:T(8,128)(2,1)} %refs_0_.5), channel_id=1, source_target_pairs={{0,16},{8,24},{16,0},{24,8},{1,17},{9,25},{17,1},{25,9},{2,18},{10... | collective-permute-start | bytes 1376264 | tf_op jit(solution)/shard_map/ppermute | solution.py:257
  11.0 1.0 %copy-start.1 = (bf16[32,4096]{1,0:T(8,128)(2,1)S(1)}, bf16[32,4096]{1,0:T(8,128)(2,1)}, u32[]{:S(2)}) copy-start(bf16[32,4096]{1,0:T(8,128)(2,1)} %refs_0_.3) | copy-start | bytes 786436
  12.0 7.3 %collective-permute-start.3 = (bf16[64,4096]{1,0:T(8,128)(2,1)S(1)}, bf16[64,4096]{1,0:T(8,128)(2,1)S(1)}, u32[]{:S(2)}, u32[]{:S(2)}) collective-permute-start(bf16[64,4096]{1,0:T(8,128)(2,1)S(1)} %stacked.2.refs_2_.refs_1_), channel_id=1, source_target_pairs={{0,1},{1,0},{2,3},{3,2},{4,5},{5,4},{6,7},{7,6},{8,9},{9,8},{10,11... | collective-permute-start | bytes 1572872 | tf_op jit(solution)/shard_map/ppermute | solution.py:257
  17.3 2.0 %collective-permute-start.4 = (bf16[64,4096]{1,0:T(8,128)(2,1)S(1)}, bf16[64,4096]{1,0:T(8,128)(2,1)S(1)}, u32[]{:S(2)}, u32[]{:S(2)}) collective-permute-start(bf16[64,4096]{1,0:T(8,128)(2,1)S(1)} %stacked.3.refs_2_), channel_id=1, source_target_pairs={{0,1},{1,0},{2,3},{3,2},{4,5},{5,4},{6,7},{7,6},{8,9},{9,8},{10,11... | collective-permute-start | bytes 1572872 | tf_op jit(solution)/shard_map/ppermute | solution.py:257
  27.3 12.7 %collective-permute-start.8 = (s16[128,1664]{1,0:T(8,128)(2,1)S(1)}, s16[128,1664]{1,0:T(8,128)(2,1)S(1)}, u32[]{:S(2)}, u32[]{:S(2)}) collective-permute-start(s16[128,1664]{1,0:T(8,128)(2,1)S(1)} %get-tuple-element.18), channel_id=1, source_target_pairs={{0,8},{8,0},{16,24},{24,16},{1,9},{9,1},{17,25},{25,17},{2,10},{10... | collective-permute-start | bytes 1277960 | tf_op jit(solution)/shard_map/ppermute | solution.py:257
  29.4 25.1 %collective-permute-start.7 = (bf16[64,3584]{1,0:T(8,128)(2,1)S(1)}, bf16[64,3584]{1,0:T(8,128)(2,1)S(1)}, u32[]{:S(2)}, u32[]{:S(2)}) collective-permute-start(bf16[64,3584]{1,0:T(8,128)(2,1)S(1)} %handed_on.1.refs_1_), channel_id=1, source_target_pairs={{0,8},{8,0},{16,24},{24,16},{1,9},{9,1},{17,25},{25,17},{2,10},{10... | collective-permute-start | bytes 1376264 | tf_op jit(solution)/shard_map/ppermute | solution.py:257
  40.6 35.7 %collective-permute-start.10 = (s16[64,1664]{1,0:T(8,128)(2,1)S(1)}, s16[64,1664]{1,0:T(8,128)(2,1)S(1)}, u32[]{:S(2)}, u32[]{:S(2)}) collective-permute-start(s16[64,1664]{1,0:T(8,128)(2,1)S(1)} %get-tuple-element.20.refs_3_), channel_id=1, source_target_pairs={{0,16},{8,24},{16,0},{24,8},{1,17},{9,25},{17,1},{25,9},{2,18},{10... | collective-permute-start | bytes 638984 | tf_op jit(solution)/shard_map/ppermute | solution.py:257
  43.3 12.9 %copy-start = (bf16[64,3584]{1,0:T(8,128)(2,1)S(1)}, bf16[64,3584]{1,0:T(8,128)(2,1)}, u32[]{:S(2)}) copy-start(bf16[64,3584]{1,0:T(8,128)(2,1)} %refs_0_.5) | copy-start | bytes 1376260
  43.3 20.6 %collective-permute-start.9 = (s16[128,1152]{1,0:T(8,128)(2,1)S(1)}, s16[128,1152]{1,0:T(8,128)(2,1)S(1)}, u32[]{:S(2)}, u32[]{:S(2)}) collective-permute-start(s16[128,1152]{1,0:T(8,128)(2,1)S(1)} %get-tuple-element.23), channel_id=1, source_target_pairs={{0,8},{8,0},{16,24},{24,16},{1,9},{9,1},{17,25},{25,17},{2,10},{10... | collective-permute-start | bytes 884744 | tf_op jit(solution)/shard_map/ppermute | solution.py:257
  50.0 26.3 %collective-permute-start.13 = (s16[64,1152]{1,0:T(8,128)(2,1)S(1)}, s16[64,1152]{1,0:T(8,128)(2,1)S(1)}, u32[]{:S(2)}, u32[]{:S(2)}) collective-permute-start(s16[64,1152]{1,0:T(8,128)(2,1)S(1)} %get-tuple-element.28), channel_id=1, source_target_pairs={{0,8},{8,0},{16,24},{24,16},{1,9},{9,1},{17,25},{25,17},{2,10},{10... | collective-permute-start | bytes 442376 | tf_op jit(solution)/shard_map/ppermute | solution.py:257
  50.6 25.8 %collective-permute-start.14 = (s16[64,1152]{1,0:T(8,128)(2,1)S(1)}, s16[64,1152]{1,0:T(8,128)(2,1)S(1)}, u32[]{:S(2)}, u32[]{:S(2)}) collective-permute-start(s16[64,1152]{1,0:T(8,128)(2,1)S(1)} %get-tuple-element.29), channel_id=1, source_target_pairs={{0,24},{8,16},{16,8},{24,0},{1,25},{9,17},{17,9},{25,1},{2,26},{10... | collective-permute-start | bytes 442376 | tf_op jit(solution)/shard_map/ppermute | solution.py:257
  54.5 21.9 %collective-permute-start.12 = (s16[64,1152]{1,0:T(8,128)(2,1)S(1)}, s16[64,1152]{1,0:T(8,128)(2,1)S(1)}, u32[]{:S(2)}, u32[]{:S(2)}) collective-permute-start(s16[64,1152]{1,0:T(8,128)(2,1)S(1)} %get-tuple-element.21.refs_4_), channel_id=1, source_target_pairs={{0,16},{8,24},{16,0},{24,8},{1,17},{9,25},{17,1},{25,9},{2,18},{10... | collective-permute-start | bytes 442376 | tf_op jit(solution)/shard_map/ppermute | solution.py:257
  64.3 13.6 %collective-permute-start.11 = (s16[64,1152]{1,0:T(8,128)(2,1)S(1)}, s16[64,1152]{1,0:T(8,128)(2,1)S(1)}, u32[]{:S(2)}, u32[]{:S(2)}) collective-permute-start(s16[64,1152]{1,0:T(8,128)(2,1)S(1)} %get-tuple-element.24.refs_5_), channel_id=1, source_target_pairs={{0,16},{8,24},{16,0},{24,8},{1,17},{9,25},{17,1},{25,9},{2,18},{10... | collective-permute-start | bytes 442376 | tf_op jit(solution)/shard_map/ppermute | solution.py:257

commit v15 on v13

--- a/solution.py
+++ b/solution.py
@@ -8,6 +8,7 @@
 from jax.sharding import PartitionSpec as P
 
 LANES = 128
+LEVEL_ROWS = 16
 STEPS_PER_OCTAVE = 128.0
 TOP = 32766.0
 LEAST = 2.0 ** -120
@@ -37,12 +38,34 @@
 
 
 def decode(codes, levels):
-    scale = jnp.exp2(levels.astype(jnp.int32).astype(jnp.float32) * (1.0 / STEPS_PER_OCTAVE)) * (1.0 / TOP)
-    return codes.astype(jnp.int32).astype(jnp.float32) * scale
-
-
-def to_levels(levels):
-    return levels.astype(jnp.int32).astype(jnp.int16)
+    return codes.astype(jnp.int32).astype(jnp.float32) * (jnp.exp2(levels * (1.0 / STEPS_PER_OCTAVE)) * (1.0 / TOP))
+
+
+def message_shape(rows, width):
+    return (width // LANES * rows + pl.cdiv(rows, LANES) * LEVEL_ROWS, LANES)
+
+
+def turned_levels(levels):
+    blocks = []
+    for at in range(0, levels.shape[0], LANES):
+        block = levels[at:at + LANES]
+        if block.shape[0] < LANES:
+            block = jnp.concatenate([block, jnp.zeros((LANES - block.shape[0], LANES), jnp.float32)], axis=0)
+        blocks.append(block.T[:LEVEL_ROWS])
+    return jnp.concatenate(blocks, axis=0).astype(jnp.int32).astype(jnp.int16)
+
+
+def levels_of(message_ref, rows, width):
+    turned = message_ref[width // LANES * rows:].astype(jnp.int32).astype(jnp.float32)
+    blocks = []
+    for at in range(0, turned.shape[0], LEVEL_ROWS):
+        block = turned[at:at + LEVEL_ROWS]
+        blocks.append(jnp.concatenate([block, jnp.zeros((LANES - LEVEL_ROWS, LANES), jnp.float32)], axis=0).T)
+    return jnp.concatenate(blocks, axis=0)[:rows]
+
+
+def codes_of(message_ref, rows, first, count):
+    return jnp.concatenate([message_ref[at * rows:(at + 1) * rows] for at in range(first, first + count)], axis=1)
 
 
 def params(limit=VMEM_LIMIT):
@@ -77,7 +100,7 @@
     sent = [refs.pop(0) for _ in sent_rows]
     levels_ref, = refs
     step = pl.program_id(0)
-    width = sent[0].shape[1] - LANES
+    per_tile = tile // LANES
 
     @pl.when(step == 0)
     def _():
@@ -89,20 +112,24 @@
     levels = levels_ref[...]
     for part in range(n_blocks):
         at = step * n_blocks + part
-        cols = pl.ds(pl.multiple_of(at * tile, tile), tile)
         values = dot(aligned_ref[...], weights[part][...], ((1,), (1,)))
         for ref, rows in zip(kept, kept_rows):
             ref[:, part * tile:(part + 1) * tile] = values[rows]
         codes, level = encode(values[coded:])
         levels = jnp.where(lane == at, level, levels)
         for ref, rows in zip(sent, sent_rows):
-            ref[:, cols] = codes[rows.start - coded:rows.stop - coded]
+            height = rows.stop - rows.start
+            for col in range(per_tile):
+                here = pl.ds(pl.multiple_of((at * per_tile + col) * height, height), height)
+                ref[here] = codes[rows.start - coded:rows.stop - coded, col * LANES:(col + 1) * LANES]
     levels_ref[...] = levels
 
     @pl.when(step == pl.num_programs(0) - 1)
     def _():
         for ref, rows in zip(sent, sent_rows):
-            ref[:, width:] = to_levels(levels[rows.start - coded:rows.stop - coded])
+            height = rows.stop - rows.start
+            turned = turned_levels(levels[rows.start - coded:rows.stop - coded])
+            ref[ref.shape[0] - turned.shape[0]:] = turned
 
 
 def partial_sums(aligned, align, weight, tile, first, count, kept_rows, sent_rows, later_than, name):
@@ -119,9 +146,9 @@
     in_specs += [pl.BlockSpec((tile, depth), block_at(part)) for part in range(n_blocks)]
     in_specs += [pl.BlockSpec(memory_space=pl.ANY)] * len(later_than)
     out_specs = [pl.BlockSpec((height, n_blocks * tile), lambda i: (0, i)) for height in heights(kept_rows)]
-    out_specs += [pl.BlockSpec((height, width + LANES), whole) for height in heights(sent_rows)]
+    out_specs += [pl.BlockSpec(message_shape(height, width), whole) for height in heights(sent_rows)]
     out_shape = [jax.ShapeDtypeStruct((height, width), jnp.float32) for height in heights(kept_rows)]
-    out_shape += [jax.ShapeDtypeStruct((height, width + LANES), jnp.int16) for height in heights(sent_rows)]
+    out_shape += [jax.ShapeDtypeStruct(message_shape(height, width), jnp.int16) for height in heights(sent_rows)]
     if aligned is None:
         out_specs.insert(0, pl.BlockSpec((total, depth), whole))
         out_shape.insert(0, jax.ShapeDtypeStruct((total, depth), jnp.bfloat16))
@@ -192,20 +219,23 @@
 
 def fold_kernel(n_others, kept_ref, got_ref, *refs):
     next_ref, sent_ref = refs[n_others:n_others + 2]
-    width = kept_ref.shape[1]
+    rows, width = kept_ref.shape
     half = next_ref.shape[0]
     sub = tile_of(width, SUB)
+    per_tile = sub // LANES
     lane = lax.broadcasted_iota(jnp.int32, (half, LANES), 1)
     levels = jnp.zeros(lane.shape, jnp.float32)
-    got_levels = got_ref[:, width:]
+    got_levels = levels_of(got_ref, rows, width)
     for at in range(width // sub):
         cols = slice(at * sub, (at + 1) * sub)
-        total = kept_ref[:, cols] + decode(got_ref[:, cols], got_levels[:, at:at + 1])
+        total = kept_ref[:, cols] + decode(codes_of(got_ref, rows, at * per_tile, per_tile), got_levels[:, at:at + 1])
         next_ref[:, cols] = total[:half]
         codes, level = encode(total[half:])
-        sent_ref[:, cols] = codes
+        for col in range(per_tile):
+            first = (at * per_tile + col) * half
+            sent_ref[first:first + half] = codes[:, col * LANES:(col + 1) * LANES]
         levels = jnp.where(lane == at, level, levels)
-    sent_ref[:, width:] = to_levels(levels)
+    sent_ref[width // LANES * half:] = turned_levels(levels)
 
 
 def fold(kept, got, passed, later_than):
@@ -216,7 +246,7 @@
         functools.partial(fold_kernel, len(others)),
         in_specs=[vmem] * 2 + [anywhere] * len(others),
         out_specs=[vmem] * 2 + [anywhere] * len(passed),
-        out_shape=[jax.ShapeDtypeStruct((rows // 2, width), kept.dtype), jax.ShapeDtypeStruct((rows // 2, got.shape[1]), got.dtype)]
+        out_shape=[jax.ShapeDtypeStruct((rows // 2, width), kept.dtype), jax.ShapeDtypeStruct(message_shape(rows // 2, width), got.dtype)]
         + [jax.ShapeDtypeStruct(array.shape, array.dtype) for array in passed],
         input_output_aliases={2 + at: 2 + at for at in range(len(passed))},
         compiler_params=params(), cost_estimate=cost(kept.size * 20, kept.size * 12), name="fold",
@@ -232,11 +262,13 @@
         kept_ref, got, refs = refs[0], refs[1:count], refs[count:]
         rows, width = kept_ref.shape
         sub = tile_of(width, SUB)
+        per_tile = sub // LANES
+        levels = [levels_of(ref, rows, width) for ref in got]
         for at in range(width // sub):
             cols = slice(at * sub, (at + 1) * sub)
             total = kept_ref[:, cols]
-            for ref in got:
-                total = total + decode(ref[:rows, cols], ref[:rows, width:][:, at:at + 1])
+            for ref, level in zip(got, levels):
+                total = total + decode(codes_of(ref, rows, at * per_tile, per_tile), level[:, at:at + 1])
             out_ref[:, base + at * sub:base + (at + 1) * sub] = total.astype(jnp.bfloat16)
         base += width
 

time: 78.3 us -> 75.7 us (0.967)
  waiting for transfers between devices: 18 us -> 15.9 us
  starting transfers between devices: 22.7 us -> 21.6 us
    ppermute x15, waiting for transfers between devices: 18 us -> 15.9 us  [send(): return lax.ppermute(value, axis, [(i, i ^ flip) for i in range(size)])]
    ppermute x15, starting transfers between devices: 22.7 us -> 21.6 us  [send(): return lax.ppermute(value, axis, [(i, i ^ flip) for i in range(size)])]
  transfers between devices with their start and end apart: 15 -> 15, of which waited for: 5 -> 5; matrix products, arithmetic and copies ran while one was open for 2% -> 2% of each run, Pallas kernels for 42% -> 44%
where the time goes in v15:
time: 75.7 us; the launch traced here: 75.5 us
  Pallas kernels  34.6 us (46%)
  starting transfers between devices  21.6 us (29%)
  waiting for transfers between devices  15.9 us (21%)
  local copies, waits for them, and re-layouts  1.8 us (2%)
  other arithmetic  0.91 us (1%)
  between operations  0.76 us (1%)
    ppermute x15, starting transfers between devices, send(): return lax.ppermute(value, axis, [(i, i ^ flip) for i in range(size)])  21.6 us
    pallas_call x3, Pallas kernels, partial_sums(): pl.pallas_call(functools.partial(sums_kernel, 0 if aligned is not None el...  18.7 us
    ppermute x15, waiting for transfers between devices, send(): return lax.ppermute(value, axis, [(i, i ^ flip) for i in range(size)])  15.9 us
    pallas_call x2, Pallas kernels, weight_grads(): pl.pallas_call(functools.partial(weight_kernel, len(pieces), first, len(l...  13.4 us
  transfers between devices with their start and end apart: 15, of which 5 were waited for; matrix products, arithmetic and copies ran while one was open for 2% of the time, Pallas kernels for 44%

profile of v15, /device:TPU:0, one launch (start us, length us, event | category | flops | bytes accessed | tf_op | source)
XLA Modules:
  0.0 75.5 jit_solution(8160092148120923429)
XLA Ops:
  0.6 3.0 %collective-permute-start = (bf16[32,4096]{1,0:T(8,128)(2,1)}, bf16[32,4096]{1,0:T(8,128)(2,1)S(1)}, u32[]{:S(2)}, u32[]{:S(2)}) collective-permute-start(bf16[32,4096]{1,0:T(8,128)(2,1)} %refs_0_.3), channel_id=1, source_target_pairs={{0,2},{1,3},{2,0},{3,1},{4,6},{5,7},{6,4},{7,5},{8,10},{9,11},{10,... | collective-permute-start | bytes 786440 | tf_op jit(solution)/shard_map/ppermute | solution.py:289
  3.6 1.5 %collective-permute-start.2 = (bf16[32,4096]{1,0:T(8,128)(2,1)}, bf16[32,4096]{1,0:T(8,128)(2,1)S(1)}, u32[]{:S(2)}, u32[]{:S(2)}) collective-permute-start(bf16[32,4096]{1,0:T(8,128)(2,1)} %refs_0_.3), channel_id=1, source_target_pairs={{0,4},{1,5},{2,6},{3,7},{4,0},{5,1},{6,2},{7,3},{8,12},{9,13},{10,... | collective-permute-start | bytes 786440 | tf_op jit(solution)/shard_map/ppermute | solution.py:289
  5.2 2.0 %collective-permute-start.6 = (bf16[64,3584]{1,0:T(8,128)(2,1)}, bf16[64,3584]{1,0:T(8,128)(2,1)S(1)}, u32[]{:S(2)}, u32[]{:S(2)}) collective-permute-start(bf16[64,3584]{1,0:T(8,128)(2,1)} %refs_0_.5), channel_id=1, source_target_pairs={{0,8},{8,0},{16,24},{24,16},{1,9},{9,1},{17,25},{25,17},{2,10},{10... | collective-permute-start | bytes 1376264 | tf_op jit(solution)/shard_map/ppermute | solution.py:289
  7.2 2.6 %collective-permute-start.5 = (bf16[64,3584]{1,0:T(8,128)(2,1)}, bf16[64,3584]{1,0:T(8,128)(2,1)S(1)}, u32[]{:S(2)}, u32[]{:S(2)}) collective-permute-start(bf16[64,3584]{1,0:T(8,128)(2,1)} %refs_0_.5), channel_id=1, source_target_pairs={{0,16},{8,24},{16,0},{24,8},{1,17},{9,25},{17,1},{25,9},{2,18},{10... | collective-permute-start | bytes 1376264 | tf_op jit(solution)/shard_map/ppermute | solution.py:289
  9.8 0.8 %reshape.24 = s32[4,64]{1,0:T(4,128)S(1)} reshape(s32[256]{0:T(256)} %param.8) | data formatting | bytes 2048 | tf_op jit(solution)/shard_map/reshape | solution.py:365
  10.6 0.7 xor_multiply_fusion
  11.2 0.9 %copy-done.1 = bf16[32,4096]{1,0:T(8,128)(2,1)S(1)} copy-done((bf16[32,4096]{1,0:T(8,128)(2,1)S(1)}, bf16[32,4096]{1,0:T(8,128)(2,1)}, u32[]{:S(2)}) %copy-start.1) | copy-done | bytes 262168
  12.2 0.1 collective-permute-start.3
  12.3 4.9 %collective-permute-done.2.refs_1_ = bf16[32,4096]{1,0:T(8,128)(2,1)S(1)} collective-permute-done((bf16[32,4096]{1,0:T(8,128)(2,1)}, bf16[32,4096]{1,0:T(8,128)(2,1)S(1)}, u32[]{:S(2)}, u32[]{:S(2)}) %collective-permute-start.2) | collective-permute-done | bytes 262176 | tf_op jit(solution)/shard_map/ppermute | solution.py:289
  17.3 0.1 collective-permute-start.4
  17.4 0.1 pad_add_fusion
  17.5 0.1 add.40
  17.6 0.1 compare_convert_fusion.refs_0_
  17.7 1.6 %collective-permute-done.4.refs_4_ = bf16[64,4096]{1,0:T(8,128)(2,1)S(1)} collective-permute-done((bf16[64,4096]{1,0:T(8,128)(2,1)S(1)}, bf16[64,4096]{1,0:T(8,128)(2,1)S(1)}, u32[]{:S(2)}, u32[]{:S(2)}) %collective-permute-start.4) | collective-permute-done | bytes 524320 | tf_op jit(solution)/shard_map/ppermute | solution.py:289
  19.2 6.0 %sums_first.1 = (bf16[256,4096]{1,0:T(8,128)(2,1)S(1)}, f32[128,1024]{1,0:T(8,128)S(1)}, s16[1040,128]{1,0:T(8,128)(2,1)S(1)}) custom-call(bf16[256,256]{1,0:T(8,128)(2,1)S(1)} %compare_convert_fusion.refs_0_, bf16[64,4096]{1,0:T(8,128)(2,1)S(1)} %stacked.2.refs_2_.refs_1_, bf16[64,4096]{1,0:T(8,128)(2,1)S(1)} %stacked.3.refs_2_, ...), custom_call_target="tpu_custom_call" | custom-call | flops 2147483648 | bytes 8388608 | tf_op jit(solution)/shard_map/sums_first/pallas_call | solution.py:155
  25.2 1.6 %collective-permute-start.8 = (s16[1040,128]{1,0:T(8,128)(2,1)S(1)}, s16[1040,128]{1,0:T(8,128)(2,1)S(1)}, u32[]{:S(2)}, u32[]{:S(2)}) collective-permute-start(s16[1040,128]{1,0:T(8,128)(2,1)S(1)} %get-tuple-element.18), channel_id=1, source_target_pairs={{0,8},{8,0},{16,24},{24,16},{1,9},{9,1},{17,25},{25,17},{2,10},{10... | collective-permute-start | bytes 798728 | tf_op jit(solution)/shard_map/ppermute | solution.py:289
  26.9 2.6 %collective-permute-done.5.refs_0_ = bf16[64,3584]{1,0:T(8,128)(2,1)S(1)} collective-permute-done((bf16[64,3584]{1,0:T(8,128)(2,1)}, bf16[64,3584]{1,0:T(8,128)(2,1)S(1)}, u32[]{:S(2)}, u32[]{:S(2)}) %collective-permute-start.5) | collective-permute-done | bytes 458784 | tf_op jit(solution)/shard_map/ppermute | solution.py:289
  29.5 0.3 collective-permute-start.7
  29.8 7.4 %sums_second.1 = (f32[128,1536]{1,0:T(8,128)S(1)}, s16[1552,128]{1,0:T(8,128)(2,1)S(1)}) custom-call(bf16[256,4096]{1,0:T(8,128)(2,1)S(1)} %get-tuple-element.16.refs_1_.refs_0_.aligned_ref, bf16[3584,4096]{1,0:T(8,128)(2,1)} %refs_2_.3, bf16[3584,4096]{1,0:T(8,128)(2,1)} %refs_2_.3, bf16[64,3584]{1,0:T(8,128)(2,1)S(1)} %collective-permute-done.6.refs_3_.refs_2_), custom_call_target="tpu_custom_call" | custom-call | flops 3221225472 | bytes 12582912 | tf_op jit(solution)/shard_map/sums_second/pallas_call | solution.py:155
  37.3 0.5 fold.2
  37.7 2.6 %collective-permute-start.10 = (s16[528,128]{1,0:T(8,128)(2,1)S(1)}, s16[528,128]{1,0:T(8,128)(2,1)S(1)}, u32[]{:S(2)}, u32[]{:S(2)}) collective-permute-start(s16[528,128]{1,0:T(8,128)(2,1)S(1)} %get-tuple-element.20.refs_3_), channel_id=1, source_target_pairs={{0,16},{8,24},{16,0},{24,8},{1,17},{9,25},{17,1},{25,9},{2,18},{10... | collective-permute-start | bytes 405512 | tf_op jit(solution)/shard_map/ppermute | solution.py:289
  40.4 5.3 %sums_last.1 = (f32[64,1024]{1,0:T(8,128)S(1)}, s16[528,128]{1,0:T(8,128)(2,1)S(1)}, s16[528,128]{1,0:T(8,128)(2,1)S(1)}, s16[528,128]{1,0:T(8,128)(2,1)S(1)}) custom-call(bf16[256,4096]{1,0:T(8,128)(2,1)S(1)} %get-tuple-element.16.refs_1_.refs_0_.aligned_ref, bf16[3584,4096]{1,0:T(8,128)(2,1)} %refs_2_.3, bf16[3584,4096]{1,0:T(8,128)(2,1)} %refs_2_.3, ...), custom_call_target="tpu_custom_call" | custom-call | flops 2147483648 | bytes 8388608 | tf_op jit(solution)/shard_map/sums_last/pallas_call | solution.py:155
  45.7 2.0 %collective-permute-start.13 = (s16[528,128]{1,0:T(8,128)(2,1)S(1)}, s16[528,128]{1,0:T(8,128)(2,1)S(1)}, u32[]{:S(2)}, u32[]{:S(2)}) collective-permute-start(s16[528,128]{1,0:T(8,128)(2,1)S(1)} %get-tuple-element.28), channel_id=1, source_target_pairs={{0,8},{8,0},{16,24},{24,16},{1,9},{9,1},{17,25},{25,17},{2,10},{10... | collective-permute-start | bytes 405512 | tf_op jit(solution)/shard_map/ppermute | solution.py:289
  47.7 1.4 %collective-permute-start.14 = (s16[528,128]{1,0:T(8,128)(2,1)S(1)}, s16[528,128]{1,0:T(8,128)(2,1)S(1)}, u32[]{:S(2)}, u32[]{:S(2)}) collective-permute-start(s16[528,128]{1,0:T(8,128)(2,1)S(1)} %get-tuple-element.29), channel_id=1, source_target_pairs={{0,24},{8,16},{16,8},{24,0},{1,25},{9,17},{17,9},{25,1},{2,26},{10... | collective-permute-start | bytes 405512 | tf_op jit(solution)/shard_map/ppermute | solution.py:289
  49.2 0.1 collective-permute-start.12
  49.3 5.9 %weight_grads.2.refs_0_.refs_4_ = bf16[3584,4096]{1,0:T(8,128)(2,1)} custom-call(bf16[256,4096]{1,0:T(8,128)(2,1)S(1)} %get-tuple-element.16.refs_1_.refs_0_.aligned_ref, bf16[64,3584]{1,0:T(8,128)(2,1)S(1)} %copy-done, bf16[64,3584]{1,0:T(8,128)(2,1)S(1)} %handed_on.1.refs_1_, bf16[64,3584]{1,0:T(8,128)(2,1)S(1)} %collective-permute-done.6.refs_3_.refs_2_, ...), custom_call_target="tpu_custom_call" | custom-call | flops 3221225472 | bytes 12582912 | tf_op jit(solution)/shard_map/weight_grads/pallas_call | solution.py:205
  55.2 3.6 %collective-permute-done.9.got_ref = s16[1552,128]{1,0:T(8,128)(2,1)S(1)} collective-permute-done((s16[1552,128]{1,0:T(8,128)(2,1)S(1)}, s16[1552,128]{1,0:T(8,128)(2,1)S(1)}, u32[]{:S(2)}, u32[]{:S(2)}) %collective-permute-start.9) | collective-permute-done | bytes 397344 | tf_op jit(solution)/shard_map/ppermute | solution.py:289
  58.8 0.6 fold.3
  59.4 4.1 %collective-permute-start.11 = (s16[784,128]{1,0:T(8,128)(2,1)S(1)}, s16[784,128]{1,0:T(8,128)(2,1)S(1)}, u32[]{:S(2)}, u32[]{:S(2)}) collective-permute-start(s16[784,128]{1,0:T(8,128)(2,1)S(1)} %get-tuple-element.24.refs_5_), channel_id=1, source_target_pairs={{0,16},{8,24},{16,0},{24,8},{1,17},{9,25},{17,1},{25,9},{2,18},{10... | collective-permute-start | bytes 602120 | tf_op jit(solution)/shard_map/ppermute | solution.py:289
  63.6 7.5 %weight_grads.3.refs_8_ = bf16[3584,4096]{1,0:T(8,128)(2,1)} custom-call(bf16[256,4096]{1,0:T(8,128)(2,1)S(1)} %get-tuple-element.16.refs_1_.refs_0_.aligned_ref, bf16[64,3584]{1,0:T(8,128)(2,1)S(1)} %copy-done, bf16[64,3584]{1,0:T(8,128)(2,1)S(1)} %handed_on.1.refs_1_, ...), custom_call_target="tpu_custom_call", output_to_operand_aliasing={{}: (5, {})} | custom-call | flops 4294967296 | bytes 16777216 | tf_op jit(solution)/shard_map/weight_grads/pallas_call | solution.py:205
  71.1 3.2 %collective-permute-done.11.refs_3_ = s16[784,128]{1,0:T(8,128)(2,1)S(1)} collective-permute-done((s16[784,128]{1,0:T(8,128)(2,1)S(1)}, s16[784,128]{1,0:T(8,128)(2,1)S(1)}, u32[]{:S(2)}, u32[]{:S(2)}) %collective-permute-start.11) | collective-permute-done | bytes 200736 | tf_op jit(solution)/shard_map/ppermute | solution.py:289
  74.3 1.2 %totals.1 = bf16[64,3584]{1,0:T(8,128)(2,1)} custom-call(f32[64,1024]{1,0:T(8,128)S(1)} %get-tuple-element.25.refs_0_, s16[528,128]{1,0:T(8,128)(2,1)S(1)} %collective-permute-done.10.refs_1_, f32[64,1536]{1,0:T(8,128)S(1)} %get-tuple-element.26.refs_2_, s16[784,128]{1,0:T(8,128)(2,1)S(1)} %collective-permute-done.11.refs_3_, ...), custom_call_target="tpu_custom_call" | custom-call | flops 9175040 | bytes 3211264 | tf_op jit(solution)/shard_map/totals/pallas_call | solution.py:280
  (20 shorter events, 0.2 us)
Async XLA Ops:
  0.6 10.6 %collective-permute-start = (bf16[32,4096]{1,0:T(8,128)(2,1)}, bf16[32,4096]{1,0:T(8,128)(2,1)S(1)}, u32[]{:S(2)}, u32[]{:S(2)}) collective-permute-start(bf16[32,4096]{1,0:T(8,128)(2,1)} %refs_0_.3), channel_id=1, source_target_pairs={{0,2},{1,3},{2,0},{3,1},{4,6},{5,7},{6,4},{7,5},{8,10},{9,11},{10,... | collective-permute-start | bytes 786440 | tf_op jit(solution)/shard_map/ppermute | solution.py:289
  3.6 13.6 %collective-permute-start.2 = (bf16[32,4096]{1,0:T(8,128)(2,1)}, bf16[32,4096]{1,0:T(8,128)(2,1)S(1)}, u32[]{:S(2)}, u32[]{:S(2)}) collective-permute-start(bf16[32,4096]{1,0:T(8,128)(2,1)} %refs_0_.3), channel_id=1, source_target_pairs={{0,4},{1,5},{2,6},{3,7},{4,0},{5,1},{6,2},{7,3},{8,12},{9,13},{10,... | collective-permute-start | bytes 786440 | tf_op jit(solution)/shard_map/ppermute | solution.py:289
  5.2 12.1 %collective-permute-start.1 = (bf16[32,4096]{1,0:T(8,128)(2,1)}, bf16[32,4096]{1,0:T(8,128)(2,1)S(1)}, u32[]{:S(2)}, u32[]{:S(2)}) collective-permute-start(bf16[32,4096]{1,0:T(8,128)(2,1)} %refs_0_.3), channel_id=1, source_target_pairs={{0,6},{1,7},{2,4},{3,5},{4,2},{5,3},{6,0},{7,1},{8,14},{9,15},{10,... | collective-permute-start | bytes 786440 | tf_op jit(solution)/shard_map/ppermute | solution.py:289
  5.2 24.6 %collective-permute-start.6 = (bf16[64,3584]{1,0:T(8,128)(2,1)}, bf16[64,3584]{1,0:T(8,128)(2,1)S(1)}, u32[]{:S(2)}, u32[]{:S(2)}) collective-permute-start(bf16[64,3584]{1,0:T(8,128)(2,1)} %refs_0_.5), channel_id=1, source_target_pairs={{0,8},{8,0},{16,24},{24,16},{1,9},{9,1},{17,25},{25,17},{2,10},{10... | collective-permute-start | bytes 1376264 | tf_op jit(solution)/shard_map/ppermute | solution.py:289
  7.2 22.2 %collective-permute-start.5 = (bf16[64,3584]{1,0:T(8,128)(2,1)}, bf16[64,3584]{1,0:T(8,128)(2,1)S(1)}, u32[]{:S(2)}, u32[]{:S(2)}) collective-permute-start(bf16[64,3584]{1,0:T(8,128)(2,1)} %refs_0_.5), channel_id=1, source_target_pairs={{0,16},{8,24},{16,0},{24,8},{1,17},{9,25},{17,1},{25,9},{2,18},{10... | collective-permute-start | bytes 1376264 | tf_op jit(solution)/shard_map/ppermute | solution.py:289
  11.2 1.0 %copy-start.1 = (bf16[32,4096]{1,0:T(8,128)(2,1)S(1)}, bf16[32,4096]{1,0:T(8,128)(2,1)}, u32[]{:S(2)}) copy-start(bf16[32,4096]{1,0:T(8,128)(2,1)} %refs_0_.3) | copy-start | bytes 786436
  12.2 7.0 %collective-permute-start.3 = (bf16[64,4096]{1,0:T(8,128)(2,1)S(1)}, bf16[64,4096]{1,0:T(8,128)(2,1)S(1)}, u32[]{:S(2)}, u32[]{:S(2)}) collective-permute-start(bf16[64,4096]{1,0:T(8,128)(2,1)S(1)} %stacked.2.refs_2_.refs_1_), channel_id=1, source_target_pairs={{0,1},{1,0},{2,3},{3,2},{4,5},{5,4},{6,7},{7,6},{8,9},{9,8},{10,11... | collective-permute-start | bytes 1572872 | tf_op jit(solution)/shard_map/ppermute | solution.py:289
  17.3 2.0 %collective-permute-start.4 = (bf16[64,4096]{1,0:T(8,128)(2,1)S(1)}, bf16[64,4096]{1,0:T(8,128)(2,1)S(1)}, u32[]{:S(2)}, u32[]{:S(2)}) collective-permute-start(bf16[64,4096]{1,0:T(8,128)(2,1)S(1)} %stacked.3.refs_2_), channel_id=1, source_target_pairs={{0,1},{1,0},{2,3},{3,2},{4,5},{5,4},{6,7},{7,6},{8,9},{9,8},{10,11... | collective-permute-start | bytes 1572872 | tf_op jit(solution)/shard_map/ppermute | solution.py:289
  25.2 12.0 %collective-permute-start.8 = (s16[1040,128]{1,0:T(8,128)(2,1)S(1)}, s16[1040,128]{1,0:T(8,128)(2,1)S(1)}, u32[]{:S(2)}, u32[]{:S(2)}) collective-permute-start(s16[1040,128]{1,0:T(8,128)(2,1)S(1)} %get-tuple-element.18), channel_id=1, source_target_pairs={{0,8},{8,0},{16,24},{24,16},{1,9},{9,1},{17,25},{25,17},{2,10},{10... | collective-permute-start | bytes 798728 | tf_op jit(solution)/shard_map/ppermute | solution.py:289
  29.5 19.7 %collective-permute-start.7 = (bf16[64,3584]{1,0:T(8,128)(2,1)S(1)}, bf16[64,3584]{1,0:T(8,128)(2,1)S(1)}, u32[]{:S(2)}, u32[]{:S(2)}) collective-permute-start(bf16[64,3584]{1,0:T(8,128)(2,1)S(1)} %handed_on.1.refs_1_), channel_id=1, source_target_pairs={{0,8},{8,0},{16,24},{24,16},{1,9},{9,1},{17,25},{25,17},{2,10},{10... | collective-permute-start | bytes 1376264 | tf_op jit(solution)/shard_map/ppermute | solution.py:289
  37.7 33.4 %collective-permute-start.10 = (s16[528,128]{1,0:T(8,128)(2,1)S(1)}, s16[528,128]{1,0:T(8,128)(2,1)S(1)}, u32[]{:S(2)}, u32[]{:S(2)}) collective-permute-start(s16[528,128]{1,0:T(8,128)(2,1)S(1)} %get-tuple-element.20.refs_3_), channel_id=1, source_target_pairs={{0,16},{8,24},{16,0},{24,8},{1,17},{9,25},{17,1},{25,9},{2,18},{10... | collective-permute-start | bytes 405512 | tf_op jit(solution)/shard_map/ppermute | solution.py:289
  40.4 8.9 %copy-start = (bf16[64,3584]{1,0:T(8,128)(2,1)S(1)}, bf16[64,3584]{1,0:T(8,128)(2,1)}, u32[]{:S(2)}) copy-start(bf16[64,3584]{1,0:T(8,128)(2,1)} %refs_0_.5) | copy-start | bytes 1376260
  40.4 18.4 %collective-permute-start.9 = (s16[1552,128]{1,0:T(8,128)(2,1)S(1)}, s16[1552,128]{1,0:T(8,128)(2,1)S(1)}, u32[]{:S(2)}, u32[]{:S(2)}) collective-permute-start(s16[1552,128]{1,0:T(8,128)(2,1)S(1)} %get-tuple-element.23), channel_id=1, source_target_pairs={{0,8},{8,0},{16,24},{24,16},{1,9},{9,1},{17,25},{25,17},{2,10},{10... | collective-permute-start | bytes 1191944 | tf_op jit(solution)/shard_map/ppermute | solution.py:289
  45.7 25.4 %collective-permute-start.13 = (s16[528,128]{1,0:T(8,128)(2,1)S(1)}, s16[528,128]{1,0:T(8,128)(2,1)S(1)}, u32[]{:S(2)}, u32[]{:S(2)}) collective-permute-start(s16[528,128]{1,0:T(8,128)(2,1)S(1)} %get-tuple-element.28), channel_id=1, source_target_pairs={{0,8},{8,0},{16,24},{24,16},{1,9},{9,1},{17,25},{25,17},{2,10},{10... | collective-permute-start | bytes 405512 | tf_op jit(solution)/shard_map/ppermute | solution.py:289
  47.7 23.4 %collective-permute-start.14 = (s16[528,128]{1,0:T(8,128)(2,1)S(1)}, s16[528,128]{1,0:T(8,128)(2,1)S(1)}, u32[]{:S(2)}, u32[]{:S(2)}) collective-permute-start(s16[528,128]{1,0:T(8,128)(2,1)S(1)} %get-tuple-element.29), channel_id=1, source_target_pairs={{0,24},{8,16},{16,8},{24,0},{1,25},{9,17},{17,9},{25,1},{2,26},{10... | collective-permute-start | bytes 405512 | tf_op jit(solution)/shard_map/ppermute | solution.py:289
  49.2 21.9 %collective-permute-start.12 = (s16[528,128]{1,0:T(8,128)(2,1)S(1)}, s16[528,128]{1,0:T(8,128)(2,1)S(1)}, u32[]{:S(2)}, u32[]{:S(2)}) collective-permute-start(s16[528,128]{1,0:T(8,128)(2,1)S(1)} %get-tuple-element.21.refs_4_), channel_id=1, source_target_pairs={{0,16},{8,24},{16,0},{24,8},{1,17},{9,25},{17,1},{25,9},{2,18},{10... | collective-permute-start | bytes 405512 | tf_op jit(solution)/shard_map/ppermute | solution.py:289
  59.4 14.9 %collective-permute-start.11 = (s16[784,128]{1,0:T(8,128)(2,1)S(1)}, s16[784,128]{1,0:T(8,128)(2,1)S(1)}, u32[]{:S(2)}, u32[]{:S(2)}) collective-permute-start(s16[784,128]{1,0:T(8,128)(2,1)S(1)} %get-tuple-element.24.refs_5_), channel_id=1, source_target_pairs={{0,16},{8,24},{16,0},{24,8},{1,17},{9,25},{17,1},{25,9},{2,18},{10... | collective-permute-start | bytes 602120 | tf_op jit(solution)/shard_map/ppermute | solution.py:289

commit v16 on v15

--- a/solution.py
+++ b/solution.py
@@ -390,13 +390,15 @@
     spans = [slice(at * rows, (at + 1) * rows) for at in range(n_row)]
     _, [kept_c], sent_c = partial_sums(
         aligned, None, down_weight, tile, *parts[2], spans[:1], spans[1:], crossed, "sums_last")
-    done_c = [kept_c] + [send(message, "row", o, n_row) for message, o in zip(sent_c, offsets[1:])]
+    sent_c = dict(zip(offsets[1:], sent_c))
+    done_c = [kept_c] + [send(sent_c[o], "row", o, n_row) for o in offsets[1:] if o != 1]
 
     grad_pieces = [act_pieces[o] for o in offsets]
     grad_tile = tile_of(hidden, 256)
     (first_a, count_a), (first_b, count_b) = part_slices(hidden // grad_tile, (3, 4))
-    grad = weight_grads(aligned, grad_pieces, grad_tile, first_a, count_a, None, sent_c[:1])
+    grad = weight_grads(aligned, grad_pieces, grad_tile, first_a, count_a, None, [sent_c[offsets[1]]])
     done_b, crossed_b, _ = halved(kept_b, got_b, [], [grad], n_row)
+    done_c.append(send(handed_on([sent_c[1]], crossed_b)[0], "row", 1, n_row))
     weight_grad = weight_grads(aligned, grad_pieces, grad_tile, first_b, count_b, grad, crossed_b)
     return weight_grad, totals([done_a, done_b, done_c], [weight_grad])
 

time: 75.7 us -> 74.7 us (0.987)
  waiting for transfers between devices: 15.9 us -> 14.8 us
    ppermute x15, waiting for transfers between devices: 15.9 us -> 14.8 us  [send(): return lax.ppermute(value, axis, [(i, i ^ flip) for i in range(size)])]
  transfers between devices with their start and end apart: 15 -> 15, of which waited for: 5 -> 4; matrix products, arithmetic and copies ran while one was open for 2% -> 2% of each run, Pallas kernels for 44% -> 45%
where the time goes in v16:
time: 74.7 us; the launch traced here: 74.5 us
  Pallas kernels  34.6 us (46%)
  starting transfers between devices  21.7 us (29%)
  waiting for transfers between devices  14.8 us (20%)
  local copies, waits for them, and re-layouts  1.8 us (2%)
  other arithmetic  0.91 us (1%)
  between operations  0.77 us (1%)
    ppermute x15, starting transfers between devices, send(): return lax.ppermute(value, axis, [(i, i ^ flip) for i in range(size)])  21.7 us
    pallas_call x3, Pallas kernels, partial_sums(): pl.pallas_call(functools.partial(sums_kernel, 0 if aligned is not None el...  18.7 us
    ppermute x15, waiting for transfers between devices, send(): return lax.ppermute(value, axis, [(i, i ^ flip) for i in range(size)])  14.8 us
    pallas_call x2, Pallas kernels, weight_grads(): pl.pallas_call(functools.partial(weight_kernel, len(pieces), first, len(l...  13.4 us
  transfers between devices with their start and end apart: 15, of which 4 were waited for; matrix products, arithmetic and copies ran while one was open for 2% of the time, Pallas kernels for 45%

profile of v16, /device:TPU:0, one launch (start us, length us, event | category | flops | bytes accessed | tf_op | source)
XLA Modules:
  0.0 74.5 jit_solution(13356589586496351007)
XLA Ops:
  0.6 3.0 %collective-permute-start = (bf16[32,4096]{1,0:T(8,128)(2,1)}, bf16[32,4096]{1,0:T(8,128)(2,1)S(1)}, u32[]{:S(2)}, u32[]{:S(2)}) collective-permute-start(bf16[32,4096]{1,0:T(8,128)(2,1)} %refs_0_.3), channel_id=1, source_target_pairs={{0,2},{1,3},{2,0},{3,1},{4,6},{5,7},{6,4},{7,5},{8,10},{9,11},{10,... | collective-permute-start | bytes 786440 | tf_op jit(solution)/shard_map/ppermute | solution.py:289
  3.6 1.5 %collective-permute-start.2 = (bf16[32,4096]{1,0:T(8,128)(2,1)}, bf16[32,4096]{1,0:T(8,128)(2,1)S(1)}, u32[]{:S(2)}, u32[]{:S(2)}) collective-permute-start(bf16[32,4096]{1,0:T(8,128)(2,1)} %refs_0_.3), channel_id=1, source_target_pairs={{0,4},{1,5},{2,6},{3,7},{4,0},{5,1},{6,2},{7,3},{8,12},{9,13},{10,... | collective-permute-start | bytes 786440 | tf_op jit(solution)/shard_map/ppermute | solution.py:289
  5.2 2.0 %collective-permute-start.6 = (bf16[64,3584]{1,0:T(8,128)(2,1)}, bf16[64,3584]{1,0:T(8,128)(2,1)S(1)}, u32[]{:S(2)}, u32[]{:S(2)}) collective-permute-start(bf16[64,3584]{1,0:T(8,128)(2,1)} %refs_0_.5), channel_id=1, source_target_pairs={{0,8},{8,0},{16,24},{24,16},{1,9},{9,1},{17,25},{25,17},{2,10},{10... | collective-permute-start | bytes 1376264 | tf_op jit(solution)/shard_map/ppermute | solution.py:289
  7.2 2.6 %collective-permute-start.5 = (bf16[64,3584]{1,0:T(8,128)(2,1)}, bf16[64,3584]{1,0:T(8,128)(2,1)S(1)}, u32[]{:S(2)}, u32[]{:S(2)}) collective-permute-start(bf16[64,3584]{1,0:T(8,128)(2,1)} %refs_0_.5), channel_id=1, source_target_pairs={{0,16},{8,24},{16,0},{24,8},{1,17},{9,25},{17,1},{25,9},{2,18},{10... | collective-permute-start | bytes 1376264 | tf_op jit(solution)/shard_map/ppermute | solution.py:289
  9.8 0.8 %reshape.24 = s32[4,64]{1,0:T(4,128)S(1)} reshape(s32[256]{0:T(256)} %param.8) | data formatting | bytes 2048 | tf_op jit(solution)/shard_map/reshape | solution.py:365
  10.6 0.7 xor_multiply_fusion
  11.2 0.9 %copy-done.1 = bf16[32,4096]{1,0:T(8,128)(2,1)S(1)} copy-done((bf16[32,4096]{1,0:T(8,128)(2,1)S(1)}, bf16[32,4096]{1,0:T(8,128)(2,1)}, u32[]{:S(2)}) %copy-start.1) | copy-done | bytes 262168
  12.2 0.1 collective-permute-start.3
  12.3 4.9 %collective-permute-done.2.refs_1_ = bf16[32,4096]{1,0:T(8,128)(2,1)S(1)} collective-permute-done((bf16[32,4096]{1,0:T(8,128)(2,1)}, bf16[32,4096]{1,0:T(8,128)(2,1)S(1)}, u32[]{:S(2)}, u32[]{:S(2)}) %collective-permute-start.2) | collective-permute-done | bytes 262176 | tf_op jit(solution)/shard_map/ppermute | solution.py:289
  17.3 0.1 collective-permute-start.4
  17.3 0.1 iota_add_fusion
  17.4 0.1 pad_add_fusion
  17.5 0.1 add.40
  17.6 0.1 compare_convert_fusion.refs_0_
  17.7 1.6 %collective-permute-done.4.refs_4_ = bf16[64,4096]{1,0:T(8,128)(2,1)S(1)} collective-permute-done((bf16[64,4096]{1,0:T(8,128)(2,1)S(1)}, bf16[64,4096]{1,0:T(8,128)(2,1)S(1)}, u32[]{:S(2)}, u32[]{:S(2)}) %collective-permute-start.4) | collective-permute-done | bytes 524320 | tf_op jit(solution)/shard_map/ppermute | solution.py:289
  19.2 6.0 %sums_first.1 = (bf16[256,4096]{1,0:T(8,128)(2,1)S(1)}, f32[128,1024]{1,0:T(8,128)S(1)}, s16[1040,128]{1,0:T(8,128)(2,1)S(1)}) custom-call(bf16[256,256]{1,0:T(8,128)(2,1)S(1)} %compare_convert_fusion.refs_0_, bf16[64,4096]{1,0:T(8,128)(2,1)S(1)} %stacked.2.refs_2_.refs_1_, bf16[64,4096]{1,0:T(8,128)(2,1)S(1)} %stacked.3.refs_2_, ...), custom_call_target="tpu_custom_call" | custom-call | flops 2147483648 | bytes 8388608 | tf_op jit(solution)/shard_map/sums_first/pallas_call | solution.py:155
  25.2 1.6 %collective-permute-start.8 = (s16[1040,128]{1,0:T(8,128)(2,1)S(1)}, s16[1040,128]{1,0:T(8,128)(2,1)S(1)}, u32[]{:S(2)}, u32[]{:S(2)}) collective-permute-start(s16[1040,128]{1,0:T(8,128)(2,1)S(1)} %get-tuple-element.18), channel_id=1, source_target_pairs={{0,8},{8,0},{16,24},{24,16},{1,9},{9,1},{17,25},{25,17},{2,10},{10... | collective-permute-start | bytes 798728 | tf_op jit(solution)/shard_map/ppermute | solution.py:289
  26.9 2.6 %collective-permute-done.5.refs_0_ = bf16[64,3584]{1,0:T(8,128)(2,1)S(1)} collective-permute-done((bf16[64,3584]{1,0:T(8,128)(2,1)}, bf16[64,3584]{1,0:T(8,128)(2,1)S(1)}, u32[]{:S(2)}, u32[]{:S(2)}) %collective-permute-start.5) | collective-permute-done | bytes 458784 | tf_op jit(solution)/shard_map/ppermute | solution.py:289
  29.5 0.3 collective-permute-start.7
  29.8 7.4 %sums_second.1 = (f32[128,1536]{1,0:T(8,128)S(1)}, s16[1552,128]{1,0:T(8,128)(2,1)S(1)}) custom-call(bf16[256,4096]{1,0:T(8,128)(2,1)S(1)} %get-tuple-element.16.refs_1_.refs_0_.aligned_ref, bf16[3584,4096]{1,0:T(8,128)(2,1)} %refs_2_.3, bf16[3584,4096]{1,0:T(8,128)(2,1)} %refs_2_.3, bf16[64,3584]{1,0:T(8,128)(2,1)S(1)} %collective-permute-done.6.refs_3_.refs_2_), custom_call_target="tpu_custom_call" | custom-call | flops 3221225472 | bytes 12582912 | tf_op jit(solution)/shard_map/sums_second/pallas_call | solution.py:155
  37.3 0.5 fold.2
  37.7 2.6 %collective-permute-start.10 = (s16[528,128]{1,0:T(8,128)(2,1)S(1)}, s16[528,128]{1,0:T(8,128)(2,1)S(1)}, u32[]{:S(2)}, u32[]{:S(2)}) collective-permute-start(s16[528,128]{1,0:T(8,128)(2,1)S(1)} %get-tuple-element.20.refs_3_), channel_id=1, source_target_pairs={{0,16},{8,24},{16,0},{24,8},{1,17},{9,25},{17,1},{25,9},{2,18},{10... | collective-permute-start | bytes 405512 | tf_op jit(solution)/shard_map/ppermute | solution.py:289
  40.4 5.3 %sums_last.1 = (f32[64,1024]{1,0:T(8,128)S(1)}, s16[528,128]{1,0:T(8,128)(2,1)S(1)}, s16[528,128]{1,0:T(8,128)(2,1)S(1)}, s16[528,128]{1,0:T(8,128)(2,1)S(1)}) custom-call(bf16[256,4096]{1,0:T(8,128)(2,1)S(1)} %get-tuple-element.16.refs_1_.refs_0_.aligned_ref, bf16[3584,4096]{1,0:T(8,128)(2,1)} %refs_2_.3, bf16[3584,4096]{1,0:T(8,128)(2,1)} %refs_2_.3, ...), custom_call_target="tpu_custom_call" | custom-call | flops 2147483648 | bytes 8388608 | tf_op jit(solution)/shard_map/sums_last/pallas_call | solution.py:155
  45.7 1.8 %collective-permute-start.13 = (s16[528,128]{1,0:T(8,128)(2,1)S(1)}, s16[528,128]{1,0:T(8,128)(2,1)S(1)}, u32[]{:S(2)}, u32[]{:S(2)}) collective-permute-start(s16[528,128]{1,0:T(8,128)(2,1)S(1)} %get-tuple-element.28), channel_id=1, source_target_pairs={{0,24},{8,16},{16,8},{24,0},{1,25},{9,17},{17,9},{25,1},{2,26},{10... | collective-permute-start | bytes 405512 | tf_op jit(solution)/shard_map/ppermute | solution.py:289
  47.5 1.7 %collective-permute-start.12 = (s16[528,128]{1,0:T(8,128)(2,1)S(1)}, s16[528,128]{1,0:T(8,128)(2,1)S(1)}, u32[]{:S(2)}, u32[]{:S(2)}) collective-permute-start(s16[528,128]{1,0:T(8,128)(2,1)S(1)} %get-tuple-element.21.refs_4_), channel_id=1, source_target_pairs={{0,16},{8,24},{16,0},{24,8},{1,17},{9,25},{17,1},{25,9},{2,18},{10... | collective-permute-start | bytes 405512 | tf_op jit(solution)/shard_map/ppermute | solution.py:289
  49.2 5.9 %weight_grads.2.refs_0_.refs_4_ = bf16[3584,4096]{1,0:T(8,128)(2,1)} custom-call(bf16[256,4096]{1,0:T(8,128)(2,1)S(1)} %get-tuple-element.16.refs_1_.refs_0_.aligned_ref, bf16[64,3584]{1,0:T(8,128)(2,1)S(1)} %copy-done, bf16[64,3584]{1,0:T(8,128)(2,1)S(1)} %handed_on.2.refs_1_, bf16[64,3584]{1,0:T(8,128)(2,1)S(1)} %collective-permute-done.6.refs_3_.refs_2_, ...), custom_call_target="tpu_custom_call" | custom-call | flops 3221225472 | bytes 12582912 | tf_op jit(solution)/shard_map/weight_grads/pallas_call | solution.py:205
  55.2 5.7 %collective-permute-done.9.got_ref = s16[1552,128]{1,0:T(8,128)(2,1)S(1)} collective-permute-done((s16[1552,128]{1,0:T(8,128)(2,1)S(1)}, s16[1552,128]{1,0:T(8,128)(2,1)S(1)}, u32[]{:S(2)}, u32[]{:S(2)}) %collective-permute-start.9) | collective-permute-done | bytes 397344 | tf_op jit(solution)/shard_map/ppermute | solution.py:289
  60.9 0.6 fold.3
  61.5 1.8 %collective-permute-start.11 = (s16[784,128]{1,0:T(8,128)(2,1)S(1)}, s16[784,128]{1,0:T(8,128)(2,1)S(1)}, u32[]{:S(2)}, u32[]{:S(2)}) collective-permute-start(s16[784,128]{1,0:T(8,128)(2,1)S(1)} %get-tuple-element.24.refs_5_.refs_1_), channel_id=1, source_target_pairs={{0,16},{8,24},{16,0},{24,8},{1,17},{9,25},{17,1},{25,9},{2,18},{10... | collective-permute-start | bytes 602120 | tf_op jit(solution)/shard_map/ppermute | solution.py:289
  63.3 2.5 %collective-permute-start.14 = (s16[528,128]{1,0:T(8,128)(2,1)S(1)}, s16[528,128]{1,0:T(8,128)(2,1)S(1)}, u32[]{:S(2)}, u32[]{:S(2)}) collective-permute-start(s16[528,128]{1,0:T(8,128)(2,1)S(1)} %handed_on.3), channel_id=1, source_target_pairs={{0,8},{8,0},{16,24},{24,16},{1,9},{9,1},{17,25},{25,17},{2,10},{10... | collective-permute-start | bytes 405512 | tf_op jit(solution)/shard_map/ppermute | solution.py:289
  65.8 7.5 %weight_grads.3.refs_8_ = bf16[3584,4096]{1,0:T(8,128)(2,1)} custom-call(bf16[256,4096]{1,0:T(8,128)(2,1)S(1)} %get-tuple-element.16.refs_1_.refs_0_.aligned_ref, bf16[64,3584]{1,0:T(8,128)(2,1)S(1)} %copy-done, bf16[64,3584]{1,0:T(8,128)(2,1)S(1)} %handed_on.2.refs_1_, ...), custom_call_target="tpu_custom_call", output_to_operand_aliasing={{}: (5, {})} | custom-call | flops 4294967296 | bytes 16777216 | tf_op jit(solution)/shard_map/weight_grads/pallas_call | solution.py:205
  73.3 1.2 %totals.1 = bf16[64,3584]{1,0:T(8,128)(2,1)} custom-call(f32[64,1024]{1,0:T(8,128)S(1)} %get-tuple-element.25.refs_0_, s16[528,128]{1,0:T(8,128)(2,1)S(1)} %collective-permute-done.10.refs_1_, f32[64,1536]{1,0:T(8,128)S(1)} %get-tuple-element.26.refs_2_, s16[784,128]{1,0:T(8,128)(2,1)S(1)} %collective-permute-done.11.refs_3_, ...), custom_call_target="tpu_custom_call" | custom-call | flops 9175040 | bytes 3211264 | tf_op jit(solution)/shard_map/totals/pallas_call | solution.py:280
  (21 shorter events, 0.2 us)
Async XLA Ops:
  0.6 10.6 %collective-permute-start = (bf16[32,4096]{1,0:T(8,128)(2,1)}, bf16[32,4096]{1,0:T(8,128)(2,1)S(1)}, u32[]{:S(2)}, u32[]{:S(2)}) collective-permute-start(bf16[32,4096]{1,0:T(8,128)(2,1)} %refs_0_.3), channel_id=1, source_target_pairs={{0,2},{1,3},{2,0},{3,1},{4,6},{5,7},{6,4},{7,5},{8,10},{9,11},{10,... | collective-permute-start | bytes 786440 | tf_op jit(solution)/shard_map/ppermute | solution.py:289
  3.6 13.6 %collective-permute-start.2 = (bf16[32,4096]{1,0:T(8,128)(2,1)}, bf16[32,4096]{1,0:T(8,128)(2,1)S(1)}, u32[]{:S(2)}, u32[]{:S(2)}) collective-permute-start(bf16[32,4096]{1,0:T(8,128)(2,1)} %refs_0_.3), channel_id=1, source_target_pairs={{0,4},{1,5},{2,6},{3,7},{4,0},{5,1},{6,2},{7,3},{8,12},{9,13},{10,... | collective-permute-start | bytes 786440 | tf_op jit(solution)/shard_map/ppermute | solution.py:289
  5.2 12.1 %collective-permute-start.1 = (bf16[32,4096]{1,0:T(8,128)(2,1)}, bf16[32,4096]{1,0:T(8,128)(2,1)S(1)}, u32[]{:S(2)}, u32[]{:S(2)}) collective-permute-start(bf16[32,4096]{1,0:T(8,128)(2,1)} %refs_0_.3), channel_id=1, source_target_pairs={{0,6},{1,7},{2,4},{3,5},{4,2},{5,3},{6,0},{7,1},{8,14},{9,15},{10,... | collective-permute-start | bytes 786440 | tf_op jit(solution)/shard_map/ppermute | solution.py:289
  5.2 24.6 %collective-permute-start.6 = (bf16[64,3584]{1,0:T(8,128)(2,1)}, bf16[64,3584]{1,0:T(8,128)(2,1)S(1)}, u32[]{:S(2)}, u32[]{:S(2)}) collective-permute-start(bf16[64,3584]{1,0:T(8,128)(2,1)} %refs_0_.5), channel_id=1, source_target_pairs={{0,8},{8,0},{16,24},{24,16},{1,9},{9,1},{17,25},{25,17},{2,10},{10... | collective-permute-start | bytes 1376264 | tf_op jit(solution)/shard_map/ppermute | solution.py:289
  7.2 22.2 %collective-permute-start.5 = (bf16[64,3584]{1,0:T(8,128)(2,1)}, bf16[64,3584]{1,0:T(8,128)(2,1)S(1)}, u32[]{:S(2)}, u32[]{:S(2)}) collective-permute-start(bf16[64,3584]{1,0:T(8,128)(2,1)} %refs_0_.5), channel_id=1, source_target_pairs={{0,16},{8,24},{16,0},{24,8},{1,17},{9,25},{17,1},{25,9},{2,18},{10... | collective-permute-start | bytes 1376264 | tf_op jit(solution)/shard_map/ppermute | solution.py:289
  11.2 1.0 %copy-start.1 = (bf16[32,4096]{1,0:T(8,128)(2,1)S(1)}, bf16[32,4096]{1,0:T(8,128)(2,1)}, u32[]{:S(2)}) copy-start(bf16[32,4096]{1,0:T(8,128)(2,1)} %refs_0_.3) | copy-start | bytes 786436
  12.2 7.0 %collective-permute-start.3 = (bf16[64,4096]{1,0:T(8,128)(2,1)S(1)}, bf16[64,4096]{1,0:T(8,128)(2,1)S(1)}, u32[]{:S(2)}, u32[]{:S(2)}) collective-permute-start(bf16[64,4096]{1,0:T(8,128)(2,1)S(1)} %stacked.2.refs_2_.refs_1_), channel_id=1, source_target_pairs={{0,1},{1,0},{2,3},{3,2},{4,5},{5,4},{6,7},{7,6},{8,9},{9,8},{10,11... | collective-permute-start | bytes 1572872 | tf_op jit(solution)/shard_map/ppermute | solution.py:289
  17.3 2.0 %collective-permute-start.4 = (bf16[64,4096]{1,0:T(8,128)(2,1)S(1)}, bf16[64,4096]{1,0:T(8,128)(2,1)S(1)}, u32[]{:S(2)}, u32[]{:S(2)}) collective-permute-start(bf16[64,4096]{1,0:T(8,128)(2,1)S(1)} %stacked.3.refs_2_), channel_id=1, source_target_pairs={{0,1},{1,0},{2,3},{3,2},{4,5},{5,4},{6,7},{7,6},{8,9},{9,8},{10,11... | collective-permute-start | bytes 1572872 | tf_op jit(solution)/shard_map/ppermute | solution.py:289
  25.2 12.0 %collective-permute-start.8 = (s16[1040,128]{1,0:T(8,128)(2,1)S(1)}, s16[1040,128]{1,0:T(8,128)(2,1)S(1)}, u32[]{:S(2)}, u32[]{:S(2)}) collective-permute-start(s16[1040,128]{1,0:T(8,128)(2,1)S(1)} %get-tuple-element.18), channel_id=1, source_target_pairs={{0,8},{8,0},{16,24},{24,16},{1,9},{9,1},{17,25},{25,17},{2,10},{10... | collective-permute-start | bytes 798728 | tf_op jit(solution)/shard_map/ppermute | solution.py:289
  29.5 19.7 %collective-permute-start.7 = (bf16[64,3584]{1,0:T(8,128)(2,1)S(1)}, bf16[64,3584]{1,0:T(8,128)(2,1)S(1)}, u32[]{:S(2)}, u32[]{:S(2)}) collective-permute-start(bf16[64,3584]{1,0:T(8,128)(2,1)S(1)} %handed_on.2.refs_1_), channel_id=1, source_target_pairs={{0,8},{8,0},{16,24},{24,16},{1,9},{9,1},{17,25},{25,17},{2,10},{10... | collective-permute-start | bytes 1376264 | tf_op jit(solution)/shard_map/ppermute | solution.py:289
  37.7 35.5 %collective-permute-start.10 = (s16[528,128]{1,0:T(8,128)(2,1)S(1)}, s16[528,128]{1,0:T(8,128)(2,1)S(1)}, u32[]{:S(2)}, u32[]{:S(2)}) collective-permute-start(s16[528,128]{1,0:T(8,128)(2,1)S(1)} %get-tuple-element.20.refs_3_), channel_id=1, source_target_pairs={{0,16},{8,24},{16,0},{24,8},{1,17},{9,25},{17,1},{25,9},{2,18},{10... | collective-permute-start | bytes 405512 | tf_op jit(solution)/shard_map/ppermute | solution.py:289
  40.4 8.8 %copy-start = (bf16[64,3584]{1,0:T(8,128)(2,1)S(1)}, bf16[64,3584]{1,0:T(8,128)(2,1)}, u32[]{:S(2)}) copy-start(bf16[64,3584]{1,0:T(8,128)(2,1)} %refs_0_.5) | copy-start | bytes 1376260
  40.4 20.5 %collective-permute-start.9 = (s16[1552,128]{1,0:T(8,128)(2,1)S(1)}, s16[1552,128]{1,0:T(8,128)(2,1)S(1)}, u32[]{:S(2)}, u32[]{:S(2)}) collective-permute-start(s16[1552,128]{1,0:T(8,128)(2,1)S(1)} %get-tuple-element.23), channel_id=1, source_target_pairs={{0,8},{8,0},{16,24},{24,16},{1,9},{9,1},{17,25},{25,17},{2,10},{10... | collective-permute-start | bytes 1191944 | tf_op jit(solution)/shard_map/ppermute | solution.py:289
  45.7 27.6 %collective-permute-start.13 = (s16[528,128]{1,0:T(8,128)(2,1)S(1)}, s16[528,128]{1,0:T(8,128)(2,1)S(1)}, u32[]{:S(2)}, u32[]{:S(2)}) collective-permute-start(s16[528,128]{1,0:T(8,128)(2,1)S(1)} %get-tuple-element.28), channel_id=1, source_target_pairs={{0,24},{8,16},{16,8},{24,0},{1,25},{9,17},{17,9},{25,1},{2,26},{10... | collective-permute-start | bytes 405512 | tf_op jit(solution)/shard_map/ppermute | solution.py:289
  47.5 25.8 %collective-permute-start.12 = (s16[528,128]{1,0:T(8,128)(2,1)S(1)}, s16[528,128]{1,0:T(8,128)(2,1)S(1)}, u32[]{:S(2)}, u32[]{:S(2)}) collective-permute-start(s16[528,128]{1,0:T(8,128)(2,1)S(1)} %get-tuple-element.21.refs_4_), channel_id=1, source_target_pairs={{0,16},{8,24},{16,0},{24,8},{1,17},{9,25},{17,1},{25,9},{2,18},{10... | collective-permute-start | bytes 405512 | tf_op jit(solution)/shard_map/ppermute | solution.py:289
  61.5 11.8 %collective-permute-start.11 = (s16[784,128]{1,0:T(8,128)(2,1)S(1)}, s16[784,128]{1,0:T(8,128)(2,1)S(1)}, u32[]{:S(2)}, u32[]{:S(2)}) collective-permute-start(s16[784,128]{1,0:T(8,128)(2,1)S(1)} %get-tuple-element.24.refs_5_.refs_1_), channel_id=1, source_target_pairs={{0,16},{8,24},{16,0},{24,8},{1,17},{9,25},{17,1},{25,9},{2,18},{10... | collective-permute-start | bytes 602120 | tf_op jit(solution)/shard_map/ppermute | solution.py:289
  63.3 10.0 %collective-permute-start.14 = (s16[528,128]{1,0:T(8,128)(2,1)S(1)}, s16[528,128]{1,0:T(8,128)(2,1)S(1)}, u32[]{:S(2)}, u32[]{:S(2)}) collective-permute-start(s16[528,128]{1,0:T(8,128)(2,1)S(1)} %handed_on.3), channel_id=1, source_target_pairs={{0,8},{8,0},{16,24},{24,16},{1,9},{9,1},{17,25},{25,17},{2,10},{10... | collective-permute-start | bytes 405512 | tf_op jit(solution)/shard_map/ppermute | solution.py:289

commit v17 on v16

--- a/solution.py
+++ b/solution.py
@@ -165,7 +165,8 @@
     return aligned, outs[:len(kept_rows)], outs[len(kept_rows):]
 
 
-def weight_kernel(n_pieces, first, n_later, tile, aligned_ref, *refs):
+def weight_kernel(offsets, first, n_later, tile, aligned_ref, *refs):
+    n_pieces = len(offsets)
     pieces = [ref[...] for ref in refs[:n_pieces]]
     out_ref, held_ref, left_sem = refs[n_pieces + n_later:]
     step = pl.program_id(0)
@@ -181,7 +182,7 @@
     def _():
         leave(step - slots).wait()
 
-    left = jnp.concatenate(pieces, axis=0)
+    left = jnp.concatenate([pieces[o] for o in offsets], axis=0)
     depth = aligned_ref.shape[1]
     chunk = tile_of(depth, 1024)
     block = held_ref.at[lax.rem(step, slots)]
@@ -198,12 +199,12 @@
                 leave(last - back).wait()
 
 
-def weight_grads(aligned, pieces, tile, first, count, filled, later_than):
+def weight_grads(aligned, pieces, offsets, tile, first, count, filled, later_than):
     total, depth = aligned.shape
     rows, hidden = pieces[0].shape
     later = ([] if filled is None else [filled]) + list(later_than)
     return pl.pallas_call(
-        functools.partial(weight_kernel, len(pieces), first, len(later), tile),
+        functools.partial(weight_kernel, offsets, first, len(later), tile),
         grid=(count,),
         in_specs=[pl.BlockSpec((total, depth), lambda i: (0, 0))]
         + [pl.BlockSpec((rows, tile), lambda i: (0, i + first))] * len(pieces)
@@ -393,13 +394,13 @@
     sent_c = dict(zip(offsets[1:], sent_c))
     done_c = [kept_c] + [send(sent_c[o], "row", o, n_row) for o in offsets[1:] if o != 1]
 
-    grad_pieces = [act_pieces[o] for o in offsets]
+    grad_pieces = [act_pieces[o] for o in range(n_row)]
     grad_tile = tile_of(hidden, 256)
-    (first_a, count_a), (first_b, count_b) = part_slices(hidden // grad_tile, (3, 4))
-    grad = weight_grads(aligned, grad_pieces, grad_tile, first_a, count_a, None, [sent_c[offsets[1]]])
+    (first_a, count_a), (first_b, count_b) = part_slices(hidden // grad_tile, (5, 2))
+    grad = weight_grads(aligned, grad_pieces, offsets, grad_tile, first_a, count_a, None, [sent_c[offsets[1]]])
     done_b, crossed_b, _ = halved(kept_b, got_b, [], [grad], n_row)
     done_c.append(send(handed_on([sent_c[1]], crossed_b)[0], "row", 1, n_row))
-    weight_grad = weight_grads(aligned, grad_pieces, grad_tile, first_b, count_b, grad, crossed_b)
+    weight_grad = weight_grads(aligned, grad_pieces, offsets, grad_tile, first_b, count_b, grad, crossed_b)
     return weight_grad, totals([done_a, done_b, done_c], [weight_grad])
 
 

time: 74.7 us -> 74.3 us (level)
  waiting for transfers between devices: 14.8 us -> 13.7 us
    ppermute x15, waiting for transfers between devices: 14.8 us -> 13.7 us  [send(): return lax.ppermute(value, axis, [(i, i ^ flip) for i in range(size)])]
    ppermute x15, starting transfers between devices: 21.7 us -> 22.4 us  [send(): return lax.ppermute(value, axis, [(i, i ^ flip) for i in range(size)])]
  transfers between devices with their start and end apart: 15 -> 15, of which waited for: 4 -> 5; matrix products, arithmetic and copies ran while one was open for 2% -> 2% of each run, Pallas kernels for 45% -> 45%
where the time goes in v17:
time: 74.3 us; the launch traced here: 74.1 us
  Pallas kernels  34.5 us (46%)
  starting transfers between devices  22.4 us (30%)
  waiting for transfers between devices  13.7 us (18%)
  local copies, waits for them, and re-layouts  1.8 us (2%)
  other arithmetic  0.91 us (1%)
  between operations  0.76 us (1%)
    ppermute x15, starting transfers between devices, send(): return lax.ppermute(value, axis, [(i, i ^ flip) for i in range(size)])  22.4 us
    pallas_call x3, Pallas kernels, partial_sums(): pl.pallas_call(functools.partial(sums_kernel, 0 if aligned is not None el...  18.7 us
    ppermute x15, waiting for transfers between devices, send(): return lax.ppermute(value, axis, [(i, i ^ flip) for i in range(size)])  13.7 us
    pallas_call x2, Pallas kernels, weight_grads(): pl.pallas_call(functools.partial(weight_kernel, offsets, first, len(later...  13.4 us
  transfers between devices with their start and end apart: 15, of which 5 were waited for; matrix products, arithmetic and copies ran while one was open for 2% of the time, Pallas kernels for 45%

profile of v17, /device:TPU:0, one launch (start us, length us, event | category | flops | bytes accessed | tf_op | source)
XLA Modules:
  0.0 74.1 jit_solution(2333035552089214354)
XLA Ops:
  0.6 3.0 %collective-permute-start = (bf16[32,4096]{1,0:T(8,128)(2,1)}, bf16[32,4096]{1,0:T(8,128)(2,1)S(1)}, u32[]{:S(2)}, u32[]{:S(2)}) collective-permute-start(bf16[32,4096]{1,0:T(8,128)(2,1)} %refs_0_.3), channel_id=1, source_target_pairs={{0,2},{1,3},{2,0},{3,1},{4,6},{5,7},{6,4},{7,5},{8,10},{9,11},{10,... | collective-permute-start | bytes 786440 | tf_op jit(solution)/shard_map/ppermute | solution.py:290
  3.6 1.5 %collective-permute-start.2 = (bf16[32,4096]{1,0:T(8,128)(2,1)}, bf16[32,4096]{1,0:T(8,128)(2,1)S(1)}, u32[]{:S(2)}, u32[]{:S(2)}) collective-permute-start(bf16[32,4096]{1,0:T(8,128)(2,1)} %refs_0_.3), channel_id=1, source_target_pairs={{0,4},{1,5},{2,6},{3,7},{4,0},{5,1},{6,2},{7,3},{8,12},{9,13},{10,... | collective-permute-start | bytes 786440 | tf_op jit(solution)/shard_map/ppermute | solution.py:290
  5.2 3.0 %collective-permute-start.6 = (bf16[64,3584]{1,0:T(8,128)(2,1)}, bf16[64,3584]{1,0:T(8,128)(2,1)S(1)}, u32[]{:S(2)}, u32[]{:S(2)}) collective-permute-start(bf16[64,3584]{1,0:T(8,128)(2,1)} %refs_0_.5), channel_id=1, source_target_pairs={{0,16},{8,24},{16,0},{24,8},{1,17},{9,25},{17,1},{25,9},{2,18},{10... | collective-permute-start | bytes 1376264 | tf_op jit(solution)/shard_map/ppermute | solution.py:290
  8.2 1.6 %collective-permute-start.5 = (bf16[64,3584]{1,0:T(8,128)(2,1)}, bf16[64,3584]{1,0:T(8,128)(2,1)S(1)}, u32[]{:S(2)}, u32[]{:S(2)}) collective-permute-start(bf16[64,3584]{1,0:T(8,128)(2,1)} %refs_0_.5), channel_id=1, source_target_pairs={{0,8},{8,0},{16,24},{24,16},{1,9},{9,1},{17,25},{25,17},{2,10},{10... | collective-permute-start | bytes 1376264 | tf_op jit(solution)/shard_map/ppermute | solution.py:290
  9.8 0.8 %reshape.24 = s32[4,64]{1,0:T(4,128)S(1)} reshape(s32[256]{0:T(256)} %param.8) | data formatting | bytes 2048 | tf_op jit(solution)/shard_map/reshape | solution.py:366
  10.6 0.7 xor_multiply_fusion
  11.2 0.9 %copy-done.1 = bf16[32,4096]{1,0:T(8,128)(2,1)S(1)} copy-done((bf16[32,4096]{1,0:T(8,128)(2,1)S(1)}, bf16[32,4096]{1,0:T(8,128)(2,1)}, u32[]{:S(2)}) %copy-start.1) | copy-done | bytes 262168
  12.2 0.1 collective-permute-start.3
  12.3 4.9 %collective-permute-done.2.refs_1_ = bf16[32,4096]{1,0:T(8,128)(2,1)S(1)} collective-permute-done((bf16[32,4096]{1,0:T(8,128)(2,1)}, bf16[32,4096]{1,0:T(8,128)(2,1)S(1)}, u32[]{:S(2)}, u32[]{:S(2)}) %collective-permute-start.2) | collective-permute-done | bytes 262176 | tf_op jit(solution)/shard_map/ppermute | solution.py:290
  17.3 0.1 collective-permute-start.4
  17.4 0.1 pad_add_fusion
  17.5 0.1 add.40
  17.6 0.1 compare_convert_fusion.refs_0_
  17.7 1.6 %collective-permute-done.4.refs_4_ = bf16[64,4096]{1,0:T(8,128)(2,1)S(1)} collective-permute-done((bf16[64,4096]{1,0:T(8,128)(2,1)S(1)}, bf16[64,4096]{1,0:T(8,128)(2,1)S(1)}, u32[]{:S(2)}, u32[]{:S(2)}) %collective-permute-start.4) | collective-permute-done | bytes 524320 | tf_op jit(solution)/shard_map/ppermute | solution.py:290
  19.2 6.0 %sums_first.1 = (bf16[256,4096]{1,0:T(8,128)(2,1)S(1)}, f32[128,1024]{1,0:T(8,128)S(1)}, s16[1040,128]{1,0:T(8,128)(2,1)S(1)}) custom-call(bf16[256,256]{1,0:T(8,128)(2,1)S(1)} %compare_convert_fusion.refs_0_, bf16[64,4096]{1,0:T(8,128)(2,1)S(1)} %stacked.2.refs_2_.refs_1_, bf16[64,4096]{1,0:T(8,128)(2,1)S(1)} %stacked.3.refs_2_, ...), custom_call_target="tpu_custom_call" | custom-call | flops 2147483648 | bytes 8388608 | tf_op jit(solution)/shard_map/sums_first/pallas_call | solution.py:155
  25.2 1.6 %collective-permute-start.8 = (s16[1040,128]{1,0:T(8,128)(2,1)S(1)}, s16[1040,128]{1,0:T(8,128)(2,1)S(1)}, u32[]{:S(2)}, u32[]{:S(2)}) collective-permute-start(s16[1040,128]{1,0:T(8,128)(2,1)S(1)} %get-tuple-element.18), channel_id=1, source_target_pairs={{0,8},{8,0},{16,24},{24,16},{1,9},{9,1},{17,25},{25,17},{2,10},{10... | collective-permute-start | bytes 798728 | tf_op jit(solution)/shard_map/ppermute | solution.py:290
  26.9 1.2 %collective-permute-done.6.refs_0_ = bf16[64,3584]{1,0:T(8,128)(2,1)S(1)} collective-permute-done((bf16[64,3584]{1,0:T(8,128)(2,1)}, bf16[64,3584]{1,0:T(8,128)(2,1)S(1)}, u32[]{:S(2)}, u32[]{:S(2)}) %collective-permute-start.6) | collective-permute-done | bytes 458784 | tf_op jit(solution)/shard_map/ppermute | solution.py:290
  28.0 0.7 collective-permute-start.7
  28.8 7.4 %sums_second.1 = (f32[128,1536]{1,0:T(8,128)S(1)}, s16[1552,128]{1,0:T(8,128)(2,1)S(1)}) custom-call(bf16[256,4096]{1,0:T(8,128)(2,1)S(1)} %get-tuple-element.16.refs_1_.refs_0_.aligned_ref, bf16[3584,4096]{1,0:T(8,128)(2,1)} %refs_2_.3, bf16[3584,4096]{1,0:T(8,128)(2,1)} %refs_2_.3, bf16[64,3584]{1,0:T(8,128)(2,1)S(1)} %collective-permute-done.5.refs_3_.refs_1_), custom_call_target="tpu_custom_call" | custom-call | flops 3221225472 | bytes 12582912 | tf_op jit(solution)/shard_map/sums_second/pallas_call | solution.py:155
  36.2 0.5 fold.2
  36.7 3.3 %collective-permute-start.10 = (s16[528,128]{1,0:T(8,128)(2,1)S(1)}, s16[528,128]{1,0:T(8,128)(2,1)S(1)}, u32[]{:S(2)}, u32[]{:S(2)}) collective-permute-start(s16[528,128]{1,0:T(8,128)(2,1)S(1)} %get-tuple-element.20.refs_3_), channel_id=1, source_target_pairs={{0,16},{8,24},{16,0},{24,8},{1,17},{9,25},{17,1},{25,9},{2,18},{10... | collective-permute-start | bytes 405512 | tf_op jit(solution)/shard_map/ppermute | solution.py:290
  40.0 5.3 %sums_last.1 = (f32[64,1024]{1,0:T(8,128)S(1)}, s16[528,128]{1,0:T(8,128)(2,1)S(1)}, s16[528,128]{1,0:T(8,128)(2,1)S(1)}, s16[528,128]{1,0:T(8,128)(2,1)S(1)}) custom-call(bf16[256,4096]{1,0:T(8,128)(2,1)S(1)} %get-tuple-element.16.refs_1_.refs_0_.aligned_ref, bf16[3584,4096]{1,0:T(8,128)(2,1)} %refs_2_.3, bf16[3584,4096]{1,0:T(8,128)(2,1)} %refs_2_.3, ...), custom_call_target="tpu_custom_call" | custom-call | flops 2147483648 | bytes 8388608 | tf_op jit(solution)/shard_map/sums_last/pallas_call | solution.py:155
  45.4 1.6 %collective-permute-start.13 = (s16[528,128]{1,0:T(8,128)(2,1)S(1)}, s16[528,128]{1,0:T(8,128)(2,1)S(1)}, u32[]{:S(2)}, u32[]{:S(2)}) collective-permute-start(s16[528,128]{1,0:T(8,128)(2,1)S(1)} %get-tuple-element.28), channel_id=1, source_target_pairs={{0,24},{8,16},{16,8},{24,0},{1,25},{9,17},{17,9},{25,1},{2,26},{10... | collective-permute-start | bytes 405512 | tf_op jit(solution)/shard_map/ppermute | solution.py:290
  46.9 1.9 %collective-permute-start.12 = (s16[528,128]{1,0:T(8,128)(2,1)S(1)}, s16[528,128]{1,0:T(8,128)(2,1)S(1)}, u32[]{:S(2)}, u32[]{:S(2)}) collective-permute-start(s16[528,128]{1,0:T(8,128)(2,1)S(1)} %get-tuple-element.21.refs_4_), channel_id=1, source_target_pairs={{0,16},{8,24},{16,0},{24,8},{1,17},{9,25},{17,1},{25,9},{2,18},{10... | collective-permute-start | bytes 405512 | tf_op jit(solution)/shard_map/ppermute | solution.py:290
  48.9 9.0 %weight_grads.2.refs_0_.refs_4_ = bf16[3584,4096]{1,0:T(8,128)(2,1)} custom-call(bf16[256,4096]{1,0:T(8,128)(2,1)S(1)} %get-tuple-element.16.refs_1_.refs_0_.aligned_ref, bf16[64,3584]{1,0:T(8,128)(2,1)S(1)} %copy-done, bf16[64,3584]{1,0:T(8,128)(2,1)S(1)} %collective-permute-done.5.refs_3_.refs_1_, bf16[64,3584]{1,0:T(8,128)(2,1)S(1)} %handed_on.2.refs_2_, ...), custom_call_target="tpu_custom_call" | custom-call | flops 5368709120 | bytes 20971520 | tf_op jit(solution)/shard_map/weight_grads/pallas_call | solution.py:206
  57.9 3.1 %collective-permute-done.9.got_ref = s16[1552,128]{1,0:T(8,128)(2,1)S(1)} collective-permute-done((s16[1552,128]{1,0:T(8,128)(2,1)S(1)}, s16[1552,128]{1,0:T(8,128)(2,1)S(1)}, u32[]{:S(2)}, u32[]{:S(2)}) %collective-permute-start.9) | collective-permute-done | bytes 397344 | tf_op jit(solution)/shard_map/ppermute | solution.py:290
  61.0 0.6 fold.3
  61.6 1.5 %collective-permute-start.11 = (s16[784,128]{1,0:T(8,128)(2,1)S(1)}, s16[784,128]{1,0:T(8,128)(2,1)S(1)}, u32[]{:S(2)}, u32[]{:S(2)}) collective-permute-start(s16[784,128]{1,0:T(8,128)(2,1)S(1)} %get-tuple-element.24.refs_5_.refs_1_), channel_id=1, source_target_pairs={{0,16},{8,24},{16,0},{24,8},{1,17},{9,25},{17,1},{25,9},{2,18},{10... | collective-permute-start | bytes 602120 | tf_op jit(solution)/shard_map/ppermute | solution.py:290
  63.1 2.5 %collective-permute-start.14 = (s16[528,128]{1,0:T(8,128)(2,1)S(1)}, s16[528,128]{1,0:T(8,128)(2,1)S(1)}, u32[]{:S(2)}, u32[]{:S(2)}) collective-permute-start(s16[528,128]{1,0:T(8,128)(2,1)S(1)} %handed_on.3), channel_id=1, source_target_pairs={{0,8},{8,0},{16,24},{24,16},{1,9},{9,1},{17,25},{25,17},{2,10},{10... | collective-permute-start | bytes 405512 | tf_op jit(solution)/shard_map/ppermute | solution.py:290
  65.6 4.4 %weight_grads.3.refs_8_ = bf16[3584,4096]{1,0:T(8,128)(2,1)} custom-call(bf16[256,4096]{1,0:T(8,128)(2,1)S(1)} %get-tuple-element.16.refs_1_.refs_0_.aligned_ref, bf16[64,3584]{1,0:T(8,128)(2,1)S(1)} %copy-done, bf16[64,3584]{1,0:T(8,128)(2,1)S(1)} %collective-permute-done.5.refs_3_.refs_1_, ...), custom_call_target="tpu_custom_call", output_to_operand_aliasing={{}: (5, {})} | custom-call | flops 2147483648 | bytes 8388608 | tf_op jit(solution)/shard_map/weight_grads/pallas_call | solution.py:206
  70.1 2.9 %collective-permute-done.11.refs_3_ = s16[784,128]{1,0:T(8,128)(2,1)S(1)} collective-permute-done((s16[784,128]{1,0:T(8,128)(2,1)S(1)}, s16[784,128]{1,0:T(8,128)(2,1)S(1)}, u32[]{:S(2)}, u32[]{:S(2)}) %collective-permute-start.11) | collective-permute-done | bytes 200736 | tf_op jit(solution)/shard_map/ppermute | solution.py:290
  72.9 1.2 %totals.1 = bf16[64,3584]{1,0:T(8,128)(2,1)} custom-call(f32[64,1024]{1,0:T(8,128)S(1)} %get-tuple-element.25.refs_0_, s16[528,128]{1,0:T(8,128)(2,1)S(1)} %collective-permute-done.10.refs_1_, f32[64,1536]{1,0:T(8,128)S(1)} %get-tuple-element.26.refs_2_, s16[784,128]{1,0:T(8,128)(2,1)S(1)} %collective-permute-done.11.refs_3_, ...), custom_call_target="tpu_custom_call" | custom-call | flops 9175040 | bytes 3211264 | tf_op jit(solution)/shard_map/totals/pallas_call | solution.py:281
  (21 shorter events, 0.2 us)
Async XLA Ops:
  0.6 10.6 %collective-permute-start = (bf16[32,4096]{1,0:T(8,128)(2,1)}, bf16[32,4096]{1,0:T(8,128)(2,1)S(1)}, u32[]{:S(2)}, u32[]{:S(2)}) collective-permute-start(bf16[32,4096]{1,0:T(8,128)(2,1)} %refs_0_.3), channel_id=1, source_target_pairs={{0,2},{1,3},{2,0},{3,1},{4,6},{5,7},{6,4},{7,5},{8,10},{9,11},{10,... | collective-permute-start | bytes 786440 | tf_op jit(solution)/shard_map/ppermute | solution.py:290
  3.6 13.6 %collective-permute-start.2 = (bf16[32,4096]{1,0:T(8,128)(2,1)}, bf16[32,4096]{1,0:T(8,128)(2,1)S(1)}, u32[]{:S(2)}, u32[]{:S(2)}) collective-permute-start(bf16[32,4096]{1,0:T(8,128)(2,1)} %refs_0_.3), channel_id=1, source_target_pairs={{0,4},{1,5},{2,6},{3,7},{4,0},{5,1},{6,2},{7,3},{8,12},{9,13},{10,... | collective-permute-start | bytes 786440 | tf_op jit(solution)/shard_map/ppermute | solution.py:290
  5.2 12.1 %collective-permute-start.1 = (bf16[32,4096]{1,0:T(8,128)(2,1)}, bf16[32,4096]{1,0:T(8,128)(2,1)S(1)}, u32[]{:S(2)}, u32[]{:S(2)}) collective-permute-start(bf16[32,4096]{1,0:T(8,128)(2,1)} %refs_0_.3), channel_id=1, source_target_pairs={{0,6},{1,7},{2,4},{3,5},{4,2},{5,3},{6,0},{7,1},{8,14},{9,15},{10,... | collective-permute-start | bytes 786440 | tf_op jit(solution)/shard_map/ppermute | solution.py:290
  5.2 22.9 %collective-permute-start.6 = (bf16[64,3584]{1,0:T(8,128)(2,1)}, bf16[64,3584]{1,0:T(8,128)(2,1)S(1)}, u32[]{:S(2)}, u32[]{:S(2)}) collective-permute-start(bf16[64,3584]{1,0:T(8,128)(2,1)} %refs_0_.5), channel_id=1, source_target_pairs={{0,16},{8,24},{16,0},{24,8},{1,17},{9,25},{17,1},{25,9},{2,18},{10... | collective-permute-start | bytes 1376264 | tf_op jit(solution)/shard_map/ppermute | solution.py:290
  8.2 20.6 %collective-permute-start.5 = (bf16[64,3584]{1,0:T(8,128)(2,1)}, bf16[64,3584]{1,0:T(8,128)(2,1)S(1)}, u32[]{:S(2)}, u32[]{:S(2)}) collective-permute-start(bf16[64,3584]{1,0:T(8,128)(2,1)} %refs_0_.5), channel_id=1, source_target_pairs={{0,8},{8,0},{16,24},{24,16},{1,9},{9,1},{17,25},{25,17},{2,10},{10... | collective-permute-start | bytes 1376264 | tf_op jit(solution)/shard_map/ppermute | solution.py:290
  11.2 1.0 %copy-start.1 = (bf16[32,4096]{1,0:T(8,128)(2,1)S(1)}, bf16[32,4096]{1,0:T(8,128)(2,1)}, u32[]{:S(2)}) copy-start(bf16[32,4096]{1,0:T(8,128)(2,1)} %refs_0_.3) | copy-start | bytes 786436
  12.2 7.0 %collective-permute-start.3 = (bf16[64,4096]{1,0:T(8,128)(2,1)S(1)}, bf16[64,4096]{1,0:T(8,128)(2,1)S(1)}, u32[]{:S(2)}, u32[]{:S(2)}) collective-permute-start(bf16[64,4096]{1,0:T(8,128)(2,1)S(1)} %stacked.2.refs_2_.refs_1_), channel_id=1, source_target_pairs={{0,1},{1,0},{2,3},{3,2},{4,5},{5,4},{6,7},{7,6},{8,9},{9,8},{10,11... | collective-permute-start | bytes 1572872 | tf_op jit(solution)/shard_map/ppermute | solution.py:290
  17.3 2.0 %collective-permute-start.4 = (bf16[64,4096]{1,0:T(8,128)(2,1)S(1)}, bf16[64,4096]{1,0:T(8,128)(2,1)S(1)}, u32[]{:S(2)}, u32[]{:S(2)}) collective-permute-start(bf16[64,4096]{1,0:T(8,128)(2,1)S(1)} %stacked.3.refs_2_), channel_id=1, source_target_pairs={{0,1},{1,0},{2,3},{3,2},{4,5},{5,4},{6,7},{7,6},{8,9},{9,8},{10,11... | collective-permute-start | bytes 1572872 | tf_op jit(solution)/shard_map/ppermute | solution.py:290
  25.2 11.0 %collective-permute-start.8 = (s16[1040,128]{1,0:T(8,128)(2,1)S(1)}, s16[1040,128]{1,0:T(8,128)(2,1)S(1)}, u32[]{:S(2)}, u32[]{:S(2)}) collective-permute-start(s16[1040,128]{1,0:T(8,128)(2,1)S(1)} %get-tuple-element.18), channel_id=1, source_target_pairs={{0,8},{8,0},{16,24},{24,16},{1,9},{9,1},{17,25},{25,17},{2,10},{10... | collective-permute-start | bytes 798728 | tf_op jit(solution)/shard_map/ppermute | solution.py:290
  28.0 20.8 %collective-permute-start.7 = (bf16[64,3584]{1,0:T(8,128)(2,1)S(1)}, bf16[64,3584]{1,0:T(8,128)(2,1)S(1)}, u32[]{:S(2)}, u32[]{:S(2)}) collective-permute-start(bf16[64,3584]{1,0:T(8,128)(2,1)S(1)} %handed_on.2.refs_2_), channel_id=1, source_target_pairs={{0,8},{8,0},{16,24},{24,16},{1,9},{9,1},{17,25},{25,17},{2,10},{10... | collective-permute-start | bytes 1376264 | tf_op jit(solution)/shard_map/ppermute | solution.py:290
  36.7 33.3 %collective-permute-start.10 = (s16[528,128]{1,0:T(8,128)(2,1)S(1)}, s16[528,128]{1,0:T(8,128)(2,1)S(1)}, u32[]{:S(2)}, u32[]{:S(2)}) collective-permute-start(s16[528,128]{1,0:T(8,128)(2,1)S(1)} %get-tuple-element.20.refs_3_), channel_id=1, source_target_pairs={{0,16},{8,24},{16,0},{24,8},{1,17},{9,25},{17,1},{25,9},{2,18},{10... | collective-permute-start | bytes 405512 | tf_op jit(solution)/shard_map/ppermute | solution.py:290
  40.0 8.8 %copy-start = (bf16[64,3584]{1,0:T(8,128)(2,1)S(1)}, bf16[64,3584]{1,0:T(8,128)(2,1)}, u32[]{:S(2)}) copy-start(bf16[64,3584]{1,0:T(8,128)(2,1)} %refs_0_.5) | copy-start | bytes 1376260
  40.0 21.0 %collective-permute-start.9 = (s16[1552,128]{1,0:T(8,128)(2,1)S(1)}, s16[1552,128]{1,0:T(8,128)(2,1)S(1)}, u32[]{:S(2)}, u32[]{:S(2)}) collective-permute-start(s16[1552,128]{1,0:T(8,128)(2,1)S(1)} %get-tuple-element.23), channel_id=1, source_target_pairs={{0,8},{8,0},{16,24},{24,16},{1,9},{9,1},{17,25},{25,17},{2,10},{10... | collective-permute-start | bytes 1191944 | tf_op jit(solution)/shard_map/ppermute | solution.py:290
  45.4 24.7 %collective-permute-start.13 = (s16[528,128]{1,0:T(8,128)(2,1)S(1)}, s16[528,128]{1,0:T(8,128)(2,1)S(1)}, u32[]{:S(2)}, u32[]{:S(2)}) collective-permute-start(s16[528,128]{1,0:T(8,128)(2,1)S(1)} %get-tuple-element.28), channel_id=1, source_target_pairs={{0,24},{8,16},{16,8},{24,0},{1,25},{9,17},{17,9},{25,1},{2,26},{10... | collective-permute-start | bytes 405512 | tf_op jit(solution)/shard_map/ppermute | solution.py:290
  46.9 23.1 %collective-permute-start.12 = (s16[528,128]{1,0:T(8,128)(2,1)S(1)}, s16[528,128]{1,0:T(8,128)(2,1)S(1)}, u32[]{:S(2)}, u32[]{:S(2)}) collective-permute-start(s16[528,128]{1,0:T(8,128)(2,1)S(1)} %get-tuple-element.21.refs_4_), channel_id=1, source_target_pairs={{0,16},{8,24},{16,0},{24,8},{1,17},{9,25},{17,1},{25,9},{2,18},{10... | collective-permute-start | bytes 405512 | tf_op jit(solution)/shard_map/ppermute | solution.py:290
  61.6 11.3 %collective-permute-start.11 = (s16[784,128]{1,0:T(8,128)(2,1)S(1)}, s16[784,128]{1,0:T(8,128)(2,1)S(1)}, u32[]{:S(2)}, u32[]{:S(2)}) collective-permute-start(s16[784,128]{1,0:T(8,128)(2,1)S(1)} %get-tuple-element.24.refs_5_.refs_1_), channel_id=1, source_target_pairs={{0,16},{8,24},{16,0},{24,8},{1,17},{9,25},{17,1},{25,9},{2,18},{10... | collective-permute-start | bytes 602120 | tf_op jit(solution)/shard_map/ppermute | solution.py:290
  63.1 6.9 %collective-permute-start.14 = (s16[528,128]{1,0:T(8,128)(2,1)S(1)}, s16[528,128]{1,0:T(8,128)(2,1)S(1)}, u32[]{:S(2)}, u32[]{:S(2)}) collective-permute-start(s16[528,128]{1,0:T(8,128)(2,1)S(1)} %handed_on.3), channel_id=1, source_target_pairs={{0,8},{8,0},{16,24},{24,16},{1,9},{9,1},{17,25},{25,17},{2,10},{10... | collective-permute-start | bytes 405512 | tf_op jit(solution)/shard_map/ppermute | solution.py:290

commit v18 on v17

--- a/solution.py
+++ b/solution.py
@@ -15,7 +15,7 @@
 VMEM_LIMIT = 48 * 1024 * 1024
 SMALL_LIMIT = 8 * 1024 * 1024
 SLOTS = 4
-SHARES = (2, 3, 2)
+SHARES = (2, 2, 3)
 SUB = 256
 
 

time: 74.3 us -> 73.8 us (level)
  transfers between devices with their start and end apart: 15 -> 15, of which waited for: 5 -> 8; matrix products, arithmetic and copies ran while one was open for 2% -> 2% of each run, Pallas kernels for 45% -> 45%
where the time goes in v18:
time: 73.8 us; the launch traced here: 73.6 us
  Pallas kernels  34.4 us (47%)
  starting transfers between devices  22.1 us (30%)
  waiting for transfers between devices  13.7 us (19%)
  local copies, waits for them, and re-layouts  1.8 us (2%)
  other arithmetic  0.91 us (1%)
  between operations  0.75 us (1%)
    ppermute x15, starting transfers between devices, send(): return lax.ppermute(value, axis, [(i, i ^ flip) for i in range(size)])  22.1 us
    pallas_call x3, Pallas kernels, partial_sums(): pl.pallas_call(functools.partial(sums_kernel, 0 if aligned is not None el...  18.7 us
    ppermute x15, waiting for transfers between devices, send(): return lax.ppermute(value, axis, [(i, i ^ flip) for i in range(size)])  13.7 us
    pallas_call x2, Pallas kernels, weight_grads(): pl.pallas_call(functools.partial(weight_kernel, offsets, first, len(later...  13.4 us
  transfers between devices with their start and end apart: 15, of which 8 were waited for; matrix products, arithmetic and copies ran while one was open for 2% of the time, Pallas kernels for 45%

profile of v18, /device:TPU:0, one launch (start us, length us, event | category | flops | bytes accessed | tf_op | source)
XLA Modules:
  0.0 73.6 jit_solution(2473555159234990279)
XLA Ops:
  0.6 3.0 %collective-permute-start = (bf16[32,4096]{1,0:T(8,128)(2,1)}, bf16[32,4096]{1,0:T(8,128)(2,1)S(1)}, u32[]{:S(2)}, u32[]{:S(2)}) collective-permute-start(bf16[32,4096]{1,0:T(8,128)(2,1)} %refs_0_.3), channel_id=1, source_target_pairs={{0,2},{1,3},{2,0},{3,1},{4,6},{5,7},{6,4},{7,5},{8,10},{9,11},{10,... | collective-permute-start | bytes 786440 | tf_op jit(solution)/shard_map/ppermute | solution.py:290
  3.6 1.5 %collective-permute-start.2 = (bf16[32,4096]{1,0:T(8,128)(2,1)}, bf16[32,4096]{1,0:T(8,128)(2,1)S(1)}, u32[]{:S(2)}, u32[]{:S(2)}) collective-permute-start(bf16[32,4096]{1,0:T(8,128)(2,1)} %refs_0_.3), channel_id=1, source_target_pairs={{0,4},{1,5},{2,6},{3,7},{4,0},{5,1},{6,2},{7,3},{8,12},{9,13},{10,... | collective-permute-start | bytes 786440 | tf_op jit(solution)/shard_map/ppermute | solution.py:290
  5.2 3.0 %collective-permute-start.6 = (bf16[64,3584]{1,0:T(8,128)(2,1)}, bf16[64,3584]{1,0:T(8,128)(2,1)S(1)}, u32[]{:S(2)}, u32[]{:S(2)}) collective-permute-start(bf16[64,3584]{1,0:T(8,128)(2,1)} %refs_0_.5), channel_id=1, source_target_pairs={{0,16},{8,24},{16,0},{24,8},{1,17},{9,25},{17,1},{25,9},{2,18},{10... | collective-permute-start | bytes 1376264 | tf_op jit(solution)/shard_map/ppermute | solution.py:290
  8.2 1.6 %collective-permute-start.5 = (bf16[64,3584]{1,0:T(8,128)(2,1)}, bf16[64,3584]{1,0:T(8,128)(2,1)S(1)}, u32[]{:S(2)}, u32[]{:S(2)}) collective-permute-start(bf16[64,3584]{1,0:T(8,128)(2,1)} %refs_0_.5), channel_id=1, source_target_pairs={{0,8},{8,0},{16,24},{24,16},{1,9},{9,1},{17,25},{25,17},{2,10},{10... | collective-permute-start | bytes 1376264 | tf_op jit(solution)/shard_map/ppermute | solution.py:290
  9.8 0.7 xor_multiply_fusion
  10.5 0.5 collective-permute-done.refs_1_
  11.0 0.9 %copy-done.1 = bf16[32,4096]{1,0:T(8,128)(2,1)S(1)} copy-done((bf16[32,4096]{1,0:T(8,128)(2,1)S(1)}, bf16[32,4096]{1,0:T(8,128)(2,1)}, u32[]{:S(2)}) %copy-start.1) | copy-done | bytes 262168
  12.0 5.2 %collective-permute-done.2.refs_1_ = bf16[32,4096]{1,0:T(8,128)(2,1)S(1)} collective-permute-done((bf16[32,4096]{1,0:T(8,128)(2,1)}, bf16[32,4096]{1,0:T(8,128)(2,1)S(1)}, u32[]{:S(2)}, u32[]{:S(2)}) %collective-permute-start.2) | collective-permute-done | bytes 262176 | tf_op jit(solution)/shard_map/ppermute | solution.py:290
  17.4 0.8 %reshape.24 = s32[4,64]{1,0:T(4,128)S(1)} reshape(s32[256]{0:T(256)} %param.8) | data formatting | bytes 2048 | tf_op jit(solution)/shard_map/reshape | solution.py:366
  18.3 0.1 compare_convert_fusion.refs_0_
  18.5 0.8 %collective-permute-done.4.refs_4_ = bf16[64,4096]{1,0:T(8,128)(2,1)S(1)} collective-permute-done((bf16[64,4096]{1,0:T(8,128)(2,1)S(1)}, bf16[64,4096]{1,0:T(8,128)(2,1)S(1)}, u32[]{:S(2)}, u32[]{:S(2)}) %collective-permute-start.4) | collective-permute-done | bytes 524320 | tf_op jit(solution)/shard_map/ppermute | solution.py:290
  19.2 6.0 %sums_first.1 = (bf16[256,4096]{1,0:T(8,128)(2,1)S(1)}, f32[128,1024]{1,0:T(8,128)S(1)}, s16[1040,128]{1,0:T(8,128)(2,1)S(1)}) custom-call(bf16[256,256]{1,0:T(8,128)(2,1)S(1)} %compare_convert_fusion.refs_0_, bf16[64,4096]{1,0:T(8,128)(2,1)S(1)} %stacked.2.refs_2_.refs_1_, bf16[64,4096]{1,0:T(8,128)(2,1)S(1)} %stacked.3.refs_2_, ...), custom_call_target="tpu_custom_call" | custom-call | flops 2147483648 | bytes 8388608 | tf_op jit(solution)/shard_map/sums_first/pallas_call | solution.py:155
  25.2 1.6 %collective-permute-start.8 = (s16[1040,128]{1,0:T(8,128)(2,1)S(1)}, s16[1040,128]{1,0:T(8,128)(2,1)S(1)}, u32[]{:S(2)}, u32[]{:S(2)}) collective-permute-start(s16[1040,128]{1,0:T(8,128)(2,1)S(1)} %get-tuple-element.18), channel_id=1, source_target_pairs={{0,8},{8,0},{16,24},{24,16},{1,9},{9,1},{17,25},{25,17},{2,10},{10... | collective-permute-start | bytes 798728 | tf_op jit(solution)/shard_map/ppermute | solution.py:290
  26.9 1.2 %collective-permute-done.6.refs_0_ = bf16[64,3584]{1,0:T(8,128)(2,1)S(1)} collective-permute-done((bf16[64,3584]{1,0:T(8,128)(2,1)}, bf16[64,3584]{1,0:T(8,128)(2,1)S(1)}, u32[]{:S(2)}, u32[]{:S(2)}) %collective-permute-start.6) | collective-permute-done | bytes 458784 | tf_op jit(solution)/shard_map/ppermute | solution.py:290
  28.0 0.7 collective-permute-start.7
  28.8 5.2 %sums_second.1 = (f32[128,1024]{1,0:T(8,128)S(1)}, s16[1040,128]{1,0:T(8,128)(2,1)S(1)}) custom-call(bf16[256,4096]{1,0:T(8,128)(2,1)S(1)} %get-tuple-element.16.refs_1_.refs_0_.aligned_ref, bf16[3584,4096]{1,0:T(8,128)(2,1)} %refs_2_.3, bf16[3584,4096]{1,0:T(8,128)(2,1)} %refs_2_.3, bf16[64,3584]{1,0:T(8,128)(2,1)S(1)} %collective-permute-done.5.refs_3_.refs_1_), custom_call_target="tpu_custom_call" | custom-call | flops 2147483648 | bytes 8388608 | tf_op jit(solution)/shard_map/sums_second/pallas_call | solution.py:155
  34.0 0.5 collective-permute-done.8.got_ref
  34.5 0.5 fold.2
  35.0 2.8 %collective-permute-start.10 = (s16[528,128]{1,0:T(8,128)(2,1)S(1)}, s16[528,128]{1,0:T(8,128)(2,1)S(1)}, u32[]{:S(2)}, u32[]{:S(2)}) collective-permute-start(s16[528,128]{1,0:T(8,128)(2,1)S(1)} %get-tuple-element.20.refs_3_), channel_id=1, source_target_pairs={{0,16},{8,24},{16,0},{24,8},{1,17},{9,25},{17,1},{25,9},{2,18},{10... | collective-permute-start | bytes 405512 | tf_op jit(solution)/shard_map/ppermute | solution.py:290
  37.8 1.4 %collective-permute-start.9 = (s16[1040,128]{1,0:T(8,128)(2,1)S(1)}, s16[1040,128]{1,0:T(8,128)(2,1)S(1)}, u32[]{:S(2)}, u32[]{:S(2)}) collective-permute-start(s16[1040,128]{1,0:T(8,128)(2,1)S(1)} %get-tuple-element.23), channel_id=1, source_target_pairs={{0,8},{8,0},{16,24},{24,16},{1,9},{9,1},{17,25},{25,17},{2,10},{10... | collective-permute-start | bytes 798728 | tf_op jit(solution)/shard_map/ppermute | solution.py:290
  39.2 7.5 %sums_last.1 = (f32[64,1536]{1,0:T(8,128)S(1)}, s16[784,128]{1,0:T(8,128)(2,1)S(1)}, s16[784,128]{1,0:T(8,128)(2,1)S(1)}, s16[784,128]{1,0:T(8,128)(2,1)S(1)}) custom-call(bf16[256,4096]{1,0:T(8,128)(2,1)S(1)} %get-tuple-element.16.refs_1_.refs_0_.aligned_ref, bf16[3584,4096]{1,0:T(8,128)(2,1)} %refs_2_.3, bf16[3584,4096]{1,0:T(8,128)(2,1)} %refs_2_.3, ...), custom_call_target="tpu_custom_call" | custom-call | flops 3221225472 | bytes 12582912 | tf_op jit(solution)/shard_map/sums_last/pallas_call | solution.py:155
  46.7 0.3 collective-permute-start.13
  47.0 1.9 %collective-permute-start.12 = (s16[784,128]{1,0:T(8,128)(2,1)S(1)}, s16[784,128]{1,0:T(8,128)(2,1)S(1)}, u32[]{:S(2)}, u32[]{:S(2)}) collective-permute-start(s16[784,128]{1,0:T(8,128)(2,1)S(1)} %get-tuple-element.21.refs_4_), channel_id=1, source_target_pairs={{0,16},{8,24},{16,0},{24,8},{1,17},{9,25},{17,1},{25,9},{2,18},{10... | collective-permute-start | bytes 602120 | tf_op jit(solution)/shard_map/ppermute | solution.py:290
  48.9 9.0 %weight_grads.2.refs_0_.refs_4_ = bf16[3584,4096]{1,0:T(8,128)(2,1)} custom-call(bf16[256,4096]{1,0:T(8,128)(2,1)S(1)} %get-tuple-element.16.refs_1_.refs_0_.aligned_ref, bf16[64,3584]{1,0:T(8,128)(2,1)S(1)} %copy-done, bf16[64,3584]{1,0:T(8,128)(2,1)S(1)} %collective-permute-done.5.refs_3_.refs_1_, bf16[64,3584]{1,0:T(8,128)(2,1)S(1)} %handed_on.2.refs_2_, ...), custom_call_target="tpu_custom_call" | custom-call | flops 5368709120 | bytes 20971520 | tf_op jit(solution)/shard_map/weight_grads/pallas_call | solution.py:206
  57.9 0.5 fold.3
  58.3 1.6 %collective-permute-start.11 = (s16[528,128]{1,0:T(8,128)(2,1)S(1)}, s16[528,128]{1,0:T(8,128)(2,1)S(1)}, u32[]{:S(2)}, u32[]{:S(2)}) collective-permute-start(s16[528,128]{1,0:T(8,128)(2,1)S(1)} %get-tuple-element.24.refs_5_.refs_1_), channel_id=1, source_target_pairs={{0,16},{8,24},{16,0},{24,8},{1,17},{9,25},{17,1},{25,9},{2,18},{10... | collective-permute-start | bytes 405512 | tf_op jit(solution)/shard_map/ppermute | solution.py:290
  60.0 2.5 %collective-permute-start.14 = (s16[784,128]{1,0:T(8,128)(2,1)S(1)}, s16[784,128]{1,0:T(8,128)(2,1)S(1)}, u32[]{:S(2)}, u32[]{:S(2)}) collective-permute-start(s16[784,128]{1,0:T(8,128)(2,1)S(1)} %handed_on.3), channel_id=1, source_target_pairs={{0,8},{8,0},{16,24},{24,16},{1,9},{9,1},{17,25},{25,17},{2,10},{10... | collective-permute-start | bytes 602120 | tf_op jit(solution)/shard_map/ppermute | solution.py:290
  62.4 4.4 %weight_grads.3.refs_8_ = bf16[3584,4096]{1,0:T(8,128)(2,1)} custom-call(bf16[256,4096]{1,0:T(8,128)(2,1)S(1)} %get-tuple-element.16.refs_1_.refs_0_.aligned_ref, bf16[64,3584]{1,0:T(8,128)(2,1)S(1)} %copy-done, bf16[64,3584]{1,0:T(8,128)(2,1)S(1)} %collective-permute-done.5.refs_3_.refs_1_, ...), custom_call_target="tpu_custom_call", output_to_operand_aliasing={{}: (5, {})} | custom-call | flops 2147483648 | bytes 8388608 | tf_op jit(solution)/shard_map/weight_grads/pallas_call | solution.py:206
  66.9 3.7 %collective-permute-done.12.refs_5_ = s16[784,128]{1,0:T(8,128)(2,1)S(1)} collective-permute-done((s16[784,128]{1,0:T(8,128)(2,1)S(1)}, s16[784,128]{1,0:T(8,128)(2,1)S(1)}, u32[]{:S(2)}, u32[]{:S(2)}) %collective-permute-start.12) | collective-permute-done | bytes 200736 | tf_op jit(solution)/shard_map/ppermute | solution.py:290
  70.6 1.5 %collective-permute-done.11.refs_3_ = s16[528,128]{1,0:T(8,128)(2,1)S(1)} collective-permute-done((s16[528,128]{1,0:T(8,128)(2,1)S(1)}, s16[528,128]{1,0:T(8,128)(2,1)S(1)}, u32[]{:S(2)}, u32[]{:S(2)}) %collective-permute-start.11) | collective-permute-done | bytes 135200 | tf_op jit(solution)/shard_map/ppermute | solution.py:290
  72.0 0.3 collective-permute-done.14.refs_7_
  72.3 1.3 %totals.1 = bf16[64,3584]{1,0:T(8,128)(2,1)} custom-call(f32[64,1024]{1,0:T(8,128)S(1)} %get-tuple-element.25.refs_0_, s16[528,128]{1,0:T(8,128)(2,1)S(1)} %collective-permute-done.10.refs_1_, f32[64,1024]{1,0:T(8,128)S(1)} %get-tuple-element.26.refs_2_, s16[528,128]{1,0:T(8,128)(2,1)S(1)} %collective-permute-done.11.refs_3_, ...), custom_call_target="tpu_custom_call" | custom-call | flops 9175040 | bytes 3211264 | tf_op jit(solution)/shard_map/totals/pallas_call | solution.py:281
  (21 shorter events, 0.5 us)
Async XLA Ops:
  0.6 10.4 %collective-permute-start = (bf16[32,4096]{1,0:T(8,128)(2,1)}, bf16[32,4096]{1,0:T(8,128)(2,1)S(1)}, u32[]{:S(2)}, u32[]{:S(2)}) collective-permute-start(bf16[32,4096]{1,0:T(8,128)(2,1)} %refs_0_.3), channel_id=1, source_target_pairs={{0,2},{1,3},{2,0},{3,1},{4,6},{5,7},{6,4},{7,5},{8,10},{9,11},{10,... | collective-permute-start | bytes 786440 | tf_op jit(solution)/shard_map/ppermute | solution.py:290
  3.6 13.6 %collective-permute-start.2 = (bf16[32,4096]{1,0:T(8,128)(2,1)}, bf16[32,4096]{1,0:T(8,128)(2,1)S(1)}, u32[]{:S(2)}, u32[]{:S(2)}) collective-permute-start(bf16[32,4096]{1,0:T(8,128)(2,1)} %refs_0_.3), channel_id=1, source_target_pairs={{0,4},{1,5},{2,6},{3,7},{4,0},{5,1},{6,2},{7,3},{8,12},{9,13},{10,... | collective-permute-start | bytes 786440 | tf_op jit(solution)/shard_map/ppermute | solution.py:290
  5.2 12.1 %collective-permute-start.1 = (bf16[32,4096]{1,0:T(8,128)(2,1)}, bf16[32,4096]{1,0:T(8,128)(2,1)S(1)}, u32[]{:S(2)}, u32[]{:S(2)}) collective-permute-start(bf16[32,4096]{1,0:T(8,128)(2,1)} %refs_0_.3), channel_id=1, source_target_pairs={{0,6},{1,7},{2,4},{3,5},{4,2},{5,3},{6,0},{7,1},{8,14},{9,15},{10,... | collective-permute-start | bytes 786440 | tf_op jit(solution)/shard_map/ppermute | solution.py:290
  5.2 22.9 %collective-permute-start.6 = (bf16[64,3584]{1,0:T(8,128)(2,1)}, bf16[64,3584]{1,0:T(8,128)(2,1)S(1)}, u32[]{:S(2)}, u32[]{:S(2)}) collective-permute-start(bf16[64,3584]{1,0:T(8,128)(2,1)} %refs_0_.5), channel_id=1, source_target_pairs={{0,16},{8,24},{16,0},{24,8},{1,17},{9,25},{17,1},{25,9},{2,18},{10... | collective-permute-start | bytes 1376264 | tf_op jit(solution)/shard_map/ppermute | solution.py:290
  8.2 20.6 %collective-permute-start.5 = (bf16[64,3584]{1,0:T(8,128)(2,1)}, bf16[64,3584]{1,0:T(8,128)(2,1)S(1)}, u32[]{:S(2)}, u32[]{:S(2)}) collective-permute-start(bf16[64,3584]{1,0:T(8,128)(2,1)} %refs_0_.5), channel_id=1, source_target_pairs={{0,8},{8,0},{16,24},{24,16},{1,9},{9,1},{17,25},{25,17},{2,10},{10... | collective-permute-start | bytes 1376264 | tf_op jit(solution)/shard_map/ppermute | solution.py:290
  11.0 1.0 %copy-start.1 = (bf16[32,4096]{1,0:T(8,128)(2,1)S(1)}, bf16[32,4096]{1,0:T(8,128)(2,1)}, u32[]{:S(2)}) copy-start(bf16[32,4096]{1,0:T(8,128)(2,1)} %refs_0_.3) | copy-start | bytes 786436
  12.0 7.3 %collective-permute-start.3 = (bf16[64,4096]{1,0:T(8,128)(2,1)S(1)}, bf16[64,4096]{1,0:T(8,128)(2,1)S(1)}, u32[]{:S(2)}, u32[]{:S(2)}) collective-permute-start(bf16[64,4096]{1,0:T(8,128)(2,1)S(1)} %stacked.2.refs_2_.refs_1_), channel_id=1, source_target_pairs={{0,1},{1,0},{2,3},{3,2},{4,5},{5,4},{6,7},{7,6},{8,9},{9,8},{10,11... | collective-permute-start | bytes 1572872 | tf_op jit(solution)/shard_map/ppermute | solution.py:290
  17.3 2.0 %collective-permute-start.4 = (bf16[64,4096]{1,0:T(8,128)(2,1)S(1)}, bf16[64,4096]{1,0:T(8,128)(2,1)S(1)}, u32[]{:S(2)}, u32[]{:S(2)}) collective-permute-start(bf16[64,4096]{1,0:T(8,128)(2,1)S(1)} %stacked.3.refs_2_), channel_id=1, source_target_pairs={{0,1},{1,0},{2,3},{3,2},{4,5},{5,4},{6,7},{7,6},{8,9},{9,8},{10,11... | collective-permute-start | bytes 1572872 | tf_op jit(solution)/shard_map/ppermute | solution.py:290
  25.2 9.3 %collective-permute-start.8 = (s16[1040,128]{1,0:T(8,128)(2,1)S(1)}, s16[1040,128]{1,0:T(8,128)(2,1)S(1)}, u32[]{:S(2)}, u32[]{:S(2)}) collective-permute-start(s16[1040,128]{1,0:T(8,128)(2,1)S(1)} %get-tuple-element.18), channel_id=1, source_target_pairs={{0,8},{8,0},{16,24},{24,16},{1,9},{9,1},{17,25},{25,17},{2,10},{10... | collective-permute-start | bytes 798728 | tf_op jit(solution)/shard_map/ppermute | solution.py:290
  28.0 20.8 %collective-permute-start.7 = (bf16[64,3584]{1,0:T(8,128)(2,1)S(1)}, bf16[64,3584]{1,0:T(8,128)(2,1)S(1)}, u32[]{:S(2)}, u32[]{:S(2)}) collective-permute-start(bf16[64,3584]{1,0:T(8,128)(2,1)S(1)} %handed_on.2.refs_2_), channel_id=1, source_target_pairs={{0,8},{8,0},{16,24},{24,16},{1,9},{9,1},{17,25},{25,17},{2,10},{10... | collective-permute-start | bytes 1376264 | tf_op jit(solution)/shard_map/ppermute | solution.py:290
  35.0 31.9 %collective-permute-start.10 = (s16[528,128]{1,0:T(8,128)(2,1)S(1)}, s16[528,128]{1,0:T(8,128)(2,1)S(1)}, u32[]{:S(2)}, u32[]{:S(2)}) collective-permute-start(s16[528,128]{1,0:T(8,128)(2,1)S(1)} %get-tuple-element.20.refs_3_), channel_id=1, source_target_pairs={{0,16},{8,24},{16,0},{24,8},{1,17},{9,25},{17,1},{25,9},{2,18},{10... | collective-permute-start | bytes 405512 | tf_op jit(solution)/shard_map/ppermute | solution.py:290
  37.8 11.1 %copy-start = (bf16[64,3584]{1,0:T(8,128)(2,1)S(1)}, bf16[64,3584]{1,0:T(8,128)(2,1)}, u32[]{:S(2)}) copy-start(bf16[64,3584]{1,0:T(8,128)(2,1)} %refs_0_.5) | copy-start | bytes 1376260
  37.8 20.1 %collective-permute-start.9 = (s16[1040,128]{1,0:T(8,128)(2,1)S(1)}, s16[1040,128]{1,0:T(8,128)(2,1)S(1)}, u32[]{:S(2)}, u32[]{:S(2)}) collective-permute-start(s16[1040,128]{1,0:T(8,128)(2,1)S(1)} %get-tuple-element.23), channel_id=1, source_target_pairs={{0,8},{8,0},{16,24},{24,16},{1,9},{9,1},{17,25},{25,17},{2,10},{10... | collective-permute-start | bytes 798728 | tf_op jit(solution)/shard_map/ppermute | solution.py:290
  46.7 20.2 %collective-permute-start.13 = (s16[784,128]{1,0:T(8,128)(2,1)S(1)}, s16[784,128]{1,0:T(8,128)(2,1)S(1)}, u32[]{:S(2)}, u32[]{:S(2)}) collective-permute-start(s16[784,128]{1,0:T(8,128)(2,1)S(1)} %get-tuple-element.28), channel_id=1, source_target_pairs={{0,24},{8,16},{16,8},{24,0},{1,25},{9,17},{17,9},{25,1},{2,26},{10... | collective-permute-start | bytes 602120 | tf_op jit(solution)/shard_map/ppermute | solution.py:290
  47.0 23.6 %collective-permute-start.12 = (s16[784,128]{1,0:T(8,128)(2,1)S(1)}, s16[784,128]{1,0:T(8,128)(2,1)S(1)}, u32[]{:S(2)}, u32[]{:S(2)}) collective-permute-start(s16[784,128]{1,0:T(8,128)(2,1)S(1)} %get-tuple-element.21.refs_4_), channel_id=1, source_target_pairs={{0,16},{8,24},{16,0},{24,8},{1,17},{9,25},{17,1},{25,9},{2,18},{10... | collective-permute-start | bytes 602120 | tf_op jit(solution)/shard_map/ppermute | solution.py:290
  58.3 13.7 %collective-permute-start.11 = (s16[528,128]{1,0:T(8,128)(2,1)S(1)}, s16[528,128]{1,0:T(8,128)(2,1)S(1)}, u32[]{:S(2)}, u32[]{:S(2)}) collective-permute-start(s16[528,128]{1,0:T(8,128)(2,1)S(1)} %get-tuple-element.24.refs_5_.refs_1_), channel_id=1, source_target_pairs={{0,16},{8,24},{16,0},{24,8},{1,17},{9,25},{17,1},{25,9},{2,18},{10... | collective-permute-start | bytes 405512 | tf_op jit(solution)/shard_map/ppermute | solution.py:290
  60.0 12.4 %collective-permute-start.14 = (s16[784,128]{1,0:T(8,128)(2,1)S(1)}, s16[784,128]{1,0:T(8,128)(2,1)S(1)}, u32[]{:S(2)}, u32[]{:S(2)}) collective-permute-start(s16[784,128]{1,0:T(8,128)(2,1)S(1)} %handed_on.3), channel_id=1, source_target_pairs={{0,8},{8,0},{16,24},{24,16},{1,9},{9,1},{17,25},{25,17},{2,10},{10... | collective-permute-start | bytes 602120 | tf_op jit(solution)/shard_map/ppermute | solution.py:290

commit v19 on v18

--- a/solution.py
+++ b/solution.py
@@ -396,7 +396,7 @@
 
     grad_pieces = [act_pieces[o] for o in range(n_row)]
     grad_tile = tile_of(hidden, 256)
-    (first_a, count_a), (first_b, count_b) = part_slices(hidden // grad_tile, (5, 2))
+    (first_a, count_a), (first_b, count_b) = part_slices(hidden // grad_tile, (4, 3))
     grad = weight_grads(aligned, grad_pieces, offsets, grad_tile, first_a, count_a, None, [sent_c[offsets[1]]])
     done_b, crossed_b, _ = halved(kept_b, got_b, [], [grad], n_row)
     done_c.append(send(handed_on([sent_c[1]], crossed_b)[0], "row", 1, n_row))

time: 73.8 us -> 73.8 us (level)
  waiting for transfers between devices: 13.7 us -> 12.1 us
  starting transfers between devices: 22.1 us -> 23.7 us
    ppermute x15, waiting for transfers between devices: 13.7 us -> 12.1 us  [send(): return lax.ppermute(value, axis, [(i, i ^ flip) for i in range(size)])]
    ppermute x15, starting transfers between devices: 22.1 us -> 23.7 us  [send(): return lax.ppermute(value, axis, [(i, i ^ flip) for i in range(size)])]
where the time goes in v19:
time: 73.8 us; the launch traced here: 73.6 us
  Pallas kernels  34.4 us (47%)
  starting transfers between devices  23.7 us (32%)
  waiting for transfers between devices  12.1 us (16%)
  local copies, waits for them, and re-layouts  1.8 us (2%)
  other arithmetic  0.91 us (1%)
  between operations  0.75 us (1%)
    ppermute x15, starting transfers between devices, send(): return lax.ppermute(value, axis, [(i, i ^ flip) for i in range(size)])  23.7 us
    pallas_call x3, Pallas kernels, partial_sums(): pl.pallas_call(functools.partial(sums_kernel, 0 if aligned is not None el...  18.7 us
    pallas_call x2, Pallas kernels, weight_grads(): pl.pallas_call(functools.partial(weight_kernel, offsets, first, len(later...  13.4 us
    ppermute x15, waiting for transfers between devices, send(): return lax.ppermute(value, axis, [(i, i ^ flip) for i in range(size)])  12.1 us
  transfers between devices with their start and end apart: 15, of which 8 were waited for; matrix products, arithmetic and copies ran while one was open for 2% of the time, Pallas kernels for 45%

profile of v19, /device:TPU:0, one launch (start us, length us, event | category | flops | bytes accessed | tf_op | source)
XLA Modules:
  0.0 73.6 jit_solution(6595099834547288742)
XLA Ops:
  0.6 3.0 %collective-permute-start = (bf16[32,4096]{1,0:T(8,128)(2,1)}, bf16[32,4096]{1,0:T(8,128)(2,1)S(1)}, u32[]{:S(2)}, u32[]{:S(2)}) collective-permute-start(bf16[32,4096]{1,0:T(8,128)(2,1)} %refs_0_.3), channel_id=1, source_target_pairs={{0,2},{1,3},{2,0},{3,1},{4,6},{5,7},{6,4},{7,5},{8,10},{9,11},{10,... | collective-permute-start | bytes 786440 | tf_op jit(solution)/shard_map/ppermute | solution.py:290
  3.6 1.5 %collective-permute-start.2 = (bf16[32,4096]{1,0:T(8,128)(2,1)}, bf16[32,4096]{1,0:T(8,128)(2,1)S(1)}, u32[]{:S(2)}, u32[]{:S(2)}) collective-permute-start(bf16[32,4096]{1,0:T(8,128)(2,1)} %refs_0_.3), channel_id=1, source_target_pairs={{0,4},{1,5},{2,6},{3,7},{4,0},{5,1},{6,2},{7,3},{8,12},{9,13},{10,... | collective-permute-start | bytes 786440 | tf_op jit(solution)/shard_map/ppermute | solution.py:290
  5.2 3.0 %collective-permute-start.6 = (bf16[64,3584]{1,0:T(8,128)(2,1)}, bf16[64,3584]{1,0:T(8,128)(2,1)S(1)}, u32[]{:S(2)}, u32[]{:S(2)}) collective-permute-start(bf16[64,3584]{1,0:T(8,128)(2,1)} %refs_0_.5), channel_id=1, source_target_pairs={{0,16},{8,24},{16,0},{24,8},{1,17},{9,25},{17,1},{25,9},{2,18},{10... | collective-permute-start | bytes 1376264 | tf_op jit(solution)/shard_map/ppermute | solution.py:290
  8.2 1.6 %collective-permute-start.5 = (bf16[64,3584]{1,0:T(8,128)(2,1)}, bf16[64,3584]{1,0:T(8,128)(2,1)S(1)}, u32[]{:S(2)}, u32[]{:S(2)}) collective-permute-start(bf16[64,3584]{1,0:T(8,128)(2,1)} %refs_0_.5), channel_id=1, source_target_pairs={{0,8},{8,0},{16,24},{24,16},{1,9},{9,1},{17,25},{25,17},{2,10},{10... | collective-permute-start | bytes 1376264 | tf_op jit(solution)/shard_map/ppermute | solution.py:290
  9.8 0.7 xor_multiply_fusion
  10.5 0.5 collective-permute-done.refs_1_
  11.0 0.9 %copy-done.1 = bf16[32,4096]{1,0:T(8,128)(2,1)S(1)} copy-done((bf16[32,4096]{1,0:T(8,128)(2,1)S(1)}, bf16[32,4096]{1,0:T(8,128)(2,1)}, u32[]{:S(2)}) %copy-start.1) | copy-done | bytes 262168
  12.0 5.2 %collective-permute-done.2.refs_1_ = bf16[32,4096]{1,0:T(8,128)(2,1)S(1)} collective-permute-done((bf16[32,4096]{1,0:T(8,128)(2,1)}, bf16[32,4096]{1,0:T(8,128)(2,1)S(1)}, u32[]{:S(2)}, u32[]{:S(2)}) %collective-permute-start.2) | collective-permute-done | bytes 262176 | tf_op jit(solution)/shard_map/ppermute | solution.py:290
  17.4 0.8 %reshape.24 = s32[4,64]{1,0:T(4,128)S(1)} reshape(s32[256]{0:T(256)} %param.8) | data formatting | bytes 2048 | tf_op jit(solution)/shard_map/reshape | solution.py:366
  18.3 0.1 compare_convert_fusion.refs_0_
  18.5 0.8 %collective-permute-done.4.refs_4_ = bf16[64,4096]{1,0:T(8,128)(2,1)S(1)} collective-permute-done((bf16[64,4096]{1,0:T(8,128)(2,1)S(1)}, bf16[64,4096]{1,0:T(8,128)(2,1)S(1)}, u32[]{:S(2)}, u32[]{:S(2)}) %collective-permute-start.4) | collective-permute-done | bytes 524320 | tf_op jit(solution)/shard_map/ppermute | solution.py:290
  19.2 6.0 %sums_first.1 = (bf16[256,4096]{1,0:T(8,128)(2,1)S(1)}, f32[128,1024]{1,0:T(8,128)S(1)}, s16[1040,128]{1,0:T(8,128)(2,1)S(1)}) custom-call(bf16[256,256]{1,0:T(8,128)(2,1)S(1)} %compare_convert_fusion.refs_0_, bf16[64,4096]{1,0:T(8,128)(2,1)S(1)} %stacked.2.refs_2_.refs_1_, bf16[64,4096]{1,0:T(8,128)(2,1)S(1)} %stacked.3.refs_2_, ...), custom_call_target="tpu_custom_call" | custom-call | flops 2147483648 | bytes 8388608 | tf_op jit(solution)/shard_map/sums_first/pallas_call | solution.py:155
  25.2 1.6 %collective-permute-start.8 = (s16[1040,128]{1,0:T(8,128)(2,1)S(1)}, s16[1040,128]{1,0:T(8,128)(2,1)S(1)}, u32[]{:S(2)}, u32[]{:S(2)}) collective-permute-start(s16[1040,128]{1,0:T(8,128)(2,1)S(1)} %get-tuple-element.18), channel_id=1, source_target_pairs={{0,8},{8,0},{16,24},{24,16},{1,9},{9,1},{17,25},{25,17},{2,10},{10... | collective-permute-start | bytes 798728 | tf_op jit(solution)/shard_map/ppermute | solution.py:290
  26.9 1.2 %collective-permute-done.6.refs_0_ = bf16[64,3584]{1,0:T(8,128)(2,1)S(1)} collective-permute-done((bf16[64,3584]{1,0:T(8,128)(2,1)}, bf16[64,3584]{1,0:T(8,128)(2,1)S(1)}, u32[]{:S(2)}, u32[]{:S(2)}) %collective-permute-start.6) | collective-permute-done | bytes 458784 | tf_op jit(solution)/shard_map/ppermute | solution.py:290
  28.0 0.7 collective-permute-start.7
  28.8 5.2 %sums_second.1 = (f32[128,1024]{1,0:T(8,128)S(1)}, s16[1040,128]{1,0:T(8,128)(2,1)S(1)}) custom-call(bf16[256,4096]{1,0:T(8,128)(2,1)S(1)} %get-tuple-element.16.refs_1_.refs_0_.aligned_ref, bf16[3584,4096]{1,0:T(8,128)(2,1)} %refs_2_.3, bf16[3584,4096]{1,0:T(8,128)(2,1)} %refs_2_.3, bf16[64,3584]{1,0:T(8,128)(2,1)S(1)} %collective-permute-done.5.refs_3_.refs_1_), custom_call_target="tpu_custom_call" | custom-call | flops 2147483648 | bytes 8388608 | tf_op jit(solution)/shard_map/sums_second/pallas_call | solution.py:155
  34.0 0.5 collective-permute-done.8.got_ref
  34.5 0.5 fold.2
  35.0 2.8 %collective-permute-start.10 = (s16[528,128]{1,0:T(8,128)(2,1)S(1)}, s16[528,128]{1,0:T(8,128)(2,1)S(1)}, u32[]{:S(2)}, u32[]{:S(2)}) collective-permute-start(s16[528,128]{1,0:T(8,128)(2,1)S(1)} %get-tuple-element.20.refs_3_), channel_id=1, source_target_pairs={{0,16},{8,24},{16,0},{24,8},{1,17},{9,25},{17,1},{25,9},{2,18},{10... | collective-permute-start | bytes 405512 | tf_op jit(solution)/shard_map/ppermute | solution.py:290
  37.8 1.4 %collective-permute-start.9 = (s16[1040,128]{1,0:T(8,128)(2,1)S(1)}, s16[1040,128]{1,0:T(8,128)(2,1)S(1)}, u32[]{:S(2)}, u32[]{:S(2)}) collective-permute-start(s16[1040,128]{1,0:T(8,128)(2,1)S(1)} %get-tuple-element.23), channel_id=1, source_target_pairs={{0,8},{8,0},{16,24},{24,16},{1,9},{9,1},{17,25},{25,17},{2,10},{10... | collective-permute-start | bytes 798728 | tf_op jit(solution)/shard_map/ppermute | solution.py:290
  39.2 7.5 %sums_last.1 = (f32[64,1536]{1,0:T(8,128)S(1)}, s16[784,128]{1,0:T(8,128)(2,1)S(1)}, s16[784,128]{1,0:T(8,128)(2,1)S(1)}, s16[784,128]{1,0:T(8,128)(2,1)S(1)}) custom-call(bf16[256,4096]{1,0:T(8,128)(2,1)S(1)} %get-tuple-element.16.refs_1_.refs_0_.aligned_ref, bf16[3584,4096]{1,0:T(8,128)(2,1)} %refs_2_.3, bf16[3584,4096]{1,0:T(8,128)(2,1)} %refs_2_.3, ...), custom_call_target="tpu_custom_call" | custom-call | flops 3221225472 | bytes 12582912 | tf_op jit(solution)/shard_map/sums_last/pallas_call | solution.py:155
  46.7 0.3 collective-permute-start.13
  47.0 1.9 %collective-permute-start.12 = (s16[784,128]{1,0:T(8,128)(2,1)S(1)}, s16[784,128]{1,0:T(8,128)(2,1)S(1)}, u32[]{:S(2)}, u32[]{:S(2)}) collective-permute-start(s16[784,128]{1,0:T(8,128)(2,1)S(1)} %get-tuple-element.21.refs_4_), channel_id=1, source_target_pairs={{0,16},{8,24},{16,0},{24,8},{1,17},{9,25},{17,1},{25,9},{2,18},{10... | collective-permute-start | bytes 602120 | tf_op jit(solution)/shard_map/ppermute | solution.py:290
  48.9 7.5 %weight_grads.2.refs_0_.refs_4_ = bf16[3584,4096]{1,0:T(8,128)(2,1)} custom-call(bf16[256,4096]{1,0:T(8,128)(2,1)S(1)} %get-tuple-element.16.refs_1_.refs_0_.aligned_ref, bf16[64,3584]{1,0:T(8,128)(2,1)S(1)} %copy-done, bf16[64,3584]{1,0:T(8,128)(2,1)S(1)} %collective-permute-done.5.refs_3_.refs_1_, bf16[64,3584]{1,0:T(8,128)(2,1)S(1)} %handed_on.2.refs_2_, ...), custom_call_target="tpu_custom_call" | custom-call | flops 4294967296 | bytes 16777216 | tf_op jit(solution)/shard_map/weight_grads/pallas_call | solution.py:206
  56.3 0.5 fold.3
  56.8 3.1 %collective-permute-start.11 = (s16[528,128]{1,0:T(8,128)(2,1)S(1)}, s16[528,128]{1,0:T(8,128)(2,1)S(1)}, u32[]{:S(2)}, u32[]{:S(2)}) collective-permute-start(s16[528,128]{1,0:T(8,128)(2,1)S(1)} %get-tuple-element.24.refs_5_.refs_1_), channel_id=1, source_target_pairs={{0,16},{8,24},{16,0},{24,8},{1,17},{9,25},{17,1},{25,9},{2,18},{10... | collective-permute-start | bytes 405512 | tf_op jit(solution)/shard_map/ppermute | solution.py:290
  60.0 2.5 %collective-permute-start.14 = (s16[784,128]{1,0:T(8,128)(2,1)S(1)}, s16[784,128]{1,0:T(8,128)(2,1)S(1)}, u32[]{:S(2)}, u32[]{:S(2)}) collective-permute-start(s16[784,128]{1,0:T(8,128)(2,1)S(1)} %handed_on.3), channel_id=1, source_target_pairs={{0,8},{8,0},{16,24},{24,16},{1,9},{9,1},{17,25},{25,17},{2,10},{10... | collective-permute-start | bytes 602120 | tf_op jit(solution)/shard_map/ppermute | solution.py:290
  62.4 5.9 %weight_grads.3.refs_8_ = bf16[3584,4096]{1,0:T(8,128)(2,1)} custom-call(bf16[256,4096]{1,0:T(8,128)(2,1)S(1)} %get-tuple-element.16.refs_1_.refs_0_.aligned_ref, bf16[64,3584]{1,0:T(8,128)(2,1)S(1)} %copy-done, bf16[64,3584]{1,0:T(8,128)(2,1)S(1)} %collective-permute-done.5.refs_3_.refs_1_, ...), custom_call_target="tpu_custom_call", output_to_operand_aliasing={{}: (5, {})} | custom-call | flops 3221225472 | bytes 12582912 | tf_op jit(solution)/shard_map/weight_grads/pallas_call | solution.py:206
  68.4 2.2 %collective-permute-done.12.refs_5_ = s16[784,128]{1,0:T(8,128)(2,1)S(1)} collective-permute-done((s16[784,128]{1,0:T(8,128)(2,1)S(1)}, s16[784,128]{1,0:T(8,128)(2,1)S(1)}, u32[]{:S(2)}, u32[]{:S(2)}) %collective-permute-start.12) | collective-permute-done | bytes 200736 | tf_op jit(solution)/shard_map/ppermute | solution.py:290
  70.6 1.5 %collective-permute-done.11.refs_3_ = s16[528,128]{1,0:T(8,128)(2,1)S(1)} collective-permute-done((s16[528,128]{1,0:T(8,128)(2,1)S(1)}, s16[528,128]{1,0:T(8,128)(2,1)S(1)}, u32[]{:S(2)}, u32[]{:S(2)}) %collective-permute-start.11) | collective-permute-done | bytes 135200 | tf_op jit(solution)/shard_map/ppermute | solution.py:290
  72.0 0.3 collective-permute-done.14.refs_7_
  72.3 1.3 %totals.1 = bf16[64,3584]{1,0:T(8,128)(2,1)} custom-call(f32[64,1024]{1,0:T(8,128)S(1)} %get-tuple-element.25.refs_0_, s16[528,128]{1,0:T(8,128)(2,1)S(1)} %collective-permute-done.10.refs_1_, f32[64,1024]{1,0:T(8,128)S(1)} %get-tuple-element.26.refs_2_, s16[528,128]{1,0:T(8,128)(2,1)S(1)} %collective-permute-done.11.refs_3_, ...), custom_call_target="tpu_custom_call" | custom-call | flops 9175040 | bytes 3211264 | tf_op jit(solution)/shard_map/totals/pallas_call | solution.py:281
  (21 shorter events, 0.5 us)
Async XLA Ops:
  0.6 10.4 %collective-permute-start = (bf16[32,4096]{1,0:T(8,128)(2,1)}, bf16[32,4096]{1,0:T(8,128)(2,1)S(1)}, u32[]{:S(2)}, u32[]{:S(2)}) collective-permute-start(bf16[32,4096]{1,0:T(8,128)(2,1)} %refs_0_.3), channel_id=1, source_target_pairs={{0,2},{1,3},{2,0},{3,1},{4,6},{5,7},{6,4},{7,5},{8,10},{9,11},{10,... | collective-permute-start | bytes 786440 | tf_op jit(solution)/shard_map/ppermute | solution.py:290
  3.6 13.6 %collective-permute-start.2 = (bf16[32,4096]{1,0:T(8,128)(2,1)}, bf16[32,4096]{1,0:T(8,128)(2,1)S(1)}, u32[]{:S(2)}, u32[]{:S(2)}) collective-permute-start(bf16[32,4096]{1,0:T(8,128)(2,1)} %refs_0_.3), channel_id=1, source_target_pairs={{0,4},{1,5},{2,6},{3,7},{4,0},{5,1},{6,2},{7,3},{8,12},{9,13},{10,... | collective-permute-start | bytes 786440 | tf_op jit(solution)/shard_map/ppermute | solution.py:290
  5.2 12.1 %collective-permute-start.1 = (bf16[32,4096]{1,0:T(8,128)(2,1)}, bf16[32,4096]{1,0:T(8,128)(2,1)S(1)}, u32[]{:S(2)}, u32[]{:S(2)}) collective-permute-start(bf16[32,4096]{1,0:T(8,128)(2,1)} %refs_0_.3), channel_id=1, source_target_pairs={{0,6},{1,7},{2,4},{3,5},{4,2},{5,3},{6,0},{7,1},{8,14},{9,15},{10,... | collective-permute-start | bytes 786440 | tf_op jit(solution)/shard_map/ppermute | solution.py:290
  5.2 22.9 %collective-permute-start.6 = (bf16[64,3584]{1,0:T(8,128)(2,1)}, bf16[64,3584]{1,0:T(8,128)(2,1)S(1)}, u32[]{:S(2)}, u32[]{:S(2)}) collective-permute-start(bf16[64,3584]{1,0:T(8,128)(2,1)} %refs_0_.5), channel_id=1, source_target_pairs={{0,16},{8,24},{16,0},{24,8},{1,17},{9,25},{17,1},{25,9},{2,18},{10... | collective-permute-start | bytes 1376264 | tf_op jit(solution)/shard_map/ppermute | solution.py:290
  8.2 20.6 %collective-permute-start.5 = (bf16[64,3584]{1,0:T(8,128)(2,1)}, bf16[64,3584]{1,0:T(8,128)(2,1)S(1)}, u32[]{:S(2)}, u32[]{:S(2)}) collective-permute-start(bf16[64,3584]{1,0:T(8,128)(2,1)} %refs_0_.5), channel_id=1, source_target_pairs={{0,8},{8,0},{16,24},{24,16},{1,9},{9,1},{17,25},{25,17},{2,10},{10... | collective-permute-start | bytes 1376264 | tf_op jit(solution)/shard_map/ppermute | solution.py:290
  11.0 1.0 %copy-start.1 = (bf16[32,4096]{1,0:T(8,128)(2,1)S(1)}, bf16[32,4096]{1,0:T(8,128)(2,1)}, u32[]{:S(2)}) copy-start(bf16[32,4096]{1,0:T(8,128)(2,1)} %refs_0_.3) | copy-start | bytes 786436
  12.0 7.3 %collective-permute-start.3 = (bf16[64,4096]{1,0:T(8,128)(2,1)S(1)}, bf16[64,4096]{1,0:T(8,128)(2,1)S(1)}, u32[]{:S(2)}, u32[]{:S(2)}) collective-permute-start(bf16[64,4096]{1,0:T(8,128)(2,1)S(1)} %stacked.2.refs_2_.refs_1_), channel_id=1, source_target_pairs={{0,1},{1,0},{2,3},{3,2},{4,5},{5,4},{6,7},{7,6},{8,9},{9,8},{10,11... | collective-permute-start | bytes 1572872 | tf_op jit(solution)/shard_map/ppermute | solution.py:290
  17.3 2.0 %collective-permute-start.4 = (bf16[64,4096]{1,0:T(8,128)(2,1)S(1)}, bf16[64,4096]{1,0:T(8,128)(2,1)S(1)}, u32[]{:S(2)}, u32[]{:S(2)}) collective-permute-start(bf16[64,4096]{1,0:T(8,128)(2,1)S(1)} %stacked.3.refs_2_), channel_id=1, source_target_pairs={{0,1},{1,0},{2,3},{3,2},{4,5},{5,4},{6,7},{7,6},{8,9},{9,8},{10,11... | collective-permute-start | bytes 1572872 | tf_op jit(solution)/shard_map/ppermute | solution.py:290
  25.2 9.3 %collective-permute-start.8 = (s16[1040,128]{1,0:T(8,128)(2,1)S(1)}, s16[1040,128]{1,0:T(8,128)(2,1)S(1)}, u32[]{:S(2)}, u32[]{:S(2)}) collective-permute-start(s16[1040,128]{1,0:T(8,128)(2,1)S(1)} %get-tuple-element.18), channel_id=1, source_target_pairs={{0,8},{8,0},{16,24},{24,16},{1,9},{9,1},{17,25},{25,17},{2,10},{10... | collective-permute-start | bytes 798728 | tf_op jit(solution)/shard_map/ppermute | solution.py:290
  28.0 20.8 %collective-permute-start.7 = (bf16[64,3584]{1,0:T(8,128)(2,1)S(1)}, bf16[64,3584]{1,0:T(8,128)(2,1)S(1)}, u32[]{:S(2)}, u32[]{:S(2)}) collective-permute-start(bf16[64,3584]{1,0:T(8,128)(2,1)S(1)} %handed_on.2.refs_2_), channel_id=1, source_target_pairs={{0,8},{8,0},{16,24},{24,16},{1,9},{9,1},{17,25},{25,17},{2,10},{10... | collective-permute-start | bytes 1376264 | tf_op jit(solution)/shard_map/ppermute | solution.py:290
  35.0 33.4 %collective-permute-start.10 = (s16[528,128]{1,0:T(8,128)(2,1)S(1)}, s16[528,128]{1,0:T(8,128)(2,1)S(1)}, u32[]{:S(2)}, u32[]{:S(2)}) collective-permute-start(s16[528,128]{1,0:T(8,128)(2,1)S(1)} %get-tuple-element.20.refs_3_), channel_id=1, source_target_pairs={{0,16},{8,24},{16,0},{24,8},{1,17},{9,25},{17,1},{25,9},{2,18},{10... | collective-permute-start | bytes 405512 | tf_op jit(solution)/shard_map/ppermute | solution.py:290
  37.8 11.1 %copy-start = (bf16[64,3584]{1,0:T(8,128)(2,1)S(1)}, bf16[64,3584]{1,0:T(8,128)(2,1)}, u32[]{:S(2)}) copy-start(bf16[64,3584]{1,0:T(8,128)(2,1)} %refs_0_.5) | copy-start | bytes 1376260
  37.8 18.5 %collective-permute-start.9 = (s16[1040,128]{1,0:T(8,128)(2,1)S(1)}, s16[1040,128]{1,0:T(8,128)(2,1)S(1)}, u32[]{:S(2)}, u32[]{:S(2)}) collective-permute-start(s16[1040,128]{1,0:T(8,128)(2,1)S(1)} %get-tuple-element.23), channel_id=1, source_target_pairs={{0,8},{8,0},{16,24},{24,16},{1,9},{9,1},{17,25},{25,17},{2,10},{10... | collective-permute-start | bytes 798728 | tf_op jit(solution)/shard_map/ppermute | solution.py:290
  46.7 21.7 %collective-permute-start.13 = (s16[784,128]{1,0:T(8,128)(2,1)S(1)}, s16[784,128]{1,0:T(8,128)(2,1)S(1)}, u32[]{:S(2)}, u32[]{:S(2)}) collective-permute-start(s16[784,128]{1,0:T(8,128)(2,1)S(1)} %get-tuple-element.28), channel_id=1, source_target_pairs={{0,24},{8,16},{16,8},{24,0},{1,25},{9,17},{17,9},{25,1},{2,26},{10... | collective-permute-start | bytes 602120 | tf_op jit(solution)/shard_map/ppermute | solution.py:290
  47.0 23.6 %collective-permute-start.12 = (s16[784,128]{1,0:T(8,128)(2,1)S(1)}, s16[784,128]{1,0:T(8,128)(2,1)S(1)}, u32[]{:S(2)}, u32[]{:S(2)}) collective-permute-start(s16[784,128]{1,0:T(8,128)(2,1)S(1)} %get-tuple-element.21.refs_4_), channel_id=1, source_target_pairs={{0,16},{8,24},{16,0},{24,8},{1,17},{9,25},{17,1},{25,9},{2,18},{10... | collective-permute-start | bytes 602120 | tf_op jit(solution)/shard_map/ppermute | solution.py:290
  56.8 15.2 %collective-permute-start.11 = (s16[528,128]{1,0:T(8,128)(2,1)S(1)}, s16[528,128]{1,0:T(8,128)(2,1)S(1)}, u32[]{:S(2)}, u32[]{:S(2)}) collective-permute-start(s16[528,128]{1,0:T(8,128)(2,1)S(1)} %get-tuple-element.24.refs_5_.refs_1_), channel_id=1, source_target_pairs={{0,16},{8,24},{16,0},{24,8},{1,17},{9,25},{17,1},{25,9},{2,18},{10... | collective-permute-start | bytes 405512 | tf_op jit(solution)/shard_map/ppermute | solution.py:290
  60.0 12.4 %collective-permute-start.14 = (s16[784,128]{1,0:T(8,128)(2,1)S(1)}, s16[784,128]{1,0:T(8,128)(2,1)S(1)}, u32[]{:S(2)}, u32[]{:S(2)}) collective-permute-start(s16[784,128]{1,0:T(8,128)(2,1)S(1)} %handed_on.3), channel_id=1, source_target_pairs={{0,8},{8,0},{16,24},{24,16},{1,9},{9,1},{17,25},{25,17},{2,10},{10... | collective-permute-start | bytes 602120 | tf_op jit(solution)/shard_map/ppermute | solution.py:290

commit v20 on v19

--- a/solution.py
+++ b/solution.py
@@ -15,7 +15,7 @@
 VMEM_LIMIT = 48 * 1024 * 1024
 SMALL_LIMIT = 8 * 1024 * 1024
 SLOTS = 4
-SHARES = (2, 2, 3)
+SHARES = (3, 2, 2)
 SUB = 256
 
 

time: 73.8 us -> 76.4 us (1.035)
  waiting for transfers between devices: 12.1 us -> 16.5 us
  starting transfers between devices: 23.7 us -> 21.8 us
    ppermute x15, waiting for transfers between devices: 12.1 us -> 16.5 us  [send(): return lax.ppermute(value, axis, [(i, i ^ flip) for i in range(size)])]
    ppermute x15, starting transfers between devices: 23.7 us -> 21.8 us  [send(): return lax.ppermute(value, axis, [(i, i ^ flip) for i in range(size)])]
  transfers between devices with their start and end apart: 15 -> 15, of which waited for: 8 -> 6; matrix products, arithmetic and copies ran while one was open for 2% -> 2% of each run, Pallas kernels for 45% -> 44%
where the time goes in v20:
time: 76.4 us; the launch traced here: 76.2 us
  Pallas kernels  34.5 us (45%)
  starting transfers between devices  21.8 us (29%)
  waiting for transfers between devices  16.5 us (22%)
  local copies, waits for them, and re-layouts  1.8 us (2%)
  other arithmetic  0.91 us (1%)
    ppermute x15, starting transfers between devices, send(): return lax.ppermute(value, axis, [(i, i ^ flip) for i in range(size)])  21.8 us
    pallas_call x3, Pallas kernels, partial_sums(): pl.pallas_call(functools.partial(sums_kernel, 0 if aligned is not None el...  18.7 us
    ppermute x15, waiting for transfers between devices, send(): return lax.ppermute(value, axis, [(i, i ^ flip) for i in range(size)])  16.5 us
    pallas_call x2, Pallas kernels, weight_grads(): pl.pallas_call(functools.partial(weight_kernel, offsets, first, len(later...  13.4 us
  transfers between devices with their start and end apart: 15, of which 6 were waited for; matrix products, arithmetic and copies ran while one was open for 2% of the time, Pallas kernels for 44%

profile of v20, /device:TPU:0, one launch (start us, length us, event | category | flops | bytes accessed | tf_op | source)
XLA Modules:
  0.0 76.2 jit_solution(3449022853156348355)
XLA Ops:
  0.6 3.0 %collective-permute-start = (bf16[32,4096]{1,0:T(8,128)(2,1)}, bf16[32,4096]{1,0:T(8,128)(2,1)S(1)}, u32[]{:S(2)}, u32[]{:S(2)}) collective-permute-start(bf16[32,4096]{1,0:T(8,128)(2,1)} %refs_0_.3), channel_id=1, source_target_pairs={{0,2},{1,3},{2,0},{3,1},{4,6},{5,7},{6,4},{7,5},{8,10},{9,11},{10,... | collective-permute-start | bytes 786440 | tf_op jit(solution)/shard_map/ppermute | solution.py:290
  3.6 1.5 %collective-permute-start.2 = (bf16[32,4096]{1,0:T(8,128)(2,1)}, bf16[32,4096]{1,0:T(8,128)(2,1)S(1)}, u32[]{:S(2)}, u32[]{:S(2)}) collective-permute-start(bf16[32,4096]{1,0:T(8,128)(2,1)} %refs_0_.3), channel_id=1, source_target_pairs={{0,4},{1,5},{2,6},{3,7},{4,0},{5,1},{6,2},{7,3},{8,12},{9,13},{10,... | collective-permute-start | bytes 786440 | tf_op jit(solution)/shard_map/ppermute | solution.py:290
  5.2 3.0 %collective-permute-start.6 = (bf16[64,3584]{1,0:T(8,128)(2,1)}, bf16[64,3584]{1,0:T(8,128)(2,1)S(1)}, u32[]{:S(2)}, u32[]{:S(2)}) collective-permute-start(bf16[64,3584]{1,0:T(8,128)(2,1)} %refs_0_.5), channel_id=1, source_target_pairs={{0,16},{8,24},{16,0},{24,8},{1,17},{9,25},{17,1},{25,9},{2,18},{10... | collective-permute-start | bytes 1376264 | tf_op jit(solution)/shard_map/ppermute | solution.py:290
  8.2 1.6 %collective-permute-start.5 = (bf16[64,3584]{1,0:T(8,128)(2,1)}, bf16[64,3584]{1,0:T(8,128)(2,1)S(1)}, u32[]{:S(2)}, u32[]{:S(2)}) collective-permute-start(bf16[64,3584]{1,0:T(8,128)(2,1)} %refs_0_.5), channel_id=1, source_target_pairs={{0,8},{8,0},{16,24},{24,16},{1,9},{9,1},{17,25},{25,17},{2,10},{10... | collective-permute-start | bytes 1376264 | tf_op jit(solution)/shard_map/ppermute | solution.py:290
  9.8 0.7 xor_multiply_fusion
  10.5 0.5 collective-permute-done.refs_1_
  11.0 0.9 %copy-done.1 = bf16[32,4096]{1,0:T(8,128)(2,1)S(1)} copy-done((bf16[32,4096]{1,0:T(8,128)(2,1)S(1)}, bf16[32,4096]{1,0:T(8,128)(2,1)}, u32[]{:S(2)}) %copy-start.1) | copy-done | bytes 262168
  12.0 5.2 %collective-permute-done.2.refs_1_ = bf16[32,4096]{1,0:T(8,128)(2,1)S(1)} collective-permute-done((bf16[32,4096]{1,0:T(8,128)(2,1)}, bf16[32,4096]{1,0:T(8,128)(2,1)S(1)}, u32[]{:S(2)}, u32[]{:S(2)}) %collective-permute-start.2) | collective-permute-done | bytes 262176 | tf_op jit(solution)/shard_map/ppermute | solution.py:290
  17.4 0.8 reshape.24
  18.2 0.1 add.40
  18.3 0.1 pad_add_fusion
  18.3 0.1 compare_convert_fusion.refs_0_
  18.5 0.8 %collective-permute-done.4.refs_4_ = bf16[64,4096]{1,0:T(8,128)(2,1)S(1)} collective-permute-done((bf16[64,4096]{1,0:T(8,128)(2,1)S(1)}, bf16[64,4096]{1,0:T(8,128)(2,1)S(1)}, u32[]{:S(2)}, u32[]{:S(2)}) %collective-permute-start.4) | collective-permute-done | bytes 524320 | tf_op jit(solution)/shard_map/ppermute | solution.py:290
  19.2 8.2 %sums_first.1 = (bf16[256,4096]{1,0:T(8,128)(2,1)S(1)}, f32[128,1536]{1,0:T(8,128)S(1)}, s16[1552,128]{1,0:T(8,128)(2,1)S(1)}) custom-call(bf16[256,256]{1,0:T(8,128)(2,1)S(1)} %compare_convert_fusion.refs_0_, bf16[64,4096]{1,0:T(8,128)(2,1)S(1)} %stacked.2.refs_2_.refs_1_, bf16[64,4096]{1,0:T(8,128)(2,1)S(1)} %stacked.3.refs_2_, ...), custom_call_target="tpu_custom_call" | custom-call | flops 3221225472 | bytes 12582912 | tf_op jit(solution)/shard_map/sums_first/pallas_call | solution.py:155
  27.4 1.6 %collective-permute-start.8 = (s16[1552,128]{1,0:T(8,128)(2,1)S(1)}, s16[1552,128]{1,0:T(8,128)(2,1)S(1)}, u32[]{:S(2)}, u32[]{:S(2)}) collective-permute-start(s16[1552,128]{1,0:T(8,128)(2,1)S(1)} %get-tuple-element.18), channel_id=1, source_target_pairs={{0,8},{8,0},{16,24},{24,16},{1,9},{9,1},{17,25},{25,17},{2,10},{10... | collective-permute-start | bytes 1191944 | tf_op jit(solution)/shard_map/ppermute | solution.py:290
  29.1 0.4 collective-permute-start.7
  29.5 5.2 %sums_second.1 = (f32[128,1024]{1,0:T(8,128)S(1)}, s16[1040,128]{1,0:T(8,128)(2,1)S(1)}) custom-call(bf16[256,4096]{1,0:T(8,128)(2,1)S(1)} %get-tuple-element.16.refs_1_.refs_0_.aligned_ref, bf16[3584,4096]{1,0:T(8,128)(2,1)} %refs_2_.3, bf16[3584,4096]{1,0:T(8,128)(2,1)} %refs_2_.3, bf16[64,3584]{1,0:T(8,128)(2,1)S(1)} %collective-permute-done.5.refs_3_.refs_1_), custom_call_target="tpu_custom_call" | custom-call | flops 2147483648 | bytes 8388608 | tf_op jit(solution)/shard_map/sums_second/pallas_call | solution.py:155
  34.8 4.8 %collective-permute-done.8.got_ref = s16[1552,128]{1,0:T(8,128)(2,1)S(1)} collective-permute-done((s16[1552,128]{1,0:T(8,128)(2,1)S(1)}, s16[1552,128]{1,0:T(8,128)(2,1)S(1)}, u32[]{:S(2)}, u32[]{:S(2)}) %collective-permute-start.8) | collective-permute-done | bytes 397344 | tf_op jit(solution)/shard_map/ppermute | solution.py:290
  39.5 0.6 fold.2
  40.2 2.6 %collective-permute-start.10 = (s16[784,128]{1,0:T(8,128)(2,1)S(1)}, s16[784,128]{1,0:T(8,128)(2,1)S(1)}, u32[]{:S(2)}, u32[]{:S(2)}) collective-permute-start(s16[784,128]{1,0:T(8,128)(2,1)S(1)} %get-tuple-element.20.refs_3_), channel_id=1, source_target_pairs={{0,16},{8,24},{16,0},{24,8},{1,17},{9,25},{17,1},{25,9},{2,18},{10... | collective-permute-start | bytes 602120 | tf_op jit(solution)/shard_map/ppermute | solution.py:290
  42.8 1.6 %collective-permute-start.9 = (s16[1040,128]{1,0:T(8,128)(2,1)S(1)}, s16[1040,128]{1,0:T(8,128)(2,1)S(1)}, u32[]{:S(2)}, u32[]{:S(2)}) collective-permute-start(s16[1040,128]{1,0:T(8,128)(2,1)S(1)} %get-tuple-element.23), channel_id=1, source_target_pairs={{0,8},{8,0},{16,24},{24,16},{1,9},{9,1},{17,25},{25,17},{2,10},{10... | collective-permute-start | bytes 798728 | tf_op jit(solution)/shard_map/ppermute | solution.py:290
  44.4 5.3 %sums_last.1 = (f32[64,1024]{1,0:T(8,128)S(1)}, s16[528,128]{1,0:T(8,128)(2,1)S(1)}, s16[528,128]{1,0:T(8,128)(2,1)S(1)}, s16[528,128]{1,0:T(8,128)(2,1)S(1)}) custom-call(bf16[256,4096]{1,0:T(8,128)(2,1)S(1)} %get-tuple-element.16.refs_1_.refs_0_.aligned_ref, bf16[3584,4096]{1,0:T(8,128)(2,1)} %refs_2_.3, bf16[3584,4096]{1,0:T(8,128)(2,1)} %refs_2_.3, ...), custom_call_target="tpu_custom_call" | custom-call | flops 2147483648 | bytes 8388608 | tf_op jit(solution)/shard_map/sums_last/pallas_call | solution.py:155
  49.7 0.3 collective-permute-start.13
  49.9 1.7 %collective-permute-start.12 = (s16[528,128]{1,0:T(8,128)(2,1)S(1)}, s16[528,128]{1,0:T(8,128)(2,1)S(1)}, u32[]{:S(2)}, u32[]{:S(2)}) collective-permute-start(s16[528,128]{1,0:T(8,128)(2,1)S(1)} %get-tuple-element.21.refs_4_), channel_id=1, source_target_pairs={{0,16},{8,24},{16,0},{24,8},{1,17},{9,25},{17,1},{25,9},{2,18},{10... | collective-permute-start | bytes 405512 | tf_op jit(solution)/shard_map/ppermute | solution.py:290
  51.6 2.0 %collective-permute-done.7.refs_3_ = bf16[64,3584]{1,0:T(8,128)(2,1)S(1)} collective-permute-done((bf16[64,3584]{1,0:T(8,128)(2,1)S(1)}, bf16[64,3584]{1,0:T(8,128)(2,1)S(1)}, u32[]{:S(2)}, u32[]{:S(2)}) %collective-permute-start.7) | collective-permute-done | bytes 458784 | tf_op jit(solution)/shard_map/ppermute | solution.py:290
  53.7 7.5 %weight_grads.2.refs_0_.refs_4_ = bf16[3584,4096]{1,0:T(8,128)(2,1)} custom-call(bf16[256,4096]{1,0:T(8,128)(2,1)S(1)} %get-tuple-element.16.refs_1_.refs_0_.aligned_ref, bf16[64,3584]{1,0:T(8,128)(2,1)S(1)} %copy-done, bf16[64,3584]{1,0:T(8,128)(2,1)S(1)} %collective-permute-done.5.refs_3_.refs_1_, bf16[64,3584]{1,0:T(8,128)(2,1)S(1)} %handed_on.2.refs_2_, ...), custom_call_target="tpu_custom_call" | custom-call | flops 4294967296 | bytes 16777216 | tf_op jit(solution)/shard_map/weight_grads/pallas_call | solution.py:206
  61.2 3.2 %collective-permute-done.9.got_ref = s16[1040,128]{1,0:T(8,128)(2,1)S(1)} collective-permute-done((s16[1040,128]{1,0:T(8,128)(2,1)S(1)}, s16[1040,128]{1,0:T(8,128)(2,1)S(1)}, u32[]{:S(2)}, u32[]{:S(2)}) %collective-permute-start.9) | collective-permute-done | bytes 266272 | tf_op jit(solution)/shard_map/ppermute | solution.py:290
  64.4 0.5 fold.3
  64.8 1.7 %collective-permute-start.11 = (s16[528,128]{1,0:T(8,128)(2,1)S(1)}, s16[528,128]{1,0:T(8,128)(2,1)S(1)}, u32[]{:S(2)}, u32[]{:S(2)}) collective-permute-start(s16[528,128]{1,0:T(8,128)(2,1)S(1)} %get-tuple-element.24.refs_5_.refs_1_), channel_id=1, source_target_pairs={{0,16},{8,24},{16,0},{24,8},{1,17},{9,25},{17,1},{25,9},{2,18},{10... | collective-permute-start | bytes 405512 | tf_op jit(solution)/shard_map/ppermute | solution.py:290
  66.5 2.5 %collective-permute-start.14 = (s16[528,128]{1,0:T(8,128)(2,1)S(1)}, s16[528,128]{1,0:T(8,128)(2,1)S(1)}, u32[]{:S(2)}, u32[]{:S(2)}) collective-permute-start(s16[528,128]{1,0:T(8,128)(2,1)S(1)} %handed_on.3), channel_id=1, source_target_pairs={{0,8},{8,0},{16,24},{24,16},{1,9},{9,1},{17,25},{25,17},{2,10},{10... | collective-permute-start | bytes 405512 | tf_op jit(solution)/shard_map/ppermute | solution.py:290
  69.0 5.9 %weight_grads.3.refs_8_ = bf16[3584,4096]{1,0:T(8,128)(2,1)} custom-call(bf16[256,4096]{1,0:T(8,128)(2,1)S(1)} %get-tuple-element.16.refs_1_.refs_0_.aligned_ref, bf16[64,3584]{1,0:T(8,128)(2,1)S(1)} %copy-done, bf16[64,3584]{1,0:T(8,128)(2,1)S(1)} %collective-permute-done.5.refs_3_.refs_1_, ...), custom_call_target="tpu_custom_call", output_to_operand_aliasing={{}: (5, {})} | custom-call | flops 3221225472 | bytes 12582912 | tf_op jit(solution)/shard_map/weight_grads/pallas_call | solution.py:206
  75.0 1.2 %totals.1 = bf16[64,3584]{1,0:T(8,128)(2,1)} custom-call(f32[64,1536]{1,0:T(8,128)S(1)} %get-tuple-element.25.refs_0_, s16[784,128]{1,0:T(8,128)(2,1)S(1)} %collective-permute-done.10.refs_1_, f32[64,1024]{1,0:T(8,128)S(1)} %get-tuple-element.26.refs_2_, s16[528,128]{1,0:T(8,128)(2,1)S(1)} %collective-permute-done.11.refs_3_, ...), custom_call_target="tpu_custom_call" | custom-call | flops 9175040 | bytes 3211264 | tf_op jit(solution)/shard_map/totals/pallas_call | solution.py:281
  (21 shorter events, 0.3 us)
Async XLA Ops:
  0.6 10.4 %collective-permute-start = (bf16[32,4096]{1,0:T(8,128)(2,1)}, bf16[32,4096]{1,0:T(8,128)(2,1)S(1)}, u32[]{:S(2)}, u32[]{:S(2)}) collective-permute-start(bf16[32,4096]{1,0:T(8,128)(2,1)} %refs_0_.3), channel_id=1, source_target_pairs={{0,2},{1,3},{2,0},{3,1},{4,6},{5,7},{6,4},{7,5},{8,10},{9,11},{10,... | collective-permute-start | bytes 786440 | tf_op jit(solution)/shard_map/ppermute | solution.py:290
  3.6 13.6 %collective-permute-start.2 = (bf16[32,4096]{1,0:T(8,128)(2,1)}, bf16[32,4096]{1,0:T(8,128)(2,1)S(1)}, u32[]{:S(2)}, u32[]{:S(2)}) collective-permute-start(bf16[32,4096]{1,0:T(8,128)(2,1)} %refs_0_.3), channel_id=1, source_target_pairs={{0,4},{1,5},{2,6},{3,7},{4,0},{5,1},{6,2},{7,3},{8,12},{9,13},{10,... | collective-permute-start | bytes 786440 | tf_op jit(solution)/shard_map/ppermute | solution.py:290
  5.2 12.1 %collective-permute-start.1 = (bf16[32,4096]{1,0:T(8,128)(2,1)}, bf16[32,4096]{1,0:T(8,128)(2,1)S(1)}, u32[]{:S(2)}, u32[]{:S(2)}) collective-permute-start(bf16[32,4096]{1,0:T(8,128)(2,1)} %refs_0_.3), channel_id=1, source_target_pairs={{0,6},{1,7},{2,4},{3,5},{4,2},{5,3},{6,0},{7,1},{8,14},{9,15},{10,... | collective-permute-start | bytes 786440 | tf_op jit(solution)/shard_map/ppermute | solution.py:290
  5.2 23.9 %collective-permute-start.6 = (bf16[64,3584]{1,0:T(8,128)(2,1)}, bf16[64,3584]{1,0:T(8,128)(2,1)S(1)}, u32[]{:S(2)}, u32[]{:S(2)}) collective-permute-start(bf16[64,3584]{1,0:T(8,128)(2,1)} %refs_0_.5), channel_id=1, source_target_pairs={{0,16},{8,24},{16,0},{24,8},{1,17},{9,25},{17,1},{25,9},{2,18},{10... | collective-permute-start | bytes 1376264 | tf_op jit(solution)/shard_map/ppermute | solution.py:290
  8.2 21.3 %collective-permute-start.5 = (bf16[64,3584]{1,0:T(8,128)(2,1)}, bf16[64,3584]{1,0:T(8,128)(2,1)S(1)}, u32[]{:S(2)}, u32[]{:S(2)}) collective-permute-start(bf16[64,3584]{1,0:T(8,128)(2,1)} %refs_0_.5), channel_id=1, source_target_pairs={{0,8},{8,0},{16,24},{24,16},{1,9},{9,1},{17,25},{25,17},{2,10},{10... | collective-permute-start | bytes 1376264 | tf_op jit(solution)/shard_map/ppermute | solution.py:290
  11.0 1.0 %copy-start.1 = (bf16[32,4096]{1,0:T(8,128)(2,1)S(1)}, bf16[32,4096]{1,0:T(8,128)(2,1)}, u32[]{:S(2)}) copy-start(bf16[32,4096]{1,0:T(8,128)(2,1)} %refs_0_.3) | copy-start | bytes 786436
  12.0 7.3 %collective-permute-start.3 = (bf16[64,4096]{1,0:T(8,128)(2,1)S(1)}, bf16[64,4096]{1,0:T(8,128)(2,1)S(1)}, u32[]{:S(2)}, u32[]{:S(2)}) collective-permute-start(bf16[64,4096]{1,0:T(8,128)(2,1)S(1)} %stacked.2.refs_2_.refs_1_), channel_id=1, source_target_pairs={{0,1},{1,0},{2,3},{3,2},{4,5},{5,4},{6,7},{7,6},{8,9},{9,8},{10,11... | collective-permute-start | bytes 1572872 | tf_op jit(solution)/shard_map/ppermute | solution.py:290
  17.3 2.0 %collective-permute-start.4 = (bf16[64,4096]{1,0:T(8,128)(2,1)S(1)}, bf16[64,4096]{1,0:T(8,128)(2,1)S(1)}, u32[]{:S(2)}, u32[]{:S(2)}) collective-permute-start(bf16[64,4096]{1,0:T(8,128)(2,1)S(1)} %stacked.3.refs_2_), channel_id=1, source_target_pairs={{0,1},{1,0},{2,3},{3,2},{4,5},{5,4},{6,7},{7,6},{8,9},{9,8},{10,11... | collective-permute-start | bytes 1572872 | tf_op jit(solution)/shard_map/ppermute | solution.py:290
  27.4 12.1 %collective-permute-start.8 = (s16[1552,128]{1,0:T(8,128)(2,1)S(1)}, s16[1552,128]{1,0:T(8,128)(2,1)S(1)}, u32[]{:S(2)}, u32[]{:S(2)}) collective-permute-start(s16[1552,128]{1,0:T(8,128)(2,1)S(1)} %get-tuple-element.18), channel_id=1, source_target_pairs={{0,8},{8,0},{16,24},{24,16},{1,9},{9,1},{17,25},{25,17},{2,10},{10... | collective-permute-start | bytes 1191944 | tf_op jit(solution)/shard_map/ppermute | solution.py:290
  29.1 24.6 %collective-permute-start.7 = (bf16[64,3584]{1,0:T(8,128)(2,1)S(1)}, bf16[64,3584]{1,0:T(8,128)(2,1)S(1)}, u32[]{:S(2)}, u32[]{:S(2)}) collective-permute-start(bf16[64,3584]{1,0:T(8,128)(2,1)S(1)} %handed_on.2.refs_2_), channel_id=1, source_target_pairs={{0,8},{8,0},{16,24},{24,16},{1,9},{9,1},{17,25},{25,17},{2,10},{10... | collective-permute-start | bytes 1376264 | tf_op jit(solution)/shard_map/ppermute | solution.py:290
  40.2 34.8 %collective-permute-start.10 = (s16[784,128]{1,0:T(8,128)(2,1)S(1)}, s16[784,128]{1,0:T(8,128)(2,1)S(1)}, u32[]{:S(2)}, u32[]{:S(2)}) collective-permute-start(s16[784,128]{1,0:T(8,128)(2,1)S(1)} %get-tuple-element.20.refs_3_), channel_id=1, source_target_pairs={{0,16},{8,24},{16,0},{24,8},{1,17},{9,25},{17,1},{25,9},{2,18},{10... | collective-permute-start | bytes 602120 | tf_op jit(solution)/shard_map/ppermute | solution.py:290
  42.8 10.9 %copy-start = (bf16[64,3584]{1,0:T(8,128)(2,1)S(1)}, bf16[64,3584]{1,0:T(8,128)(2,1)}, u32[]{:S(2)}) copy-start(bf16[64,3584]{1,0:T(8,128)(2,1)} %refs_0_.5) | copy-start | bytes 1376260
  42.8 21.6 %collective-permute-start.9 = (s16[1040,128]{1,0:T(8,128)(2,1)S(1)}, s16[1040,128]{1,0:T(8,128)(2,1)S(1)}, u32[]{:S(2)}, u32[]{:S(2)}) collective-permute-start(s16[1040,128]{1,0:T(8,128)(2,1)S(1)} %get-tuple-element.23), channel_id=1, source_target_pairs={{0,8},{8,0},{16,24},{24,16},{1,9},{9,1},{17,25},{25,17},{2,10},{10... | collective-permute-start | bytes 798728 | tf_op jit(solution)/shard_map/ppermute | solution.py:290
  49.7 25.3 %collective-permute-start.13 = (s16[528,128]{1,0:T(8,128)(2,1)S(1)}, s16[528,128]{1,0:T(8,128)(2,1)S(1)}, u32[]{:S(2)}, u32[]{:S(2)}) collective-permute-start(s16[528,128]{1,0:T(8,128)(2,1)S(1)} %get-tuple-element.28), channel_id=1, source_target_pairs={{0,24},{8,16},{16,8},{24,0},{1,25},{9,17},{17,9},{25,1},{2,26},{10... | collective-permute-start | bytes 405512 | tf_op jit(solution)/shard_map/ppermute | solution.py:290
  49.9 25.0 %collective-permute-start.12 = (s16[528,128]{1,0:T(8,128)(2,1)S(1)}, s16[528,128]{1,0:T(8,128)(2,1)S(1)}, u32[]{:S(2)}, u32[]{:S(2)}) collective-permute-start(s16[528,128]{1,0:T(8,128)(2,1)S(1)} %get-tuple-element.21.refs_4_), channel_id=1, source_target_pairs={{0,16},{8,24},{16,0},{24,8},{1,17},{9,25},{17,1},{25,9},{2,18},{10... | collective-permute-start | bytes 405512 | tf_op jit(solution)/shard_map/ppermute | solution.py:290
  64.8 10.2 %collective-permute-start.11 = (s16[528,128]{1,0:T(8,128)(2,1)S(1)}, s16[528,128]{1,0:T(8,128)(2,1)S(1)}, u32[]{:S(2)}, u32[]{:S(2)}) collective-permute-start(s16[528,128]{1,0:T(8,128)(2,1)S(1)} %get-tuple-element.24.refs_5_.refs_1_), channel_id=1, source_target_pairs={{0,16},{8,24},{16,0},{24,8},{1,17},{9,25},{17,1},{25,9},{2,18},{10... | collective-permute-start | bytes 405512 | tf_op jit(solution)/shard_map/ppermute | solution.py:290
  66.5 8.5 %collective-permute-start.14 = (s16[528,128]{1,0:T(8,128)(2,1)S(1)}, s16[528,128]{1,0:T(8,128)(2,1)S(1)}, u32[]{:S(2)}, u32[]{:S(2)}) collective-permute-start(s16[528,128]{1,0:T(8,128)(2,1)S(1)} %handed_on.3), channel_id=1, source_target_pairs={{0,8},{8,0},{16,24},{24,16},{1,9},{9,1},{17,25},{25,17},{2,10},{10... | collective-permute-start | bytes 405512 | tf_op jit(solution)/shard_map/ppermute | solution.py:290
